TPU v7x, 32 devices: a whole 2x2x4 slice. The times are simulated.
32 devices in a mesh: row: 4 (over z), col: 8 (over y, x, core).
Axes of the slice: x: 2, y: 2, z: 4, core: 2. Of those that a mesh axis runs over, the one named last changes fastest.
Arguments:
- counts: int32 [8192, 16384], P('row', 'col'), may hold values from 0 to 512
- block_mask: int32 [32, 64], P('row', 'col'), may hold values from 0 to 1
- row_perm: int32 [8192], P('row'), may hold values from 0 to 8191, as said below
- col_perm: int32 [16384], P('col'), may hold values from 0 to 16383, as said below
- row_logm: float32 [8192], P('row'), may hold values from 0 to 3
- col_logm: float32 [16384], P('col'), may hold values from 0 to 3
- row_emb: bfloat16 [8192, 512], P(('row', 'col')), may hold values from -1.1953125 to 1.1953125
- col_emb: bfloat16 [16384, 512], P(('col', 'row')), may hold values from -1.1953125 to 1.1953125
Outputs:
- row_grad: float32 [8192, 512], P(('row', 'col'))
- col_grad: float32 [16384, 512], P(('col', 'row'))
Inputs may be any that keep to these rules, and one draw needn't show every extreme that they name: `row_perm`: each aligned block of 2048 entries is a permutation of that block's own index range. `col_perm`: each aligned block of 2048 entries is a permutation of that block's own index range.
All inputs are finite; a program needn't handle non-finite values.
Results may differ from a plain program's by a relative error of at most 0.0022.
Values may be sent and summed in bfloat16 or wider, within the bound.
No kernel may reach another device: no remote copies, remote signals or barrier semaphores. Data moves between devices by JAX's collectives and lax.ppermute only.
A program may use at most 128 MiB of HBM per device.

v0:
```python
import functools

import jax
import jax.numpy as jnp
import numpy as np
from jax import lax
from jax.experimental import pallas as pl
from jax.experimental.pallas import tpu as pltpu
from jax.sharding import PartitionSpec as P

F32 = jnp.float32
BF16 = jnp.bfloat16
LANES = 128
MIB = 1 << 20


def cell_delta(score, count, active, row_part, col_part):
    real_count = count.astype(F32)
    safe = jnp.maximum(real_count, 1.0)
    pmi = jnp.log(safe) - row_part[:, None] - col_part[None, :]
    confid = 0.1 + 0.25 * jnp.sqrt(safe)
    positive = confid * (score - pmi)
    zeroed = jax.nn.sigmoid(score - pmi)
    deriv = jnp.where(count > 0, positive, zeroed)
    return (active.astype(F32) * deriv).astype(BF16)


def plain_shards(counts, block_mask, row_perm, col_perm, row_logm, col_logm, row_emb, col_emb):
    shard_rows, shard_cols = counts.shape
    all_cols = shard_cols * lax.axis_size("col")
    all_rows = shard_rows * lax.axis_size("row")
    block_side = shard_rows // block_mask.shape[0]
    row_group = lax.all_gather(row_emb, "col", axis=0, tiled=True)
    col_group = lax.all_gather(col_emb, "row", axis=0, tiled=True)
    row_local = row_perm - lax.axis_index("row") * shard_rows
    col_local = col_perm - lax.axis_index("col") * shard_cols
    wvec = jnp.take(row_group, row_local, axis=0)
    cvec = jnp.take(col_group, col_local, axis=0)
    score = lax.dot_general(wvec, cvec, (((1,), (1,)), ((), ())), preferred_element_type=F32)
    active = jnp.repeat(jnp.repeat(block_mask, block_side, axis=0), block_side, axis=1)
    delta = cell_delta(score, counts, active, row_logm, col_logm)
    gshard = jnp.dot(delta, cvec, preferred_element_type=F32) / jnp.sqrt(F32(all_cols))
    ordered = jnp.zeros(gshard.shape, F32).at[row_local].set(gshard)
    row_grad = lax.psum_scatter(ordered, "col", scatter_dimension=0, tiled=True)
    hshard = lax.dot_general(
        delta, wvec, (((0,), (0,)), ((), ())), preferred_element_type=F32
    ) / jnp.sqrt(F32(all_rows))
    col_ordered = jnp.zeros(hshard.shape, F32).at[col_local].set(hshard)
    col_grad = lax.psum_scatter(col_ordered, "row", scatter_dimension=0, tiled=True)
    return (row_grad, col_grad)


ROW_AT, COL_AT = 0, 1

WHOLE = pl.BlockSpec(memory_space=pltpu.VMEM)
SCALARS = pl.BlockSpec(memory_space=pltpu.SMEM)


def params(mib):
    return pltpu.CompilerParams(vmem_limit_bytes=mib * MIB)


def cost(flops, moved):
    return pl.CostEstimate(flops=flops, bytes_accessed=moved, transcendentals=0)


def onehot(flag):
    return jnp.where(flag, 1.0, 0.0).astype(BF16)


def pieces_of(value):
    high = value.astype(BF16)
    rest = value - high.astype(F32)
    middle = rest.astype(BF16)
    low = (rest - middle.astype(F32)).astype(BF16)
    return high, middle, low


def along_sublanes(value):
    fill = jnp.zeros((LANES - value.shape[0], LANES), F32)
    return jnp.concatenate([value, fill], axis=0).T


def copies(pairs, sems):
    made = [pltpu.make_async_copy(src, dst, sems.at[at]) for at, (src, dst) in enumerate(pairs)]
    for copy in made:
        copy.start()
    return made


def fill_pick(pick, columns, base, groups):
    vocab = (lax.broadcasted_iota(jnp.int32, (LANES, pick.shape[1]), 1) + base).astype(F32)
    for group in groups:
        pick[pl.ds(group * LANES, LANES), :] = onehot(columns[:, group : group + 1] == vocab)


def chunk_base(scalars, offset, width):
    return jnp.bitwise_xor(scalars[ROW_AT], offset) * width


def move_values(values, pick, aux_ref):
    moved = jnp.dot(values, pick[...], preferred_element_type=F32)
    rows = values.shape[0] - 24
    aux_ref[pl.ds(0, rows), :] = moved[:rows]
    aux_ref[pl.ds(rows, 8), :] = moved[rows : rows + 8] + moved[rows + 8 : rows + 16] + moved[rows + 16 :]


def order_first_kernel(offsets, scalars, perm_hbm, mask_hbm, logm_hbm, count_hbm, *refs):
    parts = len(offsets)
    outs, auxes, refs = refs[:parts], refs[parts : 2 * parts], refs[2 * parts :]
    shifted_ref, columns_ref, values_ref, perm, mask_ref, logm_ref, tiles, pick, sems, tile_sems = refs
    depth = pick.shape[1]
    width = pick.shape[2]
    rows = outs[0].shape[0]
    step = tiles.shape[1]
    steps = rows // step

    slots = tiles.shape[0]

    def tile_copy(at):
        slot = lax.rem(at, slots)
        return pltpu.make_async_copy(
            count_hbm.at[pl.ds(pl.multiple_of(at * step, step), step)], tiles.at[slot], tile_sems.at[slot]
        )

    small = copies([(perm_hbm, perm), (mask_hbm, mask_ref), (logm_hbm, logm_ref)], sems)
    for at in range(slots):
        tile_copy(at).start()
    for copy in small:
        copy.wait()
    columns = along_sublanes((perm[...] - scalars[COL_AT] * depth).astype(F32))
    columns_ref[...] = columns
    blocks_r, blocks_c = mask_ref.shape
    mask = mask_ref[...].astype(F32)
    side = (blocks_r, depth // blocks_c)
    active = jnp.concatenate(
        [jnp.broadcast_to(mask[:, at : at + 1], side) for at in range(blocks_c)], axis=1
    )
    logm = jnp.broadcast_to(logm_ref[...], (8, depth))
    values = jnp.concatenate([active, *[piece.astype(F32) for piece in pieces_of(logm)]], axis=0)
    values_ref[...] = values
    values = values.astype(BF16)
    for part, offset in enumerate(offsets):
        fill_pick(pick.at[part], columns, chunk_base(scalars, offset, width), range(depth // LANES))
        move_values(values, pick.at[part], auxes[part])

    @pl.loop(0, steps)
    def _(at):
        here = pl.ds(pl.multiple_of(at * step, step), step)
        tile_copy(at).wait()
        shifted = (tiles[lax.rem(at, slots)] - 256).astype(F32).astype(BF16)
        shifted_ref[here, :] = shifted

        @pl.when(at + slots < steps)
        def _():
            tile_copy(at + slots).start()

        for part in range(parts):
            moved = jnp.dot(shifted, pick[part], preferred_element_type=F32)
            outs[part][here, :] = moved.astype(BF16)


def in_hbm(value):
    return pltpu.with_memory_space_constraint(value, pltpu.HBM)


def order_first(scalars, col_perm, block_mask, col_logm, counts, offsets, width):
    rows, cols = counts.shape
    parts = len(offsets)
    blocks = block_mask.shape[0]
    outside = pl.BlockSpec(memory_space=pltpu.HBM)
    step = 512
    return pl.pallas_call(
        functools.partial(order_first_kernel, offsets),
        in_specs=[SCALARS] + [outside] * 4,
        out_specs=[WHOLE] * (2 * parts + 3),
        out_shape=[jax.ShapeDtypeStruct((rows, width), BF16)] * parts
        + [jax.ShapeDtypeStruct((blocks + 8, width), F32)] * parts
        + [
            jax.ShapeDtypeStruct((rows, cols), BF16),
            jax.ShapeDtypeStruct((LANES, LANES), F32),
            jax.ShapeDtypeStruct((blocks + 24, cols), F32),
        ],
        scratch_shapes=[
            pltpu.VMEM((cols // LANES, LANES), jnp.int32),
            pltpu.VMEM(block_mask.shape, jnp.int32),
            pltpu.VMEM((1, cols), F32),
            pltpu.VMEM((2, step, cols), jnp.int32),
            pltpu.VMEM((parts, cols, width), BF16),
            pltpu.SemaphoreType.DMA((3,)),
            pltpu.SemaphoreType.DMA((2,)),
        ],
        compiler_params=params(28),
        cost_estimate=cost(2 * parts * rows * cols * width, 4 * rows * cols),
        name="order_first",
    )(scalars, *[in_hbm(each) for each in (col_perm.reshape(-1, LANES), block_mask, col_logm[None, :], counts)])


def order_next_kernel(offsets, scalars, shifted_ref, columns_ref, values_ref, *refs):
    parts = len(offsets)
    outs, auxes, pick = refs[:parts], refs[parts : 2 * parts], refs[-1]
    depth, width = pick.shape[1:]
    values = values_ref[...].astype(BF16)
    for part, offset in enumerate(offsets):
        base = chunk_base(scalars, offset, width)
        fill_pick(pick.at[part], columns_ref[...], base, range(depth // LANES))
        move_values(values, pick.at[part], auxes[part])
    step = 512

    @pl.loop(0, shifted_ref.shape[0] // step)
    def _(at):
        here = pl.ds(pl.multiple_of(at * step, step), step)
        for part in range(parts):
            moved = jnp.dot(shifted_ref[here, :], pick[part], preferred_element_type=F32)
            outs[part][here, :] = moved.astype(BF16)


def order_next(scalars, shifted, columns, values, offsets, width):
    rows, cols = shifted.shape
    parts = len(offsets)
    return pl.pallas_call(
        functools.partial(order_next_kernel, offsets),
        in_specs=[SCALARS] + [WHOLE] * 3,
        out_specs=[WHOLE] * (2 * parts),
        out_shape=[jax.ShapeDtypeStruct((rows, width), BF16)] * parts
        + [jax.ShapeDtypeStruct((values.shape[0] - 16, width), F32)] * parts,
        scratch_shapes=[pltpu.VMEM((parts, cols, width), BF16)],
        compiler_params=params(24),
        cost_estimate=cost(rows * width, rows * width),
        name="order_next",
    )(scalars, shifted, columns, values)


def take_kernel(scalars, perm_ref, logm_ref, *refs):
    own, from_x, from_y, from_xy, from_core, out_ref, turned_ref, logm_out, group, pick = refs
    side = own.shape[0]
    mine = [own, from_x, from_y, from_xy]
    blocks = [(2 * at, mine[at]) for at in range(4)] + [(2 * at + 1, from_core.at[at]) for at in range(4)]
    for offset, block in blocks:
        first = pl.multiple_of(jnp.bitwise_xor(scalars[COL_AT], offset) * side, side)
        group[pl.ds(first, side), :] = block[...]
    rows = out_ref.shape[0]
    depth = group.shape[0]
    groups = rows // LANES
    index = (perm_ref[...] - scalars[ROW_AT] * rows).astype(F32)
    columns = along_sublanes(jnp.concatenate([index, logm_ref[...]], axis=0))
    step = pick.shape[1]
    vocab = lax.broadcasted_iota(jnp.int32, (LANES, depth), 1).astype(F32)
    for first in range(0, rows, step):
        slot = (first // step) % pick.shape[0]
        for inner in range(0, step, LANES):
            at = (first + inner) // LANES
            pick[slot, pl.ds(inner, LANES), :] = onehot(columns[:, at : at + 1] == vocab)
            logm_out[pl.ds(first + inner, LANES), :] = jnp.broadcast_to(
                columns[:, groups + at : groups + at + 1], (LANES, LANES)
            )
        taken = jnp.dot(pick[slot], group[...], preferred_element_type=F32).astype(BF16)
        out_ref[pl.ds(first, step), :] = taken
        turned_ref[:, pl.ds(first, step)] = taken.T


def take_rows(scalars, row_perm, row_logm, blocks):
    rows = row_perm.shape[0]
    side, width = blocks[0].shape
    return pl.pallas_call(
        take_kernel,
        in_specs=[SCALARS] + [WHOLE] * 7,
        out_specs=[WHOLE] * 3,
        out_shape=[
            jax.ShapeDtypeStruct((rows, width), BF16),
            jax.ShapeDtypeStruct((width, rows), BF16),
            jax.ShapeDtypeStruct((rows, LANES), F32),
        ],
        scratch_shapes=[pltpu.VMEM((8 * side, width), BF16), pltpu.VMEM((2, 512, 8 * side), BF16)],
        compiler_params=params(24),
        cost_estimate=cost(2 * rows * rows * width, 4 * rows * width),
        name="take_rows",
    )(scalars, row_perm.reshape(-1, LANES), row_logm.reshape(-1, LANES), *blocks)


def cells_kernel(has_sum, chunk, wvec_ref, turned_ref, count_ref, aux_ref, logm_ref, *refs):
    if has_sum:
        before_ref, refs = refs[0], refs[1:]
    grad_ref, term_ref, sent_ref, chunk_turned, delta_ref, sum_ref = refs
    chunk_turned[...] = chunk[...].T
    rows = wvec_ref.shape[0]
    width = chunk.shape[0]
    blocks = aux_ref.shape[0] - 8
    tile = rows // blocks
    col_logm = aux_ref[blocks : blocks + 1, :]

    def rows_at(at, count=1):
        return pl.ds(pl.multiple_of(at * tile, tile), count * tile)

    def score_of(at):
        return jnp.dot(wvec_ref[rows_at(at), :], chunk_turned[...], preferred_element_type=F32)

    def delta_of(at, score):
        here = rows_at(at)
        count = count_ref[here, :].astype(F32) + 256.0
        safe = jnp.maximum(count, 1.0)
        row_logm = jnp.concatenate([logm_ref[here, :]] * (width // LANES), axis=1)
        gap = score + ((row_logm + col_logm) - jnp.log(safe))
        confid = 0.1 + 0.25 * (safe * lax.rsqrt(safe))
        zeroed = 0.5 * jnp.tanh(0.5 * gap) + 0.5
        deriv = jnp.where(count > 0.0, confid * gap, zeroed)
        delta_ref[here, :] = (deriv * aux_ref[pl.ds(at, 1), :]).astype(BF16)

    def grad_of(at):
        here = rows_at(at)
        grad = jnp.dot(delta_ref[here, :], chunk[...], preferred_element_type=F32)
        if has_sum:
            grad = grad + before_ref[here, :]
        grad_ref[here, :] = grad

    def term_of(at, count):
        here = rows_at(at, count)
        sum_ref[...] += jnp.dot(turned_ref[:, here], delta_ref[here, :], preferred_element_type=F32)

    joined = 4
    sum_ref[...] = jnp.zeros_like(sum_ref)

    @pl.loop(0, blocks // joined)
    def _(group):
        first = group * joined
        ahead = score_of(first)
        for at in range(joined):
            score = ahead
            if at + 1 < joined:
                ahead = score_of(first + at + 1)
            delta_of(first + at, score)
            if at:
                grad_of(first + at - 1)
            if at == joined // 2:
                term_of(first, joined // 2)
        grad_of(first + joined - 1)
        term_of(first + joined // 2, joined // 2)

    total = sum_ref[...].T
    term_ref[...] = total
    sent_ref[...] = total.astype(BF16)


def cells(chunk, wvec, turned, ordered, aux, logm, before):
    rows, depth = wvec.shape
    width = chunk.shape[0]
    args = [chunk, wvec, turned, ordered, aux, logm]
    aliases = {}
    if before is not None:
        aliases = {len(args): 0}
        args.append(before)
    return pl.pallas_call(
        functools.partial(cells_kernel, before is not None),
        in_specs=[WHOLE] * len(args),
        out_specs=[WHOLE] * 3,
        out_shape=[
            jax.ShapeDtypeStruct((rows, depth), F32),
            jax.ShapeDtypeStruct((width, depth), F32),
            jax.ShapeDtypeStruct((width, depth), BF16),
        ],
        scratch_shapes=[
            pltpu.VMEM((depth, width), BF16),
            pltpu.VMEM((rows, width), BF16),
            pltpu.VMEM((depth, width), F32),
        ],
        input_output_aliases=aliases,
        compiler_params=params(24),
        cost_estimate=cost(rows * width * depth, rows * depth),
        name="cells",
    )(*args)


def put_kernel(offsets, exact, scalars, perm_ref, grad_ref, out_ref):
    grad = grad_ref[...]
    rows, width = grad.shape
    high = grad.astype(BF16)
    moving = high
    if exact:
        moving = jnp.concatenate([high, (grad - high.astype(F32)).astype(BF16)], axis=1)
    side = out_ref.shape[1]
    index = jnp.broadcast_to((perm_ref[...] - scalars[ROW_AT] * rows).astype(F32), (8, rows))[:1]
    vocab = lax.broadcasted_iota(jnp.int32, (side, rows), 0)
    for at, offset in enumerate(offsets):
        base = jnp.bitwise_xor(scalars[COL_AT], offset) * side
        pick = onehot(index == (vocab + base).astype(F32))
        moved = jnp.dot(pick, moving, preferred_element_type=F32)
        if exact:
            moved = moved[:, :width] + moved[:, width:]
        out_ref[at] = moved.astype(out_ref.dtype)


def put_rows(scalars, row_perm, grad, offsets, side, exact):
    width = grad.shape[1]
    return pl.pallas_call(
        functools.partial(put_kernel, offsets, exact),
        in_specs=[SCALARS, WHOLE, WHOLE],
        out_specs=WHOLE,
        out_shape=jax.ShapeDtypeStruct((len(offsets), side, width), F32 if exact else BF16),
        compiler_params=params(24),
        cost_estimate=cost((4096 if exact else 1) * grad.size, grad.size),
        name="put_rows",
    )(scalars, row_perm[None, :], grad)


def swap(value, axis, bit):
    pairs = [(at, at ^ bit) for at in range(lax.axis_size(axis))]
    return lax.ppermute(value, axis, pairs)


def together(values):
    return lax.optimization_barrier(values)


def line_shards(counts, block_mask, row_perm, col_perm, row_logm, col_logm, row_emb, col_emb):
    shard_rows, shard_cols = counts.shape
    side = row_emb.shape[0]
    width = col_emb.shape[0]
    scalars = jnp.stack([lax.axis_index("row"), lax.axis_index("col")]).astype(jnp.int32)

    cross = swap(col_emb, "row", 2)
    near = swap(col_emb, "row", 1)
    count_far, aux_far, shifted, columns, values = order_first(
        scalars, col_perm, block_mask, col_logm, counts, (3,), width
    )
    ordered = functools.partial(order_next, scalars)
    row_block, shifted = together((row_emb, shifted))
    from_x = swap(row_block, "col", 2)
    from_y = swap(row_block, "col", 4)
    from_xy = swap(row_block, "col", 6)
    count_cross, count_near, aux_cross, aux_near = ordered(shifted, columns, values, (2, 1), width)
    cross, near, from_x, from_y, from_xy, count_near, shifted = together(
        (cross, near, from_x, from_y, from_xy, count_near, shifted)
    )
    far = swap(cross, "row", 1)
    from_core = swap(jnp.stack([row_emb, from_x, from_y, from_xy]), "col", 1)
    count_own, aux_own = ordered(shifted, columns, values, (0,), width)
    count_own, near = together((count_own, near))
    blocks = [row_emb, from_x, from_y, from_xy, from_core]
    wvec, turned, logm = take_rows(scalars, row_perm, row_logm, blocks)

    grad, term_near, sent_near = cells(near, wvec, turned, count_near, aux_near, logm, None)
    grad, far = together((grad, far))
    grad, _, sent_far = cells(far, wvec, turned, count_far, aux_far, logm, grad)
    got_far = swap(sent_far, "row", 1)
    grad, term_cross, _ = cells(cross, wvec, turned, count_cross, aux_cross, logm, grad)
    got_near = swap(sent_near, "row", 1)
    grad, got_near = together((grad, got_near))
    grad, term_own, _ = cells(col_emb, wvec, turned, count_own, aux_own, logm, grad)

    grad, got_far = together((grad, got_far))
    sum_cross = (term_cross + got_far.astype(F32)).astype(BF16)
    got_cross = swap(sum_cross, "row", 2)
    grad, sum_cross = together((grad, sum_cross))
    away = put_rows(scalars, row_perm, grad, (1, 3, 5, 7), side, False)
    core = swap(away, "col", 1)
    grad, away = together((grad, away))
    home = put_rows(scalars, row_perm, grad, (0, 2, 4, 6), side, True)
    both = home + core.astype(F32)
    got_x = swap(both[1].astype(BF16), "col", 2)
    got_y = swap(both[2].astype(BF16), "col", 4)
    got_xy = swap(both[3].astype(BF16), "col", 6)
    row_sum = both[0] + got_x.astype(F32) + got_y.astype(F32) + got_xy.astype(F32)
    col_sum = term_own + got_near.astype(F32) + got_cross.astype(F32)
    row_scale = np.float32(1.0 / np.sqrt(shard_cols * 8))
    col_scale = np.float32(1.0 / np.sqrt(shard_rows * 4))
    return (row_sum * row_scale, col_sum * col_scale)


def solution(mesh):
    in_specs = (
        P("row", "col"),
        P("row", "col"),
        P("row"),
        P("col"),
        P("row"),
        P("col"),
        P(("row", "col"), None),
        P(("col", "row"), None),
    )
    out_specs = (P(("row", "col"), None), P(("col", "row"), None))
    line = mesh.shape["row"] == 4 and mesh.shape["col"] == 8
    body = line_shards if line else plain_shards
    return jax.shard_map(body, mesh=mesh, in_specs=in_specs, out_specs=out_specs, check_vma=False)
```

profile of v0, /device:TPU:0, one launch (start us, length us, event | category | flops | bytes accessed | tf_op | source)
XLA Modules:
  0.0 108.1 jit_solution(6418015210458087193)
XLA Ops:
  0.6 4.1 %collective-permute-start = (bf16[512,512]{1,0:T(8,128)(2,1)}, bf16[512,512]{1,0:T(8,128)(2,1)S(1)}, u32[]{:S(2)}, u32[]{:S(2)}) collective-permute-start(bf16[512,512]{1,0:T(8,128)(2,1)} %chunk.1), channel_id=1, source_target_pairs={{0,16},{8,24},{16,0},{24,8},{1,17},{9,25},{17,1},{25,9},{2,18},{10... | collective-permute-start | bytes 1572872 | tf_op jit(solution)/shard_map/ppermute | solution.py:407
  4.7 1.6 %collective-permute-start.1 = (bf16[512,512]{1,0:T(8,128)(2,1)}, bf16[512,512]{1,0:T(8,128)(2,1)S(1)}, u32[]{:S(2)}, u32[]{:S(2)}) collective-permute-start(bf16[512,512]{1,0:T(8,128)(2,1)} %chunk.1), channel_id=1, source_target_pairs={{0,8},{8,0},{16,24},{24,16},{1,9},{9,1},{17,25},{25,17},{2,10},{10... | collective-permute-start | bytes 1572872 | tf_op jit(solution)/shard_map/ppermute | solution.py:407
  6.3 0.1 pad_add_fusion.scalars
  6.4 0.0 copy-start.1
  6.4 9.5 %order_first.1 = (bf16[2048,512]{1,0:T(8,128)(2,1)S(1)}, f32[16,512]{1,0:T(8,128)S(1)}, bf16[2048,2048]{1,0:T(8,128)(2,1)S(1)}, f32[128,128]{1,0:T(8,128)S(1)}, f32[32,2048]{1,0:T(8,128)S(1)}) custom-call(s32[2]{0:T(128)S(1)} %pad_add_fusion.scalars, s32[16,128]{1,0:T(8,128)} %bitcast.35, s32[8,8]{1,0:T(8,128)} %mask_hbm.1, f32[1,2048]{1,0:T(1,128)} %bitcast.36, ...), custom_call_target="tpu_custom_call" | custom-call | flops 4294967296 | bytes 16777216 | tf_op jit(solution)/shard_map/order_first/pallas_call | solution.py:173
  15.9 0.0 copy-done.1
  15.9 2.5 %collective-permute-start.4 = (bf16[256,512]{1,0:T(8,128)(2,1)S(1)}, bf16[256,512]{1,0:T(8,128)(2,1)S(1)}, u32[]{:S(2)}, u32[]{:S(2)}) collective-permute-start(bf16[256,512]{1,0:T(8,128)(2,1)S(1)} %copy-done.1), channel_id=1, source_target_pairs={{0,6},{1,7},{2,4},{3,5},{4,2},{5,3},{6,0},{7,1},{8,14},{9,15},{10,... | collective-permute-start | bytes 786440 | tf_op jit(solution)/shard_map/ppermute | solution.py:407
  18.4 0.5 collective-permute-start.3
  18.9 0.5 collective-permute-start.2
  19.4 11.2 %order_next.2 = (bf16[2048,512]{1,0:T(8,128)(2,1)S(1)}, bf16[2048,512]{1,0:T(8,128)(2,1)S(1)}, f32[16,512]{1,0:T(8,128)S(1)}, f32[16,512]{1,0:T(8,128)S(1)}) custom-call(s32[2]{0:T(128)S(1)} %pad_add_fusion.scalars, bf16[2048,2048]{1,0:T(8,128)(2,1)S(1)} %get-tuple-element.54.shifted_ref, f32[128,128]{1,0:T(8,128)S(1)} %get-tuple-element.46.columns_ref, ...), custom_call_target="tpu_custom_call" | custom-call | flops 1048576 | bytes 1048576 | tf_op jit(solution)/shard_map/order_next/pallas_call | solution.py:221
  30.6 0.0 collective-permute-done.4.refs_3_
  30.6 0.0 collective-permute-done.3.refs_2_
  30.6 0.0 collective-permute-done.2.refs_1_
  30.6 0.0 collective-permute-done.chunk
  30.6 0.0 collective-permute-done.1.chunk
  30.7 0.1 pad_maximum_fusion
  30.8 0.0 copy-start.2
  30.8 0.0 copy-start.3
  30.8 0.1 collective-permute-start.5
  30.9 0.5 collective-permute-start.6
  31.4 6.2 %order_next.3 = (bf16[2048,512]{1,0:T(8,128)(2,1)S(1)}, f32[16,512]{1,0:T(8,128)S(1)}) custom-call(s32[2]{0:T(128)S(1)} %pad_add_fusion.scalars, bf16[2048,2048]{1,0:T(8,128)(2,1)S(1)} %get-tuple-element.54.shifted_ref, f32[128,128]{1,0:T(8,128)S(1)} %get-tuple-element.46.columns_ref, f32[32,2048]{1,0:T(8,128)S(1)} %get-tuple-element.47.values_ref), custom_call_target="tpu_custom_call" | custom-call | flops 1048576 | bytes 1048576 | tf_op jit(solution)/shard_map/order_next/pallas_call | solution.py:221
  37.7 0.0 collective-permute-done.5.refs_4_
  37.7 0.0 copy-done.2
  37.7 0.0 copy-done.3
  37.7 5.3 %take_rows.1 = (bf16[2048,512]{1,0:T(8,128)(2,1)S(1)}, bf16[512,2048]{1,0:T(8,128)(2,1)S(1)}, f32[2048,128]{1,0:T(8,128)S(1)}) custom-call(s32[2]{0:T(128)S(1)} %pad_add_fusion.scalars, s32[16,128]{1,0:T(8,128)S(1)} %bitcast.31, f32[16,128]{1,0:T(8,128)S(1)} %bitcast.34, bf16[256,512]{1,0:T(8,128)(2,1)S(1)} %copy-done.1, ...), custom_call_target="tpu_custom_call" | custom-call | flops 4294967296 | bytes 4194304 | tf_op jit(solution)/shard_map/take_rows/pallas_call | solution.py:265
  43.0 7.8 %cells.4 = (f32[2048,512]{1,0:T(8,128)S(1)}, f32[512,512]{1,0:T(8,128)}, bf16[512,512]{1,0:T(8,128)(2,1)S(1)}) custom-call(bf16[512,512]{1,0:T(8,128)(2,1)S(1)} %collective-permute-done.1.chunk, bf16[2048,512]{1,0:T(8,128)(2,1)S(1)} %get-tuple-element.52.wvec_ref, bf16[512,2048]{1,0:T(8,128)(2,1)S(1)} %get-tuple-element.53.turned_ref, ...), custom_call_target="tpu_custom_call" | custom-call | flops 536870912 | bytes 1048576 | tf_op jit(solution)/shard_map/cells/pallas_call | solution.py:352
  50.8 1.6 %collective-permute-start.7 = (bf16[512,512]{1,0:T(8,128)(2,1)S(1)}, bf16[512,512]{1,0:T(8,128)(2,1)S(1)}, u32[]{:S(2)}, u32[]{:S(2)}) collective-permute-start(bf16[512,512]{1,0:T(8,128)(2,1)S(1)} %get-tuple-element.73), channel_id=1, source_target_pairs={{0,8},{8,0},{16,24},{24,16},{1,9},{9,1},{17,25},{25,17},{2,10},{10... | collective-permute-start | bytes 1572872 | tf_op jit(solution)/shard_map/ppermute | solution.py:407
  52.4 0.0 collective-permute-done.6.chunk
  52.4 8.0 %cells.5 = (f32[2048,512]{1,0:T(8,128)S(1)}, f32[512,512]{1,0:T(8,128)}, bf16[512,512]{1,0:T(8,128)(2,1)S(1)}) custom-call(bf16[512,512]{1,0:T(8,128)(2,1)S(1)} %collective-permute-done.6.chunk, bf16[2048,512]{1,0:T(8,128)(2,1)S(1)} %get-tuple-element.52.wvec_ref, ...), custom_call_target="tpu_custom_call", output_to_operand_aliasing={{0}: (6, {})} | custom-call | flops 536870912 | bytes 1048576 | tf_op jit(solution)/shard_map/cells/pallas_call | solution.py:352
  60.4 0.4 collective-permute-start.8
  60.8 0.0 copy-start
  60.8 7.7 %cells.6 = (f32[2048,512]{1,0:T(8,128)S(1)}, f32[512,512]{1,0:T(8,128)S(1)}, bf16[512,512]{1,0:T(8,128)(2,1)}) custom-call(bf16[512,512]{1,0:T(8,128)(2,1)S(1)} %collective-permute-done.chunk, bf16[2048,512]{1,0:T(8,128)(2,1)S(1)} %get-tuple-element.52.wvec_ref, bf16[512,2048]{1,0:T(8,128)(2,1)S(1)} %get-tuple-element.53.turned_ref, ...), custom_call_target="tpu_custom_call", output_to_operand_aliasing={{0}: (6, {})} | custom-call | flops 536870912 | bytes 1048576 | tf_op jit(solution)/shard_map/cells/pallas_call | solution.py:352
  68.5 0.0 collective-permute-done.7
  68.5 0.0 copy-done
  68.5 7.9 %cells.7 = (f32[2048,512]{1,0:T(8,128)S(1)}, f32[512,512]{1,0:T(8,128)S(1)}, bf16[512,512]{1,0:T(8,128)(2,1)}) custom-call(bf16[512,512]{1,0:T(8,128)(2,1)S(1)} %copy-done, bf16[2048,512]{1,0:T(8,128)(2,1)S(1)} %get-tuple-element.52.wvec_ref, bf16[512,2048]{1,0:T(8,128)(2,1)S(1)} %get-tuple-element.53.turned_ref, ...), custom_call_target="tpu_custom_call", output_to_operand_aliasing={{0}: (6, {})} | custom-call | flops 536870912 | bytes 1048576 | tf_op jit(solution)/shard_map/cells/pallas_call | solution.py:352
  76.4 0.0 collective-permute-done.8
  76.4 0.2 add_convert_fusion
  76.5 2.9 %put_rows.2 = bf16[4,256,512]{2,1,0:T(8,128)(2,1)S(1)} custom-call(s32[2]{0:T(128)S(1)} %pad_add_fusion.scalars, s32[1,2048]{1,0:T(1,128)S(1)} %bitcast.32, f32[2048,512]{1,0:T(8,128)S(1)} %get-tuple-element.81.grad_ref), custom_call_target="tpu_custom_call" | custom-call | flops 1048576 | bytes 1048576 | tf_op jit(solution)/shard_map/put_rows/pallas_call | solution.py:394
  79.4 0.1 collective-permute-start.9
  79.5 1.2 %collective-permute-start.13 = (bf16[512,512]{1,0:T(8,128)(2,1)S(1)}, bf16[512,512]{1,0:T(8,128)(2,1)S(1)}, u32[]{:S(2)}, u32[]{:S(2)}) collective-permute-start(bf16[512,512]{1,0:T(8,128)(2,1)S(1)} %add_convert_fusion), channel_id=1, source_target_pairs={{0,16},{8,24},{16,0},{24,8},{1,17},{9,25},{17,1},{25,9},{2,18},{10... | collective-permute-start | bytes 1572872 | tf_op jit(solution)/shard_map/ppermute | solution.py:407
  80.6 5.0 %put_rows.3 = f32[4,256,512]{2,1,0:T(8,128)S(1)} custom-call(s32[2]{0:T(128)S(1)} %pad_add_fusion.scalars, s32[1,2048]{1,0:T(1,128)S(1)} %bitcast.33, f32[2048,512]{1,0:T(8,128)S(1)} %get-tuple-element.81.grad_ref), custom_call_target="tpu_custom_call" | custom-call | flops 4294967296 | bytes 1048576 | tf_op jit(solution)/shard_map/put_rows/pallas_call | solution.py:394
  85.7 0.0 collective-permute-done.9
  85.7 0.4 fusion.4
  86.1 0.1 slice_bitcast_fusion.3
  86.2 1.6 %collective-permute-start.10 = (bf16[256,512]{1,0:T(8,128)(2,1)S(1)}, bf16[256,512]{1,0:T(8,128)(2,1)S(1)}, u32[]{:S(2)}, u32[]{:S(2)}) collective-permute-start(bf16[256,512]{1,0:T(8,128)(2,1)S(1)} %get-tuple-element.86), channel_id=1, source_target_pairs={{0,2},{1,3},{2,0},{3,1},{4,6},{5,7},{6,4},{7,5},{8,10},{9,11},{10,... | collective-permute-start | bytes 786440 | tf_op jit(solution)/shard_map/ppermute | solution.py:407
  87.8 1.5 %collective-permute-start.12 = (bf16[256,512]{1,0:T(8,128)(2,1)S(1)}, bf16[256,512]{1,0:T(8,128)(2,1)S(1)}, u32[]{:S(2)}, u32[]{:S(2)}) collective-permute-start(bf16[256,512]{1,0:T(8,128)(2,1)S(1)} %get-tuple-element.87), channel_id=1, source_target_pairs={{0,6},{1,7},{2,4},{3,5},{4,2},{5,3},{6,0},{7,1},{8,14},{9,15},{10,... | collective-permute-start | bytes 786440 | tf_op jit(solution)/shard_map/ppermute | solution.py:407
  89.3 0.5 collective-permute-start.11
  89.8 16.2 %collective-permute-done.13 = bf16[512,512]{1,0:T(8,128)(2,1)S(1)} collective-permute-done((bf16[512,512]{1,0:T(8,128)(2,1)S(1)}, bf16[512,512]{1,0:T(8,128)(2,1)S(1)}, u32[]{:S(2)}, u32[]{:S(2)}) %collective-permute-start.13) | collective-permute-done | bytes 524320 | tf_op jit(solution)/shard_map/ppermute | solution.py:407
  106.0 1.2 %add_multiply_fusion = f32[512,512]{1,0:T(8,128)} fusion(bf16[512,512]{1,0:T(8,128)(2,1)S(1)} %collective-permute-done.13, f32[512,512]{1,0:T(8,128)S(1)} %get-tuple-element.82, bf16[512,512]{1,0:T(8,128)(2,1)S(1)} %collective-permute-done.7), kind=kLoop, calls=%fused_computation.2 | loop fusion | flops 1310720 | bytes 3145728 | tf_op jit(solution)/shard_map/mul | solution.py:466
  107.2 0.0 collective-permute-done.10
  107.2 0.0 collective-permute-done.12
  107.2 0.0 collective-permute-done.11
  107.2 0.9 fusion.3
Async XLA Ops:
  0.6 30.0 %collective-permute-start = (bf16[512,512]{1,0:T(8,128)(2,1)}, bf16[512,512]{1,0:T(8,128)(2,1)S(1)}, u32[]{:S(2)}, u32[]{:S(2)}) collective-permute-start(bf16[512,512]{1,0:T(8,128)(2,1)} %chunk.1), channel_id=1, source_target_pairs={{0,16},{8,24},{16,0},{24,8},{1,17},{9,25},{17,1},{25,9},{2,18},{10... | collective-permute-start | bytes 1572872 | tf_op jit(solution)/shard_map/ppermute | solution.py:407
  4.7 25.9 %collective-permute-start.1 = (bf16[512,512]{1,0:T(8,128)(2,1)}, bf16[512,512]{1,0:T(8,128)(2,1)S(1)}, u32[]{:S(2)}, u32[]{:S(2)}) collective-permute-start(bf16[512,512]{1,0:T(8,128)(2,1)} %chunk.1), channel_id=1, source_target_pairs={{0,8},{8,0},{16,24},{24,16},{1,9},{9,1},{17,25},{25,17},{2,10},{10... | collective-permute-start | bytes 1572872 | tf_op jit(solution)/shard_map/ppermute | solution.py:407
  6.4 9.5 %copy-start.1 = (bf16[256,512]{1,0:T(8,128)(2,1)S(1)}, bf16[256,512]{1,0:T(8,128)(2,1)}, u32[]{:S(2)}) copy-start(bf16[256,512]{1,0:T(8,128)(2,1)} %refs_0_.1) | copy-start | bytes 786436
  15.9 14.7 %collective-permute-start.4 = (bf16[256,512]{1,0:T(8,128)(2,1)S(1)}, bf16[256,512]{1,0:T(8,128)(2,1)S(1)}, u32[]{:S(2)}, u32[]{:S(2)}) collective-permute-start(bf16[256,512]{1,0:T(8,128)(2,1)S(1)} %copy-done.1), channel_id=1, source_target_pairs={{0,6},{1,7},{2,4},{3,5},{4,2},{5,3},{6,0},{7,1},{8,14},{9,15},{10,... | collective-permute-start | bytes 786440 | tf_op jit(solution)/shard_map/ppermute | solution.py:407
  18.4 12.2 %collective-permute-start.3 = (bf16[256,512]{1,0:T(8,128)(2,1)S(1)}, bf16[256,512]{1,0:T(8,128)(2,1)S(1)}, u32[]{:S(2)}, u32[]{:S(2)}) collective-permute-start(bf16[256,512]{1,0:T(8,128)(2,1)S(1)} %copy-done.1), channel_id=1, source_target_pairs={{0,4},{1,5},{2,6},{3,7},{4,0},{5,1},{6,2},{7,3},{8,12},{9,13},{10,... | collective-permute-start | bytes 786440 | tf_op jit(solution)/shard_map/ppermute | solution.py:407
  18.9 11.7 %collective-permute-start.2 = (bf16[256,512]{1,0:T(8,128)(2,1)S(1)}, bf16[256,512]{1,0:T(8,128)(2,1)S(1)}, u32[]{:S(2)}, u32[]{:S(2)}) collective-permute-start(bf16[256,512]{1,0:T(8,128)(2,1)S(1)} %copy-done.1), channel_id=1, source_target_pairs={{0,2},{1,3},{2,0},{3,1},{4,6},{5,7},{6,4},{7,5},{8,10},{9,11},{10,... | collective-permute-start | bytes 786440 | tf_op jit(solution)/shard_map/ppermute | solution.py:407
  30.8 6.9 %copy-start.2 = (s32[2048]{0:T(1024)S(1)}, s32[2048]{0:T(1024)}, u32[]{:S(2)}) copy-start(s32[2048]{0:T(1024)} %param.10) | copy-start | bytes 24580
  30.8 6.9 %copy-start.3 = (f32[2048]{0:T(1024)S(1)}, f32[2048]{0:T(1024)}, u32[]{:S(2)}) copy-start(f32[2048]{0:T(1024)} %param.12) | copy-start | bytes 24580
  30.8 6.9 %collective-permute-start.5 = (bf16[4,256,512]{2,1,0:T(8,128)(2,1)S(1)}, bf16[4,256,512]{2,1,0:T(8,128)(2,1)S(1)}, u32[]{:S(2)}, u32[]{:S(2)}) collective-permute-start(bf16[4,256,512]{2,1,0:T(8,128)(2,1)S(1)} %pad_maximum_fusion), channel_id=1, source_target_pairs={{0,1},{1,0},{2,3},{3,2},{4,5},{5,4},{6,7},{7,6},{8,9},{9,8},{10,11... | collective-permute-start | bytes 3145736 | tf_op jit(solution)/shard_map/ppermute | solution.py:407
  30.9 21.5 %collective-permute-start.6 = (bf16[512,512]{1,0:T(8,128)(2,1)S(1)}, bf16[512,512]{1,0:T(8,128)(2,1)S(1)}, u32[]{:S(2)}, u32[]{:S(2)}) collective-permute-start(bf16[512,512]{1,0:T(8,128)(2,1)S(1)} %collective-permute-done.chunk), channel_id=1, source_target_pairs={{0,8},{8,0},{16,24},{24,16},{1,9},{9,1},{17,25},{25,17},{2,10},{10... | collective-permute-start | bytes 1572872 | tf_op jit(solution)/shard_map/ppermute | solution.py:407
  50.8 17.7 %collective-permute-start.7 = (bf16[512,512]{1,0:T(8,128)(2,1)S(1)}, bf16[512,512]{1,0:T(8,128)(2,1)S(1)}, u32[]{:S(2)}, u32[]{:S(2)}) collective-permute-start(bf16[512,512]{1,0:T(8,128)(2,1)S(1)} %get-tuple-element.73), channel_id=1, source_target_pairs={{0,8},{8,0},{16,24},{24,16},{1,9},{9,1},{17,25},{25,17},{2,10},{10... | collective-permute-start | bytes 1572872 | tf_op jit(solution)/shard_map/ppermute | solution.py:407
  60.4 16.0 %collective-permute-start.8 = (bf16[512,512]{1,0:T(8,128)(2,1)S(1)}, bf16[512,512]{1,0:T(8,128)(2,1)S(1)}, u32[]{:S(2)}, u32[]{:S(2)}) collective-permute-start(bf16[512,512]{1,0:T(8,128)(2,1)S(1)} %get-tuple-element.76), channel_id=1, source_target_pairs={{0,8},{8,0},{16,24},{24,16},{1,9},{9,1},{17,25},{25,17},{2,10},{10... | collective-permute-start | bytes 1572872 | tf_op jit(solution)/shard_map/ppermute | solution.py:407
  60.8 7.7 %copy-start = (bf16[512,512]{1,0:T(8,128)(2,1)S(1)}, bf16[512,512]{1,0:T(8,128)(2,1)}, u32[]{:S(2)}) copy-start(bf16[512,512]{1,0:T(8,128)(2,1)} %chunk.1) | copy-start | bytes 1572868
  79.4 6.3 %collective-permute-start.9 = (bf16[4,256,512]{2,1,0:T(8,128)(2,1)S(1)}, bf16[4,256,512]{2,1,0:T(8,128)(2,1)S(1)}, u32[]{:S(2)}, u32[]{:S(2)}) collective-permute-start(bf16[4,256,512]{2,1,0:T(8,128)(2,1)S(1)} %put_rows.2), channel_id=1, source_target_pairs={{0,1},{1,0},{2,3},{3,2},{4,5},{5,4},{6,7},{7,6},{8,9},{9,8},{10,11... | collective-permute-start | bytes 3145736 | tf_op jit(solution)/shard_map/ppermute | solution.py:407
  79.5 26.5 %collective-permute-start.13 = (bf16[512,512]{1,0:T(8,128)(2,1)S(1)}, bf16[512,512]{1,0:T(8,128)(2,1)S(1)}, u32[]{:S(2)}, u32[]{:S(2)}) collective-permute-start(bf16[512,512]{1,0:T(8,128)(2,1)S(1)} %add_convert_fusion), channel_id=1, source_target_pairs={{0,16},{8,24},{16,0},{24,8},{1,17},{9,25},{17,1},{25,9},{2,18},{10... | collective-permute-start | bytes 1572872 | tf_op jit(solution)/shard_map/ppermute | solution.py:407
  86.2 21.0 %collective-permute-start.10 = (bf16[256,512]{1,0:T(8,128)(2,1)S(1)}, bf16[256,512]{1,0:T(8,128)(2,1)S(1)}, u32[]{:S(2)}, u32[]{:S(2)}) collective-permute-start(bf16[256,512]{1,0:T(8,128)(2,1)S(1)} %get-tuple-element.86), channel_id=1, source_target_pairs={{0,2},{1,3},{2,0},{3,1},{4,6},{5,7},{6,4},{7,5},{8,10},{9,11},{10,... | collective-permute-start | bytes 786440 | tf_op jit(solution)/shard_map/ppermute | solution.py:407
  87.8 19.4 %collective-permute-start.12 = (bf16[256,512]{1,0:T(8,128)(2,1)S(1)}, bf16[256,512]{1,0:T(8,128)(2,1)S(1)}, u32[]{:S(2)}, u32[]{:S(2)}) collective-permute-start(bf16[256,512]{1,0:T(8,128)(2,1)S(1)} %get-tuple-element.87), channel_id=1, source_target_pairs={{0,6},{1,7},{2,4},{3,5},{4,2},{5,3},{6,0},{7,1},{8,14},{9,15},{10,... | collective-permute-start | bytes 786440 | tf_op jit(solution)/shard_map/ppermute | solution.py:407
  89.3 17.9 %collective-permute-start.11 = (bf16[256,512]{1,0:T(8,128)(2,1)S(1)}, bf16[256,512]{1,0:T(8,128)(2,1)S(1)}, u32[]{:S(2)}, u32[]{:S(2)}) collective-permute-start(bf16[256,512]{1,0:T(8,128)(2,1)S(1)} %get-tuple-element.88), channel_id=1, source_target_pairs={{0,4},{1,5},{2,6},{3,7},{4,0},{5,1},{6,2},{7,3},{8,12},{9,13},{10,... | collective-permute-start | bytes 786440 | tf_op jit(solution)/shard_map/ppermute | solution.py:407
where the time goes:
time: 108 us
  Pallas kernels  71.4 us (66%)
  starting transfers between devices  16.6 us (15%)
  waiting for transfers between devices  16.2 us (15%)
  other arithmetic  2.96 us (3%)
    pallas_call x4, Pallas kernels, cells(): pl.pallas_call(functools.partial(cells_kernel, before is not None), in_sp...  31.3 us
    pallas_call x2, Pallas kernels, order_next(): pl.pallas_call(functools.partial(order_next_kernel, offsets), in_specs=[S...  17.4 us
    ppermute x14, starting transfers between devices, swap(): return lax.ppermute(value, axis, pairs)  16.6 us
    ppermute x14, waiting for transfers between devices, swap(): return lax.ppermute(value, axis, pairs)  16.2 us
    pallas_call x1, Pallas kernels, order_first(): pl.pallas_call(functools.partial(order_first_kernel, offsets), in_specs=[...  9.47 us
    pallas_call x2, Pallas kernels, put_rows(): pl.pallas_call(functools.partial(put_kernel, offsets, exact), in_specs=[S...  7.92 us
    pallas_call x1, Pallas kernels, take_rows(): pl.pallas_call(take_kernel, in_specs=[SCALARS] + [WHOLE] * 7, out_specs=[...  5.32 us
    mul x2, other arithmetic, line_shards(): return (row_sum * row_scale, col_sum * col_scale)  2.17 us
  transfers between devices with their start and end apart: 14, of which 1 were waited for; matrix products, arithmetic and copies ran while one was open for 2% of the time, Pallas kernels for 63%

commit v1 on v0

--- a/solution.py
+++ b/solution.py
@@ -278,70 +278,75 @@
     )(scalars, row_perm.reshape(-1, LANES), row_logm.reshape(-1, LANES), *blocks)
 
 
-def cells_kernel(has_sum, chunk, wvec_ref, turned_ref, count_ref, aux_ref, logm_ref, *refs):
+def cells_kernel(has_sum, pieces, chunk, wvec_ref, turned_ref, count_ref, aux_ref, logm_ref, *refs):
     if has_sum:
         before_ref, refs = refs[0], refs[1:]
-    grad_ref, term_ref, sent_ref, chunk_turned, delta_ref, sum_ref = refs
+    grad_ref, term_ref, sent_refs = refs[0], refs[1], refs[2 : 2 + pieces]
+    chunk_turned, delta_ref, sum_ref = refs[2 + pieces :]
     chunk_turned[...] = chunk[...].T
     rows = wvec_ref.shape[0]
     width = chunk.shape[0]
     blocks = aux_ref.shape[0] - 8
     tile = rows // blocks
+    joined = delta_ref.shape[0] // tile
+    half = joined // 2
     col_logm = aux_ref[blocks : blocks + 1, :]
-
-    def rows_at(at, count=1):
-        return pl.ds(pl.multiple_of(at * tile, tile), count * tile)
-
-    def score_of(at):
-        return jnp.dot(wvec_ref[rows_at(at), :], chunk_turned[...], preferred_element_type=F32)
-
-    def delta_of(at, score):
-        here = rows_at(at)
-        count = count_ref[here, :].astype(F32) + 256.0
-        safe = jnp.maximum(count, 1.0)
-        row_logm = jnp.concatenate([logm_ref[here, :]] * (width // LANES), axis=1)
-        gap = score + ((row_logm + col_logm) - jnp.log(safe))
-        confid = 0.1 + 0.25 * (safe * lax.rsqrt(safe))
-        zeroed = 0.5 * jnp.tanh(0.5 * gap) + 0.5
-        deriv = jnp.where(count > 0.0, confid * gap, zeroed)
-        delta_ref[here, :] = (deriv * aux_ref[pl.ds(at, 1), :]).astype(BF16)
-
-    def grad_of(at):
-        here = rows_at(at)
-        grad = jnp.dot(delta_ref[here, :], chunk[...], preferred_element_type=F32)
-        if has_sum:
-            grad = grad + before_ref[here, :]
-        grad_ref[here, :] = grad
-
-    def term_of(at, count):
-        here = rows_at(at, count)
-        sum_ref[...] += jnp.dot(turned_ref[:, here], delta_ref[here, :], preferred_element_type=F32)
-
-    joined = 4
     sum_ref[...] = jnp.zeros_like(sum_ref)
 
     @pl.loop(0, blocks // joined)
     def _(group):
-        first = group * joined
-        ahead = score_of(first)
+        def rows_at(at, count=1):
+            return pl.ds(pl.multiple_of((group * joined + at) * tile, tile), count * tile)
+
+        def held(at, count=1):
+            return delta_ref[pl.ds(at * tile, count * tile), :]
+
+        def score_of(at):
+            return jnp.dot(wvec_ref[rows_at(at), :], chunk_turned[...], preferred_element_type=F32)
+
+        def delta_of(at, score):
+            here = rows_at(at)
+            count = count_ref[here, :].astype(F32) + 256.0
+            log = jnp.log(jnp.maximum(count, 1.0))
+            row_logm = jnp.concatenate([logm_ref[here, :]] * (width // LANES), axis=1)
+            gap = score + ((row_logm + col_logm) - log)
+            confid = 0.1 + 0.25 * jnp.exp2(log * np.float32(0.5 / np.log(2.0)))
+            zeroed = 0.5 * jnp.tanh(0.5 * gap) + 0.5
+            deriv = jnp.where(count > 0.0, confid * gap, zeroed)
+            active = aux_ref[pl.ds(group * joined + at, 1), :]
+            delta_ref[pl.ds(at * tile, tile), :] = (deriv * active).astype(BF16)
+
+        def grad_of(at):
+            grad = jnp.dot(held(at), chunk[...], preferred_element_type=F32)
+            if has_sum:
+                grad = grad + before_ref[rows_at(at), :]
+            grad_ref[rows_at(at), :] = grad
+
+        def term_of(at):
+            turned = turned_ref[:, rows_at(at, half)]
+            sum_ref[...] += jnp.dot(turned, held(at, half), preferred_element_type=F32)
+
+        ahead = score_of(0)
         for at in range(joined):
             score = ahead
             if at + 1 < joined:
-                ahead = score_of(first + at + 1)
-            delta_of(first + at, score)
+                ahead = score_of(at + 1)
+            delta_of(at, score)
             if at:
-                grad_of(first + at - 1)
-            if at == joined // 2:
-                term_of(first, joined // 2)
-        grad_of(first + joined - 1)
-        term_of(first + joined // 2, joined // 2)
+                grad_of(at - 1)
+            if at == half:
+                term_of(0)
+        grad_of(joined - 1)
+        term_of(half)
 
     total = sum_ref[...].T
     term_ref[...] = total
-    sent_ref[...] = total.astype(BF16)
-
-
-def cells(chunk, wvec, turned, ordered, aux, logm, before):
+    for at, sent_ref in enumerate(sent_refs):
+        size = sent_ref.shape[0]
+        sent_ref[...] = total[at * size : (at + 1) * size].astype(BF16)
+
+
+def cells(chunk, wvec, turned, ordered, aux, logm, before, pieces):
     rows, depth = wvec.shape
     width = chunk.shape[0]
     args = [chunk, wvec, turned, ordered, aux, logm]
@@ -350,22 +355,22 @@
         aliases = {len(args): 0}
         args.append(before)
     return pl.pallas_call(
-        functools.partial(cells_kernel, before is not None),
+        functools.partial(cells_kernel, before is not None, pieces),
         in_specs=[WHOLE] * len(args),
-        out_specs=[WHOLE] * 3,
+        out_specs=[WHOLE] * (2 + pieces),
         out_shape=[
             jax.ShapeDtypeStruct((rows, depth), F32),
             jax.ShapeDtypeStruct((width, depth), F32),
-            jax.ShapeDtypeStruct((width, depth), BF16),
-        ],
+        ]
+        + [jax.ShapeDtypeStruct((width // pieces, depth), BF16) for _ in range(pieces)],
         scratch_shapes=[
             pltpu.VMEM((depth, width), BF16),
-            pltpu.VMEM((rows, width), BF16),
+            pltpu.VMEM((rows // 2, width), BF16),
             pltpu.VMEM((depth, width), F32),
         ],
         input_output_aliases=aliases,
         compiler_params=params(24),
-        cost_estimate=cost(rows * width * depth, rows * depth),
+        cost_estimate=cost(rows * width, rows * depth),
         name="cells",
     )(*args)
 
@@ -434,23 +439,27 @@
     far = swap(cross, "row", 1)
     from_core = swap(jnp.stack([row_emb, from_x, from_y, from_xy]), "col", 1)
     count_own, aux_own = ordered(shifted, columns, values, (0,), width)
-    count_own, near = together((count_own, near))
+    count_own, row_perm = together((count_own, row_perm))
     blocks = [row_emb, from_x, from_y, from_xy, from_core]
     wvec, turned, logm = take_rows(scalars, row_perm, row_logm, blocks)
 
-    grad, term_near, sent_near = cells(near, wvec, turned, count_near, aux_near, logm, None)
-    grad, far = together((grad, far))
-    grad, _, sent_far = cells(far, wvec, turned, count_far, aux_far, logm, grad)
-    got_far = swap(sent_far, "row", 1)
-    grad, term_cross, _ = cells(cross, wvec, turned, count_cross, aux_cross, logm, grad)
+    grad, _, sent_0, sent_1 = cells(far, wvec, turned, count_far, aux_far, logm, None, 2)
+    far_0 = swap(sent_0, "row", 1)
+    far_1 = swap(sent_1, "row", 1)
+    grad, term_cross = cells(cross, wvec, turned, count_cross, aux_cross, logm, grad, 0)
+    grad, far_0 = together((grad, far_0))
+
+    half = width // 2
+    sum_0 = (term_cross[:half] + far_0.astype(F32)).astype(BF16)
+    cross_0 = swap(sum_0, "row", 2)
+    grad, sum_0 = together((grad, sum_0))
+    grad, _, sent_near = cells(near, wvec, turned, count_near, aux_near, logm, grad, 1)
     got_near = swap(sent_near, "row", 1)
-    grad, got_near = together((grad, got_near))
-    grad, term_own, _ = cells(col_emb, wvec, turned, count_own, aux_own, logm, grad)
-
-    grad, got_far = together((grad, got_far))
-    sum_cross = (term_cross + got_far.astype(F32)).astype(BF16)
-    got_cross = swap(sum_cross, "row", 2)
-    grad, sum_cross = together((grad, sum_cross))
+    grad, term_own = cells(col_emb, wvec, turned, count_own, aux_own, logm, grad, 0)
+    grad, far_1, cross_0 = together((grad, far_1, cross_0))
+    sum_1 = (term_cross[half:] + far_1.astype(F32)).astype(BF16)
+    cross_1 = swap(sum_1, "row", 2)
+    grad, sum_1 = together((grad, sum_1))
     away = put_rows(scalars, row_perm, grad, (1, 3, 5, 7), side, False)
     core = swap(away, "col", 1)
     grad, away = together((grad, away))
@@ -460,7 +469,8 @@
     got_y = swap(both[2].astype(BF16), "col", 4)
     got_xy = swap(both[3].astype(BF16), "col", 6)
     row_sum = both[0] + got_x.astype(F32) + got_y.astype(F32) + got_xy.astype(F32)
-    col_sum = term_own + got_near.astype(F32) + got_cross.astype(F32)
+    got_cross = jnp.concatenate([cross_0, cross_1]).astype(F32)
+    col_sum = term_own + got_near.astype(F32) + got_cross
     row_scale = np.float32(1.0 / np.sqrt(shard_cols * 8))
     col_scale = np.float32(1.0 / np.sqrt(shard_rows * 4))
     return (row_sum * row_scale, col_sum * col_scale)

time: 108 us -> 104 us (0.963)
  Pallas kernels: 71.4 us -> 66.4 us
  starting transfers between devices: 16.6 us -> 19 us
  waiting for transfers between devices: 16.2 us -> 14.6 us
    pallas_call x4, Pallas kernels: 31.3 us -> 26.3 us  [cells(): pl.pallas_call(functools.partial(cells_kernel, before is not None, pieces...]
    ppermute x14 -> x16, starting transfers between devices: 16.6 us -> 19 us  [swap(): return lax.ppermute(value, axis, pairs)]
    ppermute x14 -> x16, waiting for transfers between devices: 16.2 us -> 14.6 us  [swap(): return lax.ppermute(value, axis, pairs)]
  transfers between devices with their start and end apart: 14 -> 16, of which waited for: 1 -> 6; matrix products, arithmetic and copies ran while one was open for 2% -> 2% of each run, Pallas kernels for 63% -> 55%
where the time goes in v1:
time: 104 us
  Pallas kernels  66.4 us (64%)
  starting transfers between devices  19 us (18%)
  waiting for transfers between devices  14.6 us (14%)
  other arithmetic  2.92 us (3%)
    pallas_call x4, Pallas kernels, cells(): pl.pallas_call(functools.partial(cells_kernel, before is not None, pieces...  26.3 us
    ppermute x16, starting transfers between devices, swap(): return lax.ppermute(value, axis, pairs)  19 us
    pallas_call x2, Pallas kernels, order_next(): pl.pallas_call(functools.partial(order_next_kernel, offsets), in_specs=[S...  17.4 us
    ppermute x16, waiting for transfers between devices, swap(): return lax.ppermute(value, axis, pairs)  14.6 us
    pallas_call x1, Pallas kernels, order_first(): pl.pallas_call(functools.partial(order_first_kernel, offsets), in_specs=[...  9.47 us
    pallas_call x2, Pallas kernels, put_rows(): pl.pallas_call(functools.partial(put_kernel, offsets, exact), in_specs=[S...  7.91 us
    pallas_call x1, Pallas kernels, take_rows(): pl.pallas_call(take_kernel, in_specs=[SCALARS] + [WHOLE] * 7, out_specs=[...  5.32 us
    mul x2, other arithmetic, line_shards(): return (row_sum * row_scale, col_sum * col_scale)  2.15 us
  transfers between devices with their start and end apart: 16, of which 6 were waited for; matrix products, arithmetic and copies ran while one was open for 2% of the time, Pallas kernels for 55%

profile of v1, /device:TPU:0, one launch (start us, length us, event | category | flops | bytes accessed | tf_op | source)
XLA Modules:
  0.0 103.8 jit_solution(10567906342805815589)
XLA Ops:
  0.6 4.1 %collective-permute-start = (bf16[512,512]{1,0:T(8,128)(2,1)}, bf16[512,512]{1,0:T(8,128)(2,1)S(1)}, u32[]{:S(2)}, u32[]{:S(2)}) collective-permute-start(bf16[512,512]{1,0:T(8,128)(2,1)} %chunk.1), channel_id=1, source_target_pairs={{0,16},{8,24},{16,0},{24,8},{1,17},{9,25},{17,1},{25,9},{2,18},{10... | collective-permute-start | bytes 1572872 | tf_op jit(solution)/shard_map/ppermute | solution.py:412
  4.7 1.6 %collective-permute-start.1 = (bf16[512,512]{1,0:T(8,128)(2,1)}, bf16[512,512]{1,0:T(8,128)(2,1)S(1)}, u32[]{:S(2)}, u32[]{:S(2)}) collective-permute-start(bf16[512,512]{1,0:T(8,128)(2,1)} %chunk.1), channel_id=1, source_target_pairs={{0,8},{8,0},{16,24},{24,16},{1,9},{9,1},{17,25},{25,17},{2,10},{10... | collective-permute-start | bytes 1572872 | tf_op jit(solution)/shard_map/ppermute | solution.py:412
  6.3 0.1 pad_add_fusion.scalars
  6.4 0.0 copy-start.1
  6.4 9.5 %order_first.1 = (bf16[2048,512]{1,0:T(8,128)(2,1)S(1)}, f32[16,512]{1,0:T(8,128)S(1)}, bf16[2048,2048]{1,0:T(8,128)(2,1)S(1)}, f32[128,128]{1,0:T(8,128)S(1)}, f32[32,2048]{1,0:T(8,128)S(1)}) custom-call(s32[2]{0:T(128)S(1)} %pad_add_fusion.scalars, s32[16,128]{1,0:T(8,128)} %bitcast.35, s32[8,8]{1,0:T(8,128)} %mask_hbm.1, f32[1,2048]{1,0:T(1,128)} %bitcast.36, ...), custom_call_target="tpu_custom_call" | custom-call | flops 4294967296 | bytes 16777216 | tf_op jit(solution)/shard_map/order_first/pallas_call | solution.py:173
  15.9 0.0 copy-done.1
  15.9 2.5 %collective-permute-start.4 = (bf16[256,512]{1,0:T(8,128)(2,1)S(1)}, bf16[256,512]{1,0:T(8,128)(2,1)S(1)}, u32[]{:S(2)}, u32[]{:S(2)}) collective-permute-start(bf16[256,512]{1,0:T(8,128)(2,1)S(1)} %copy-done.1), channel_id=1, source_target_pairs={{0,6},{1,7},{2,4},{3,5},{4,2},{5,3},{6,0},{7,1},{8,14},{9,15},{10,... | collective-permute-start | bytes 786440 | tf_op jit(solution)/shard_map/ppermute | solution.py:412
  18.4 0.5 collective-permute-start.3
  18.9 0.5 collective-permute-start.2
  19.4 11.2 %order_next.2 = (bf16[2048,512]{1,0:T(8,128)(2,1)S(1)}, bf16[2048,512]{1,0:T(8,128)(2,1)S(1)}, f32[16,512]{1,0:T(8,128)S(1)}, f32[16,512]{1,0:T(8,128)S(1)}) custom-call(s32[2]{0:T(128)S(1)} %pad_add_fusion.scalars, bf16[2048,2048]{1,0:T(8,128)(2,1)S(1)} %get-tuple-element.50.shifted_ref, f32[128,128]{1,0:T(8,128)S(1)} %get-tuple-element.47.columns_ref, ...), custom_call_target="tpu_custom_call" | custom-call | flops 1048576 | bytes 1048576 | tf_op jit(solution)/shard_map/order_next/pallas_call | solution.py:221
  30.6 0.0 collective-permute-done.4.refs_3_
  30.6 0.0 collective-permute-done.3.refs_2_
  30.6 0.0 collective-permute-done.2.refs_1_
  30.6 0.0 collective-permute-done.chunk
  30.6 0.0 collective-permute-done.1.chunk
  30.7 0.1 pad_maximum_fusion
  30.8 0.0 copy-start.2
  30.8 0.0 copy-start.3
  30.8 0.1 collective-permute-start.5
  30.9 0.5 collective-permute-start.6
  31.4 6.2 %order_next.3 = (bf16[2048,512]{1,0:T(8,128)(2,1)S(1)}, f32[16,512]{1,0:T(8,128)S(1)}) custom-call(s32[2]{0:T(128)S(1)} %pad_add_fusion.scalars, bf16[2048,2048]{1,0:T(8,128)(2,1)S(1)} %get-tuple-element.50.shifted_ref, f32[128,128]{1,0:T(8,128)S(1)} %get-tuple-element.47.columns_ref, f32[32,2048]{1,0:T(8,128)S(1)} %get-tuple-element.48.values_ref), custom_call_target="tpu_custom_call" | custom-call | flops 1048576 | bytes 1048576 | tf_op jit(solution)/shard_map/order_next/pallas_call | solution.py:221
  37.7 0.0 collective-permute-done.5.refs_4_
  37.7 0.0 copy-done.2
  37.7 0.0 copy-done.3
  37.7 5.3 %take_rows.1 = (bf16[2048,512]{1,0:T(8,128)(2,1)S(1)}, bf16[512,2048]{1,0:T(8,128)(2,1)S(1)}, f32[2048,128]{1,0:T(8,128)S(1)}) custom-call(s32[2]{0:T(128)S(1)} %pad_add_fusion.scalars, s32[16,128]{1,0:T(8,128)S(1)} %bitcast.31, f32[16,128]{1,0:T(8,128)S(1)} %bitcast.34, bf16[256,512]{1,0:T(8,128)(2,1)S(1)} %copy-done.1, ...), custom_call_target="tpu_custom_call" | custom-call | flops 4294967296 | bytes 4194304 | tf_op jit(solution)/shard_map/take_rows/pallas_call | solution.py:265
  43.0 2.2 %collective-permute-done.6.chunk = bf16[512,512]{1,0:T(8,128)(2,1)S(1)} collective-permute-done((bf16[512,512]{1,0:T(8,128)(2,1)S(1)}, bf16[512,512]{1,0:T(8,128)(2,1)S(1)}, u32[]{:S(2)}, u32[]{:S(2)}) %collective-permute-start.6) | collective-permute-done | bytes 524320 | tf_op jit(solution)/shard_map/ppermute | solution.py:412
  45.2 6.7 %cells.4 = (f32[2048,512]{1,0:T(8,128)S(1)}, f32[512,512]{1,0:T(8,128)}, bf16[256,512]{1,0:T(8,128)(2,1)S(1)}, bf16[256,512]{1,0:T(8,128)(2,1)S(1)}) custom-call(bf16[512,512]{1,0:T(8,128)(2,1)S(1)} %collective-permute-done.6.chunk, bf16[2048,512]{1,0:T(8,128)(2,1)S(1)} %get-tuple-element.56.wvec_ref, bf16[512,2048]{1,0:T(8,128)(2,1)S(1)} %get-tuple-element.57.turned_ref, ...), custom_call_target="tpu_custom_call" | custom-call | flops 1048576 | bytes 1048576 | tf_op jit(solution)/shard_map/cells/pallas_call | solution.py:357
  51.9 0.4 collective-permute-start.7
  52.4 1.6 %collective-permute-start.8 = (bf16[256,512]{1,0:T(8,128)(2,1)S(1)}, bf16[256,512]{1,0:T(8,128)(2,1)S(1)}, u32[]{:S(2)}, u32[]{:S(2)}) collective-permute-start(bf16[256,512]{1,0:T(8,128)(2,1)S(1)} %get-tuple-element.78), channel_id=1, source_target_pairs={{0,8},{8,0},{16,24},{24,16},{1,9},{9,1},{17,25},{25,17},{2,10},{10... | collective-permute-start | bytes 786440 | tf_op jit(solution)/shard_map/ppermute | solution.py:412
  53.9 6.2 %cells.5 = (f32[2048,512]{1,0:T(8,128)S(1)}, f32[512,512]{1,0:T(8,128)S(1)}) custom-call(bf16[512,512]{1,0:T(8,128)(2,1)S(1)} %collective-permute-done.chunk, bf16[2048,512]{1,0:T(8,128)(2,1)S(1)} %get-tuple-element.56.wvec_ref, bf16[512,2048]{1,0:T(8,128)(2,1)S(1)} %get-tuple-element.57.turned_ref, ...), custom_call_target="tpu_custom_call", output_to_operand_aliasing={{0}: (6, {})} | custom-call | flops 1048576 | bytes 1048576 | tf_op jit(solution)/shard_map/cells/pallas_call | solution.py:357
  60.2 0.9 collective-permute-done.7
  61.1 0.1 add_convert_fusion.1
  61.2 0.4 collective-permute-start.9
  61.6 0.0 copy-start
  61.6 7.1 %cells.6 = (f32[2048,512]{1,0:T(8,128)S(1)}, f32[512,512]{1,0:T(8,128)}, bf16[512,512]{1,0:T(8,128)(2,1)S(1)}) custom-call(bf16[512,512]{1,0:T(8,128)(2,1)S(1)} %collective-permute-done.1.chunk, bf16[2048,512]{1,0:T(8,128)(2,1)S(1)} %get-tuple-element.56.wvec_ref, ...), custom_call_target="tpu_custom_call", output_to_operand_aliasing={{0}: (6, {})} | custom-call | flops 1048576 | bytes 1048576 | tf_op jit(solution)/shard_map/cells/pallas_call | solution.py:357
  68.7 0.0 copy-done
  68.7 6.3 %cells.7 = (f32[2048,512]{1,0:T(8,128)S(1)}, f32[512,512]{1,0:T(8,128)S(1)}) custom-call(bf16[512,512]{1,0:T(8,128)(2,1)S(1)} %copy-done, bf16[2048,512]{1,0:T(8,128)(2,1)S(1)} %get-tuple-element.56.wvec_ref, bf16[512,2048]{1,0:T(8,128)(2,1)S(1)} %get-tuple-element.57.turned_ref, ...), custom_call_target="tpu_custom_call", output_to_operand_aliasing={{0}: (6, {})} | custom-call | flops 1048576 | bytes 1048576 | tf_op jit(solution)/shard_map/cells/pallas_call | solution.py:357
  75.0 0.0 collective-permute-done.8
  75.0 0.0 collective-permute-done.9
  75.0 0.1 add_convert_fusion
  75.1 2.9 %put_rows.2 = bf16[4,256,512]{2,1,0:T(8,128)(2,1)S(1)} custom-call(s32[2]{0:T(128)S(1)} %pad_add_fusion.scalars, s32[1,2048]{1,0:T(1,128)S(1)} %bitcast.32, f32[2048,512]{1,0:T(8,128)S(1)} %get-tuple-element.82.grad_ref), custom_call_target="tpu_custom_call" | custom-call | flops 1048576 | bytes 1048576 | tf_op jit(solution)/shard_map/put_rows/pallas_call | solution.py:399
  77.9 0.1 collective-permute-start.10
  78.0 1.3 %collective-permute-start.14 = (bf16[512,512]{1,0:T(8,128)(2,1)S(1)}, bf16[512,512]{1,0:T(8,128)(2,1)S(1)}, u32[]{:S(2)}, u32[]{:S(2)}) collective-permute-start(bf16[512,512]{1,0:T(8,128)(2,1)S(1)} %get-tuple-element.84), channel_id=1, source_target_pairs={{0,8},{8,0},{16,24},{24,16},{1,9},{9,1},{17,25},{25,17},{2,10},{10... | collective-permute-start | bytes 1572872 | tf_op jit(solution)/shard_map/ppermute | solution.py:412
  79.3 1.8 %collective-permute-start.15 = (bf16[256,512]{1,0:T(8,128)(2,1)S(1)}, bf16[256,512]{1,0:T(8,128)(2,1)S(1)}, u32[]{:S(2)}, u32[]{:S(2)}) collective-permute-start(bf16[256,512]{1,0:T(8,128)(2,1)S(1)} %add_convert_fusion), channel_id=1, source_target_pairs={{0,16},{8,24},{16,0},{24,8},{1,17},{9,25},{17,1},{25,9},{2,18},{10... | collective-permute-start | bytes 786440 | tf_op jit(solution)/shard_map/ppermute | solution.py:412
  81.1 5.0 %put_rows.3 = f32[4,256,512]{2,1,0:T(8,128)S(1)} custom-call(s32[2]{0:T(128)S(1)} %pad_add_fusion.scalars, s32[1,2048]{1,0:T(1,128)S(1)} %bitcast.33, f32[2048,512]{1,0:T(8,128)S(1)} %get-tuple-element.82.grad_ref), custom_call_target="tpu_custom_call" | custom-call | flops 4294967296 | bytes 1048576 | tf_op jit(solution)/shard_map/put_rows/pallas_call | solution.py:399
  86.2 0.0 collective-permute-done.10
  86.2 0.4 fusion.4
  86.6 0.1 slice_bitcast_fusion.3
  86.7 1.5 %collective-permute-start.11 = (bf16[256,512]{1,0:T(8,128)(2,1)S(1)}, bf16[256,512]{1,0:T(8,128)(2,1)S(1)}, u32[]{:S(2)}, u32[]{:S(2)}) collective-permute-start(bf16[256,512]{1,0:T(8,128)(2,1)S(1)} %get-tuple-element.88), channel_id=1, source_target_pairs={{0,2},{1,3},{2,0},{3,1},{4,6},{5,7},{6,4},{7,5},{8,10},{9,11},{10,... | collective-permute-start | bytes 786440 | tf_op jit(solution)/shard_map/ppermute | solution.py:412
  88.2 1.5 %collective-permute-start.13 = (bf16[256,512]{1,0:T(8,128)(2,1)S(1)}, bf16[256,512]{1,0:T(8,128)(2,1)S(1)}, u32[]{:S(2)}, u32[]{:S(2)}) collective-permute-start(bf16[256,512]{1,0:T(8,128)(2,1)S(1)} %get-tuple-element.89), channel_id=1, source_target_pairs={{0,6},{1,7},{2,4},{3,5},{4,2},{5,3},{6,0},{7,1},{8,14},{9,15},{10,... | collective-permute-start | bytes 786440 | tf_op jit(solution)/shard_map/ppermute | solution.py:412
  89.7 0.5 collective-permute-start.12
  90.2 6.5 %collective-permute-done.15 = bf16[256,512]{1,0:T(8,128)(2,1)S(1)} collective-permute-done((bf16[256,512]{1,0:T(8,128)(2,1)S(1)}, bf16[256,512]{1,0:T(8,128)(2,1)S(1)}, u32[]{:S(2)}, u32[]{:S(2)}) %collective-permute-start.15) | collective-permute-done | bytes 262176 | tf_op jit(solution)/shard_map/ppermute | solution.py:412
  96.7 1.3 %collective-permute-done.14 = bf16[512,512]{1,0:T(8,128)(2,1)S(1)} collective-permute-done((bf16[512,512]{1,0:T(8,128)(2,1)S(1)}, bf16[512,512]{1,0:T(8,128)(2,1)S(1)}, u32[]{:S(2)}, u32[]{:S(2)}) %collective-permute-start.14) | collective-permute-done | bytes 524320 | tf_op jit(solution)/shard_map/ppermute | solution.py:412
  98.0 1.2 %add_multiply_fusion = f32[512,512]{1,0:T(8,128)} fusion(f32[512,512]{1,0:T(8,128)S(1)} %get-tuple-element.83, bf16[512,512]{1,0:T(8,128)(2,1)S(1)} %collective-permute-done.14, bf16[256,512]{1,0:T(8,128)(2,1)S(1)} %collective-permute-done.15, bf16[256,512]{1,0:T(8,128)(2,1)S(1)} %collective-permute-done.9), kind=kLoop, calls=%fused_computation.2 | loop fusion | flops 2097152 | bytes 3145728 | tf_op jit(solution)/shard_map/mul | solution.py:476
  99.2 0.0 collective-permute-done.11
  99.2 2.3 %collective-permute-done.13 = bf16[256,512]{1,0:T(8,128)(2,1)S(1)} collective-permute-done((bf16[256,512]{1,0:T(8,128)(2,1)S(1)}, bf16[256,512]{1,0:T(8,128)(2,1)S(1)}, u32[]{:S(2)}, u32[]{:S(2)}) %collective-permute-start.13) | collective-permute-done | bytes 262176 | tf_op jit(solution)/shard_map/ppermute | solution.py:412
  101.5 1.4 %collective-permute-done.12 = bf16[256,512]{1,0:T(8,128)(2,1)S(1)} collective-permute-done((bf16[256,512]{1,0:T(8,128)(2,1)S(1)}, bf16[256,512]{1,0:T(8,128)(2,1)S(1)}, u32[]{:S(2)}, u32[]{:S(2)}) %collective-permute-start.12) | collective-permute-done | bytes 262176 | tf_op jit(solution)/shard_map/ppermute | solution.py:412
  102.9 0.9 fusion.3
Async XLA Ops:
  0.6 30.0 %collective-permute-start = (bf16[512,512]{1,0:T(8,128)(2,1)}, bf16[512,512]{1,0:T(8,128)(2,1)S(1)}, u32[]{:S(2)}, u32[]{:S(2)}) collective-permute-start(bf16[512,512]{1,0:T(8,128)(2,1)} %chunk.1), channel_id=1, source_target_pairs={{0,16},{8,24},{16,0},{24,8},{1,17},{9,25},{17,1},{25,9},{2,18},{10... | collective-permute-start | bytes 1572872 | tf_op jit(solution)/shard_map/ppermute | solution.py:412
  4.7 25.9 %collective-permute-start.1 = (bf16[512,512]{1,0:T(8,128)(2,1)}, bf16[512,512]{1,0:T(8,128)(2,1)S(1)}, u32[]{:S(2)}, u32[]{:S(2)}) collective-permute-start(bf16[512,512]{1,0:T(8,128)(2,1)} %chunk.1), channel_id=1, source_target_pairs={{0,8},{8,0},{16,24},{24,16},{1,9},{9,1},{17,25},{25,17},{2,10},{10... | collective-permute-start | bytes 1572872 | tf_op jit(solution)/shard_map/ppermute | solution.py:412
  6.4 9.5 %copy-start.1 = (bf16[256,512]{1,0:T(8,128)(2,1)S(1)}, bf16[256,512]{1,0:T(8,128)(2,1)}, u32[]{:S(2)}) copy-start(bf16[256,512]{1,0:T(8,128)(2,1)} %refs_0_.1) | copy-start | bytes 786436
  15.9 14.7 %collective-permute-start.4 = (bf16[256,512]{1,0:T(8,128)(2,1)S(1)}, bf16[256,512]{1,0:T(8,128)(2,1)S(1)}, u32[]{:S(2)}, u32[]{:S(2)}) collective-permute-start(bf16[256,512]{1,0:T(8,128)(2,1)S(1)} %copy-done.1), channel_id=1, source_target_pairs={{0,6},{1,7},{2,4},{3,5},{4,2},{5,3},{6,0},{7,1},{8,14},{9,15},{10,... | collective-permute-start | bytes 786440 | tf_op jit(solution)/shard_map/ppermute | solution.py:412
  18.4 12.2 %collective-permute-start.3 = (bf16[256,512]{1,0:T(8,128)(2,1)S(1)}, bf16[256,512]{1,0:T(8,128)(2,1)S(1)}, u32[]{:S(2)}, u32[]{:S(2)}) collective-permute-start(bf16[256,512]{1,0:T(8,128)(2,1)S(1)} %copy-done.1), channel_id=1, source_target_pairs={{0,4},{1,5},{2,6},{3,7},{4,0},{5,1},{6,2},{7,3},{8,12},{9,13},{10,... | collective-permute-start | bytes 786440 | tf_op jit(solution)/shard_map/ppermute | solution.py:412
  18.9 11.7 %collective-permute-start.2 = (bf16[256,512]{1,0:T(8,128)(2,1)S(1)}, bf16[256,512]{1,0:T(8,128)(2,1)S(1)}, u32[]{:S(2)}, u32[]{:S(2)}) collective-permute-start(bf16[256,512]{1,0:T(8,128)(2,1)S(1)} %copy-done.1), channel_id=1, source_target_pairs={{0,2},{1,3},{2,0},{3,1},{4,6},{5,7},{6,4},{7,5},{8,10},{9,11},{10,... | collective-permute-start | bytes 786440 | tf_op jit(solution)/shard_map/ppermute | solution.py:412
  30.8 6.9 %copy-start.2 = (s32[2048]{0:T(1024)S(1)}, s32[2048]{0:T(1024)}, u32[]{:S(2)}) copy-start(s32[2048]{0:T(1024)} %param.10) | copy-start | bytes 24580
  30.8 6.9 %copy-start.3 = (f32[2048]{0:T(1024)S(1)}, f32[2048]{0:T(1024)}, u32[]{:S(2)}) copy-start(f32[2048]{0:T(1024)} %param.12) | copy-start | bytes 24580
  30.8 6.9 %collective-permute-start.5 = (bf16[4,256,512]{2,1,0:T(8,128)(2,1)S(1)}, bf16[4,256,512]{2,1,0:T(8,128)(2,1)S(1)}, u32[]{:S(2)}, u32[]{:S(2)}) collective-permute-start(bf16[4,256,512]{2,1,0:T(8,128)(2,1)S(1)} %pad_maximum_fusion), channel_id=1, source_target_pairs={{0,1},{1,0},{2,3},{3,2},{4,5},{5,4},{6,7},{7,6},{8,9},{9,8},{10,11... | collective-permute-start | bytes 3145736 | tf_op jit(solution)/shard_map/ppermute | solution.py:412
  30.9 14.3 %collective-permute-start.6 = (bf16[512,512]{1,0:T(8,128)(2,1)S(1)}, bf16[512,512]{1,0:T(8,128)(2,1)S(1)}, u32[]{:S(2)}, u32[]{:S(2)}) collective-permute-start(bf16[512,512]{1,0:T(8,128)(2,1)S(1)} %collective-permute-done.chunk), channel_id=1, source_target_pairs={{0,8},{8,0},{16,24},{24,16},{1,9},{9,1},{17,25},{25,17},{2,10},{10... | collective-permute-start | bytes 1572872 | tf_op jit(solution)/shard_map/ppermute | solution.py:412
  51.9 9.2 %collective-permute-start.7 = (bf16[256,512]{1,0:T(8,128)(2,1)S(1)}, bf16[256,512]{1,0:T(8,128)(2,1)S(1)}, u32[]{:S(2)}, u32[]{:S(2)}) collective-permute-start(bf16[256,512]{1,0:T(8,128)(2,1)S(1)} %get-tuple-element.71), channel_id=1, source_target_pairs={{0,8},{8,0},{16,24},{24,16},{1,9},{9,1},{17,25},{25,17},{2,10},{10... | collective-permute-start | bytes 786440 | tf_op jit(solution)/shard_map/ppermute | solution.py:412
  52.4 22.6 %collective-permute-start.8 = (bf16[256,512]{1,0:T(8,128)(2,1)S(1)}, bf16[256,512]{1,0:T(8,128)(2,1)S(1)}, u32[]{:S(2)}, u32[]{:S(2)}) collective-permute-start(bf16[256,512]{1,0:T(8,128)(2,1)S(1)} %get-tuple-element.78), channel_id=1, source_target_pairs={{0,8},{8,0},{16,24},{24,16},{1,9},{9,1},{17,25},{25,17},{2,10},{10... | collective-permute-start | bytes 786440 | tf_op jit(solution)/shard_map/ppermute | solution.py:412
  61.2 13.8 %collective-permute-start.9 = (bf16[256,512]{1,0:T(8,128)(2,1)S(1)}, bf16[256,512]{1,0:T(8,128)(2,1)S(1)}, u32[]{:S(2)}, u32[]{:S(2)}) collective-permute-start(bf16[256,512]{1,0:T(8,128)(2,1)S(1)} %add_convert_fusion.1), channel_id=1, source_target_pairs={{0,16},{8,24},{16,0},{24,8},{1,17},{9,25},{17,1},{25,9},{2,18},{10... | collective-permute-start | bytes 786440 | tf_op jit(solution)/shard_map/ppermute | solution.py:412
  61.6 7.1 %copy-start = (bf16[512,512]{1,0:T(8,128)(2,1)S(1)}, bf16[512,512]{1,0:T(8,128)(2,1)}, u32[]{:S(2)}) copy-start(bf16[512,512]{1,0:T(8,128)(2,1)} %chunk.1) | copy-start | bytes 1572868
  77.9 8.3 %collective-permute-start.10 = (bf16[4,256,512]{2,1,0:T(8,128)(2,1)S(1)}, bf16[4,256,512]{2,1,0:T(8,128)(2,1)S(1)}, u32[]{:S(2)}, u32[]{:S(2)}) collective-permute-start(bf16[4,256,512]{2,1,0:T(8,128)(2,1)S(1)} %put_rows.2), channel_id=1, source_target_pairs={{0,1},{1,0},{2,3},{3,2},{4,5},{5,4},{6,7},{7,6},{8,9},{9,8},{10,11... | collective-permute-start | bytes 3145736 | tf_op jit(solution)/shard_map/ppermute | solution.py:412
  78.0 20.0 %collective-permute-start.14 = (bf16[512,512]{1,0:T(8,128)(2,1)S(1)}, bf16[512,512]{1,0:T(8,128)(2,1)S(1)}, u32[]{:S(2)}, u32[]{:S(2)}) collective-permute-start(bf16[512,512]{1,0:T(8,128)(2,1)S(1)} %get-tuple-element.84), channel_id=1, source_target_pairs={{0,8},{8,0},{16,24},{24,16},{1,9},{9,1},{17,25},{25,17},{2,10},{10... | collective-permute-start | bytes 1572872 | tf_op jit(solution)/shard_map/ppermute | solution.py:412
  79.3 17.4 %collective-permute-start.15 = (bf16[256,512]{1,0:T(8,128)(2,1)S(1)}, bf16[256,512]{1,0:T(8,128)(2,1)S(1)}, u32[]{:S(2)}, u32[]{:S(2)}) collective-permute-start(bf16[256,512]{1,0:T(8,128)(2,1)S(1)} %add_convert_fusion), channel_id=1, source_target_pairs={{0,16},{8,24},{16,0},{24,8},{1,17},{9,25},{17,1},{25,9},{2,18},{10... | collective-permute-start | bytes 786440 | tf_op jit(solution)/shard_map/ppermute | solution.py:412
  86.7 12.5 %collective-permute-start.11 = (bf16[256,512]{1,0:T(8,128)(2,1)S(1)}, bf16[256,512]{1,0:T(8,128)(2,1)S(1)}, u32[]{:S(2)}, u32[]{:S(2)}) collective-permute-start(bf16[256,512]{1,0:T(8,128)(2,1)S(1)} %get-tuple-element.88), channel_id=1, source_target_pairs={{0,2},{1,3},{2,0},{3,1},{4,6},{5,7},{6,4},{7,5},{8,10},{9,11},{10,... | collective-permute-start | bytes 786440 | tf_op jit(solution)/shard_map/ppermute | solution.py:412
  88.2 13.3 %collective-permute-start.13 = (bf16[256,512]{1,0:T(8,128)(2,1)S(1)}, bf16[256,512]{1,0:T(8,128)(2,1)S(1)}, u32[]{:S(2)}, u32[]{:S(2)}) collective-permute-start(bf16[256,512]{1,0:T(8,128)(2,1)S(1)} %get-tuple-element.89), channel_id=1, source_target_pairs={{0,6},{1,7},{2,4},{3,5},{4,2},{5,3},{6,0},{7,1},{8,14},{9,15},{10,... | collective-permute-start | bytes 786440 | tf_op jit(solution)/shard_map/ppermute | solution.py:412
  89.7 13.2 %collective-permute-start.12 = (bf16[256,512]{1,0:T(8,128)(2,1)S(1)}, bf16[256,512]{1,0:T(8,128)(2,1)S(1)}, u32[]{:S(2)}, u32[]{:S(2)}) collective-permute-start(bf16[256,512]{1,0:T(8,128)(2,1)S(1)} %get-tuple-element.90), channel_id=1, source_target_pairs={{0,4},{1,5},{2,6},{3,7},{4,0},{5,1},{6,2},{7,3},{8,12},{9,13},{10,... | collective-permute-start | bytes 786440 | tf_op jit(solution)/shard_map/ppermute | solution.py:412

commit v2 on v1

--- a/solution.py
+++ b/solution.py
@@ -278,11 +278,9 @@
     )(scalars, row_perm.reshape(-1, LANES), row_logm.reshape(-1, LANES), *blocks)
 
 
-def cells_kernel(has_sum, pieces, chunk, wvec_ref, turned_ref, count_ref, aux_ref, logm_ref, *refs):
-    if has_sum:
-        before_ref, refs = refs[0], refs[1:]
-    grad_ref, term_ref, sent_refs = refs[0], refs[1], refs[2 : 2 + pieces]
-    chunk_turned, delta_ref, sum_ref = refs[2 + pieces :]
+def chunk_work(
+    chunk, wvec_ref, turned_ref, count_ref, aux_ref, logm_ref, before_ref, grad_ref, term_ref, chunk_turned, delta_ref
+):
     chunk_turned[...] = chunk[...].T
     rows = wvec_ref.shape[0]
     width = chunk.shape[0]
@@ -291,7 +289,7 @@
     joined = delta_ref.shape[0] // tile
     half = joined // 2
     col_logm = aux_ref[blocks : blocks + 1, :]
-    sum_ref[...] = jnp.zeros_like(sum_ref)
+    term_ref[...] = jnp.zeros_like(term_ref)
 
     @pl.loop(0, blocks // joined)
     def _(group):
@@ -318,13 +316,13 @@
 
         def grad_of(at):
             grad = jnp.dot(held(at), chunk[...], preferred_element_type=F32)
-            if has_sum:
+            if before_ref is not None:
                 grad = grad + before_ref[rows_at(at), :]
             grad_ref[rows_at(at), :] = grad
 
         def term_of(at):
             turned = turned_ref[:, rows_at(at, half)]
-            sum_ref[...] += jnp.dot(turned, held(at, half), preferred_element_type=F32)
+            term_ref[...] += jnp.dot(turned, held(at, half), preferred_element_type=F32)
 
         ahead = score_of(0)
         for at in range(joined):
@@ -339,30 +337,52 @@
         grad_of(joined - 1)
         term_of(half)
 
-    total = sum_ref[...].T
-    term_ref[...] = total
-    for at, sent_ref in enumerate(sent_refs):
-        size = sent_ref.shape[0]
-        sent_ref[...] = total[at * size : (at + 1) * size].astype(BF16)
-
-
-def cells(chunk, wvec, turned, ordered, aux, logm, before, pieces):
+
+def cells_kernel(has_sum, sends, *refs):
+    chunks = len(sends)
+    wvec_ref, turned_ref, logm_ref, refs = *refs[:3], refs[3:]
+    chunk_refs, count_refs, aux_refs = refs[:chunks], refs[chunks : 2 * chunks], refs[2 * chunks : 3 * chunks]
+    refs = refs[3 * chunks :]
+    before_ref = None
+    if has_sum:
+        before_ref, refs = refs[0], refs[1:]
+    grad_ref, refs = refs[0], refs[1:]
+    chunk_turned, delta_ref, sum_ref = refs[-3:]
+    for at, pieces in enumerate(sends):
+        term_ref = sum_ref
+        if not pieces:
+            term_ref, refs = refs[0], refs[1:]
+        chunk_work(
+            chunk_refs[at], wvec_ref, turned_ref, count_refs[at], aux_refs[at], logm_ref,
+            before_ref, grad_ref, term_ref, chunk_turned, delta_ref,
+        )
+        before_ref = grad_ref
+        for piece in range(pieces):
+            sent_ref, refs = refs[0], refs[1:]
+            size = sent_ref.shape[0]
+            sent_ref[...] = term_ref[pl.ds(piece * size, size), :].astype(BF16)
+
+
+def cells(rows_in, chunks, before, sends):
+    wvec = rows_in[0]
     rows, depth = wvec.shape
-    width = chunk.shape[0]
-    args = [chunk, wvec, turned, ordered, aux, logm]
+    width = chunks[0][0].shape[0]
+    args = [*rows_in, *[each for kind in zip(*chunks) for each in kind]]
     aliases = {}
     if before is not None:
         aliases = {len(args): 0}
         args.append(before)
+    out_shape = [jax.ShapeDtypeStruct((rows, depth), F32)]
+    for pieces in sends:
+        if pieces:
+            out_shape += [jax.ShapeDtypeStruct((depth // pieces, width), BF16) for _ in range(pieces)]
+        else:
+            out_shape.append(jax.ShapeDtypeStruct((depth, width), F32))
     return pl.pallas_call(
-        functools.partial(cells_kernel, before is not None, pieces),
+        functools.partial(cells_kernel, before is not None, sends),
         in_specs=[WHOLE] * len(args),
-        out_specs=[WHOLE] * (2 + pieces),
-        out_shape=[
-            jax.ShapeDtypeStruct((rows, depth), F32),
-            jax.ShapeDtypeStruct((width, depth), F32),
-        ]
-        + [jax.ShapeDtypeStruct((width // pieces, depth), BF16) for _ in range(pieces)],
+        out_specs=[WHOLE] * len(out_shape),
+        out_shape=out_shape,
         scratch_shapes=[
             pltpu.VMEM((depth, width), BF16),
             pltpu.VMEM((rows // 2, width), BF16),
@@ -373,6 +393,27 @@
         cost_estimate=cost(rows * width, rows * depth),
         name="cells",
     )(*args)
+
+
+def finish_kernel(scale, *refs):
+    own_ref, near_ref, cross_refs, out_ref = refs[0], refs[1], refs[2:-1], refs[-1]
+    size = cross_refs[0].shape[0]
+    for at, cross_ref in enumerate(cross_refs):
+        here = pl.ds(at * size, size)
+        total = own_ref[here, :] + near_ref[here, :].astype(F32) + cross_ref[...].astype(F32)
+        out_ref[:, here] = (total * scale).T
+
+
+def finish(scale, own, near, *crosses):
+    return pl.pallas_call(
+        functools.partial(finish_kernel, scale),
+        in_specs=[WHOLE] * (2 + len(crosses)),
+        out_specs=WHOLE,
+        out_shape=jax.ShapeDtypeStruct(own.shape[::-1], F32),
+        compiler_params=params(8),
+        cost_estimate=cost(own.size, own.size // 16),
+        name="finish",
+    )(own, near, *crosses)
 
 
 def put_kernel(offsets, exact, scalars, perm_ref, grad_ref, out_ref):
@@ -402,7 +443,7 @@
         out_specs=WHOLE,
         out_shape=jax.ShapeDtypeStruct((len(offsets), side, width), F32 if exact else BF16),
         compiler_params=params(24),
-        cost_estimate=cost((4096 if exact else 1) * grad.size, grad.size),
+        cost_estimate=cost((4096 if exact and len(offsets) > 1 else 1) * grad.size, grad.size // 16),
         name="put_rows",
     )(scalars, row_perm[None, :], grad)
 
@@ -443,37 +484,42 @@
     blocks = [row_emb, from_x, from_y, from_xy, from_core]
     wvec, turned, logm = take_rows(scalars, row_perm, row_logm, blocks)
 
-    grad, _, sent_0, sent_1 = cells(far, wvec, turned, count_far, aux_far, logm, None, 2)
+    rows_in = (wvec, turned, logm)
+    of_far, of_cross = (far, count_far, aux_far), (cross, count_cross, aux_cross)
+    of_near, of_own = (near, count_near, aux_near), (col_emb, count_own, aux_own)
+    grad, sent_0, sent_1 = cells(rows_in, [of_far], None, (2,))
     far_0 = swap(sent_0, "row", 1)
     far_1 = swap(sent_1, "row", 1)
-    grad, term_cross = cells(cross, wvec, turned, count_cross, aux_cross, logm, grad, 0)
+    grad, term_cross = cells(rows_in, [of_cross], grad, (0,))
     grad, far_0 = together((grad, far_0))
 
-    half = width // 2
+    half = term_cross.shape[0] // 2
     sum_0 = (term_cross[:half] + far_0.astype(F32)).astype(BF16)
     cross_0 = swap(sum_0, "row", 2)
     grad, sum_0 = together((grad, sum_0))
-    grad, _, sent_near = cells(near, wvec, turned, count_near, aux_near, logm, grad, 1)
+    grad, sent_near, term_own = cells(rows_in, [of_near, of_own], grad, (1, 0))
     got_near = swap(sent_near, "row", 1)
-    grad, term_own = cells(col_emb, wvec, turned, count_own, aux_own, logm, grad, 0)
     grad, far_1, cross_0 = together((grad, far_1, cross_0))
     sum_1 = (term_cross[half:] + far_1.astype(F32)).astype(BF16)
     cross_1 = swap(sum_1, "row", 2)
     grad, sum_1 = together((grad, sum_1))
-    away = put_rows(scalars, row_perm, grad, (1, 3, 5, 7), side, False)
+
+    ordered = functools.partial(put_rows, scalars, row_perm)
+    away = ordered(grad, (1, 3, 5, 7), side, False)
     core = swap(away, "col", 1)
     grad, away = together((grad, away))
-    home = put_rows(scalars, row_perm, grad, (0, 2, 4, 6), side, True)
-    both = home + core.astype(F32)
-    got_x = swap(both[1].astype(BF16), "col", 2)
-    got_y = swap(both[2].astype(BF16), "col", 4)
-    got_xy = swap(both[3].astype(BF16), "col", 6)
-    row_sum = both[0] + got_x.astype(F32) + got_y.astype(F32) + got_xy.astype(F32)
-    got_cross = jnp.concatenate([cross_0, cross_1]).astype(F32)
-    col_sum = term_own + got_near.astype(F32) + got_cross
+    both = ordered(grad, (2, 4, 6), side, True) + core[1:].astype(F32)
+    sends = [both[at].astype(BF16) for at in range(3)]
+    got = [swap(sent, "col", bit) for sent, bit in zip(sends, (2, 4, 6))]
+    grad, sends = together((grad, sends))
+    home = ordered(grad, (0,), side, True)
+    home, term_own = together((home, term_own))
+    row_sum = home[0] + core[0].astype(F32)
+    for each in got:
+        row_sum = row_sum + each.astype(F32)
     row_scale = np.float32(1.0 / np.sqrt(shard_cols * 8))
     col_scale = np.float32(1.0 / np.sqrt(shard_rows * 4))
-    return (row_sum * row_scale, col_sum * col_scale)
+    return (row_sum * row_scale, finish(col_scale, term_own, got_near, cross_0, cross_1))
 
 
 def solution(mesh):

time: 104 us -> 100 us (0.962)
  other arithmetic: 2.92 us -> 1.63 us
  Pallas kernels: 66.4 us -> 65.3 us
  waiting for transfers between devices: 14.6 us -> 13.5 us
    pallas_call x4, Pallas kernels: 26.3 us -> 24.5 us  [the longest x3 23.1 us: cells(): pl.pallas_call(functools.partial(cells_kernel, before is not None, sends)...]
    mul x2 -> x1, other arithmetic: 2.15 us -> 0.97 us  [line_shards(): row_sum * row_scale]
    ppermute x16, waiting for transfers between devices: 14.6 us -> 13.5 us  [swap(): return lax.ppermute(value, axis, pairs)]
    pallas_call x2 -> x3, Pallas kernels: 7.91 us -> 8.63 us  [put_rows(): pl.pallas_call(functools.partial(put_kernel, offsets, exact), in_specs=[S...]
  transfers between devices with their start and end apart: 16 -> 16, of which waited for: 6 -> 7; matrix products, arithmetic and copies ran while one was open for 2% -> 1% of each run, Pallas kernels for 55% -> 57%
where the time goes in v2:
time: 100 us
  Pallas kernels  65.3 us (65%)
  starting transfers between devices  18.7 us (19%)
  waiting for transfers between devices  13.5 us (14%)
  other arithmetic  1.63 us (2%)
    pallas_call x3, Pallas kernels, cells(): pl.pallas_call(functools.partial(cells_kernel, before is not None, sends)...  23.1 us
    ppermute x16, starting transfers between devices, swap(): return lax.ppermute(value, axis, pairs)  18.7 us
    pallas_call x2, Pallas kernels, order_next(): pl.pallas_call(functools.partial(order_next_kernel, offsets), in_specs=[S...  17.4 us
    ppermute x16, waiting for transfers between devices, swap(): return lax.ppermute(value, axis, pairs)  13.5 us
    pallas_call x1, Pallas kernels, order_first(): pl.pallas_call(functools.partial(order_first_kernel, offsets), in_specs=[...  9.47 us
    pallas_call x3, Pallas kernels, put_rows(): pl.pallas_call(functools.partial(put_kernel, offsets, exact), in_specs=[S...  8.63 us
    pallas_call x1, Pallas kernels, take_rows(): pl.pallas_call(take_kernel, in_specs=[SCALARS] + [WHOLE] * 7, out_specs=[...  5.32 us
  transfers between devices with their start and end apart: 16, of which 7 were waited for; matrix products, arithmetic and copies ran while one was open for 1% of the time, Pallas kernels for 57%

profile of v2, /device:TPU:0, one launch (start us, length us, event | category | flops | bytes accessed | tf_op | source)
XLA Modules:
  0.0 100.0 jit_solution(13067469598783779792)
XLA Ops:
  0.6 4.1 %collective-permute-start = (bf16[512,512]{1,0:T(8,128)(2,1)}, bf16[512,512]{1,0:T(8,128)(2,1)S(1)}, u32[]{:S(2)}, u32[]{:S(2)}) collective-permute-start(bf16[512,512]{1,0:T(8,128)(2,1)} %refs_4_.1), channel_id=1, source_target_pairs={{0,16},{8,24},{16,0},{24,8},{1,17},{9,25},{17,1},{25,9},{2,18},{10... | collective-permute-start | bytes 1572872 | tf_op jit(solution)/shard_map/ppermute | solution.py:453
  4.7 1.6 %collective-permute-start.1 = (bf16[512,512]{1,0:T(8,128)(2,1)}, bf16[512,512]{1,0:T(8,128)(2,1)S(1)}, u32[]{:S(2)}, u32[]{:S(2)}) collective-permute-start(bf16[512,512]{1,0:T(8,128)(2,1)} %refs_4_.1), channel_id=1, source_target_pairs={{0,8},{8,0},{16,24},{24,16},{1,9},{9,1},{17,25},{25,17},{2,10},{10... | collective-permute-start | bytes 1572872 | tf_op jit(solution)/shard_map/ppermute | solution.py:453
  6.3 0.1 pad_add_fusion.scalars
  6.4 0.0 copy-start.1
  6.4 9.5 %order_first.1 = (bf16[2048,512]{1,0:T(8,128)(2,1)S(1)}, f32[16,512]{1,0:T(8,128)S(1)}, bf16[2048,2048]{1,0:T(8,128)(2,1)S(1)}, f32[128,128]{1,0:T(8,128)S(1)}, f32[32,2048]{1,0:T(8,128)S(1)}) custom-call(s32[2]{0:T(128)S(1)} %pad_add_fusion.scalars, s32[16,128]{1,0:T(8,128)} %bitcast.34, s32[8,8]{1,0:T(8,128)} %mask_hbm.1, f32[1,2048]{1,0:T(1,128)} %bitcast.35, ...), custom_call_target="tpu_custom_call" | custom-call | flops 4294967296 | bytes 16777216 | tf_op jit(solution)/shard_map/order_first/pallas_call | solution.py:173
  15.9 0.0 copy-done.1
  15.9 2.5 %collective-permute-start.4 = (bf16[256,512]{1,0:T(8,128)(2,1)S(1)}, bf16[256,512]{1,0:T(8,128)(2,1)S(1)}, u32[]{:S(2)}, u32[]{:S(2)}) collective-permute-start(bf16[256,512]{1,0:T(8,128)(2,1)S(1)} %copy-done.1), channel_id=1, source_target_pairs={{0,6},{1,7},{2,4},{3,5},{4,2},{5,3},{6,0},{7,1},{8,14},{9,15},{10,... | collective-permute-start | bytes 786440 | tf_op jit(solution)/shard_map/ppermute | solution.py:453
  18.4 0.5 collective-permute-start.3
  18.9 0.5 collective-permute-start.2
  19.4 11.2 %order_next.2 = (bf16[2048,512]{1,0:T(8,128)(2,1)S(1)}, bf16[2048,512]{1,0:T(8,128)(2,1)S(1)}, f32[16,512]{1,0:T(8,128)S(1)}, f32[16,512]{1,0:T(8,128)S(1)}) custom-call(s32[2]{0:T(128)S(1)} %pad_add_fusion.scalars, bf16[2048,2048]{1,0:T(8,128)(2,1)S(1)} %get-tuple-element.52.shifted_ref, f32[128,128]{1,0:T(8,128)S(1)} %get-tuple-element.49.columns_ref, ...), custom_call_target="tpu_custom_call" | custom-call | flops 1048576 | bytes 1048576 | tf_op jit(solution)/shard_map/order_next/pallas_call | solution.py:221
  30.6 0.0 collective-permute-done.4.refs_3_
  30.6 0.0 collective-permute-done.3.refs_2_
  30.6 0.0 collective-permute-done.2.refs_1_
  30.6 0.0 collective-permute-done.refs_3_
  30.6 0.0 collective-permute-done.1.refs_3_
  30.7 0.1 pad_maximum_fusion
  30.8 0.0 copy-start.2
  30.8 0.0 copy-start.3
  30.8 0.1 collective-permute-start.5
  30.9 0.5 collective-permute-start.6
  31.4 6.2 %order_next.3 = (bf16[2048,512]{1,0:T(8,128)(2,1)S(1)}, f32[16,512]{1,0:T(8,128)S(1)}) custom-call(s32[2]{0:T(128)S(1)} %pad_add_fusion.scalars, bf16[2048,2048]{1,0:T(8,128)(2,1)S(1)} %get-tuple-element.52.shifted_ref, f32[128,128]{1,0:T(8,128)S(1)} %get-tuple-element.49.columns_ref, f32[32,2048]{1,0:T(8,128)S(1)} %get-tuple-element.50.values_ref), custom_call_target="tpu_custom_call" | custom-call | flops 1048576 | bytes 1048576 | tf_op jit(solution)/shard_map/order_next/pallas_call | solution.py:221
  37.7 0.0 collective-permute-done.5.refs_4_
  37.7 0.0 copy-done.2
  37.7 0.0 copy-done.3
  37.7 5.3 %take_rows.1 = (bf16[2048,512]{1,0:T(8,128)(2,1)S(1)}, bf16[512,2048]{1,0:T(8,128)(2,1)S(1)}, f32[2048,128]{1,0:T(8,128)S(1)}) custom-call(s32[2]{0:T(128)S(1)} %pad_add_fusion.scalars, s32[16,128]{1,0:T(8,128)S(1)} %bitcast.29, f32[16,128]{1,0:T(8,128)S(1)} %bitcast.33, bf16[256,512]{1,0:T(8,128)(2,1)S(1)} %copy-done.1, ...), custom_call_target="tpu_custom_call" | custom-call | flops 4294967296 | bytes 4194304 | tf_op jit(solution)/shard_map/take_rows/pallas_call | solution.py:265
  43.0 2.2 %collective-permute-done.6.refs_3_ = bf16[512,512]{1,0:T(8,128)(2,1)S(1)} collective-permute-done((bf16[512,512]{1,0:T(8,128)(2,1)S(1)}, bf16[512,512]{1,0:T(8,128)(2,1)S(1)}, u32[]{:S(2)}, u32[]{:S(2)}) %collective-permute-start.6) | collective-permute-done | bytes 524320 | tf_op jit(solution)/shard_map/ppermute | solution.py:453
  45.2 5.5 %cells.3 = (f32[2048,512]{1,0:T(8,128)S(1)}, bf16[256,512]{1,0:T(8,128)(2,1)S(1)}, bf16[256,512]{1,0:T(8,128)(2,1)S(1)}) custom-call(bf16[2048,512]{1,0:T(8,128)(2,1)S(1)} %get-tuple-element.58.refs_0_, bf16[512,2048]{1,0:T(8,128)(2,1)S(1)} %get-tuple-element.59.refs_1_, f32[2048,128]{1,0:T(8,128)S(1)} %get-tuple-element.60.refs_2_, ...), custom_call_target="tpu_custom_call" | custom-call | flops 1048576 | bytes 1048576 | tf_op jit(solution)/shard_map/cells/pallas_call | solution.py:381
  50.7 0.5 collective-permute-start.7
  51.2 1.6 %collective-permute-start.8 = (bf16[256,512]{1,0:T(8,128)(2,1)S(1)}, bf16[256,512]{1,0:T(8,128)(2,1)S(1)}, u32[]{:S(2)}, u32[]{:S(2)}) collective-permute-start(bf16[256,512]{1,0:T(8,128)(2,1)S(1)} %get-tuple-element.79), channel_id=1, source_target_pairs={{0,8},{8,0},{16,24},{24,16},{1,9},{9,1},{17,25},{25,17},{2,10},{10... | collective-permute-start | bytes 786440 | tf_op jit(solution)/shard_map/ppermute | solution.py:453
  52.8 0.0 copy-start
  52.8 5.8 %cells.4 = (f32[2048,512]{1,0:T(8,128)S(1)}, f32[512,512]{1,0:T(8,128)S(1)}) custom-call(bf16[2048,512]{1,0:T(8,128)(2,1)S(1)} %get-tuple-element.58.refs_0_, bf16[512,2048]{1,0:T(8,128)(2,1)S(1)} %get-tuple-element.59.refs_1_, f32[2048,128]{1,0:T(8,128)S(1)} %get-tuple-element.60.refs_2_, ...), custom_call_target="tpu_custom_call", output_to_operand_aliasing={{0}: (6, {})} | custom-call | flops 1048576 | bytes 1048576 | tf_op jit(solution)/shard_map/cells/pallas_call | solution.py:381
  58.6 1.4 %collective-permute-done.7 = bf16[256,512]{1,0:T(8,128)(2,1)S(1)} collective-permute-done((bf16[256,512]{1,0:T(8,128)(2,1)S(1)}, bf16[256,512]{1,0:T(8,128)(2,1)S(1)}, u32[]{:S(2)}, u32[]{:S(2)}) %collective-permute-start.7) | collective-permute-done | bytes 262176 | tf_op jit(solution)/shard_map/ppermute | solution.py:453
  60.0 0.1 add_convert_fusion.2
  60.1 0.4 collective-permute-start.9
  60.5 0.0 copy-done
  60.5 11.8 %cells.5 = (f32[2048,512]{1,0:T(8,128)S(1)}, bf16[512,512]{1,0:T(8,128)(2,1)S(1)}, f32[512,512]{1,0:T(8,128)S(1)}) custom-call(bf16[2048,512]{1,0:T(8,128)(2,1)S(1)} %get-tuple-element.58.refs_0_, bf16[512,2048]{1,0:T(8,128)(2,1)S(1)} %get-tuple-element.59.refs_1_, f32[2048,128]{1,0:T(8,128)S(1)} %get-tuple-element.60.refs_2_, ...), custom_call_target="tpu_custom_call", output_to_operand_aliasing={{0}: (9, {})} | custom-call | flops 1048576 | bytes 1048576 | tf_op jit(solution)/shard_map/cells/pallas_call | solution.py:381
  72.3 0.0 collective-permute-done.8
  72.3 0.3 collective-permute-done.9.refs_2_
  72.7 0.1 add_convert_fusion.1
  72.7 2.9 %put_rows.3 = bf16[4,256,512]{2,1,0:T(8,128)(2,1)S(1)} custom-call(s32[2]{0:T(128)S(1)} %pad_add_fusion.scalars, s32[1,2048]{1,0:T(1,128)S(1)} %bitcast.30, f32[2048,512]{1,0:T(8,128)S(1)} %get-tuple-element.84.grad_ref), custom_call_target="tpu_custom_call" | custom-call | flops 1048576 | bytes 65536 | tf_op jit(solution)/shard_map/put_rows/pallas_call | solution.py:440
  75.6 0.1 collective-permute-start.10
  75.7 1.0 collective-permute-start.14
  76.7 1.8 %collective-permute-start.15 = (bf16[256,512]{1,0:T(8,128)(2,1)S(1)}, bf16[256,512]{1,0:T(8,128)(2,1)S(1)}, u32[]{:S(2)}, u32[]{:S(2)}) collective-permute-start(bf16[256,512]{1,0:T(8,128)(2,1)S(1)} %add_convert_fusion.1), channel_id=1, source_target_pairs={{0,16},{8,24},{16,0},{24,8},{1,17},{9,25},{17,1},{25,9},{2,18},{10... | collective-permute-start | bytes 786440 | tf_op jit(solution)/shard_map/ppermute | solution.py:453
  78.5 4.0 %put_rows.4 = f32[3,256,512]{2,1,0:T(8,128)S(1)} custom-call(s32[2]{0:T(128)S(1)} %pad_add_fusion.scalars, s32[1,2048]{1,0:T(1,128)S(1)} %bitcast.31, f32[2048,512]{1,0:T(8,128)S(1)} %get-tuple-element.84.grad_ref), custom_call_target="tpu_custom_call" | custom-call | flops 4294967296 | bytes 65536 | tf_op jit(solution)/shard_map/put_rows/pallas_call | solution.py:440
  82.5 0.0 collective-permute-done.10
  82.5 0.3 add_convert_fusion
  82.8 0.1 slice_bitcast_fusion.2
  82.9 1.6 %collective-permute-start.11 = (bf16[256,512]{1,0:T(8,128)(2,1)S(1)}, bf16[256,512]{1,0:T(8,128)(2,1)S(1)}, u32[]{:S(2)}, u32[]{:S(2)}) collective-permute-start(bf16[256,512]{1,0:T(8,128)(2,1)S(1)} %get-tuple-element.90), channel_id=1, source_target_pairs={{0,2},{1,3},{2,0},{3,1},{4,6},{5,7},{6,4},{7,5},{8,10},{9,11},{10,... | collective-permute-start | bytes 786440 | tf_op jit(solution)/shard_map/ppermute | solution.py:453
  84.4 1.5 %collective-permute-start.13 = (bf16[256,512]{1,0:T(8,128)(2,1)S(1)}, bf16[256,512]{1,0:T(8,128)(2,1)S(1)}, u32[]{:S(2)}, u32[]{:S(2)}) collective-permute-start(bf16[256,512]{1,0:T(8,128)(2,1)S(1)} %get-tuple-element.91), channel_id=1, source_target_pairs={{0,6},{1,7},{2,4},{3,5},{4,2},{5,3},{6,0},{7,1},{8,14},{9,15},{10,... | collective-permute-start | bytes 786440 | tf_op jit(solution)/shard_map/ppermute | solution.py:453
  85.9 0.5 collective-permute-start.12
  86.4 1.8 %put_rows.5 = f32[1,256,512]{2,1,0:T(8,128)S(1)} custom-call(s32[2]{0:T(128)S(1)} %pad_add_fusion.scalars, s32[1,2048]{1,0:T(1,128)S(1)} %bitcast.32, f32[2048,512]{1,0:T(8,128)S(1)} %get-tuple-element.84.grad_ref), custom_call_target="tpu_custom_call" | custom-call | flops 1048576 | bytes 65536 | tf_op jit(solution)/shard_map/put_rows/pallas_call | solution.py:440
  88.2 5.9 %collective-permute-done.15.refs_3_ = bf16[256,512]{1,0:T(8,128)(2,1)S(1)} collective-permute-done((bf16[256,512]{1,0:T(8,128)(2,1)S(1)}, bf16[256,512]{1,0:T(8,128)(2,1)S(1)}, u32[]{:S(2)}, u32[]{:S(2)}) %collective-permute-start.15) | collective-permute-done | bytes 262176 | tf_op jit(solution)/shard_map/ppermute | solution.py:453
  94.1 1.6 %collective-permute-done.14.refs_1_ = bf16[512,512]{1,0:T(8,128)(2,1)S(1)} collective-permute-done((bf16[512,512]{1,0:T(8,128)(2,1)S(1)}, bf16[512,512]{1,0:T(8,128)(2,1)S(1)}, u32[]{:S(2)}, u32[]{:S(2)}) %collective-permute-start.14) | collective-permute-done | bytes 524320 | tf_op jit(solution)/shard_map/ppermute | solution.py:453
  95.7 1.3 %finish.1 = f32[512,512]{1,0:T(8,128)} custom-call(f32[512,512]{1,0:T(8,128)S(1)} %get-tuple-element.87.refs_0_, bf16[512,512]{1,0:T(8,128)(2,1)S(1)} %collective-permute-done.14.refs_1_, bf16[256,512]{1,0:T(8,128)(2,1)S(1)} %collective-permute-done.9.refs_2_, bf16[256,512]{1,0:T(8,128)(2,1)S(1)} %collective-permute-done.15.refs_3_), custom_call_target="tpu_custom_call" | custom-call | flops 262144 | bytes 16384 | tf_op jit(solution)/shard_map/finish/pallas_call | solution.py:408
  97.0 0.0 collective-permute-done.11
  97.0 0.7 collective-permute-done.13
  97.7 1.4 %collective-permute-done.12 = bf16[256,512]{1,0:T(8,128)(2,1)S(1)} collective-permute-done((bf16[256,512]{1,0:T(8,128)(2,1)S(1)}, bf16[256,512]{1,0:T(8,128)(2,1)S(1)}, u32[]{:S(2)}, u32[]{:S(2)}) %collective-permute-start.12) | collective-permute-done | bytes 262176 | tf_op jit(solution)/shard_map/ppermute | solution.py:453
  99.1 1.0 fusion.2
Async XLA Ops:
  0.6 30.0 %collective-permute-start = (bf16[512,512]{1,0:T(8,128)(2,1)}, bf16[512,512]{1,0:T(8,128)(2,1)S(1)}, u32[]{:S(2)}, u32[]{:S(2)}) collective-permute-start(bf16[512,512]{1,0:T(8,128)(2,1)} %refs_4_.1), channel_id=1, source_target_pairs={{0,16},{8,24},{16,0},{24,8},{1,17},{9,25},{17,1},{25,9},{2,18},{10... | collective-permute-start | bytes 1572872 | tf_op jit(solution)/shard_map/ppermute | solution.py:453
  4.7 25.9 %collective-permute-start.1 = (bf16[512,512]{1,0:T(8,128)(2,1)}, bf16[512,512]{1,0:T(8,128)(2,1)S(1)}, u32[]{:S(2)}, u32[]{:S(2)}) collective-permute-start(bf16[512,512]{1,0:T(8,128)(2,1)} %refs_4_.1), channel_id=1, source_target_pairs={{0,8},{8,0},{16,24},{24,16},{1,9},{9,1},{17,25},{25,17},{2,10},{10... | collective-permute-start | bytes 1572872 | tf_op jit(solution)/shard_map/ppermute | solution.py:453
  6.4 9.5 %copy-start.1 = (bf16[256,512]{1,0:T(8,128)(2,1)S(1)}, bf16[256,512]{1,0:T(8,128)(2,1)}, u32[]{:S(2)}) copy-start(bf16[256,512]{1,0:T(8,128)(2,1)} %refs_0_.1) | copy-start | bytes 786436
  15.9 14.7 %collective-permute-start.4 = (bf16[256,512]{1,0:T(8,128)(2,1)S(1)}, bf16[256,512]{1,0:T(8,128)(2,1)S(1)}, u32[]{:S(2)}, u32[]{:S(2)}) collective-permute-start(bf16[256,512]{1,0:T(8,128)(2,1)S(1)} %copy-done.1), channel_id=1, source_target_pairs={{0,6},{1,7},{2,4},{3,5},{4,2},{5,3},{6,0},{7,1},{8,14},{9,15},{10,... | collective-permute-start | bytes 786440 | tf_op jit(solution)/shard_map/ppermute | solution.py:453
  18.4 12.2 %collective-permute-start.3 = (bf16[256,512]{1,0:T(8,128)(2,1)S(1)}, bf16[256,512]{1,0:T(8,128)(2,1)S(1)}, u32[]{:S(2)}, u32[]{:S(2)}) collective-permute-start(bf16[256,512]{1,0:T(8,128)(2,1)S(1)} %copy-done.1), channel_id=1, source_target_pairs={{0,4},{1,5},{2,6},{3,7},{4,0},{5,1},{6,2},{7,3},{8,12},{9,13},{10,... | collective-permute-start | bytes 786440 | tf_op jit(solution)/shard_map/ppermute | solution.py:453
  18.9 11.7 %collective-permute-start.2 = (bf16[256,512]{1,0:T(8,128)(2,1)S(1)}, bf16[256,512]{1,0:T(8,128)(2,1)S(1)}, u32[]{:S(2)}, u32[]{:S(2)}) collective-permute-start(bf16[256,512]{1,0:T(8,128)(2,1)S(1)} %copy-done.1), channel_id=1, source_target_pairs={{0,2},{1,3},{2,0},{3,1},{4,6},{5,7},{6,4},{7,5},{8,10},{9,11},{10,... | collective-permute-start | bytes 786440 | tf_op jit(solution)/shard_map/ppermute | solution.py:453
  30.8 6.9 %copy-start.2 = (s32[2048]{0:T(1024)S(1)}, s32[2048]{0:T(1024)}, u32[]{:S(2)}) copy-start(s32[2048]{0:T(1024)} %param.10) | copy-start | bytes 24580
  30.8 6.9 %copy-start.3 = (f32[2048]{0:T(1024)S(1)}, f32[2048]{0:T(1024)}, u32[]{:S(2)}) copy-start(f32[2048]{0:T(1024)} %param.12) | copy-start | bytes 24580
  30.8 6.9 %collective-permute-start.5 = (bf16[4,256,512]{2,1,0:T(8,128)(2,1)S(1)}, bf16[4,256,512]{2,1,0:T(8,128)(2,1)S(1)}, u32[]{:S(2)}, u32[]{:S(2)}) collective-permute-start(bf16[4,256,512]{2,1,0:T(8,128)(2,1)S(1)} %pad_maximum_fusion), channel_id=1, source_target_pairs={{0,1},{1,0},{2,3},{3,2},{4,5},{5,4},{6,7},{7,6},{8,9},{9,8},{10,11... | collective-permute-start | bytes 3145736 | tf_op jit(solution)/shard_map/ppermute | solution.py:453
  30.9 14.3 %collective-permute-start.6 = (bf16[512,512]{1,0:T(8,128)(2,1)S(1)}, bf16[512,512]{1,0:T(8,128)(2,1)S(1)}, u32[]{:S(2)}, u32[]{:S(2)}) collective-permute-start(bf16[512,512]{1,0:T(8,128)(2,1)S(1)} %collective-permute-done.refs_3_), channel_id=1, source_target_pairs={{0,8},{8,0},{16,24},{24,16},{1,9},{9,1},{17,25},{25,17},{2,10},{10... | collective-permute-start | bytes 1572872 | tf_op jit(solution)/shard_map/ppermute | solution.py:453
  50.7 9.3 %collective-permute-start.7 = (bf16[256,512]{1,0:T(8,128)(2,1)S(1)}, bf16[256,512]{1,0:T(8,128)(2,1)S(1)}, u32[]{:S(2)}, u32[]{:S(2)}) collective-permute-start(bf16[256,512]{1,0:T(8,128)(2,1)S(1)} %get-tuple-element.73), channel_id=1, source_target_pairs={{0,8},{8,0},{16,24},{24,16},{1,9},{9,1},{17,25},{25,17},{2,10},{10... | collective-permute-start | bytes 786440 | tf_op jit(solution)/shard_map/ppermute | solution.py:453
  51.2 21.1 %collective-permute-start.8 = (bf16[256,512]{1,0:T(8,128)(2,1)S(1)}, bf16[256,512]{1,0:T(8,128)(2,1)S(1)}, u32[]{:S(2)}, u32[]{:S(2)}) collective-permute-start(bf16[256,512]{1,0:T(8,128)(2,1)S(1)} %get-tuple-element.79), channel_id=1, source_target_pairs={{0,8},{8,0},{16,24},{24,16},{1,9},{9,1},{17,25},{25,17},{2,10},{10... | collective-permute-start | bytes 786440 | tf_op jit(solution)/shard_map/ppermute | solution.py:453
  52.8 7.7 %copy-start = (bf16[512,512]{1,0:T(8,128)(2,1)S(1)}, bf16[512,512]{1,0:T(8,128)(2,1)}, u32[]{:S(2)}) copy-start(bf16[512,512]{1,0:T(8,128)(2,1)} %refs_4_.1) | copy-start | bytes 1572868
  60.1 12.6 %collective-permute-start.9 = (bf16[256,512]{1,0:T(8,128)(2,1)S(1)}, bf16[256,512]{1,0:T(8,128)(2,1)S(1)}, u32[]{:S(2)}, u32[]{:S(2)}) collective-permute-start(bf16[256,512]{1,0:T(8,128)(2,1)S(1)} %add_convert_fusion.2), channel_id=1, source_target_pairs={{0,16},{8,24},{16,0},{24,8},{1,17},{9,25},{17,1},{25,9},{2,18},{10... | collective-permute-start | bytes 786440 | tf_op jit(solution)/shard_map/ppermute | solution.py:453
  75.6 6.8 %collective-permute-start.10 = (bf16[4,256,512]{2,1,0:T(8,128)(2,1)S(1)}, bf16[4,256,512]{2,1,0:T(8,128)(2,1)S(1)}, u32[]{:S(2)}, u32[]{:S(2)}) collective-permute-start(bf16[4,256,512]{2,1,0:T(8,128)(2,1)S(1)} %put_rows.3), channel_id=1, source_target_pairs={{0,1},{1,0},{2,3},{3,2},{4,5},{5,4},{6,7},{7,6},{8,9},{9,8},{10,11... | collective-permute-start | bytes 3145736 | tf_op jit(solution)/shard_map/ppermute | solution.py:453
  75.7 20.0 %collective-permute-start.14 = (bf16[512,512]{1,0:T(8,128)(2,1)S(1)}, bf16[512,512]{1,0:T(8,128)(2,1)S(1)}, u32[]{:S(2)}, u32[]{:S(2)}) collective-permute-start(bf16[512,512]{1,0:T(8,128)(2,1)S(1)} %get-tuple-element.88), channel_id=1, source_target_pairs={{0,8},{8,0},{16,24},{24,16},{1,9},{9,1},{17,25},{25,17},{2,10},{10... | collective-permute-start | bytes 1572872 | tf_op jit(solution)/shard_map/ppermute | solution.py:453
  76.7 17.4 %collective-permute-start.15 = (bf16[256,512]{1,0:T(8,128)(2,1)S(1)}, bf16[256,512]{1,0:T(8,128)(2,1)S(1)}, u32[]{:S(2)}, u32[]{:S(2)}) collective-permute-start(bf16[256,512]{1,0:T(8,128)(2,1)S(1)} %add_convert_fusion.1), channel_id=1, source_target_pairs={{0,16},{8,24},{16,0},{24,8},{1,17},{9,25},{17,1},{25,9},{2,18},{10... | collective-permute-start | bytes 786440 | tf_op jit(solution)/shard_map/ppermute | solution.py:453
  82.9 14.1 %collective-permute-start.11 = (bf16[256,512]{1,0:T(8,128)(2,1)S(1)}, bf16[256,512]{1,0:T(8,128)(2,1)S(1)}, u32[]{:S(2)}, u32[]{:S(2)}) collective-permute-start(bf16[256,512]{1,0:T(8,128)(2,1)S(1)} %get-tuple-element.90), channel_id=1, source_target_pairs={{0,2},{1,3},{2,0},{3,1},{4,6},{5,7},{6,4},{7,5},{8,10},{9,11},{10,... | collective-permute-start | bytes 786440 | tf_op jit(solution)/shard_map/ppermute | solution.py:453
  84.4 13.3 %collective-permute-start.13 = (bf16[256,512]{1,0:T(8,128)(2,1)S(1)}, bf16[256,512]{1,0:T(8,128)(2,1)S(1)}, u32[]{:S(2)}, u32[]{:S(2)}) collective-permute-start(bf16[256,512]{1,0:T(8,128)(2,1)S(1)} %get-tuple-element.91), channel_id=1, source_target_pairs={{0,6},{1,7},{2,4},{3,5},{4,2},{5,3},{6,0},{7,1},{8,14},{9,15},{10,... | collective-permute-start | bytes 786440 | tf_op jit(solution)/shard_map/ppermute | solution.py:453
  85.9 13.2 %collective-permute-start.12 = (bf16[256,512]{1,0:T(8,128)(2,1)S(1)}, bf16[256,512]{1,0:T(8,128)(2,1)S(1)}, u32[]{:S(2)}, u32[]{:S(2)}) collective-permute-start(bf16[256,512]{1,0:T(8,128)(2,1)S(1)} %get-tuple-element.92), channel_id=1, source_target_pairs={{0,4},{1,5},{2,6},{3,7},{4,0},{5,1},{6,2},{7,3},{8,12},{9,13},{10,... | collective-permute-start | bytes 786440 | tf_op jit(solution)/shard_map/ppermute | solution.py:453

commit v3 on v2

--- a/solution.py
+++ b/solution.py
@@ -88,10 +88,13 @@
     return made
 
 
-def fill_pick(pick, columns, base, groups):
-    vocab = (lax.broadcasted_iota(jnp.int32, (LANES, pick.shape[1]), 1) + base).astype(F32)
-    for group in groups:
-        pick[pl.ds(group * LANES, LANES), :] = onehot(columns[:, group : group + 1] == vocab)
+def fill_pick(pick, spread, base, first, count):
+    width = pick.shape[1]
+    vocab = (lax.broadcasted_iota(jnp.int32, (LANES, width), 1) + base).astype(F32)
+    for at in range(0, count, LANES):
+        here = pl.ds(pl.multiple_of(first + at, LANES), LANES)
+        index = jnp.concatenate([spread[here, :]] * (width // LANES), axis=1)
+        pick[here, :] = onehot(index == vocab)
 
 
 def chunk_base(scalars, offset, width):
@@ -105,31 +108,29 @@
     aux_ref[pl.ds(rows, 8), :] = moved[rows : rows + 8] + moved[rows + 8 : rows + 16] + moved[rows + 16 :]
 
 
-def order_first_kernel(offsets, scalars, perm_hbm, mask_hbm, logm_hbm, count_hbm, *refs):
-    parts = len(offsets)
-    outs, auxes, refs = refs[:parts], refs[parts : 2 * parts], refs[2 * parts :]
-    shifted_ref, columns_ref, values_ref, perm, mask_ref, logm_ref, tiles, pick, sems, tile_sems = refs
-    depth = pick.shape[1]
-    width = pick.shape[2]
-    rows = outs[0].shape[0]
+def order_first_kernel(offset, scalars, perm_hbm, mask_hbm, logm_hbm, count_hbm, *refs):
+    out_ref, aux_ref, shifted_ref, spread_ref, values_ref, refs = *refs[:5], refs[5:]
+    perm, mask_ref, logm_ref, tiles, held, pick, sems, tile_sems = refs
+    depth, width = pick.shape
+    rows = out_ref.shape[0]
     step = tiles.shape[1]
-    steps = rows // step
-
-    slots = tiles.shape[0]
-
-    def tile_copy(at):
-        slot = lax.rem(at, slots)
+    pairs = rows // step // 2
+
+    def tile_copy(at, slot):
         return pltpu.make_async_copy(
             count_hbm.at[pl.ds(pl.multiple_of(at * step, step), step)], tiles.at[slot], tile_sems.at[slot]
         )
 
     small = copies([(perm_hbm, perm), (mask_hbm, mask_ref), (logm_hbm, logm_ref)], sems)
-    for at in range(slots):
-        tile_copy(at).start()
+    for slot in range(2):
+        tile_copy(slot, slot).start()
     for copy in small:
         copy.wait()
     columns = along_sublanes((perm[...] - scalars[COL_AT] * depth).astype(F32))
-    columns_ref[...] = columns
+    for group in range(depth // LANES):
+        spread_ref[pl.ds(group * LANES, LANES), :] = jnp.broadcast_to(
+            columns[:, group : group + 1], (LANES, LANES)
+        )
     blocks_r, blocks_c = mask_ref.shape
     mask = mask_ref[...].astype(F32)
     side = (blocks_r, depth // blocks_c)
@@ -139,46 +140,51 @@
     logm = jnp.broadcast_to(logm_ref[...], (8, depth))
     values = jnp.concatenate([active, *[piece.astype(F32) for piece in pieces_of(logm)]], axis=0)
     values_ref[...] = values
-    values = values.astype(BF16)
-    for part, offset in enumerate(offsets):
-        fill_pick(pick.at[part], columns, chunk_base(scalars, offset, width), range(depth // LANES))
-        move_values(values, pick.at[part], auxes[part])
-
-    @pl.loop(0, steps)
-    def _(at):
-        here = pl.ds(pl.multiple_of(at * step, step), step)
-        tile_copy(at).wait()
-        shifted = (tiles[lax.rem(at, slots)] - 256).astype(F32).astype(BF16)
-        shifted_ref[here, :] = shifted
-
-        @pl.when(at + slots < steps)
+    fill_pick(pick, spread_ref, chunk_base(scalars, offset, width), 0, depth)
+    move_values(values.astype(BF16), pick, aux_ref)
+
+    def shift(at, slot):
+        tile_copy(at, slot).wait()
+        shifted = (tiles[slot] - 256).astype(F32).astype(BF16)
+        held[slot] = shifted
+        shifted_ref[pl.ds(pl.multiple_of(at * step, step), step), :] = shifted
+
+    def move(at, slot):
+        moved = jnp.dot(held[slot], pick[...], preferred_element_type=F32)
+        out_ref[pl.ds(pl.multiple_of(at * step, step), step), :] = moved.astype(BF16)
+
+    @pl.loop(0, pairs)
+    def _(pair):
+        shift(2 * pair, 0)
+        move(2 * pair, 0)
+        shift(2 * pair + 1, 1)
+
+        @pl.when(pair + 1 < pairs)
         def _():
-            tile_copy(at + slots).start()
-
-        for part in range(parts):
-            moved = jnp.dot(shifted, pick[part], preferred_element_type=F32)
-            outs[part][here, :] = moved.astype(BF16)
+            for slot in range(2):
+                tile_copy(2 * pair + 2 + slot, slot).start()
+
+        move(2 * pair + 1, 1)
 
 
 def in_hbm(value):
     return pltpu.with_memory_space_constraint(value, pltpu.HBM)
 
 
-def order_first(scalars, col_perm, block_mask, col_logm, counts, offsets, width):
+def order_first(scalars, col_perm, block_mask, col_logm, counts, offset, width):
     rows, cols = counts.shape
-    parts = len(offsets)
     blocks = block_mask.shape[0]
     outside = pl.BlockSpec(memory_space=pltpu.HBM)
-    step = 512
+    step = 256
     return pl.pallas_call(
-        functools.partial(order_first_kernel, offsets),
+        functools.partial(order_first_kernel, offset),
         in_specs=[SCALARS] + [outside] * 4,
-        out_specs=[WHOLE] * (2 * parts + 3),
-        out_shape=[jax.ShapeDtypeStruct((rows, width), BF16)] * parts
-        + [jax.ShapeDtypeStruct((blocks + 8, width), F32)] * parts
-        + [
+        out_specs=[WHOLE] * 5,
+        out_shape=[
+            jax.ShapeDtypeStruct((rows, width), BF16),
+            jax.ShapeDtypeStruct((blocks + 8, width), F32),
             jax.ShapeDtypeStruct((rows, cols), BF16),
-            jax.ShapeDtypeStruct((LANES, LANES), F32),
+            jax.ShapeDtypeStruct((cols, LANES), F32),
             jax.ShapeDtypeStruct((blocks + 24, cols), F32),
         ],
         scratch_shapes=[
@@ -186,36 +192,39 @@
             pltpu.VMEM(block_mask.shape, jnp.int32),
             pltpu.VMEM((1, cols), F32),
             pltpu.VMEM((2, step, cols), jnp.int32),
-            pltpu.VMEM((parts, cols, width), BF16),
+            pltpu.VMEM((2, step, cols), BF16),
+            pltpu.VMEM((cols, width), BF16),
             pltpu.SemaphoreType.DMA((3,)),
             pltpu.SemaphoreType.DMA((2,)),
         ],
-        compiler_params=params(28),
-        cost_estimate=cost(2 * parts * rows * cols * width, 4 * rows * cols),
+        compiler_params=params(24),
+        cost_estimate=cost(2 * rows * cols * width, 4 * rows * cols),
         name="order_first",
     )(scalars, *[in_hbm(each) for each in (col_perm.reshape(-1, LANES), block_mask, col_logm[None, :], counts)])
 
 
-def order_next_kernel(offsets, scalars, shifted_ref, columns_ref, values_ref, *refs):
+def order_next_kernel(offsets, scalars, shifted_ref, spread_ref, values_ref, *refs):
     parts = len(offsets)
-    outs, auxes, pick = refs[:parts], refs[parts : 2 * parts], refs[-1]
-    depth, width = pick.shape[1:]
+    outs, auxes, picks = refs[:parts], refs[parts : 2 * parts], refs[2 * parts :]
+    depth, width = picks[0].shape
+    bases = [chunk_base(scalars, offset, width) for offset in offsets]
     values = values_ref[...].astype(BF16)
-    for part, offset in enumerate(offsets):
-        base = chunk_base(scalars, offset, width)
-        fill_pick(pick.at[part], columns_ref[...], base, range(depth // LANES))
-        move_values(values, pick.at[part], auxes[part])
     step = 512
-
-    @pl.loop(0, shifted_ref.shape[0] // step)
-    def _(at):
-        here = pl.ds(pl.multiple_of(at * step, step), step)
-        for part in range(parts):
-            moved = jnp.dot(shifted_ref[here, :], pick[part], preferred_element_type=F32)
+    steps = shifted_ref.shape[0] // step
+    fill_pick(picks[0], spread_ref, bases[0], 0, depth)
+    for part in range(parts):
+        move_values(values, picks[part], auxes[part])
+
+        @pl.loop(0, steps)
+        def _(at):
+            here = pl.ds(pl.multiple_of(at * step, step), step)
+            moved = jnp.dot(shifted_ref[here, :], picks[part][...], preferred_element_type=F32)
             outs[part][here, :] = moved.astype(BF16)
-
-
-def order_next(scalars, shifted, columns, values, offsets, width):
+            if part + 1 < parts:
+                fill_pick(picks[part + 1], spread_ref, bases[part + 1], at * (depth // steps), depth // steps)
+
+
+def order_next(scalars, shifted, spread, values, offsets, width):
     rows, cols = shifted.shape
     parts = len(offsets)
     return pl.pallas_call(
@@ -224,11 +233,11 @@
         out_specs=[WHOLE] * (2 * parts),
         out_shape=[jax.ShapeDtypeStruct((rows, width), BF16)] * parts
         + [jax.ShapeDtypeStruct((values.shape[0] - 16, width), F32)] * parts,
-        scratch_shapes=[pltpu.VMEM((parts, cols, width), BF16)],
+        scratch_shapes=[pltpu.VMEM((cols, width), BF16)] * parts,
         compiler_params=params(24),
         cost_estimate=cost(rows * width, rows * width),
         name="order_next",
-    )(scalars, shifted, columns, values)
+    )(scalars, shifted, spread, values)
 
 
 def take_kernel(scalars, perm_ref, logm_ref, *refs):
@@ -416,7 +425,7 @@
     )(own, near, *crosses)
 
 
-def put_kernel(offsets, exact, scalars, perm_ref, grad_ref, out_ref):
+def put_kernel(offsets, exact, scalars, perm_ref, grad_ref, out_ref, pick):
     grad = grad_ref[...]
     rows, width = grad.shape
     high = grad.astype(BF16)
@@ -428,11 +437,11 @@
     vocab = lax.broadcasted_iota(jnp.int32, (side, rows), 0)
     for at, offset in enumerate(offsets):
         base = jnp.bitwise_xor(scalars[COL_AT], offset) * side
-        pick = onehot(index == (vocab + base).astype(F32))
-        moved = jnp.dot(pick, moving, preferred_element_type=F32)
-        if exact:
-            moved = moved[:, :width] + moved[:, width:]
-        out_ref[at] = moved.astype(out_ref.dtype)
+        pick[pl.ds(at * side, side), :] = onehot(index == (vocab + base).astype(F32))
+    moved = jnp.dot(pick[...], moving, preferred_element_type=F32)
+    if exact:
+        moved = moved[:, :width] + moved[:, width:]
+    out_ref[...] = moved.astype(out_ref.dtype).reshape(out_ref.shape)
 
 
 def put_rows(scalars, row_perm, grad, offsets, side, exact):
@@ -442,6 +451,7 @@
         in_specs=[SCALARS, WHOLE, WHOLE],
         out_specs=WHOLE,
         out_shape=jax.ShapeDtypeStruct((len(offsets), side, width), F32 if exact else BF16),
+        scratch_shapes=[pltpu.VMEM((len(offsets) * side, grad.shape[0]), BF16)],
         compiler_params=params(24),
         cost_estimate=cost((4096 if exact and len(offsets) > 1 else 1) * grad.size, grad.size // 16),
         name="put_rows",
@@ -465,21 +475,21 @@
 
     cross = swap(col_emb, "row", 2)
     near = swap(col_emb, "row", 1)
-    count_far, aux_far, shifted, columns, values = order_first(
-        scalars, col_perm, block_mask, col_logm, counts, (3,), width
+    count_far, aux_far, shifted, spread, values = order_first(
+        scalars, col_perm, block_mask, col_logm, counts, 3, width
     )
     ordered = functools.partial(order_next, scalars)
     row_block, shifted = together((row_emb, shifted))
     from_x = swap(row_block, "col", 2)
     from_y = swap(row_block, "col", 4)
     from_xy = swap(row_block, "col", 6)
-    count_cross, count_near, aux_cross, aux_near = ordered(shifted, columns, values, (2, 1), width)
+    count_cross, count_near, aux_cross, aux_near = ordered(shifted, spread, values, (2, 1), width)
     cross, near, from_x, from_y, from_xy, count_near, shifted = together(
         (cross, near, from_x, from_y, from_xy, count_near, shifted)
     )
     far = swap(cross, "row", 1)
     from_core = swap(jnp.stack([row_emb, from_x, from_y, from_xy]), "col", 1)
-    count_own, aux_own = ordered(shifted, columns, values, (0,), width)
+    count_own, aux_own = ordered(shifted, spread, values, (0,), width)
     count_own, row_perm = together((count_own, row_perm))
     blocks = [row_emb, from_x, from_y, from_xy, from_core]
     wvec, turned, logm = take_rows(scalars, row_perm, row_logm, blocks)
@@ -510,7 +520,7 @@
     grad, away = together((grad, away))
     both = ordered(grad, (2, 4, 6), side, True) + core[1:].astype(F32)
     sends = [both[at].astype(BF16) for at in range(3)]
-    got = [swap(sent, "col", bit) for sent, bit in zip(sends, (2, 4, 6))]
+    got = [swap(sends[at], "col", bit) for at, bit in ((1, 4), (2, 6), (0, 2))]
     grad, sends = together((grad, sends))
     home = ordered(grad, (0,), side, True)
     home, term_own = together((home, term_own))

time: 100 us -> 103 us (1.030)
  Pallas kernels: 65.3 us -> 69.1 us
    pallas_call x1, Pallas kernels: 9.47 us -> 12.9 us  [order_first(): pl.pallas_call(functools.partial(order_first_kernel, offset), in_specs=[S...]
  transfers between devices with their start and end apart: 16 -> 16, of which waited for: 7 -> 6; matrix products, arithmetic and copies ran while one was open for 1% -> 0% of each run, Pallas kernels for 57% -> 59%
where the time goes in v3:
time: 103 us
  Pallas kernels  69.1 us (67%)
  starting transfers between devices  18.6 us (18%)
  waiting for transfers between devices  12.5 us (12%)
  other arithmetic  1.64 us (2%)
    pallas_call x3, Pallas kernels, cells(): pl.pallas_call(functools.partial(cells_kernel, before is not None, sends)...  23.1 us
    ppermute x16, starting transfers between devices, swap(): return lax.ppermute(value, axis, pairs)  18.6 us
    pallas_call x2, Pallas kernels, order_next(): pl.pallas_call(functools.partial(order_next_kernel, offsets), in_specs=[S...  18 us
    pallas_call x1, Pallas kernels, order_first(): pl.pallas_call(functools.partial(order_first_kernel, offset), in_specs=[S...  12.9 us
    ppermute x16, waiting for transfers between devices, swap(): return lax.ppermute(value, axis, pairs)  12.5 us
    pallas_call x3, Pallas kernels, put_rows(): pl.pallas_call(functools.partial(put_kernel, offsets, exact), in_specs=[S...  8.62 us
    pallas_call x1, Pallas kernels, take_rows(): pl.pallas_call(take_kernel, in_specs=[SCALARS] + [WHOLE] * 7, out_specs=[...  5.32 us
  transfers between devices with their start and end apart: 16, of which 6 were waited for; matrix products, arithmetic and copies ran while one was open for 0% of the time, Pallas kernels for 59%

profile of v3, /device:TPU:0, one launch (start us, length us, event | category | flops | bytes accessed | tf_op | source)
XLA Modules:
  0.0 102.8 jit_solution(14026145163349086985)
XLA Ops:
  0.6 4.1 %collective-permute-start = (bf16[512,512]{1,0:T(8,128)(2,1)}, bf16[512,512]{1,0:T(8,128)(2,1)S(1)}, u32[]{:S(2)}, u32[]{:S(2)}) collective-permute-start(bf16[512,512]{1,0:T(8,128)(2,1)} %refs_4_.1), channel_id=1, source_target_pairs={{0,16},{8,24},{16,0},{24,8},{1,17},{9,25},{17,1},{25,9},{2,18},{10... | collective-permute-start | bytes 1572872 | tf_op jit(solution)/shard_map/ppermute | solution.py:463
  4.7 1.6 %collective-permute-start.1 = (bf16[512,512]{1,0:T(8,128)(2,1)}, bf16[512,512]{1,0:T(8,128)(2,1)S(1)}, u32[]{:S(2)}, u32[]{:S(2)}) collective-permute-start(bf16[512,512]{1,0:T(8,128)(2,1)} %refs_4_.1), channel_id=1, source_target_pairs={{0,8},{8,0},{16,24},{24,16},{1,9},{9,1},{17,25},{25,17},{2,10},{10... | collective-permute-start | bytes 1572872 | tf_op jit(solution)/shard_map/ppermute | solution.py:463
  6.3 0.1 pad_add_fusion.scalars
  6.4 0.0 copy-start.1
  6.4 12.9 %order_first.1 = (bf16[2048,512]{1,0:T(8,128)(2,1)S(1)}, f32[16,512]{1,0:T(8,128)S(1)}, bf16[2048,2048]{1,0:T(8,128)(2,1)S(1)}, f32[2048,128]{1,0:T(8,128)S(1)}, f32[32,2048]{1,0:T(8,128)S(1)}) custom-call(s32[2]{0:T(128)S(1)} %pad_add_fusion.scalars, s32[16,128]{1,0:T(8,128)} %bitcast.34, s32[8,8]{1,0:T(8,128)} %mask_hbm.1, f32[1,2048]{1,0:T(1,128)} %bitcast.35, ...), custom_call_target="tpu_custom_call" | custom-call | flops 4294967296 | bytes 16777216 | tf_op jit(solution)/shard_map/order_first/pallas_call | solution.py:179
  19.3 0.0 copy-done.1
  19.3 2.5 %collective-permute-start.4 = (bf16[256,512]{1,0:T(8,128)(2,1)S(1)}, bf16[256,512]{1,0:T(8,128)(2,1)S(1)}, u32[]{:S(2)}, u32[]{:S(2)}) collective-permute-start(bf16[256,512]{1,0:T(8,128)(2,1)S(1)} %copy-done.1), channel_id=1, source_target_pairs={{0,6},{1,7},{2,4},{3,5},{4,2},{5,3},{6,0},{7,1},{8,14},{9,15},{10,... | collective-permute-start | bytes 786440 | tf_op jit(solution)/shard_map/ppermute | solution.py:463
  21.7 0.5 collective-permute-start.3
  22.2 0.6 collective-permute-start.2
  22.8 11.9 %order_next.2 = (bf16[2048,512]{1,0:T(8,128)(2,1)S(1)}, bf16[2048,512]{1,0:T(8,128)(2,1)S(1)}, f32[16,512]{1,0:T(8,128)S(1)}, f32[16,512]{1,0:T(8,128)S(1)}) custom-call(s32[2]{0:T(128)S(1)} %pad_add_fusion.scalars, bf16[2048,2048]{1,0:T(8,128)(2,1)S(1)} %get-tuple-element.52.shifted_ref, f32[2048,128]{1,0:T(8,128)S(1)} %get-tuple-element.49.spread_ref, ...), custom_call_target="tpu_custom_call" | custom-call | flops 1048576 | bytes 1048576 | tf_op jit(solution)/shard_map/order_next/pallas_call | solution.py:230
  34.7 0.0 collective-permute-done.4.refs_3_
  34.7 0.0 collective-permute-done.3.refs_2_
  34.7 0.0 collective-permute-done.2.refs_1_
  34.7 0.0 collective-permute-done.refs_3_
  34.7 0.0 collective-permute-done.1.refs_3_
  34.8 0.1 pad_maximum_fusion
  34.9 0.0 copy-start.2
  34.9 0.0 copy-start.3
  34.9 0.1 collective-permute-start.5
  35.0 0.5 collective-permute-start.6
  35.5 6.1 %order_next.3 = (bf16[2048,512]{1,0:T(8,128)(2,1)S(1)}, f32[16,512]{1,0:T(8,128)S(1)}) custom-call(s32[2]{0:T(128)S(1)} %pad_add_fusion.scalars, bf16[2048,2048]{1,0:T(8,128)(2,1)S(1)} %get-tuple-element.52.shifted_ref, f32[2048,128]{1,0:T(8,128)S(1)} %get-tuple-element.49.spread_ref, f32[32,2048]{1,0:T(8,128)S(1)} %get-tuple-element.50.values_ref), custom_call_target="tpu_custom_call" | custom-call | flops 1048576 | bytes 1048576 | tf_op jit(solution)/shard_map/order_next/pallas_call | solution.py:230
  41.6 0.0 collective-permute-done.5.refs_4_
  41.6 0.0 copy-done.2
  41.6 0.0 copy-done.3
  41.6 5.3 %take_rows.1 = (bf16[2048,512]{1,0:T(8,128)(2,1)S(1)}, bf16[512,2048]{1,0:T(8,128)(2,1)S(1)}, f32[2048,128]{1,0:T(8,128)S(1)}) custom-call(s32[2]{0:T(128)S(1)} %pad_add_fusion.scalars, s32[16,128]{1,0:T(8,128)S(1)} %bitcast.29, f32[16,128]{1,0:T(8,128)S(1)} %bitcast.33, bf16[256,512]{1,0:T(8,128)(2,1)S(1)} %copy-done.1, ...), custom_call_target="tpu_custom_call" | custom-call | flops 4294967296 | bytes 4194304 | tf_op jit(solution)/shard_map/take_rows/pallas_call | solution.py:274
  47.0 2.4 %collective-permute-done.6.refs_3_ = bf16[512,512]{1,0:T(8,128)(2,1)S(1)} collective-permute-done((bf16[512,512]{1,0:T(8,128)(2,1)S(1)}, bf16[512,512]{1,0:T(8,128)(2,1)S(1)}, u32[]{:S(2)}, u32[]{:S(2)}) %collective-permute-start.6) | collective-permute-done | bytes 524320 | tf_op jit(solution)/shard_map/ppermute | solution.py:463
  49.3 5.4 %cells.3 = (f32[2048,512]{1,0:T(8,128)S(1)}, bf16[256,512]{1,0:T(8,128)(2,1)S(1)}, bf16[256,512]{1,0:T(8,128)(2,1)S(1)}) custom-call(bf16[2048,512]{1,0:T(8,128)(2,1)S(1)} %get-tuple-element.58.refs_0_, bf16[512,2048]{1,0:T(8,128)(2,1)S(1)} %get-tuple-element.59.refs_1_, f32[2048,128]{1,0:T(8,128)S(1)} %get-tuple-element.60.refs_2_, ...), custom_call_target="tpu_custom_call" | custom-call | flops 1048576 | bytes 1048576 | tf_op jit(solution)/shard_map/cells/pallas_call | solution.py:390
  54.8 0.5 collective-permute-start.7
  55.3 1.6 %collective-permute-start.8 = (bf16[256,512]{1,0:T(8,128)(2,1)S(1)}, bf16[256,512]{1,0:T(8,128)(2,1)S(1)}, u32[]{:S(2)}, u32[]{:S(2)}) collective-permute-start(bf16[256,512]{1,0:T(8,128)(2,1)S(1)} %get-tuple-element.79), channel_id=1, source_target_pairs={{0,8},{8,0},{16,24},{24,16},{1,9},{9,1},{17,25},{25,17},{2,10},{10... | collective-permute-start | bytes 786440 | tf_op jit(solution)/shard_map/ppermute | solution.py:463
  56.9 0.0 copy-start
  56.9 5.8 %cells.4 = (f32[2048,512]{1,0:T(8,128)S(1)}, f32[512,512]{1,0:T(8,128)S(1)}) custom-call(bf16[2048,512]{1,0:T(8,128)(2,1)S(1)} %get-tuple-element.58.refs_0_, bf16[512,2048]{1,0:T(8,128)(2,1)S(1)} %get-tuple-element.59.refs_1_, f32[2048,128]{1,0:T(8,128)S(1)} %get-tuple-element.60.refs_2_, ...), custom_call_target="tpu_custom_call", output_to_operand_aliasing={{0}: (6, {})} | custom-call | flops 1048576 | bytes 1048576 | tf_op jit(solution)/shard_map/cells/pallas_call | solution.py:390
  62.7 1.3 %collective-permute-done.7 = bf16[256,512]{1,0:T(8,128)(2,1)S(1)} collective-permute-done((bf16[256,512]{1,0:T(8,128)(2,1)S(1)}, bf16[256,512]{1,0:T(8,128)(2,1)S(1)}, u32[]{:S(2)}, u32[]{:S(2)}) %collective-permute-start.7) | collective-permute-done | bytes 262176 | tf_op jit(solution)/shard_map/ppermute | solution.py:463
  64.1 0.1 add_convert_fusion.2
  64.1 0.4 collective-permute-start.9
  64.5 0.0 copy-done
  64.5 11.8 %cells.5 = (f32[2048,512]{1,0:T(8,128)S(1)}, bf16[512,512]{1,0:T(8,128)(2,1)S(1)}, f32[512,512]{1,0:T(8,128)S(1)}) custom-call(bf16[2048,512]{1,0:T(8,128)(2,1)S(1)} %get-tuple-element.58.refs_0_, bf16[512,2048]{1,0:T(8,128)(2,1)S(1)} %get-tuple-element.59.refs_1_, f32[2048,128]{1,0:T(8,128)S(1)} %get-tuple-element.60.refs_2_, ...), custom_call_target="tpu_custom_call", output_to_operand_aliasing={{0}: (9, {})} | custom-call | flops 1048576 | bytes 1048576 | tf_op jit(solution)/shard_map/cells/pallas_call | solution.py:390
  76.3 0.0 collective-permute-done.8
  76.3 0.4 collective-permute-done.9.refs_2_
  76.8 0.1 add_convert_fusion.1
  76.8 2.9 %put_rows.3 = bf16[4,256,512]{2,1,0:T(8,128)(2,1)S(1)} custom-call(s32[2]{0:T(128)S(1)} %pad_add_fusion.scalars, s32[1,2048]{1,0:T(1,128)S(1)} %bitcast.30, f32[2048,512]{1,0:T(8,128)S(1)} %get-tuple-element.84.grad_ref), custom_call_target="tpu_custom_call" | custom-call | flops 1048576 | bytes 65536 | tf_op jit(solution)/shard_map/put_rows/pallas_call | solution.py:449
  79.7 0.1 collective-permute-start.10
  79.8 0.1 collective-permute-start.14
  79.9 2.6 %collective-permute-start.15 = (bf16[256,512]{1,0:T(8,128)(2,1)S(1)}, bf16[256,512]{1,0:T(8,128)(2,1)S(1)}, u32[]{:S(2)}, u32[]{:S(2)}) collective-permute-start(bf16[256,512]{1,0:T(8,128)(2,1)S(1)} %add_convert_fusion.1), channel_id=1, source_target_pairs={{0,16},{8,24},{16,0},{24,8},{1,17},{9,25},{17,1},{25,9},{2,18},{10... | collective-permute-start | bytes 786440 | tf_op jit(solution)/shard_map/ppermute | solution.py:463
  82.5 3.9 %put_rows.4 = f32[3,256,512]{2,1,0:T(8,128)S(1)} custom-call(s32[2]{0:T(128)S(1)} %pad_add_fusion.scalars, s32[1,2048]{1,0:T(1,128)S(1)} %bitcast.31, f32[2048,512]{1,0:T(8,128)S(1)} %get-tuple-element.84.grad_ref), custom_call_target="tpu_custom_call" | custom-call | flops 4294967296 | bytes 65536 | tf_op jit(solution)/shard_map/put_rows/pallas_call | solution.py:449
  86.5 0.0 collective-permute-done.10
  86.5 0.3 add_convert_fusion
  86.8 0.1 slice_bitcast_fusion.1
  86.9 1.6 %collective-permute-start.11 = (bf16[256,512]{1,0:T(8,128)(2,1)S(1)}, bf16[256,512]{1,0:T(8,128)(2,1)S(1)}, u32[]{:S(2)}, u32[]{:S(2)}) collective-permute-start(bf16[256,512]{1,0:T(8,128)(2,1)S(1)} %get-tuple-element.90), channel_id=1, source_target_pairs={{0,4},{1,5},{2,6},{3,7},{4,0},{5,1},{6,2},{7,3},{8,12},{9,13},{10,... | collective-permute-start | bytes 786440 | tf_op jit(solution)/shard_map/ppermute | solution.py:463
  88.4 1.4 %collective-permute-start.12 = (bf16[256,512]{1,0:T(8,128)(2,1)S(1)}, bf16[256,512]{1,0:T(8,128)(2,1)S(1)}, u32[]{:S(2)}, u32[]{:S(2)}) collective-permute-start(bf16[256,512]{1,0:T(8,128)(2,1)S(1)} %get-tuple-element.91), channel_id=1, source_target_pairs={{0,6},{1,7},{2,4},{3,5},{4,2},{5,3},{6,0},{7,1},{8,14},{9,15},{10,... | collective-permute-start | bytes 786440 | tf_op jit(solution)/shard_map/ppermute | solution.py:463
  89.8 0.6 collective-permute-start.13
  90.4 1.8 %put_rows.5 = f32[1,256,512]{2,1,0:T(8,128)S(1)} custom-call(s32[2]{0:T(128)S(1)} %pad_add_fusion.scalars, s32[1,2048]{1,0:T(1,128)S(1)} %bitcast.32, f32[2048,512]{1,0:T(8,128)S(1)} %get-tuple-element.84.grad_ref), custom_call_target="tpu_custom_call" | custom-call | flops 1048576 | bytes 65536 | tf_op jit(solution)/shard_map/put_rows/pallas_call | solution.py:449
  92.2 5.3 %collective-permute-done.15.refs_3_ = bf16[256,512]{1,0:T(8,128)(2,1)S(1)} collective-permute-done((bf16[256,512]{1,0:T(8,128)(2,1)S(1)}, bf16[256,512]{1,0:T(8,128)(2,1)S(1)}, u32[]{:S(2)}, u32[]{:S(2)}) %collective-permute-start.15) | collective-permute-done | bytes 262176 | tf_op jit(solution)/shard_map/ppermute | solution.py:463
  97.5 2.2 %collective-permute-done.14.refs_1_ = bf16[512,512]{1,0:T(8,128)(2,1)S(1)} collective-permute-done((bf16[512,512]{1,0:T(8,128)(2,1)S(1)}, bf16[512,512]{1,0:T(8,128)(2,1)S(1)}, u32[]{:S(2)}, u32[]{:S(2)}) %collective-permute-start.14) | collective-permute-done | bytes 524320 | tf_op jit(solution)/shard_map/ppermute | solution.py:463
  99.8 1.3 %finish.1 = f32[512,512]{1,0:T(8,128)} custom-call(f32[512,512]{1,0:T(8,128)S(1)} %get-tuple-element.87.refs_0_, bf16[512,512]{1,0:T(8,128)(2,1)S(1)} %collective-permute-done.14.refs_1_, bf16[256,512]{1,0:T(8,128)(2,1)S(1)} %collective-permute-done.9.refs_2_, bf16[256,512]{1,0:T(8,128)(2,1)S(1)} %collective-permute-done.15.refs_3_), custom_call_target="tpu_custom_call" | custom-call | flops 262144 | bytes 16384 | tf_op jit(solution)/shard_map/finish/pallas_call | solution.py:417
  101.1 0.0 collective-permute-done.11
  101.1 0.0 collective-permute-done.12
  101.1 0.8 collective-permute-done.13
  101.9 1.0 fusion.2
Async XLA Ops:
  0.6 34.1 %collective-permute-start = (bf16[512,512]{1,0:T(8,128)(2,1)}, bf16[512,512]{1,0:T(8,128)(2,1)S(1)}, u32[]{:S(2)}, u32[]{:S(2)}) collective-permute-start(bf16[512,512]{1,0:T(8,128)(2,1)} %refs_4_.1), channel_id=1, source_target_pairs={{0,16},{8,24},{16,0},{24,8},{1,17},{9,25},{17,1},{25,9},{2,18},{10... | collective-permute-start | bytes 1572872 | tf_op jit(solution)/shard_map/ppermute | solution.py:463
  4.7 30.0 %collective-permute-start.1 = (bf16[512,512]{1,0:T(8,128)(2,1)}, bf16[512,512]{1,0:T(8,128)(2,1)S(1)}, u32[]{:S(2)}, u32[]{:S(2)}) collective-permute-start(bf16[512,512]{1,0:T(8,128)(2,1)} %refs_4_.1), channel_id=1, source_target_pairs={{0,8},{8,0},{16,24},{24,16},{1,9},{9,1},{17,25},{25,17},{2,10},{10... | collective-permute-start | bytes 1572872 | tf_op jit(solution)/shard_map/ppermute | solution.py:463
  6.4 12.9 %copy-start.1 = (bf16[256,512]{1,0:T(8,128)(2,1)S(1)}, bf16[256,512]{1,0:T(8,128)(2,1)}, u32[]{:S(2)}) copy-start(bf16[256,512]{1,0:T(8,128)(2,1)} %refs_0_.1) | copy-start | bytes 786436
  19.3 15.4 %collective-permute-start.4 = (bf16[256,512]{1,0:T(8,128)(2,1)S(1)}, bf16[256,512]{1,0:T(8,128)(2,1)S(1)}, u32[]{:S(2)}, u32[]{:S(2)}) collective-permute-start(bf16[256,512]{1,0:T(8,128)(2,1)S(1)} %copy-done.1), channel_id=1, source_target_pairs={{0,6},{1,7},{2,4},{3,5},{4,2},{5,3},{6,0},{7,1},{8,14},{9,15},{10,... | collective-permute-start | bytes 786440 | tf_op jit(solution)/shard_map/ppermute | solution.py:463
  21.7 13.0 %collective-permute-start.3 = (bf16[256,512]{1,0:T(8,128)(2,1)S(1)}, bf16[256,512]{1,0:T(8,128)(2,1)S(1)}, u32[]{:S(2)}, u32[]{:S(2)}) collective-permute-start(bf16[256,512]{1,0:T(8,128)(2,1)S(1)} %copy-done.1), channel_id=1, source_target_pairs={{0,4},{1,5},{2,6},{3,7},{4,0},{5,1},{6,2},{7,3},{8,12},{9,13},{10,... | collective-permute-start | bytes 786440 | tf_op jit(solution)/shard_map/ppermute | solution.py:463
  22.2 12.5 %collective-permute-start.2 = (bf16[256,512]{1,0:T(8,128)(2,1)S(1)}, bf16[256,512]{1,0:T(8,128)(2,1)S(1)}, u32[]{:S(2)}, u32[]{:S(2)}) collective-permute-start(bf16[256,512]{1,0:T(8,128)(2,1)S(1)} %copy-done.1), channel_id=1, source_target_pairs={{0,2},{1,3},{2,0},{3,1},{4,6},{5,7},{6,4},{7,5},{8,10},{9,11},{10,... | collective-permute-start | bytes 786440 | tf_op jit(solution)/shard_map/ppermute | solution.py:463
  34.9 6.7 %copy-start.2 = (s32[2048]{0:T(1024)S(1)}, s32[2048]{0:T(1024)}, u32[]{:S(2)}) copy-start(s32[2048]{0:T(1024)} %param.10) | copy-start | bytes 24580
  34.9 6.7 %copy-start.3 = (f32[2048]{0:T(1024)S(1)}, f32[2048]{0:T(1024)}, u32[]{:S(2)}) copy-start(f32[2048]{0:T(1024)} %param.12) | copy-start | bytes 24580
  34.9 6.7 %collective-permute-start.5 = (bf16[4,256,512]{2,1,0:T(8,128)(2,1)S(1)}, bf16[4,256,512]{2,1,0:T(8,128)(2,1)S(1)}, u32[]{:S(2)}, u32[]{:S(2)}) collective-permute-start(bf16[4,256,512]{2,1,0:T(8,128)(2,1)S(1)} %pad_maximum_fusion), channel_id=1, source_target_pairs={{0,1},{1,0},{2,3},{3,2},{4,5},{5,4},{6,7},{7,6},{8,9},{9,8},{10,11... | collective-permute-start | bytes 3145736 | tf_op jit(solution)/shard_map/ppermute | solution.py:463
  35.0 14.3 %collective-permute-start.6 = (bf16[512,512]{1,0:T(8,128)(2,1)S(1)}, bf16[512,512]{1,0:T(8,128)(2,1)S(1)}, u32[]{:S(2)}, u32[]{:S(2)}) collective-permute-start(bf16[512,512]{1,0:T(8,128)(2,1)S(1)} %collective-permute-done.refs_3_), channel_id=1, source_target_pairs={{0,8},{8,0},{16,24},{24,16},{1,9},{9,1},{17,25},{25,17},{2,10},{10... | collective-permute-start | bytes 1572872 | tf_op jit(solution)/shard_map/ppermute | solution.py:463
  54.8 9.3 %collective-permute-start.7 = (bf16[256,512]{1,0:T(8,128)(2,1)S(1)}, bf16[256,512]{1,0:T(8,128)(2,1)S(1)}, u32[]{:S(2)}, u32[]{:S(2)}) collective-permute-start(bf16[256,512]{1,0:T(8,128)(2,1)S(1)} %get-tuple-element.73), channel_id=1, source_target_pairs={{0,8},{8,0},{16,24},{24,16},{1,9},{9,1},{17,25},{25,17},{2,10},{10... | collective-permute-start | bytes 786440 | tf_op jit(solution)/shard_map/ppermute | solution.py:463
  55.3 21.0 %collective-permute-start.8 = (bf16[256,512]{1,0:T(8,128)(2,1)S(1)}, bf16[256,512]{1,0:T(8,128)(2,1)S(1)}, u32[]{:S(2)}, u32[]{:S(2)}) collective-permute-start(bf16[256,512]{1,0:T(8,128)(2,1)S(1)} %get-tuple-element.79), channel_id=1, source_target_pairs={{0,8},{8,0},{16,24},{24,16},{1,9},{9,1},{17,25},{25,17},{2,10},{10... | collective-permute-start | bytes 786440 | tf_op jit(solution)/shard_map/ppermute | solution.py:463
  56.9 7.6 %copy-start = (bf16[512,512]{1,0:T(8,128)(2,1)S(1)}, bf16[512,512]{1,0:T(8,128)(2,1)}, u32[]{:S(2)}) copy-start(bf16[512,512]{1,0:T(8,128)(2,1)} %refs_4_.1) | copy-start | bytes 1572868
  64.1 12.6 %collective-permute-start.9 = (bf16[256,512]{1,0:T(8,128)(2,1)S(1)}, bf16[256,512]{1,0:T(8,128)(2,1)S(1)}, u32[]{:S(2)}, u32[]{:S(2)}) collective-permute-start(bf16[256,512]{1,0:T(8,128)(2,1)S(1)} %add_convert_fusion.2), channel_id=1, source_target_pairs={{0,16},{8,24},{16,0},{24,8},{1,17},{9,25},{17,1},{25,9},{2,18},{10... | collective-permute-start | bytes 786440 | tf_op jit(solution)/shard_map/ppermute | solution.py:463
  79.7 6.7 %collective-permute-start.10 = (bf16[4,256,512]{2,1,0:T(8,128)(2,1)S(1)}, bf16[4,256,512]{2,1,0:T(8,128)(2,1)S(1)}, u32[]{:S(2)}, u32[]{:S(2)}) collective-permute-start(bf16[4,256,512]{2,1,0:T(8,128)(2,1)S(1)} %put_rows.3), channel_id=1, source_target_pairs={{0,1},{1,0},{2,3},{3,2},{4,5},{5,4},{6,7},{7,6},{8,9},{9,8},{10,11... | collective-permute-start | bytes 3145736 | tf_op jit(solution)/shard_map/ppermute | solution.py:463
  79.8 20.0 %collective-permute-start.14 = (bf16[512,512]{1,0:T(8,128)(2,1)S(1)}, bf16[512,512]{1,0:T(8,128)(2,1)S(1)}, u32[]{:S(2)}, u32[]{:S(2)}) collective-permute-start(bf16[512,512]{1,0:T(8,128)(2,1)S(1)} %get-tuple-element.88), channel_id=1, source_target_pairs={{0,8},{8,0},{16,24},{24,16},{1,9},{9,1},{17,25},{25,17},{2,10},{10... | collective-permute-start | bytes 1572872 | tf_op jit(solution)/shard_map/ppermute | solution.py:463
  79.9 17.7 %collective-permute-start.15 = (bf16[256,512]{1,0:T(8,128)(2,1)S(1)}, bf16[256,512]{1,0:T(8,128)(2,1)S(1)}, u32[]{:S(2)}, u32[]{:S(2)}) collective-permute-start(bf16[256,512]{1,0:T(8,128)(2,1)S(1)} %add_convert_fusion.1), channel_id=1, source_target_pairs={{0,16},{8,24},{16,0},{24,8},{1,17},{9,25},{17,1},{25,9},{2,18},{10... | collective-permute-start | bytes 786440 | tf_op jit(solution)/shard_map/ppermute | solution.py:463
  86.9 14.2 %collective-permute-start.11 = (bf16[256,512]{1,0:T(8,128)(2,1)S(1)}, bf16[256,512]{1,0:T(8,128)(2,1)S(1)}, u32[]{:S(2)}, u32[]{:S(2)}) collective-permute-start(bf16[256,512]{1,0:T(8,128)(2,1)S(1)} %get-tuple-element.90), channel_id=1, source_target_pairs={{0,4},{1,5},{2,6},{3,7},{4,0},{5,1},{6,2},{7,3},{8,12},{9,13},{10,... | collective-permute-start | bytes 786440 | tf_op jit(solution)/shard_map/ppermute | solution.py:463
  88.4 12.7 %collective-permute-start.12 = (bf16[256,512]{1,0:T(8,128)(2,1)S(1)}, bf16[256,512]{1,0:T(8,128)(2,1)S(1)}, u32[]{:S(2)}, u32[]{:S(2)}) collective-permute-start(bf16[256,512]{1,0:T(8,128)(2,1)S(1)} %get-tuple-element.91), channel_id=1, source_target_pairs={{0,6},{1,7},{2,4},{3,5},{4,2},{5,3},{6,0},{7,1},{8,14},{9,15},{10,... | collective-permute-start | bytes 786440 | tf_op jit(solution)/shard_map/ppermute | solution.py:463
  89.8 12.0 %collective-permute-start.13 = (bf16[256,512]{1,0:T(8,128)(2,1)S(1)}, bf16[256,512]{1,0:T(8,128)(2,1)S(1)}, u32[]{:S(2)}, u32[]{:S(2)}) collective-permute-start(bf16[256,512]{1,0:T(8,128)(2,1)S(1)} %get-tuple-element.92), channel_id=1, source_target_pairs={{0,2},{1,3},{2,0},{3,1},{4,6},{5,7},{6,4},{7,5},{8,10},{9,11},{10,... | collective-permute-start | bytes 786440 | tf_op jit(solution)/shard_map/ppermute | solution.py:463

commit v4 on v2

--- a/solution.py
+++ b/solution.py
@@ -115,16 +115,11 @@
     step = tiles.shape[1]
     steps = rows // step
 
-    slots = tiles.shape[0]
-
     def tile_copy(at):
-        slot = lax.rem(at, slots)
-        return pltpu.make_async_copy(
-            count_hbm.at[pl.ds(pl.multiple_of(at * step, step), step)], tiles.at[slot], tile_sems.at[slot]
-        )
+        return pltpu.make_async_copy(count_hbm.at[pl.ds(at * step, step)], tiles.at[at], tile_sems.at[at])
 
     small = copies([(perm_hbm, perm), (mask_hbm, mask_ref), (logm_hbm, logm_ref)], sems)
-    for at in range(slots):
+    for at in range(steps):
         tile_copy(at).start()
     for copy in small:
         copy.wait()
@@ -144,19 +139,17 @@
         fill_pick(pick.at[part], columns, chunk_base(scalars, offset, width), range(depth // LANES))
         move_values(values, pick.at[part], auxes[part])
 
-    @pl.loop(0, steps)
-    def _(at):
-        here = pl.ds(pl.multiple_of(at * step, step), step)
+    def shift(at):
         tile_copy(at).wait()
-        shifted = (tiles[lax.rem(at, slots)] - 256).astype(F32).astype(BF16)
-        shifted_ref[here, :] = shifted
-
-        @pl.when(at + slots < steps)
-        def _():
-            tile_copy(at + slots).start()
-
+        shifted_ref[pl.ds(at * step, step), :] = (tiles[at] - 256).astype(F32).astype(BF16)
+
+    shift(0)
+    for at in range(steps):
+        if at + 1 < steps:
+            shift(at + 1)
+        here = pl.ds(at * step, step)
         for part in range(parts):
-            moved = jnp.dot(shifted, pick[part], preferred_element_type=F32)
+            moved = jnp.dot(shifted_ref[here, :], pick[part], preferred_element_type=F32)
             outs[part][here, :] = moved.astype(BF16)
 
 
@@ -185,10 +178,10 @@
             pltpu.VMEM((cols // LANES, LANES), jnp.int32),
             pltpu.VMEM(block_mask.shape, jnp.int32),
             pltpu.VMEM((1, cols), F32),
-            pltpu.VMEM((2, step, cols), jnp.int32),
+            pltpu.VMEM((rows // step, step, cols), jnp.int32),
             pltpu.VMEM((parts, cols, width), BF16),
             pltpu.SemaphoreType.DMA((3,)),
-            pltpu.SemaphoreType.DMA((2,)),
+            pltpu.SemaphoreType.DMA((rows // step,)),
         ],
         compiler_params=params(28),
         cost_estimate=cost(2 * parts * rows * cols * width, 4 * rows * cols),
@@ -416,7 +409,7 @@
     )(own, near, *crosses)
 
 
-def put_kernel(offsets, exact, scalars, perm_ref, grad_ref, out_ref):
+def put_kernel(steps, other, exact, scalars, perm_ref, grad_ref, out_ref, pick):
     grad = grad_ref[...]
     rows, width = grad.shape
     high = grad.astype(BF16)
@@ -426,24 +419,38 @@
     side = out_ref.shape[1]
     index = jnp.broadcast_to((perm_ref[...] - scalars[ROW_AT] * rows).astype(F32), (8, rows))[:1]
     vocab = lax.broadcasted_iota(jnp.int32, (side, rows), 0)
-    for at, offset in enumerate(offsets):
-        base = jnp.bitwise_xor(scalars[COL_AT], offset) * side
-        pick = onehot(index == (vocab + base).astype(F32))
-        moved = jnp.dot(pick, moving, preferred_element_type=F32)
-        if exact:
-            moved = moved[:, :width] + moved[:, width:]
-        out_ref[at] = moved.astype(out_ref.dtype)
-
-
-def put_rows(scalars, row_perm, grad, offsets, side, exact):
-    width = grad.shape[1]
+    own = lax.shift_right_logical(scalars[COL_AT], 1)
+    core = jnp.bitwise_and(scalars[COL_AT], 1)
+    if other:
+        core = 1 - core
+    chips = [jnp.bitwise_xor(own, step) for step in steps]
+    for at, chip in enumerate(chips):
+        base = (2 * chip + core) * side
+        pick[pl.ds(at * side, side), :] = onehot(index == (vocab + base).astype(F32))
+    moved = jnp.dot(pick[...], moving, preferred_element_type=F32)
+    if exact:
+        moved = moved[:, :width] + moved[:, width:]
+    moved = moved.astype(out_ref.dtype)
+    if len(steps) == 1:
+        out_ref[0] = moved
+        return
+    if 0 not in steps:
+        out_ref[pl.ds(own, 1)] = jnp.zeros((1, side, width), out_ref.dtype)
+    for at, chip in enumerate(chips):
+        out_ref[pl.ds(chip, 1)] = moved[at * side : (at + 1) * side][None]
+
+
+def put_rows(scalars, row_perm, grad, steps, side, other, exact):
+    rows, width = grad.shape
+    blocks = 1 if len(steps) == 1 else 4
     return pl.pallas_call(
-        functools.partial(put_kernel, offsets, exact),
+        functools.partial(put_kernel, steps, other, exact),
         in_specs=[SCALARS, WHOLE, WHOLE],
         out_specs=WHOLE,
-        out_shape=jax.ShapeDtypeStruct((len(offsets), side, width), F32 if exact else BF16),
+        out_shape=jax.ShapeDtypeStruct((blocks, side, width), F32 if exact else BF16),
+        scratch_shapes=[pltpu.VMEM((len(steps) * side, rows), BF16)],
         compiler_params=params(24),
-        cost_estimate=cost((4096 if exact and len(offsets) > 1 else 1) * grad.size, grad.size // 16),
+        cost_estimate=cost((4096 if exact and blocks > 1 else 1) * grad.size, grad.size // 16),
         name="put_rows",
     )(scalars, row_perm[None, :], grad)
 
@@ -504,19 +511,21 @@
     cross_1 = swap(sum_1, "row", 2)
     grad, sum_1 = together((grad, sum_1))
 
-    ordered = functools.partial(put_rows, scalars, row_perm)
-    away = ordered(grad, (1, 3, 5, 7), side, False)
+    put = functools.partial(put_rows, scalars, row_perm)
+    away = put(grad, (0, 1, 2, 3), side, True, False)
     core = swap(away, "col", 1)
     grad, away = together((grad, away))
-    both = ordered(grad, (2, 4, 6), side, True) + core[1:].astype(F32)
-    sends = [both[at].astype(BF16) for at in range(3)]
-    got = [swap(sent, "col", bit) for sent, bit in zip(sends, (2, 4, 6))]
-    grad, sends = together((grad, sends))
-    home = ordered(grad, (0,), side, True)
-    home, term_own = together((home, term_own))
-    row_sum = home[0] + core[0].astype(F32)
-    for each in got:
-        row_sum = row_sum + each.astype(F32)
+    both = put(grad, (1, 2, 3), side, False, True) + core.astype(F32)
+    sends = both.astype(BF16).reshape(4 * side, -1)
+    sends, grad = together((sends, grad))
+    got = lax.all_to_all(sends, "col", 0, 0, axis_index_groups=[[0, 2, 4, 6], [1, 3, 5, 7]], tiled=True)
+    got, term_own = together((got, term_own))
+    home = put(grad, (0,), side, False, True)
+    chip = lax.axis_index("col") // 2
+    row_sum = home[0] + lax.dynamic_index_in_dim(core, chip, 0, False).astype(F32)
+    for at in range(4):
+        each = got[at * side : (at + 1) * side].astype(F32)
+        row_sum = row_sum + jnp.where(chip == at, 0.0, each)
     row_scale = np.float32(1.0 / np.sqrt(shard_cols * 8))
     col_scale = np.float32(1.0 / np.sqrt(shard_rows * 4))
     return (row_sum * row_scale, finish(col_scale, term_own, got_near, cross_0, cross_1))

time: 100 us -> 112 us (1.12)
  waiting for transfers between devices: 13.5 us -> 16.8 us
  Pallas kernels: 65.3 us -> 68.1 us
  other arithmetic: 1.63 us -> 4.04 us
  local copies, waits for them, and re-layouts: 0.07 us -> 2.22 us
    all_to_all x0 -> x1, waiting for transfers between devices: none -> 7.63 us  [line_shards(): lax.all_to_all(sends, 'col', 0, 0, axis_index_groups=[[0, 2, 4, 6], [1, 3...]
    ppermute x16 -> x13, waiting for transfers between devices: 13.5 us -> 9.13 us  [swap(): return lax.ppermute(value, axis, pairs)]
    all_to_all x0 -> x1, starting transfers between devices: none -> 4.25 us  [line_shards(): lax.all_to_all(sends, 'col', 0, 0, axis_index_groups=[[0, 2, 4, 6], [1, 3...]
    ppermute x16 -> x13, starting transfers between devices: 18.7 us -> 15.3 us  [swap(): return lax.ppermute(value, axis, pairs)]
    pallas_call x1, Pallas kernels: 9.47 us -> 11.8 us  [order_first(): pl.pallas_call(functools.partial(order_first_kernel, offsets), in_specs=[...]
    unnamed x8 -> x14, local copies, waits for them, and re-layouts: 0.02 us -> 2.22 us
    mul x1, other arithmetic: 0.97 us -> 2.34 us  [line_shards(): row_sum * row_scale]
    convert_element_type x0 -> x1, other arithmetic: none -> 1.35 us  [line_shards(): sends = both.astype(BF16).reshape(4 * side, -1)]
  transfers between devices with their start and end apart: 16 -> 14, of which waited for: 7 -> 6; matrix products, arithmetic and copies ran while one was open for 1% -> 0% of each run, Pallas kernels for 57% -> 52%
where the time goes in v4:
time: 112 us
  Pallas kernels  68.1 us (61%)
  starting transfers between devices  19.5 us (17%)
  waiting for transfers between devices  16.8 us (15%)
  other arithmetic  4.04 us (4%)
  local copies, waits for them, and re-layouts  2.22 us (2%)
    pallas_call x3, Pallas kernels, cells(): pl.pallas_call(functools.partial(cells_kernel, before is not None, sends)...  23.4 us
    pallas_call x2, Pallas kernels, order_next(): pl.pallas_call(functools.partial(order_next_kernel, offsets), in_specs=[S...  17.5 us
    ppermute x13, starting transfers between devices, swap(): return lax.ppermute(value, axis, pairs)  15.3 us
    pallas_call x1, Pallas kernels, order_first(): pl.pallas_call(functools.partial(order_first_kernel, offsets), in_specs=[...  11.8 us
    ppermute x13, waiting for transfers between devices, swap(): return lax.ppermute(value, axis, pairs)  9.13 us
    pallas_call x3, Pallas kernels, put_rows(): pl.pallas_call(functools.partial(put_kernel, steps, other, exact), in_spe...  8.84 us
    all_to_all x1, waiting for transfers between devices, line_shards(): lax.all_to_all(sends, 'col', 0, 0, axis_index_groups=[[0, 2, 4, 6], [1, 3...  7.63 us
    pallas_call x1, Pallas kernels, take_rows(): pl.pallas_call(take_kernel, in_specs=[SCALARS] + [WHOLE] * 7, out_specs=[...  5.32 us
  transfers between devices with their start and end apart: 14, of which 6 were waited for; matrix products, arithmetic and copies ran while one was open for 0% of the time, Pallas kernels for 52%

profile of v4, /device:TPU:0, one launch (start us, length us, event | category | flops | bytes accessed | tf_op | source)
XLA Modules:
  0.0 111.6 jit_solution(3254319835538021404)
XLA Ops:
  0.6 4.1 %collective-permute-start = (bf16[512,512]{1,0:T(8,128)(2,1)}, bf16[512,512]{1,0:T(8,128)(2,1)S(1)}, u32[]{:S(2)}, u32[]{:S(2)}) collective-permute-start(bf16[512,512]{1,0:T(8,128)(2,1)} %refs_4_.1), channel_id=1, source_target_pairs={{0,16},{8,24},{16,0},{24,8},{1,17},{9,25},{17,1},{25,9},{2,18},{10... | collective-permute-start | bytes 1572872 | tf_op jit(solution)/shard_map/ppermute | solution.py:460
  4.7 1.6 %collective-permute-start.1 = (bf16[512,512]{1,0:T(8,128)(2,1)}, bf16[512,512]{1,0:T(8,128)(2,1)S(1)}, u32[]{:S(2)}, u32[]{:S(2)}) collective-permute-start(bf16[512,512]{1,0:T(8,128)(2,1)} %refs_4_.1), channel_id=1, source_target_pairs={{0,8},{8,0},{16,24},{24,16},{1,9},{9,1},{17,25},{25,17},{2,10},{10... | collective-permute-start | bytes 1572872 | tf_op jit(solution)/shard_map/ppermute | solution.py:460
  6.3 0.1 pad_add_fusion.scalars
  6.4 0.0 copy-start.3
  6.4 11.8 %order_first.1 = (bf16[2048,512]{1,0:T(8,128)(2,1)S(1)}, f32[16,512]{1,0:T(8,128)S(1)}, bf16[2048,2048]{1,0:T(8,128)(2,1)S(1)}, f32[128,128]{1,0:T(8,128)S(1)}, f32[32,2048]{1,0:T(8,128)S(1)}) custom-call(s32[2]{0:T(128)S(1)} %pad_add_fusion.scalars, s32[16,128]{1,0:T(8,128)} %bitcast.33, s32[8,8]{1,0:T(8,128)} %mask_hbm.1, f32[1,2048]{1,0:T(1,128)} %bitcast.34, ...), custom_call_target="tpu_custom_call" | custom-call | flops 4294967296 | bytes 16777216 | tf_op jit(solution)/shard_map/order_first/pallas_call | solution.py:166
  18.2 0.0 copy-done.3
  18.2 1.6 %collective-permute-start.2 = (bf16[256,512]{1,0:T(8,128)(2,1)S(1)}, bf16[256,512]{1,0:T(8,128)(2,1)S(1)}, u32[]{:S(2)}, u32[]{:S(2)}) collective-permute-start(bf16[256,512]{1,0:T(8,128)(2,1)S(1)} %copy-done.3), channel_id=1, source_target_pairs={{0,2},{1,3},{2,0},{3,1},{4,6},{5,7},{6,4},{7,5},{8,10},{9,11},{10,... | collective-permute-start | bytes 786440 | tf_op jit(solution)/shard_map/ppermute | solution.py:460
  19.7 1.5 %collective-permute-start.3 = (bf16[256,512]{1,0:T(8,128)(2,1)S(1)}, bf16[256,512]{1,0:T(8,128)(2,1)S(1)}, u32[]{:S(2)}, u32[]{:S(2)}) collective-permute-start(bf16[256,512]{1,0:T(8,128)(2,1)S(1)} %copy-done.3), channel_id=1, source_target_pairs={{0,4},{1,5},{2,6},{3,7},{4,0},{5,1},{6,2},{7,3},{8,12},{9,13},{10,... | collective-permute-start | bytes 786440 | tf_op jit(solution)/shard_map/ppermute | solution.py:460
  21.2 0.5 collective-permute-start.4
  21.7 11.3 %order_next.2 = (bf16[2048,512]{1,0:T(8,128)(2,1)S(1)}, bf16[2048,512]{1,0:T(8,128)(2,1)S(1)}, f32[16,512]{1,0:T(8,128)S(1)}, f32[16,512]{1,0:T(8,128)S(1)}) custom-call(s32[2]{0:T(128)S(1)} %pad_add_fusion.scalars, bf16[2048,2048]{1,0:T(8,128)(2,1)S(1)} %get-tuple-element.53.shifted_ref, f32[128,128]{1,0:T(8,128)S(1)} %get-tuple-element.50.columns_ref, ...), custom_call_target="tpu_custom_call" | custom-call | flops 1048576 | bytes 1048576 | tf_op jit(solution)/shard_map/order_next/pallas_call | solution.py:214
  33.0 0.0 collective-permute-done.2.refs_1_
  33.0 0.0 collective-permute-done.3.refs_2_
  33.0 0.0 collective-permute-done.4.refs_3_
  33.0 0.0 collective-permute-done.refs_3_
  33.0 0.0 collective-permute-done.1.refs_3_
  33.0 0.1 pad_maximum_fusion
  33.2 0.0 copy-start.4
  33.2 0.0 copy-start.5
  33.2 0.1 collective-permute-start.5
  33.3 0.5 collective-permute-start.6
  33.8 6.3 %order_next.3 = (bf16[2048,512]{1,0:T(8,128)(2,1)S(1)}, f32[16,512]{1,0:T(8,128)S(1)}) custom-call(s32[2]{0:T(128)S(1)} %pad_add_fusion.scalars, bf16[2048,2048]{1,0:T(8,128)(2,1)S(1)} %get-tuple-element.53.shifted_ref, f32[128,128]{1,0:T(8,128)S(1)} %get-tuple-element.50.columns_ref, f32[32,2048]{1,0:T(8,128)S(1)} %get-tuple-element.51.values_ref), custom_call_target="tpu_custom_call" | custom-call | flops 1048576 | bytes 1048576 | tf_op jit(solution)/shard_map/order_next/pallas_call | solution.py:214
  40.1 0.0 collective-permute-done.5.refs_4_
  40.1 0.0 copy-done.4
  40.1 0.0 copy-done.5
  40.1 5.3 %take_rows.1 = (bf16[2048,512]{1,0:T(8,128)(2,1)S(1)}, bf16[512,2048]{1,0:T(8,128)(2,1)S(1)}, f32[2048,128]{1,0:T(8,128)S(1)}) custom-call(s32[2]{0:T(128)S(1)} %pad_add_fusion.scalars, s32[16,128]{1,0:T(8,128)S(1)} %bitcast.28, f32[16,128]{1,0:T(8,128)S(1)} %bitcast.32, bf16[256,512]{1,0:T(8,128)(2,1)S(1)} %copy-done.3, ...), custom_call_target="tpu_custom_call" | custom-call | flops 4294967296 | bytes 4194304 | tf_op jit(solution)/shard_map/take_rows/pallas_call | solution.py:258
  45.4 2.2 %collective-permute-done.6.refs_3_ = bf16[512,512]{1,0:T(8,128)(2,1)S(1)} collective-permute-done((bf16[512,512]{1,0:T(8,128)(2,1)S(1)}, bf16[512,512]{1,0:T(8,128)(2,1)S(1)}, u32[]{:S(2)}, u32[]{:S(2)}) %collective-permute-start.6) | collective-permute-done | bytes 524320 | tf_op jit(solution)/shard_map/ppermute | solution.py:460
  47.6 5.5 %cells.3 = (f32[2048,512]{1,0:T(8,128)S(1)}, bf16[256,512]{1,0:T(8,128)(2,1)S(1)}, bf16[256,512]{1,0:T(8,128)(2,1)S(1)}) custom-call(bf16[2048,512]{1,0:T(8,128)(2,1)S(1)} %get-tuple-element.59.refs_0_, bf16[512,2048]{1,0:T(8,128)(2,1)S(1)} %get-tuple-element.60.refs_1_, f32[2048,128]{1,0:T(8,128)S(1)} %get-tuple-element.61.refs_2_, ...), custom_call_target="tpu_custom_call" | custom-call | flops 1048576 | bytes 1048576 | tf_op jit(solution)/shard_map/cells/pallas_call | solution.py:374
  53.2 0.5 collective-permute-start.7
  53.7 1.6 %collective-permute-start.8 = (bf16[256,512]{1,0:T(8,128)(2,1)S(1)}, bf16[256,512]{1,0:T(8,128)(2,1)S(1)}, u32[]{:S(2)}, u32[]{:S(2)}) collective-permute-start(bf16[256,512]{1,0:T(8,128)(2,1)S(1)} %get-tuple-element.80), channel_id=1, source_target_pairs={{0,8},{8,0},{16,24},{24,16},{1,9},{9,1},{17,25},{25,17},{2,10},{10... | collective-permute-start | bytes 786440 | tf_op jit(solution)/shard_map/ppermute | solution.py:460
  55.3 0.0 copy-start.2
  55.3 5.9 %cells.4 = (f32[2048,512]{1,0:T(8,128)S(1)}, f32[512,512]{1,0:T(8,128)S(1)}) custom-call(bf16[2048,512]{1,0:T(8,128)(2,1)S(1)} %get-tuple-element.59.refs_0_, bf16[512,2048]{1,0:T(8,128)(2,1)S(1)} %get-tuple-element.60.refs_1_, f32[2048,128]{1,0:T(8,128)S(1)} %get-tuple-element.61.refs_2_, ...), custom_call_target="tpu_custom_call", output_to_operand_aliasing={{0}: (6, {})} | custom-call | flops 1048576 | bytes 1048576 | tf_op jit(solution)/shard_map/cells/pallas_call | solution.py:374
  61.1 1.3 %collective-permute-done.7 = bf16[256,512]{1,0:T(8,128)(2,1)S(1)} collective-permute-done((bf16[256,512]{1,0:T(8,128)(2,1)S(1)}, bf16[256,512]{1,0:T(8,128)(2,1)S(1)}, u32[]{:S(2)}, u32[]{:S(2)}) %collective-permute-start.7) | collective-permute-done | bytes 262176 | tf_op jit(solution)/shard_map/ppermute | solution.py:460
  62.5 0.1 add_convert_fusion.2
  62.5 0.4 collective-permute-start.9
  62.9 0.0 copy-done.2
  62.9 12.0 %cells.5 = (f32[2048,512]{1,0:T(8,128)S(1)}, bf16[512,512]{1,0:T(8,128)(2,1)S(1)}, f32[512,512]{1,0:T(8,128)S(1)}) custom-call(bf16[2048,512]{1,0:T(8,128)(2,1)S(1)} %get-tuple-element.59.refs_0_, bf16[512,2048]{1,0:T(8,128)(2,1)S(1)} %get-tuple-element.60.refs_1_, f32[2048,128]{1,0:T(8,128)S(1)} %get-tuple-element.61.refs_2_, ...), custom_call_target="tpu_custom_call", output_to_operand_aliasing={{0}: (9, {})} | custom-call | flops 1048576 | bytes 1048576 | tf_op jit(solution)/shard_map/cells/pallas_call | solution.py:374
  74.9 0.0 copy-start
  74.9 0.0 collective-permute-done.8
  74.9 0.2 collective-permute-done.9.refs_2_
  75.2 0.1 add_convert_fusion.1
  75.2 2.9 %put_rows.3 = bf16[4,256,512]{2,1,0:T(8,128)(2,1)S(1)} custom-call(s32[2]{0:T(128)S(1)} %pad_add_fusion.scalars, s32[1,2048]{1,0:T(1,128)S(1)} %bitcast.29, f32[2048,512]{1,0:T(8,128)S(1)} %get-tuple-element.85.grad_ref), custom_call_target="tpu_custom_call" | custom-call | flops 1048576 | bytes 65536 | tf_op jit(solution)/shard_map/put_rows/pallas_call | solution.py:446
  78.1 0.1 collective-permute-start.10
  78.2 0.0 copy-done
  78.2 4.0 %put_rows.4 = f32[4,256,512]{2,1,0:T(8,128)S(1)} custom-call(s32[2]{0:T(128)S(1)} %pad_add_fusion.scalars, s32[1,2048]{1,0:T(1,128)S(1)} %bitcast.30, f32[2048,512]{1,0:T(8,128)S(1)} %get-tuple-element.85.grad_ref), custom_call_target="tpu_custom_call" | custom-call | flops 4294967296 | bytes 65536 | tf_op jit(solution)/shard_map/put_rows/pallas_call | solution.py:446
  82.3 0.0 collective-permute-done.10
  82.3 0.0 copy-start.6
  82.3 1.3 %add_convert_fusion = bf16[4,256,512]{2,1,0:T(8,128)(2,1)} fusion(f32[4,256,512]{2,1,0:T(8,128)S(1)} %put_rows.4, bf16[4,256,512]{2,1,0:T(8,128)(2,1)S(1)} %collective-permute-done.10), kind=kLoop, calls=%fused_computation | loop fusion | flops 1572864 | bytes 4194304 | tf_op jit(solution)/shard_map/convert_element_type | solution.py:519
  83.6 0.0 copy-done.6
  83.6 4.3 %all-to-all-start = ((bf16[4,256,512]{2,1,0:T(8,128)(2,1)}), bf16[4,256,512]{2,1,0:T(8,128)(2,1)}, u32[]{:S(2)}, u32[]{:S(2)}) async-start(bf16[4,256,512]{2,1,0:T(8,128)(2,1)} %bitcast.13), calls=%async_computation | async-start | bytes 2097152 | tf_op jit(solution)/shard_map/all_to_all | solution.py:521
  87.9 0.2 collective-permute-start.11
  88.0 2.7 %collective-permute-start.12 = (bf16[256,512]{1,0:T(8,128)(2,1)S(1)}, bf16[256,512]{1,0:T(8,128)(2,1)S(1)}, u32[]{:S(2)}, u32[]{:S(2)}) collective-permute-start(bf16[256,512]{1,0:T(8,128)(2,1)S(1)} %add_convert_fusion.1), channel_id=1, source_target_pairs={{0,16},{8,24},{16,0},{24,8},{1,17},{9,25},{17,1},{25,9},{2,18},{10... | collective-permute-start | bytes 786440 | tf_op jit(solution)/shard_map/ppermute | solution.py:460
  90.8 0.0 copy-start.1
  90.8 2.2 %copy-done.1 = f32[2048,512]{1,0:T(8,128)S(1)} copy-done((f32[2048,512]{1,0:T(8,128)S(1)}, f32[2048,512]{1,0:T(8,128)}, u32[]{:S(2)}) %copy-start.1) | copy-done | bytes 4194328
  93.0 1.9 %put_rows.5 = f32[1,256,512]{2,1,0:T(8,128)S(1)} custom-call(s32[2]{0:T(128)S(1)} %pad_add_fusion.scalars, s32[1,2048]{1,0:T(1,128)S(1)} %bitcast.31, f32[2048,512]{1,0:T(8,128)S(1)} %copy-done.1), custom_call_target="tpu_custom_call" | custom-call | flops 1048576 | bytes 65536 | tf_op jit(solution)/shard_map/put_rows/pallas_call | solution.py:446
  94.9 7.6 %all-to-all-done = bf16[4,256,512]{2,1,0:T(8,128)(2,1)} async-done(((bf16[4,256,512]{2,1,0:T(8,128)(2,1)}), bf16[4,256,512]{2,1,0:T(8,128)(2,1)}, u32[]{:S(2)}, u32[]{:S(2)}) %all-to-all-start) | async-done | bytes 1048608 | tf_op jit(solution)/shard_map/all_to_all | solution.py:521
  102.5 3.2 %collective-permute-done.12.refs_3_ = bf16[256,512]{1,0:T(8,128)(2,1)S(1)} collective-permute-done((bf16[256,512]{1,0:T(8,128)(2,1)S(1)}, bf16[256,512]{1,0:T(8,128)(2,1)S(1)}, u32[]{:S(2)}, u32[]{:S(2)}) %collective-permute-start.12) | collective-permute-done | bytes 262176 | tf_op jit(solution)/shard_map/ppermute | solution.py:460
  105.7 2.2 %collective-permute-done.11.refs_1_ = bf16[512,512]{1,0:T(8,128)(2,1)S(1)} collective-permute-done((bf16[512,512]{1,0:T(8,128)(2,1)S(1)}, bf16[512,512]{1,0:T(8,128)(2,1)S(1)}, u32[]{:S(2)}, u32[]{:S(2)}) %collective-permute-start.11) | collective-permute-done | bytes 524320 | tf_op jit(solution)/shard_map/ppermute | solution.py:460
  107.9 1.3 %finish.1 = f32[512,512]{1,0:T(8,128)} custom-call(f32[512,512]{1,0:T(8,128)S(1)} %get-tuple-element.89.refs_0_, bf16[512,512]{1,0:T(8,128)(2,1)S(1)} %collective-permute-done.11.refs_1_, bf16[256,512]{1,0:T(8,128)(2,1)S(1)} %collective-permute-done.9.refs_2_, bf16[256,512]{1,0:T(8,128)(2,1)S(1)} %collective-permute-done.12.refs_3_), custom_call_target="tpu_custom_call" | custom-call | flops 262144 | bytes 16384 | tf_op jit(solution)/shard_map/finish/pallas_call | solution.py:401
  109.2 2.3 %fusion.3 = f32[256,512]{1,0:T(8,128)} fusion(f32[1,256,512]{2,1,0:T(8,128)S(1)} %put_rows.5, bf16[1024,512]{1,0:T(8,128)(2,1)} %bitcast.14, bf16[4,256,512]{2,1,0:T(8,128)(2,1)} %copy-done.6, s32[]{:T(128)S(6)} %select_n.36, pred[]{:T(512)S(6)} %eq.15, pred[]{:T(512)S(6)} %eq.14, pred[]{:T(512)S(6)} %eq.13, pred[]{:T(512)S(6)} %eq.12), kind=kLoop, calls=%fused_computation.6 | loop fusion | flops 1966080 | bytes 2359304 | tf_op jit(solution)/shard_map/mul | solution.py:531
Async XLA Ops:
  0.6 32.4 %collective-permute-start = (bf16[512,512]{1,0:T(8,128)(2,1)}, bf16[512,512]{1,0:T(8,128)(2,1)S(1)}, u32[]{:S(2)}, u32[]{:S(2)}) collective-permute-start(bf16[512,512]{1,0:T(8,128)(2,1)} %refs_4_.1), channel_id=1, source_target_pairs={{0,16},{8,24},{16,0},{24,8},{1,17},{9,25},{17,1},{25,9},{2,18},{10... | collective-permute-start | bytes 1572872 | tf_op jit(solution)/shard_map/ppermute | solution.py:460
  4.7 28.3 %collective-permute-start.1 = (bf16[512,512]{1,0:T(8,128)(2,1)}, bf16[512,512]{1,0:T(8,128)(2,1)S(1)}, u32[]{:S(2)}, u32[]{:S(2)}) collective-permute-start(bf16[512,512]{1,0:T(8,128)(2,1)} %refs_4_.1), channel_id=1, source_target_pairs={{0,8},{8,0},{16,24},{24,16},{1,9},{9,1},{17,25},{25,17},{2,10},{10... | collective-permute-start | bytes 1572872 | tf_op jit(solution)/shard_map/ppermute | solution.py:460
  6.4 11.8 %copy-start.3 = (bf16[256,512]{1,0:T(8,128)(2,1)S(1)}, bf16[256,512]{1,0:T(8,128)(2,1)}, u32[]{:S(2)}) copy-start(bf16[256,512]{1,0:T(8,128)(2,1)} %refs_0_.1) | copy-start | bytes 786436
  18.2 14.8 %collective-permute-start.2 = (bf16[256,512]{1,0:T(8,128)(2,1)S(1)}, bf16[256,512]{1,0:T(8,128)(2,1)S(1)}, u32[]{:S(2)}, u32[]{:S(2)}) collective-permute-start(bf16[256,512]{1,0:T(8,128)(2,1)S(1)} %copy-done.3), channel_id=1, source_target_pairs={{0,2},{1,3},{2,0},{3,1},{4,6},{5,7},{6,4},{7,5},{8,10},{9,11},{10,... | collective-permute-start | bytes 786440 | tf_op jit(solution)/shard_map/ppermute | solution.py:460
  19.7 13.3 %collective-permute-start.3 = (bf16[256,512]{1,0:T(8,128)(2,1)S(1)}, bf16[256,512]{1,0:T(8,128)(2,1)S(1)}, u32[]{:S(2)}, u32[]{:S(2)}) collective-permute-start(bf16[256,512]{1,0:T(8,128)(2,1)S(1)} %copy-done.3), channel_id=1, source_target_pairs={{0,4},{1,5},{2,6},{3,7},{4,0},{5,1},{6,2},{7,3},{8,12},{9,13},{10,... | collective-permute-start | bytes 786440 | tf_op jit(solution)/shard_map/ppermute | solution.py:460
  21.2 11.8 %collective-permute-start.4 = (bf16[256,512]{1,0:T(8,128)(2,1)S(1)}, bf16[256,512]{1,0:T(8,128)(2,1)S(1)}, u32[]{:S(2)}, u32[]{:S(2)}) collective-permute-start(bf16[256,512]{1,0:T(8,128)(2,1)S(1)} %copy-done.3), channel_id=1, source_target_pairs={{0,6},{1,7},{2,4},{3,5},{4,2},{5,3},{6,0},{7,1},{8,14},{9,15},{10,... | collective-permute-start | bytes 786440 | tf_op jit(solution)/shard_map/ppermute | solution.py:460
  33.2 6.9 %copy-start.4 = (s32[2048]{0:T(1024)S(1)}, s32[2048]{0:T(1024)}, u32[]{:S(2)}) copy-start(s32[2048]{0:T(1024)} %param.10) | copy-start | bytes 24580
  33.2 6.9 %copy-start.5 = (f32[2048]{0:T(1024)S(1)}, f32[2048]{0:T(1024)}, u32[]{:S(2)}) copy-start(f32[2048]{0:T(1024)} %param.12) | copy-start | bytes 24580
  33.2 6.9 %collective-permute-start.5 = (bf16[4,256,512]{2,1,0:T(8,128)(2,1)S(1)}, bf16[4,256,512]{2,1,0:T(8,128)(2,1)S(1)}, u32[]{:S(2)}, u32[]{:S(2)}) collective-permute-start(bf16[4,256,512]{2,1,0:T(8,128)(2,1)S(1)} %pad_maximum_fusion), channel_id=1, source_target_pairs={{0,1},{1,0},{2,3},{3,2},{4,5},{5,4},{6,7},{7,6},{8,9},{9,8},{10,11... | collective-permute-start | bytes 3145736 | tf_op jit(solution)/shard_map/ppermute | solution.py:460
  33.3 14.3 %collective-permute-start.6 = (bf16[512,512]{1,0:T(8,128)(2,1)S(1)}, bf16[512,512]{1,0:T(8,128)(2,1)S(1)}, u32[]{:S(2)}, u32[]{:S(2)}) collective-permute-start(bf16[512,512]{1,0:T(8,128)(2,1)S(1)} %collective-permute-done.refs_3_), channel_id=1, source_target_pairs={{0,8},{8,0},{16,24},{24,16},{1,9},{9,1},{17,25},{25,17},{2,10},{10... | collective-permute-start | bytes 1572872 | tf_op jit(solution)/shard_map/ppermute | solution.py:460
  53.2 9.3 %collective-permute-start.7 = (bf16[256,512]{1,0:T(8,128)(2,1)S(1)}, bf16[256,512]{1,0:T(8,128)(2,1)S(1)}, u32[]{:S(2)}, u32[]{:S(2)}) collective-permute-start(bf16[256,512]{1,0:T(8,128)(2,1)S(1)} %get-tuple-element.74), channel_id=1, source_target_pairs={{0,8},{8,0},{16,24},{24,16},{1,9},{9,1},{17,25},{25,17},{2,10},{10... | collective-permute-start | bytes 786440 | tf_op jit(solution)/shard_map/ppermute | solution.py:460
  53.7 21.2 %collective-permute-start.8 = (bf16[256,512]{1,0:T(8,128)(2,1)S(1)}, bf16[256,512]{1,0:T(8,128)(2,1)S(1)}, u32[]{:S(2)}, u32[]{:S(2)}) collective-permute-start(bf16[256,512]{1,0:T(8,128)(2,1)S(1)} %get-tuple-element.80), channel_id=1, source_target_pairs={{0,8},{8,0},{16,24},{24,16},{1,9},{9,1},{17,25},{25,17},{2,10},{10... | collective-permute-start | bytes 786440 | tf_op jit(solution)/shard_map/ppermute | solution.py:460
  55.3 7.7 %copy-start.2 = (bf16[512,512]{1,0:T(8,128)(2,1)S(1)}, bf16[512,512]{1,0:T(8,128)(2,1)}, u32[]{:S(2)}) copy-start(bf16[512,512]{1,0:T(8,128)(2,1)} %refs_4_.1) | copy-start | bytes 1572868
  62.5 12.6 %collective-permute-start.9 = (bf16[256,512]{1,0:T(8,128)(2,1)S(1)}, bf16[256,512]{1,0:T(8,128)(2,1)S(1)}, u32[]{:S(2)}, u32[]{:S(2)}) collective-permute-start(bf16[256,512]{1,0:T(8,128)(2,1)S(1)} %add_convert_fusion.2), channel_id=1, source_target_pairs={{0,16},{8,24},{16,0},{24,8},{1,17},{9,25},{17,1},{25,9},{2,18},{10... | collective-permute-start | bytes 786440 | tf_op jit(solution)/shard_map/ppermute | solution.py:460
  74.9 3.3 %copy-start = (f32[2048,512]{1,0:T(8,128)}, f32[2048,512]{1,0:T(8,128)S(1)}, u32[]{:S(2)}) copy-start(f32[2048,512]{1,0:T(8,128)S(1)} %get-tuple-element.85.grad_ref) | copy-start | bytes 12582916
  78.1 4.1 %collective-permute-start.10 = (bf16[4,256,512]{2,1,0:T(8,128)(2,1)S(1)}, bf16[4,256,512]{2,1,0:T(8,128)(2,1)S(1)}, u32[]{:S(2)}, u32[]{:S(2)}) collective-permute-start(bf16[4,256,512]{2,1,0:T(8,128)(2,1)S(1)} %put_rows.3), channel_id=1, source_target_pairs={{0,1},{1,0},{2,3},{3,2},{4,5},{5,4},{6,7},{7,6},{8,9},{9,8},{10,11... | collective-permute-start | bytes 3145736 | tf_op jit(solution)/shard_map/ppermute | solution.py:460
  82.3 1.4 %copy-start.6 = (bf16[4,256,512]{2,1,0:T(8,128)(2,1)}, bf16[4,256,512]{2,1,0:T(8,128)(2,1)S(1)}, u32[]{:S(2)}) copy-start(bf16[4,256,512]{2,1,0:T(8,128)(2,1)S(1)} %collective-permute-done.10) | copy-start | bytes 3145732
  83.6 18.9 %all-to-all-start = ((bf16[4,256,512]{2,1,0:T(8,128)(2,1)}), bf16[4,256,512]{2,1,0:T(8,128)(2,1)}, u32[]{:S(2)}, u32[]{:S(2)}) async-start(bf16[4,256,512]{2,1,0:T(8,128)(2,1)} %bitcast.13), calls=%async_computation | async-start | bytes 2097152 | tf_op jit(solution)/shard_map/all_to_all | solution.py:521
  87.9 20.0 %collective-permute-start.11 = (bf16[512,512]{1,0:T(8,128)(2,1)S(1)}, bf16[512,512]{1,0:T(8,128)(2,1)S(1)}, u32[]{:S(2)}, u32[]{:S(2)}) collective-permute-start(bf16[512,512]{1,0:T(8,128)(2,1)S(1)} %get-tuple-element.90), channel_id=1, source_target_pairs={{0,8},{8,0},{16,24},{24,16},{1,9},{9,1},{17,25},{25,17},{2,10},{10... | collective-permute-start | bytes 1572872 | tf_op jit(solution)/shard_map/ppermute | solution.py:460
  88.0 17.7 %collective-permute-start.12 = (bf16[256,512]{1,0:T(8,128)(2,1)S(1)}, bf16[256,512]{1,0:T(8,128)(2,1)S(1)}, u32[]{:S(2)}, u32[]{:S(2)}) collective-permute-start(bf16[256,512]{1,0:T(8,128)(2,1)S(1)} %add_convert_fusion.1), channel_id=1, source_target_pairs={{0,16},{8,24},{16,0},{24,8},{1,17},{9,25},{17,1},{25,9},{2,18},{10... | collective-permute-start | bytes 786440 | tf_op jit(solution)/shard_map/ppermute | solution.py:460
  90.8 2.2 %copy-start.1 = (f32[2048,512]{1,0:T(8,128)S(1)}, f32[2048,512]{1,0:T(8,128)}, u32[]{:S(2)}) copy-start(f32[2048,512]{1,0:T(8,128)} %copy-done) | copy-start | bytes 12582916

commit v5 on v2

--- a/solution.py
+++ b/solution.py
@@ -278,66 +278,6 @@
     )(scalars, row_perm.reshape(-1, LANES), row_logm.reshape(-1, LANES), *blocks)
 
 
-def chunk_work(
-    chunk, wvec_ref, turned_ref, count_ref, aux_ref, logm_ref, before_ref, grad_ref, term_ref, chunk_turned, delta_ref
-):
-    chunk_turned[...] = chunk[...].T
-    rows = wvec_ref.shape[0]
-    width = chunk.shape[0]
-    blocks = aux_ref.shape[0] - 8
-    tile = rows // blocks
-    joined = delta_ref.shape[0] // tile
-    half = joined // 2
-    col_logm = aux_ref[blocks : blocks + 1, :]
-    term_ref[...] = jnp.zeros_like(term_ref)
-
-    @pl.loop(0, blocks // joined)
-    def _(group):
-        def rows_at(at, count=1):
-            return pl.ds(pl.multiple_of((group * joined + at) * tile, tile), count * tile)
-
-        def held(at, count=1):
-            return delta_ref[pl.ds(at * tile, count * tile), :]
-
-        def score_of(at):
-            return jnp.dot(wvec_ref[rows_at(at), :], chunk_turned[...], preferred_element_type=F32)
-
-        def delta_of(at, score):
-            here = rows_at(at)
-            count = count_ref[here, :].astype(F32) + 256.0
-            log = jnp.log(jnp.maximum(count, 1.0))
-            row_logm = jnp.concatenate([logm_ref[here, :]] * (width // LANES), axis=1)
-            gap = score + ((row_logm + col_logm) - log)
-            confid = 0.1 + 0.25 * jnp.exp2(log * np.float32(0.5 / np.log(2.0)))
-            zeroed = 0.5 * jnp.tanh(0.5 * gap) + 0.5
-            deriv = jnp.where(count > 0.0, confid * gap, zeroed)
-            active = aux_ref[pl.ds(group * joined + at, 1), :]
-            delta_ref[pl.ds(at * tile, tile), :] = (deriv * active).astype(BF16)
-
-        def grad_of(at):
-            grad = jnp.dot(held(at), chunk[...], preferred_element_type=F32)
-            if before_ref is not None:
-                grad = grad + before_ref[rows_at(at), :]
-            grad_ref[rows_at(at), :] = grad
-
-        def term_of(at):
-            turned = turned_ref[:, rows_at(at, half)]
-            term_ref[...] += jnp.dot(turned, held(at, half), preferred_element_type=F32)
-
-        ahead = score_of(0)
-        for at in range(joined):
-            score = ahead
-            if at + 1 < joined:
-                ahead = score_of(at + 1)
-            delta_of(at, score)
-            if at:
-                grad_of(at - 1)
-            if at == half:
-                term_of(0)
-        grad_of(joined - 1)
-        term_of(half)
-
-
 def cells_kernel(has_sum, sends, *refs):
     chunks = len(sends)
     wvec_ref, turned_ref, logm_ref, refs = *refs[:3], refs[3:]
@@ -346,21 +286,102 @@
     before_ref = None
     if has_sum:
         before_ref, refs = refs[0], refs[1:]
-    grad_ref, refs = refs[0], refs[1:]
-    chunk_turned, delta_ref, sum_ref = refs[-3:]
-    for at, pieces in enumerate(sends):
-        term_ref = sum_ref
-        if not pieces:
-            term_ref, refs = refs[0], refs[1:]
-        chunk_work(
-            chunk_refs[at], wvec_ref, turned_ref, count_refs[at], aux_refs[at], logm_ref,
-            before_ref, grad_ref, term_ref, chunk_turned, delta_ref,
-        )
-        before_ref = grad_ref
-        for piece in range(pieces):
-            sent_ref, refs = refs[0], refs[1:]
-            size = sent_ref.shape[0]
-            sent_ref[...] = term_ref[pl.ds(piece * size, size), :].astype(BF16)
+    grad_ref, outs = refs[0], list(refs[1:-4])
+    chunk, chunk_turned, delta_ref, term_ref = refs[-4:]
+    rows = wvec_ref.shape[0]
+    width = chunk.shape[0]
+    blocks = aux_refs[0].shape[0] - 8
+    tile = rows // blocks
+    joined = delta_ref.shape[0] // tile
+    half = joined // 2
+    out_refs = [[outs.pop(0) for _ in range(max(pieces, 1))] for pieces in sends]
+
+    def work(which):
+        def chosen(several, here):
+            value = several[0][here]
+            for at in range(1, chunks):
+                value = jnp.where(which == at, several[at][here], value)
+            return value
+
+        for at in range(chunks):
+
+            @pl.when(which == at)
+            def _():
+                chunk[...] = chunk_refs[at][...]
+
+        chunk_turned[...] = chunk[...].T
+        col_logm = chosen(aux_refs, (pl.ds(blocks, 1), slice(None)))
+
+        def part(group):
+            def rows_at(at, count=1):
+                return pl.ds(pl.multiple_of((group * joined + at) * tile, tile), count * tile)
+
+            def held(at, count=1):
+                return delta_ref[pl.ds(at * tile, count * tile), :]
+
+            def score_of(at):
+                return jnp.dot(wvec_ref[rows_at(at), :], chunk_turned[...], preferred_element_type=F32)
+
+            def delta_of(at, score):
+                here = (rows_at(at), slice(None))
+                count = chosen(count_refs, here).astype(F32) + 256.0
+                log = jnp.log(jnp.maximum(count, 1.0))
+                row_logm = jnp.concatenate([logm_ref[here]] * (width // LANES), axis=1)
+                gap = score + ((row_logm + col_logm) - log)
+                confid = 0.1 + 0.25 * jnp.exp2(log * np.float32(0.5 / np.log(2.0)))
+                zeroed = 0.5 * jnp.tanh(0.5 * gap) + 0.5
+                deriv = jnp.where(count > 0.0, confid * gap, zeroed)
+                active = chosen(aux_refs, (pl.ds(group * joined + at, 1), slice(None)))
+                delta_ref[pl.ds(at * tile, tile), :] = (deriv * active).astype(BF16)
+
+            def grad_of(at):
+                here = (rows_at(at), slice(None))
+                grad = jnp.dot(held(at), chunk[...], preferred_element_type=F32)
+                if has_sum:
+                    before = before_ref[here]
+                    if chunks > 1:
+                        before = jnp.where(which == 0, before, grad_ref[here])
+                    grad = grad + before
+                grad_ref[here] = grad
+
+            def term_of(at):
+                turned = turned_ref[:, rows_at(at, half)]
+                term = jnp.dot(turned, held(at, half), preferred_element_type=F32)
+                if joined < blocks or at:
+                    term = term_ref[...] + term
+                term_ref[...] = term
+
+            ahead = score_of(0)
+            for at in range(joined):
+                score = ahead
+                if at + 1 < joined:
+                    ahead = score_of(at + 1)
+                delta_of(at, score)
+                if at:
+                    grad_of(at - 1)
+                if at == half:
+                    term_of(0)
+            grad_of(joined - 1)
+            term_of(half)
+
+        if joined < blocks:
+            term_ref[...] = jnp.zeros_like(term_ref)
+            pl.loop(0, blocks // joined)(part)
+        else:
+            part(0)
+
+        for at, pieces in enumerate(sends):
+
+            @pl.when(which == at)
+            def _():
+                for piece, out_ref in enumerate(out_refs[at]):
+                    size = out_ref.shape[0]
+                    out_ref[...] = term_ref[pl.ds(piece * size, size), :].astype(out_ref.dtype)
+
+    if chunks > 1:
+        pl.loop(0, chunks)(work)
+    else:
+        work(0)
 
 
 def cells(rows_in, chunks, before, sends):
@@ -384,8 +405,9 @@
         out_specs=[WHOLE] * len(out_shape),
         out_shape=out_shape,
         scratch_shapes=[
+            pltpu.VMEM((width, depth), BF16),
             pltpu.VMEM((depth, width), BF16),
-            pltpu.VMEM((rows // 2, width), BF16),
+            pltpu.VMEM((rows, width), BF16),
             pltpu.VMEM((depth, width), F32),
         ],
         input_output_aliases=aliases,
@@ -416,7 +438,7 @@
     )(own, near, *crosses)
 
 
-def put_kernel(offsets, exact, scalars, perm_ref, grad_ref, out_ref):
+def put_kernel(offsets, exact, scalars, perm_ref, grad_ref, out_ref, pick):
     grad = grad_ref[...]
     rows, width = grad.shape
     high = grad.astype(BF16)
@@ -428,11 +450,11 @@
     vocab = lax.broadcasted_iota(jnp.int32, (side, rows), 0)
     for at, offset in enumerate(offsets):
         base = jnp.bitwise_xor(scalars[COL_AT], offset) * side
-        pick = onehot(index == (vocab + base).astype(F32))
-        moved = jnp.dot(pick, moving, preferred_element_type=F32)
-        if exact:
-            moved = moved[:, :width] + moved[:, width:]
-        out_ref[at] = moved.astype(out_ref.dtype)
+        pick[pl.ds(at * side, side), :] = onehot(index == (vocab + base).astype(F32))
+    moved = jnp.dot(pick[...], moving, preferred_element_type=F32)
+    if exact:
+        moved = moved[:, :width] + moved[:, width:]
+    out_ref[...] = moved.astype(out_ref.dtype).reshape(out_ref.shape)
 
 
 def put_rows(scalars, row_perm, grad, offsets, side, exact):
@@ -442,6 +464,7 @@
         in_specs=[SCALARS, WHOLE, WHOLE],
         out_specs=WHOLE,
         out_shape=jax.ShapeDtypeStruct((len(offsets), side, width), F32 if exact else BF16),
+        scratch_shapes=[pltpu.VMEM((len(offsets) * side, grad.shape[0]), BF16)],
         compiler_params=params(24),
         cost_estimate=cost((4096 if exact and len(offsets) > 1 else 1) * grad.size, grad.size // 16),
         name="put_rows",
@@ -510,7 +533,7 @@
     grad, away = together((grad, away))
     both = ordered(grad, (2, 4, 6), side, True) + core[1:].astype(F32)
     sends = [both[at].astype(BF16) for at in range(3)]
-    got = [swap(sent, "col", bit) for sent, bit in zip(sends, (2, 4, 6))]
+    got = [swap(sends[at], "col", bit) for at, bit in ((1, 4), (2, 6), (0, 2))]
     grad, sends = together((grad, sends))
     home = ordered(grad, (0,), side, True)
     home, term_own = together((home, term_own))

time: 100 us -> 99.4 us (level)
  waiting for transfers between devices: 13.5 us -> 11.8 us
    ppermute x16, waiting for transfers between devices: 13.5 us -> 11.8 us  [swap(): return lax.ppermute(value, axis, pairs)]
  transfers between devices with their start and end apart: 16 -> 16, of which waited for: 7 -> 5; matrix products, arithmetic and copies ran while one was open for 1% -> 1% of each run, Pallas kernels for 57% -> 58%
where the time goes in v5:
time: 99.4 us; the launch traced here: 99.2 us
  Pallas kernels  65.8 us (66%)
  starting transfers between devices  19 us (19%)
  waiting for transfers between devices  11.8 us (12%)
  other arithmetic  1.63 us (2%)
    pallas_call x3, Pallas kernels, cells(): pl.pallas_call(functools.partial(cells_kernel, before is not None, sends)...  23.5 us
    ppermute x16, starting transfers between devices, swap(): return lax.ppermute(value, axis, pairs)  19 us
    pallas_call x2, Pallas kernels, order_next(): pl.pallas_call(functools.partial(order_next_kernel, offsets), in_specs=[S...  17.6 us
    ppermute x16, waiting for transfers between devices, swap(): return lax.ppermute(value, axis, pairs)  11.8 us
    pallas_call x1, Pallas kernels, order_first(): pl.pallas_call(functools.partial(order_first_kernel, offsets), in_specs=[...  9.47 us
    pallas_call x3, Pallas kernels, put_rows(): pl.pallas_call(functools.partial(put_kernel, offsets, exact), in_specs=[S...  8.62 us
    pallas_call x1, Pallas kernels, take_rows(): pl.pallas_call(take_kernel, in_specs=[SCALARS] + [WHOLE] * 7, out_specs=[...  5.32 us
  transfers between devices with their start and end apart: 16, of which 5 were waited for; matrix products, arithmetic and copies ran while one was open for 1% of the time, Pallas kernels for 58%

profile of v5, /device:TPU:0, one launch (start us, length us, event | category | flops | bytes accessed | tf_op | source)
XLA Modules:
  0.0 99.2 jit_solution(12670442242797848812)
XLA Ops:
  0.6 4.1 %collective-permute-start = (bf16[512,512]{1,0:T(8,128)(2,1)}, bf16[512,512]{1,0:T(8,128)(2,1)S(1)}, u32[]{:S(2)}, u32[]{:S(2)}) collective-permute-start(bf16[512,512]{1,0:T(8,128)(2,1)} %refs_4_.1), channel_id=1, source_target_pairs={{0,16},{8,24},{16,0},{24,8},{1,17},{9,25},{17,1},{25,9},{2,18},{10... | collective-permute-start | bytes 1572872 | tf_op jit(solution)/shard_map/ppermute | solution.py:476
  4.7 1.6 %collective-permute-start.1 = (bf16[512,512]{1,0:T(8,128)(2,1)}, bf16[512,512]{1,0:T(8,128)(2,1)S(1)}, u32[]{:S(2)}, u32[]{:S(2)}) collective-permute-start(bf16[512,512]{1,0:T(8,128)(2,1)} %refs_4_.1), channel_id=1, source_target_pairs={{0,8},{8,0},{16,24},{24,16},{1,9},{9,1},{17,25},{25,17},{2,10},{10... | collective-permute-start | bytes 1572872 | tf_op jit(solution)/shard_map/ppermute | solution.py:476
  6.3 0.1 pad_add_fusion.scalars
  6.4 0.0 copy-start.1
  6.4 9.5 %order_first.1 = (bf16[2048,512]{1,0:T(8,128)(2,1)S(1)}, f32[16,512]{1,0:T(8,128)S(1)}, bf16[2048,2048]{1,0:T(8,128)(2,1)S(1)}, f32[128,128]{1,0:T(8,128)S(1)}, f32[32,2048]{1,0:T(8,128)S(1)}) custom-call(s32[2]{0:T(128)S(1)} %pad_add_fusion.scalars, s32[16,128]{1,0:T(8,128)} %bitcast.34, s32[8,8]{1,0:T(8,128)} %mask_hbm.1, f32[1,2048]{1,0:T(1,128)} %bitcast.35, ...), custom_call_target="tpu_custom_call" | custom-call | flops 4294967296 | bytes 16777216 | tf_op jit(solution)/shard_map/order_first/pallas_call | solution.py:173
  15.9 0.0 copy-done.1
  15.9 2.5 %collective-permute-start.4 = (bf16[256,512]{1,0:T(8,128)(2,1)S(1)}, bf16[256,512]{1,0:T(8,128)(2,1)S(1)}, u32[]{:S(2)}, u32[]{:S(2)}) collective-permute-start(bf16[256,512]{1,0:T(8,128)(2,1)S(1)} %copy-done.1), channel_id=1, source_target_pairs={{0,6},{1,7},{2,4},{3,5},{4,2},{5,3},{6,0},{7,1},{8,14},{9,15},{10,... | collective-permute-start | bytes 786440 | tf_op jit(solution)/shard_map/ppermute | solution.py:476
  18.4 0.5 collective-permute-start.3
  18.9 0.5 collective-permute-start.2
  19.4 11.2 %order_next.2 = (bf16[2048,512]{1,0:T(8,128)(2,1)S(1)}, bf16[2048,512]{1,0:T(8,128)(2,1)S(1)}, f32[16,512]{1,0:T(8,128)S(1)}, f32[16,512]{1,0:T(8,128)S(1)}) custom-call(s32[2]{0:T(128)S(1)} %pad_add_fusion.scalars, bf16[2048,2048]{1,0:T(8,128)(2,1)S(1)} %get-tuple-element.52.shifted_ref, f32[128,128]{1,0:T(8,128)S(1)} %get-tuple-element.49.columns_ref, ...), custom_call_target="tpu_custom_call" | custom-call | flops 1048576 | bytes 1048576 | tf_op jit(solution)/shard_map/order_next/pallas_call | solution.py:221
  30.6 0.0 collective-permute-done.4.refs_3_
  30.6 0.0 collective-permute-done.3.refs_2_
  30.6 0.0 collective-permute-done.2.refs_1_
  30.6 0.0 collective-permute-done.refs_3_
  30.6 0.0 collective-permute-done.1.refs_3_
  30.7 0.1 pad_maximum_fusion
  30.8 0.0 copy-start.2
  30.8 0.0 copy-start.3
  30.8 0.1 collective-permute-start.5
  30.9 0.5 collective-permute-start.6
  31.4 6.4 %order_next.3 = (bf16[2048,512]{1,0:T(8,128)(2,1)S(1)}, f32[16,512]{1,0:T(8,128)S(1)}) custom-call(s32[2]{0:T(128)S(1)} %pad_add_fusion.scalars, bf16[2048,2048]{1,0:T(8,128)(2,1)S(1)} %get-tuple-element.52.shifted_ref, f32[128,128]{1,0:T(8,128)S(1)} %get-tuple-element.49.columns_ref, f32[32,2048]{1,0:T(8,128)S(1)} %get-tuple-element.50.values_ref), custom_call_target="tpu_custom_call" | custom-call | flops 1048576 | bytes 1048576 | tf_op jit(solution)/shard_map/order_next/pallas_call | solution.py:221
  37.9 0.0 collective-permute-done.5.refs_4_
  37.9 0.0 copy-done.2
  37.9 0.0 copy-done.3
  37.9 5.3 %take_rows.1 = (bf16[2048,512]{1,0:T(8,128)(2,1)S(1)}, bf16[512,2048]{1,0:T(8,128)(2,1)S(1)}, f32[2048,128]{1,0:T(8,128)S(1)}) custom-call(s32[2]{0:T(128)S(1)} %pad_add_fusion.scalars, s32[16,128]{1,0:T(8,128)S(1)} %bitcast.29, f32[16,128]{1,0:T(8,128)S(1)} %bitcast.33, bf16[256,512]{1,0:T(8,128)(2,1)S(1)} %copy-done.1, ...), custom_call_target="tpu_custom_call" | custom-call | flops 4294967296 | bytes 4194304 | tf_op jit(solution)/shard_map/take_rows/pallas_call | solution.py:265
  43.2 2.0 %collective-permute-done.6.refs_3_ = bf16[512,512]{1,0:T(8,128)(2,1)S(1)} collective-permute-done((bf16[512,512]{1,0:T(8,128)(2,1)S(1)}, bf16[512,512]{1,0:T(8,128)(2,1)S(1)}, u32[]{:S(2)}, u32[]{:S(2)}) %collective-permute-start.6) | collective-permute-done | bytes 524320 | tf_op jit(solution)/shard_map/ppermute | solution.py:476
  45.2 5.2 %cells.3 = (f32[2048,512]{1,0:T(8,128)S(1)}, bf16[256,512]{1,0:T(8,128)(2,1)S(1)}, bf16[256,512]{1,0:T(8,128)(2,1)S(1)}) custom-call(bf16[2048,512]{1,0:T(8,128)(2,1)S(1)} %get-tuple-element.58.refs_0_, bf16[512,2048]{1,0:T(8,128)(2,1)S(1)} %get-tuple-element.59.refs_1_, f32[2048,128]{1,0:T(8,128)S(1)} %get-tuple-element.60.refs_2_, ...), custom_call_target="tpu_custom_call" | custom-call | flops 1048576 | bytes 1048576 | tf_op jit(solution)/shard_map/cells/pallas_call | solution.py:402
  50.4 0.5 collective-permute-start.7
  50.9 1.6 %collective-permute-start.8 = (bf16[256,512]{1,0:T(8,128)(2,1)S(1)}, bf16[256,512]{1,0:T(8,128)(2,1)S(1)}, u32[]{:S(2)}, u32[]{:S(2)}) collective-permute-start(bf16[256,512]{1,0:T(8,128)(2,1)S(1)} %get-tuple-element.79), channel_id=1, source_target_pairs={{0,8},{8,0},{16,24},{24,16},{1,9},{9,1},{17,25},{25,17},{2,10},{10... | collective-permute-start | bytes 786440 | tf_op jit(solution)/shard_map/ppermute | solution.py:476
  52.5 0.0 copy-start
  52.5 5.8 %cells.4 = (f32[2048,512]{1,0:T(8,128)S(1)}, f32[512,512]{1,0:T(8,128)S(1)}) custom-call(bf16[2048,512]{1,0:T(8,128)(2,1)S(1)} %get-tuple-element.58.refs_0_, bf16[512,2048]{1,0:T(8,128)(2,1)S(1)} %get-tuple-element.59.refs_1_, f32[2048,128]{1,0:T(8,128)S(1)} %get-tuple-element.60.refs_2_, ...), custom_call_target="tpu_custom_call", output_to_operand_aliasing={{0}: (6, {})} | custom-call | flops 1048576 | bytes 1048576 | tf_op jit(solution)/shard_map/cells/pallas_call | solution.py:402
  58.3 1.4 %collective-permute-done.7 = bf16[256,512]{1,0:T(8,128)(2,1)S(1)} collective-permute-done((bf16[256,512]{1,0:T(8,128)(2,1)S(1)}, bf16[256,512]{1,0:T(8,128)(2,1)S(1)}, u32[]{:S(2)}, u32[]{:S(2)}) %collective-permute-start.7) | collective-permute-done | bytes 262176 | tf_op jit(solution)/shard_map/ppermute | solution.py:476
  59.7 0.1 add_convert_fusion.2
  59.8 0.4 collective-permute-start.9
  60.2 0.0 copy-done
  60.2 12.6 %cells.5 = (f32[2048,512]{1,0:T(8,128)S(1)}, bf16[512,512]{1,0:T(8,128)(2,1)S(1)}, f32[512,512]{1,0:T(8,128)S(1)}) custom-call(bf16[2048,512]{1,0:T(8,128)(2,1)S(1)} %get-tuple-element.58.refs_0_, bf16[512,2048]{1,0:T(8,128)(2,1)S(1)} %get-tuple-element.59.refs_1_, f32[2048,128]{1,0:T(8,128)S(1)} %get-tuple-element.60.refs_2_, ...), custom_call_target="tpu_custom_call", output_to_operand_aliasing={{0}: (9, {})} | custom-call | flops 1048576 | bytes 1048576 | tf_op jit(solution)/shard_map/cells/pallas_call | solution.py:402
  72.7 0.0 collective-permute-done.8
  72.7 0.0 collective-permute-done.9.refs_2_
  72.7 0.1 add_convert_fusion.1
  72.8 2.9 %put_rows.3 = bf16[4,256,512]{2,1,0:T(8,128)(2,1)S(1)} custom-call(s32[2]{0:T(128)S(1)} %pad_add_fusion.scalars, s32[1,2048]{1,0:T(1,128)S(1)} %bitcast.30, f32[2048,512]{1,0:T(8,128)S(1)} %get-tuple-element.84.grad_ref), custom_call_target="tpu_custom_call" | custom-call | flops 1048576 | bytes 65536 | tf_op jit(solution)/shard_map/put_rows/pallas_call | solution.py:462
  75.7 0.1 collective-permute-start.10
  75.8 1.3 %collective-permute-start.14 = (bf16[512,512]{1,0:T(8,128)(2,1)S(1)}, bf16[512,512]{1,0:T(8,128)(2,1)S(1)}, u32[]{:S(2)}, u32[]{:S(2)}) collective-permute-start(bf16[512,512]{1,0:T(8,128)(2,1)S(1)} %get-tuple-element.88), channel_id=1, source_target_pairs={{0,8},{8,0},{16,24},{24,16},{1,9},{9,1},{17,25},{25,17},{2,10},{10... | collective-permute-start | bytes 1572872 | tf_op jit(solution)/shard_map/ppermute | solution.py:476
  77.1 1.8 %collective-permute-start.15 = (bf16[256,512]{1,0:T(8,128)(2,1)S(1)}, bf16[256,512]{1,0:T(8,128)(2,1)S(1)}, u32[]{:S(2)}, u32[]{:S(2)}) collective-permute-start(bf16[256,512]{1,0:T(8,128)(2,1)S(1)} %add_convert_fusion.1), channel_id=1, source_target_pairs={{0,16},{8,24},{16,0},{24,8},{1,17},{9,25},{17,1},{25,9},{2,18},{10... | collective-permute-start | bytes 786440 | tf_op jit(solution)/shard_map/ppermute | solution.py:476
  78.9 3.9 %put_rows.4 = f32[3,256,512]{2,1,0:T(8,128)S(1)} custom-call(s32[2]{0:T(128)S(1)} %pad_add_fusion.scalars, s32[1,2048]{1,0:T(1,128)S(1)} %bitcast.31, f32[2048,512]{1,0:T(8,128)S(1)} %get-tuple-element.84.grad_ref), custom_call_target="tpu_custom_call" | custom-call | flops 4294967296 | bytes 65536 | tf_op jit(solution)/shard_map/put_rows/pallas_call | solution.py:462
  82.8 0.0 collective-permute-done.10
  82.9 0.3 add_convert_fusion
  83.2 0.1 slice_bitcast_fusion.1
  83.2 1.6 %collective-permute-start.11 = (bf16[256,512]{1,0:T(8,128)(2,1)S(1)}, bf16[256,512]{1,0:T(8,128)(2,1)S(1)}, u32[]{:S(2)}, u32[]{:S(2)}) collective-permute-start(bf16[256,512]{1,0:T(8,128)(2,1)S(1)} %get-tuple-element.90), channel_id=1, source_target_pairs={{0,4},{1,5},{2,6},{3,7},{4,0},{5,1},{6,2},{7,3},{8,12},{9,13},{10,... | collective-permute-start | bytes 786440 | tf_op jit(solution)/shard_map/ppermute | solution.py:476
  84.8 1.4 %collective-permute-start.12 = (bf16[256,512]{1,0:T(8,128)(2,1)S(1)}, bf16[256,512]{1,0:T(8,128)(2,1)S(1)}, u32[]{:S(2)}, u32[]{:S(2)}) collective-permute-start(bf16[256,512]{1,0:T(8,128)(2,1)S(1)} %get-tuple-element.91), channel_id=1, source_target_pairs={{0,6},{1,7},{2,4},{3,5},{4,2},{5,3},{6,0},{7,1},{8,14},{9,15},{10,... | collective-permute-start | bytes 786440 | tf_op jit(solution)/shard_map/ppermute | solution.py:476
  86.2 0.6 collective-permute-start.13
  86.8 1.8 %put_rows.5 = f32[1,256,512]{2,1,0:T(8,128)S(1)} custom-call(s32[2]{0:T(128)S(1)} %pad_add_fusion.scalars, s32[1,2048]{1,0:T(1,128)S(1)} %bitcast.32, f32[2048,512]{1,0:T(8,128)S(1)} %get-tuple-element.84.grad_ref), custom_call_target="tpu_custom_call" | custom-call | flops 1048576 | bytes 65536 | tf_op jit(solution)/shard_map/put_rows/pallas_call | solution.py:462
  88.6 5.9 %collective-permute-done.15.refs_3_ = bf16[256,512]{1,0:T(8,128)(2,1)S(1)} collective-permute-done((bf16[256,512]{1,0:T(8,128)(2,1)S(1)}, bf16[256,512]{1,0:T(8,128)(2,1)S(1)}, u32[]{:S(2)}, u32[]{:S(2)}) %collective-permute-start.15) | collective-permute-done | bytes 262176 | tf_op jit(solution)/shard_map/ppermute | solution.py:476
  94.5 1.3 %collective-permute-done.14.refs_1_ = bf16[512,512]{1,0:T(8,128)(2,1)S(1)} collective-permute-done((bf16[512,512]{1,0:T(8,128)(2,1)S(1)}, bf16[512,512]{1,0:T(8,128)(2,1)S(1)}, u32[]{:S(2)}, u32[]{:S(2)}) %collective-permute-start.14) | collective-permute-done | bytes 524320 | tf_op jit(solution)/shard_map/ppermute | solution.py:476
  95.7 1.3 %finish.1 = f32[512,512]{1,0:T(8,128)} custom-call(f32[512,512]{1,0:T(8,128)S(1)} %get-tuple-element.87.refs_0_, bf16[512,512]{1,0:T(8,128)(2,1)S(1)} %collective-permute-done.14.refs_1_, bf16[256,512]{1,0:T(8,128)(2,1)S(1)} %collective-permute-done.9.refs_2_, bf16[256,512]{1,0:T(8,128)(2,1)S(1)} %collective-permute-done.15.refs_3_), custom_call_target="tpu_custom_call" | custom-call | flops 262144 | bytes 16384 | tf_op jit(solution)/shard_map/finish/pallas_call | solution.py:430
  97.0 0.0 collective-permute-done.11
  97.1 0.0 collective-permute-done.12
  97.1 1.2 %collective-permute-done.13 = bf16[256,512]{1,0:T(8,128)(2,1)S(1)} collective-permute-done((bf16[256,512]{1,0:T(8,128)(2,1)S(1)}, bf16[256,512]{1,0:T(8,128)(2,1)S(1)}, u32[]{:S(2)}, u32[]{:S(2)}) %collective-permute-start.13) | collective-permute-done | bytes 262176 | tf_op jit(solution)/shard_map/ppermute | solution.py:476
  98.2 1.0 fusion.2
Async XLA Ops:
  0.6 30.0 %collective-permute-start = (bf16[512,512]{1,0:T(8,128)(2,1)}, bf16[512,512]{1,0:T(8,128)(2,1)S(1)}, u32[]{:S(2)}, u32[]{:S(2)}) collective-permute-start(bf16[512,512]{1,0:T(8,128)(2,1)} %refs_4_.1), channel_id=1, source_target_pairs={{0,16},{8,24},{16,0},{24,8},{1,17},{9,25},{17,1},{25,9},{2,18},{10... | collective-permute-start | bytes 1572872 | tf_op jit(solution)/shard_map/ppermute | solution.py:476
  4.7 25.9 %collective-permute-start.1 = (bf16[512,512]{1,0:T(8,128)(2,1)}, bf16[512,512]{1,0:T(8,128)(2,1)S(1)}, u32[]{:S(2)}, u32[]{:S(2)}) collective-permute-start(bf16[512,512]{1,0:T(8,128)(2,1)} %refs_4_.1), channel_id=1, source_target_pairs={{0,8},{8,0},{16,24},{24,16},{1,9},{9,1},{17,25},{25,17},{2,10},{10... | collective-permute-start | bytes 1572872 | tf_op jit(solution)/shard_map/ppermute | solution.py:476
  6.4 9.5 %copy-start.1 = (bf16[256,512]{1,0:T(8,128)(2,1)S(1)}, bf16[256,512]{1,0:T(8,128)(2,1)}, u32[]{:S(2)}) copy-start(bf16[256,512]{1,0:T(8,128)(2,1)} %refs_0_.1) | copy-start | bytes 786436
  15.9 14.7 %collective-permute-start.4 = (bf16[256,512]{1,0:T(8,128)(2,1)S(1)}, bf16[256,512]{1,0:T(8,128)(2,1)S(1)}, u32[]{:S(2)}, u32[]{:S(2)}) collective-permute-start(bf16[256,512]{1,0:T(8,128)(2,1)S(1)} %copy-done.1), channel_id=1, source_target_pairs={{0,6},{1,7},{2,4},{3,5},{4,2},{5,3},{6,0},{7,1},{8,14},{9,15},{10,... | collective-permute-start | bytes 786440 | tf_op jit(solution)/shard_map/ppermute | solution.py:476
  18.4 12.2 %collective-permute-start.3 = (bf16[256,512]{1,0:T(8,128)(2,1)S(1)}, bf16[256,512]{1,0:T(8,128)(2,1)S(1)}, u32[]{:S(2)}, u32[]{:S(2)}) collective-permute-start(bf16[256,512]{1,0:T(8,128)(2,1)S(1)} %copy-done.1), channel_id=1, source_target_pairs={{0,4},{1,5},{2,6},{3,7},{4,0},{5,1},{6,2},{7,3},{8,12},{9,13},{10,... | collective-permute-start | bytes 786440 | tf_op jit(solution)/shard_map/ppermute | solution.py:476
  18.9 11.7 %collective-permute-start.2 = (bf16[256,512]{1,0:T(8,128)(2,1)S(1)}, bf16[256,512]{1,0:T(8,128)(2,1)S(1)}, u32[]{:S(2)}, u32[]{:S(2)}) collective-permute-start(bf16[256,512]{1,0:T(8,128)(2,1)S(1)} %copy-done.1), channel_id=1, source_target_pairs={{0,2},{1,3},{2,0},{3,1},{4,6},{5,7},{6,4},{7,5},{8,10},{9,11},{10,... | collective-permute-start | bytes 786440 | tf_op jit(solution)/shard_map/ppermute | solution.py:476
  30.8 7.1 %copy-start.2 = (s32[2048]{0:T(1024)S(1)}, s32[2048]{0:T(1024)}, u32[]{:S(2)}) copy-start(s32[2048]{0:T(1024)} %param.10) | copy-start | bytes 24580
  30.8 7.1 %copy-start.3 = (f32[2048]{0:T(1024)S(1)}, f32[2048]{0:T(1024)}, u32[]{:S(2)}) copy-start(f32[2048]{0:T(1024)} %param.12) | copy-start | bytes 24580
  30.8 7.0 %collective-permute-start.5 = (bf16[4,256,512]{2,1,0:T(8,128)(2,1)S(1)}, bf16[4,256,512]{2,1,0:T(8,128)(2,1)S(1)}, u32[]{:S(2)}, u32[]{:S(2)}) collective-permute-start(bf16[4,256,512]{2,1,0:T(8,128)(2,1)S(1)} %pad_maximum_fusion), channel_id=1, source_target_pairs={{0,1},{1,0},{2,3},{3,2},{4,5},{5,4},{6,7},{7,6},{8,9},{9,8},{10,11... | collective-permute-start | bytes 3145736 | tf_op jit(solution)/shard_map/ppermute | solution.py:476
  30.9 14.3 %collective-permute-start.6 = (bf16[512,512]{1,0:T(8,128)(2,1)S(1)}, bf16[512,512]{1,0:T(8,128)(2,1)S(1)}, u32[]{:S(2)}, u32[]{:S(2)}) collective-permute-start(bf16[512,512]{1,0:T(8,128)(2,1)S(1)} %collective-permute-done.refs_3_), channel_id=1, source_target_pairs={{0,8},{8,0},{16,24},{24,16},{1,9},{9,1},{17,25},{25,17},{2,10},{10... | collective-permute-start | bytes 1572872 | tf_op jit(solution)/shard_map/ppermute | solution.py:476
  50.4 9.3 %collective-permute-start.7 = (bf16[256,512]{1,0:T(8,128)(2,1)S(1)}, bf16[256,512]{1,0:T(8,128)(2,1)S(1)}, u32[]{:S(2)}, u32[]{:S(2)}) collective-permute-start(bf16[256,512]{1,0:T(8,128)(2,1)S(1)} %get-tuple-element.73), channel_id=1, source_target_pairs={{0,8},{8,0},{16,24},{24,16},{1,9},{9,1},{17,25},{25,17},{2,10},{10... | collective-permute-start | bytes 786440 | tf_op jit(solution)/shard_map/ppermute | solution.py:476
  50.9 21.8 %collective-permute-start.8 = (bf16[256,512]{1,0:T(8,128)(2,1)S(1)}, bf16[256,512]{1,0:T(8,128)(2,1)S(1)}, u32[]{:S(2)}, u32[]{:S(2)}) collective-permute-start(bf16[256,512]{1,0:T(8,128)(2,1)S(1)} %get-tuple-element.79), channel_id=1, source_target_pairs={{0,8},{8,0},{16,24},{24,16},{1,9},{9,1},{17,25},{25,17},{2,10},{10... | collective-permute-start | bytes 786440 | tf_op jit(solution)/shard_map/ppermute | solution.py:476
  52.5 7.7 %copy-start = (bf16[512,512]{1,0:T(8,128)(2,1)S(1)}, bf16[512,512]{1,0:T(8,128)(2,1)}, u32[]{:S(2)}) copy-start(bf16[512,512]{1,0:T(8,128)(2,1)} %refs_4_.1) | copy-start | bytes 1572868
  59.8 13.0 %collective-permute-start.9 = (bf16[256,512]{1,0:T(8,128)(2,1)S(1)}, bf16[256,512]{1,0:T(8,128)(2,1)S(1)}, u32[]{:S(2)}, u32[]{:S(2)}) collective-permute-start(bf16[256,512]{1,0:T(8,128)(2,1)S(1)} %add_convert_fusion.2), channel_id=1, source_target_pairs={{0,16},{8,24},{16,0},{24,8},{1,17},{9,25},{17,1},{25,9},{2,18},{10... | collective-permute-start | bytes 786440 | tf_op jit(solution)/shard_map/ppermute | solution.py:476
  75.7 7.2 %collective-permute-start.10 = (bf16[4,256,512]{2,1,0:T(8,128)(2,1)S(1)}, bf16[4,256,512]{2,1,0:T(8,128)(2,1)S(1)}, u32[]{:S(2)}, u32[]{:S(2)}) collective-permute-start(bf16[4,256,512]{2,1,0:T(8,128)(2,1)S(1)} %put_rows.3), channel_id=1, source_target_pairs={{0,1},{1,0},{2,3},{3,2},{4,5},{5,4},{6,7},{7,6},{8,9},{9,8},{10,11... | collective-permute-start | bytes 3145736 | tf_op jit(solution)/shard_map/ppermute | solution.py:476
  75.8 20.0 %collective-permute-start.14 = (bf16[512,512]{1,0:T(8,128)(2,1)S(1)}, bf16[512,512]{1,0:T(8,128)(2,1)S(1)}, u32[]{:S(2)}, u32[]{:S(2)}) collective-permute-start(bf16[512,512]{1,0:T(8,128)(2,1)S(1)} %get-tuple-element.88), channel_id=1, source_target_pairs={{0,8},{8,0},{16,24},{24,16},{1,9},{9,1},{17,25},{25,17},{2,10},{10... | collective-permute-start | bytes 1572872 | tf_op jit(solution)/shard_map/ppermute | solution.py:476
  77.1 17.4 %collective-permute-start.15 = (bf16[256,512]{1,0:T(8,128)(2,1)S(1)}, bf16[256,512]{1,0:T(8,128)(2,1)S(1)}, u32[]{:S(2)}, u32[]{:S(2)}) collective-permute-start(bf16[256,512]{1,0:T(8,128)(2,1)S(1)} %add_convert_fusion.1), channel_id=1, source_target_pairs={{0,16},{8,24},{16,0},{24,8},{1,17},{9,25},{17,1},{25,9},{2,18},{10... | collective-permute-start | bytes 786440 | tf_op jit(solution)/shard_map/ppermute | solution.py:476
  83.2 13.8 %collective-permute-start.11 = (bf16[256,512]{1,0:T(8,128)(2,1)S(1)}, bf16[256,512]{1,0:T(8,128)(2,1)S(1)}, u32[]{:S(2)}, u32[]{:S(2)}) collective-permute-start(bf16[256,512]{1,0:T(8,128)(2,1)S(1)} %get-tuple-element.90), channel_id=1, source_target_pairs={{0,4},{1,5},{2,6},{3,7},{4,0},{5,1},{6,2},{7,3},{8,12},{9,13},{10,... | collective-permute-start | bytes 786440 | tf_op jit(solution)/shard_map/ppermute | solution.py:476
  84.8 12.2 %collective-permute-start.12 = (bf16[256,512]{1,0:T(8,128)(2,1)S(1)}, bf16[256,512]{1,0:T(8,128)(2,1)S(1)}, u32[]{:S(2)}, u32[]{:S(2)}) collective-permute-start(bf16[256,512]{1,0:T(8,128)(2,1)S(1)} %get-tuple-element.91), channel_id=1, source_target_pairs={{0,6},{1,7},{2,4},{3,5},{4,2},{5,3},{6,0},{7,1},{8,14},{9,15},{10,... | collective-permute-start | bytes 786440 | tf_op jit(solution)/shard_map/ppermute | solution.py:476
  86.2 12.0 %collective-permute-start.13 = (bf16[256,512]{1,0:T(8,128)(2,1)S(1)}, bf16[256,512]{1,0:T(8,128)(2,1)S(1)}, u32[]{:S(2)}, u32[]{:S(2)}) collective-permute-start(bf16[256,512]{1,0:T(8,128)(2,1)S(1)} %get-tuple-element.92), channel_id=1, source_target_pairs={{0,2},{1,3},{2,0},{3,1},{4,6},{5,7},{6,4},{7,5},{8,10},{9,11},{10,... | collective-permute-start | bytes 786440 | tf_op jit(solution)/shard_map/ppermute | solution.py:476

commit v6 on v2

--- a/solution.py
+++ b/solution.py
@@ -278,21 +278,27 @@
     )(scalars, row_perm.reshape(-1, LANES), row_logm.reshape(-1, LANES), *blocks)
 
 
-def chunk_work(
-    chunk, wvec_ref, turned_ref, count_ref, aux_ref, logm_ref, before_ref, grad_ref, term_ref, chunk_turned, delta_ref
-):
+def cells_kernel(others, pieces, *refs):
+    wvec_ref, turned_ref, logm_ref, chunk, count_ref, aux_ref, refs = *refs[:6], refs[6:]
+    chunk_refs, delta_refs, refs = refs[:others], refs[others : 2 * others], refs[2 * others :]
+    main_ref, out_refs, refs = refs[0], refs[1 : 1 + max(pieces, 1)], refs[1 + max(pieces, 1) :]
+    chunk_turned, term_ref, refs = refs[0], refs[1], refs[2:]
     chunk_turned[...] = chunk[...].T
     rows = wvec_ref.shape[0]
     width = chunk.shape[0]
     blocks = aux_ref.shape[0] - 8
     tile = rows // blocks
+    col_logm = aux_ref[pl.ds(blocks, 1), :]
+    if others:
+        delta_ref, stack = refs
+        for at, ref in enumerate([*chunk_refs, chunk]):
+            stack[pl.ds(at * width, width), :] = ref[...]
+    else:
+        delta_ref = main_ref
     joined = delta_ref.shape[0] // tile
     half = joined // 2
-    col_logm = aux_ref[blocks : blocks + 1, :]
-    term_ref[...] = jnp.zeros_like(term_ref)
-
-    @pl.loop(0, blocks // joined)
-    def _(group):
+
+    def part(group):
         def rows_at(at, count=1):
             return pl.ds(pl.multiple_of((group * joined + at) * tile, tile), count * tile)
 
@@ -314,15 +320,17 @@
             active = aux_ref[pl.ds(group * joined + at, 1), :]
             delta_ref[pl.ds(at * tile, tile), :] = (deriv * active).astype(BF16)
 
-        def grad_of(at):
-            grad = jnp.dot(held(at), chunk[...], preferred_element_type=F32)
-            if before_ref is not None:
-                grad = grad + before_ref[rows_at(at), :]
-            grad_ref[rows_at(at), :] = grad
+        def grad_of(at, count):
+            here = rows_at(at, count)
+            deltas = jnp.concatenate([ref[here, :] for ref in delta_refs] + [held(at, count)], axis=1)
+            main_ref[here, :] = jnp.dot(deltas, stack[...], preferred_element_type=F32)
 
         def term_of(at):
             turned = turned_ref[:, rows_at(at, half)]
-            term_ref[...] += jnp.dot(turned, held(at, half), preferred_element_type=F32)
+            term = jnp.dot(turned, held(at, half), preferred_element_type=F32)
+            if joined < blocks or at:
+                term = term_ref[...] + term
+            term_ref[...] = term
 
         ahead = score_of(0)
         for at in range(joined):
@@ -330,65 +338,45 @@
             if at + 1 < joined:
                 ahead = score_of(at + 1)
             delta_of(at, score)
-            if at:
-                grad_of(at - 1)
             if at == half:
                 term_of(0)
-        grad_of(joined - 1)
+                if others:
+                    grad_of(0, half)
         term_of(half)
-
-
-def cells_kernel(has_sum, sends, *refs):
-    chunks = len(sends)
-    wvec_ref, turned_ref, logm_ref, refs = *refs[:3], refs[3:]
-    chunk_refs, count_refs, aux_refs = refs[:chunks], refs[chunks : 2 * chunks], refs[2 * chunks : 3 * chunks]
-    refs = refs[3 * chunks :]
-    before_ref = None
-    if has_sum:
-        before_ref, refs = refs[0], refs[1:]
-    grad_ref, refs = refs[0], refs[1:]
-    chunk_turned, delta_ref, sum_ref = refs[-3:]
-    for at, pieces in enumerate(sends):
-        term_ref = sum_ref
-        if not pieces:
-            term_ref, refs = refs[0], refs[1:]
-        chunk_work(
-            chunk_refs[at], wvec_ref, turned_ref, count_refs[at], aux_refs[at], logm_ref,
-            before_ref, grad_ref, term_ref, chunk_turned, delta_ref,
-        )
-        before_ref = grad_ref
-        for piece in range(pieces):
-            sent_ref, refs = refs[0], refs[1:]
-            size = sent_ref.shape[0]
-            sent_ref[...] = term_ref[pl.ds(piece * size, size), :].astype(BF16)
-
-
-def cells(rows_in, chunks, before, sends):
+        if others:
+            grad_of(half, half)
+
+    if joined < blocks:
+        term_ref[...] = jnp.zeros_like(term_ref)
+        pl.loop(0, blocks // joined)(part)
+    else:
+        part(0)
+    for piece, out_ref in enumerate(out_refs):
+        size = out_ref.shape[0]
+        out_ref[...] = term_ref[pl.ds(piece * size, size), :].astype(out_ref.dtype)
+
+
+def cells(rows_in, chunk, pieces, others=()):
     wvec = rows_in[0]
     rows, depth = wvec.shape
-    width = chunks[0][0].shape[0]
-    args = [*rows_in, *[each for kind in zip(*chunks) for each in kind]]
-    aliases = {}
-    if before is not None:
-        aliases = {len(args): 0}
-        args.append(before)
-    out_shape = [jax.ShapeDtypeStruct((rows, depth), F32)]
-    for pieces in sends:
-        if pieces:
-            out_shape += [jax.ShapeDtypeStruct((depth // pieces, width), BF16) for _ in range(pieces)]
-        else:
-            out_shape.append(jax.ShapeDtypeStruct((depth, width), F32))
+    width = chunk[0].shape[0]
+    args = [*rows_in, *chunk, *[each for each, _ in others], *[delta for _, delta in others]]
+    if others:
+        main = jax.ShapeDtypeStruct((rows, depth), F32)
+        scratch = [pltpu.VMEM((rows // 2, width), BF16), pltpu.VMEM(((len(others) + 1) * width, depth), BF16)]
+    else:
+        main = jax.ShapeDtypeStruct((rows, width), BF16)
+        scratch = []
+    if pieces:
+        outs = [jax.ShapeDtypeStruct((depth // pieces, width), BF16) for _ in range(pieces)]
+    else:
+        outs = [jax.ShapeDtypeStruct((depth, width), F32)]
     return pl.pallas_call(
-        functools.partial(cells_kernel, before is not None, sends),
+        functools.partial(cells_kernel, len(others), pieces),
         in_specs=[WHOLE] * len(args),
-        out_specs=[WHOLE] * len(out_shape),
-        out_shape=out_shape,
-        scratch_shapes=[
-            pltpu.VMEM((depth, width), BF16),
-            pltpu.VMEM((rows // 2, width), BF16),
-            pltpu.VMEM((depth, width), F32),
-        ],
-        input_output_aliases=aliases,
+        out_specs=[WHOLE] * (1 + len(outs)),
+        out_shape=[main, *outs],
+        scratch_shapes=[pltpu.VMEM((depth, width), BF16), pltpu.VMEM((depth, width), F32), *scratch],
         compiler_params=params(24),
         cost_estimate=cost(rows * width, rows * depth),
         name="cells",
@@ -416,7 +404,7 @@
     )(own, near, *crosses)
 
 
-def put_kernel(offsets, exact, scalars, perm_ref, grad_ref, out_ref):
+def put_kernel(offsets, exact, scalars, perm_ref, grad_ref, out_ref, pick):
     grad = grad_ref[...]
     rows, width = grad.shape
     high = grad.astype(BF16)
@@ -428,11 +416,11 @@
     vocab = lax.broadcasted_iota(jnp.int32, (side, rows), 0)
     for at, offset in enumerate(offsets):
         base = jnp.bitwise_xor(scalars[COL_AT], offset) * side
-        pick = onehot(index == (vocab + base).astype(F32))
-        moved = jnp.dot(pick, moving, preferred_element_type=F32)
-        if exact:
-            moved = moved[:, :width] + moved[:, width:]
-        out_ref[at] = moved.astype(out_ref.dtype)
+        pick[pl.ds(at * side, side), :] = onehot(index == (vocab + base).astype(F32))
+    moved = jnp.dot(pick[...], moving, preferred_element_type=F32)
+    if exact:
+        moved = moved[:, :width] + moved[:, width:]
+    out_ref[...] = moved.astype(out_ref.dtype).reshape(out_ref.shape)
 
 
 def put_rows(scalars, row_perm, grad, offsets, side, exact):
@@ -442,6 +430,7 @@
         in_specs=[SCALARS, WHOLE, WHOLE],
         out_specs=WHOLE,
         out_shape=jax.ShapeDtypeStruct((len(offsets), side, width), F32 if exact else BF16),
+        scratch_shapes=[pltpu.VMEM((len(offsets) * side, grad.shape[0]), BF16)],
         compiler_params=params(24),
         cost_estimate=cost((4096 if exact and len(offsets) > 1 else 1) * grad.size, grad.size // 16),
         name="put_rows",
@@ -487,18 +476,21 @@
     rows_in = (wvec, turned, logm)
     of_far, of_cross = (far, count_far, aux_far), (cross, count_cross, aux_cross)
     of_near, of_own = (near, count_near, aux_near), (col_emb, count_own, aux_own)
-    grad, sent_0, sent_1 = cells(rows_in, [of_far], None, (2,))
+    delta_far, sent_0, sent_1 = cells(rows_in, of_far, 2)
     far_0 = swap(sent_0, "row", 1)
     far_1 = swap(sent_1, "row", 1)
-    grad, term_cross = cells(rows_in, [of_cross], grad, (0,))
-    grad, far_0 = together((grad, far_0))
+    rows_in, delta_far = together((rows_in, delta_far))
+    delta_cross, term_cross = cells(rows_in, of_cross, 0)
+    rows_in, term_cross, far_0 = together((rows_in, term_cross, far_0))
 
     half = term_cross.shape[0] // 2
     sum_0 = (term_cross[:half] + far_0.astype(F32)).astype(BF16)
+    rows_in, sum_0 = together((rows_in, sum_0))
     cross_0 = swap(sum_0, "row", 2)
-    grad, sum_0 = together((grad, sum_0))
-    grad, sent_near, term_own = cells(rows_in, [of_near, of_own], grad, (1, 0))
+    delta_near, sent_near = cells(rows_in, of_near, 1)
     got_near = swap(sent_near, "row", 1)
+    others = ((far, delta_far), (cross, delta_cross), (near, delta_near))
+    grad, term_own = cells(rows_in, of_own, 0, others)
     grad, far_1, cross_0 = together((grad, far_1, cross_0))
     sum_1 = (term_cross[half:] + far_1.astype(F32)).astype(BF16)
     cross_1 = swap(sum_1, "row", 2)
@@ -510,7 +502,7 @@
     grad, away = together((grad, away))
     both = ordered(grad, (2, 4, 6), side, True) + core[1:].astype(F32)
     sends = [both[at].astype(BF16) for at in range(3)]
-    got = [swap(sent, "col", bit) for sent, bit in zip(sends, (2, 4, 6))]
+    got = [swap(sends[at], "col", bit) for at, bit in ((1, 4), (2, 6), (0, 2))]
     grad, sends = together((grad, sends))
     home = ordered(grad, (0,), side, True)
     home, term_own = together((home, term_own))

time: 100 us -> 99.7 us (level)
    pallas_call x3 -> x4, Pallas kernels: 23.1 us -> 22.4 us  [cells(): pl.pallas_call(functools.partial(cells_kernel, len(others), pieces), in_s...]
  transfers between devices with their start and end apart: 16 -> 16, of which waited for: 7 -> 5; matrix products, arithmetic and copies ran while one was open for 1% -> 0% of each run, Pallas kernels for 57% -> 58%
where the time goes in v6:
time: 99.7 us; the launch traced here: 99.5 us
  Pallas kernels  64.7 us (65%)
  starting transfers between devices  19 us (19%)
  waiting for transfers between devices  13.1 us (13%)
  other arithmetic  1.61 us (2%)
    pallas_call x4, Pallas kernels, cells(): pl.pallas_call(functools.partial(cells_kernel, len(others), pieces), in_s...  22.4 us
    ppermute x16, starting transfers between devices, swap(): return lax.ppermute(value, axis, pairs)  19 us
    pallas_call x2, Pallas kernels, order_next(): pl.pallas_call(functools.partial(order_next_kernel, offsets), in_specs=[S...  17.6 us
    ppermute x16, waiting for transfers between devices, swap(): return lax.ppermute(value, axis, pairs)  13.1 us
    pallas_call x1, Pallas kernels, order_first(): pl.pallas_call(functools.partial(order_first_kernel, offsets), in_specs=[...  9.47 us
    pallas_call x3, Pallas kernels, put_rows(): pl.pallas_call(functools.partial(put_kernel, offsets, exact), in_specs=[S...  8.61 us
    pallas_call x1, Pallas kernels, take_rows(): pl.pallas_call(take_kernel, in_specs=[SCALARS] + [WHOLE] * 7, out_specs=[...  5.32 us
  transfers between devices with their start and end apart: 16, of which 5 were waited for; matrix products, arithmetic and copies ran while one was open for 0% of the time, Pallas kernels for 58%

profile of v6, /device:TPU:0, one launch (start us, length us, event | category | flops | bytes accessed | tf_op | source)
XLA Modules:
  0.0 99.5 jit_solution(17363772041894794147)
XLA Ops:
  0.6 4.1 %collective-permute-start = (bf16[512,512]{1,0:T(8,128)(2,1)}, bf16[512,512]{1,0:T(8,128)(2,1)S(1)}, u32[]{:S(2)}, u32[]{:S(2)}) collective-permute-start(bf16[512,512]{1,0:T(8,128)(2,1)} %refs_3_.1), channel_id=1, source_target_pairs={{0,16},{8,24},{16,0},{24,8},{1,17},{9,25},{17,1},{25,9},{2,18},{10... | collective-permute-start | bytes 1572872 | tf_op jit(solution)/shard_map/ppermute | solution.py:442
  4.7 1.6 %collective-permute-start.1 = (bf16[512,512]{1,0:T(8,128)(2,1)}, bf16[512,512]{1,0:T(8,128)(2,1)S(1)}, u32[]{:S(2)}, u32[]{:S(2)}) collective-permute-start(bf16[512,512]{1,0:T(8,128)(2,1)} %refs_3_.1), channel_id=1, source_target_pairs={{0,8},{8,0},{16,24},{24,16},{1,9},{9,1},{17,25},{25,17},{2,10},{10... | collective-permute-start | bytes 1572872 | tf_op jit(solution)/shard_map/ppermute | solution.py:442
  6.3 0.1 pad_add_fusion.scalars
  6.4 0.0 copy-start.1
  6.4 9.5 %order_first.1 = (bf16[2048,512]{1,0:T(8,128)(2,1)S(1)}, f32[16,512]{1,0:T(8,128)S(1)}, bf16[2048,2048]{1,0:T(8,128)(2,1)S(1)}, f32[128,128]{1,0:T(8,128)S(1)}, f32[32,2048]{1,0:T(8,128)S(1)}) custom-call(s32[2]{0:T(128)S(1)} %pad_add_fusion.scalars, s32[16,128]{1,0:T(8,128)} %bitcast.34, s32[8,8]{1,0:T(8,128)} %mask_hbm.1, f32[1,2048]{1,0:T(1,128)} %bitcast.35, ...), custom_call_target="tpu_custom_call" | custom-call | flops 4294967296 | bytes 16777216 | tf_op jit(solution)/shard_map/order_first/pallas_call | solution.py:173
  15.9 0.0 copy-done.1
  15.9 2.5 %collective-permute-start.4 = (bf16[256,512]{1,0:T(8,128)(2,1)S(1)}, bf16[256,512]{1,0:T(8,128)(2,1)S(1)}, u32[]{:S(2)}, u32[]{:S(2)}) collective-permute-start(bf16[256,512]{1,0:T(8,128)(2,1)S(1)} %copy-done.1), channel_id=1, source_target_pairs={{0,6},{1,7},{2,4},{3,5},{4,2},{5,3},{6,0},{7,1},{8,14},{9,15},{10,... | collective-permute-start | bytes 786440 | tf_op jit(solution)/shard_map/ppermute | solution.py:442
  18.4 0.5 collective-permute-start.3
  18.9 0.5 collective-permute-start.2
  19.4 11.2 %order_next.2 = (bf16[2048,512]{1,0:T(8,128)(2,1)S(1)}, bf16[2048,512]{1,0:T(8,128)(2,1)S(1)}, f32[16,512]{1,0:T(8,128)S(1)}, f32[16,512]{1,0:T(8,128)S(1)}) custom-call(s32[2]{0:T(128)S(1)} %pad_add_fusion.scalars, bf16[2048,2048]{1,0:T(8,128)(2,1)S(1)} %get-tuple-element.63.shifted_ref, f32[128,128]{1,0:T(8,128)S(1)} %get-tuple-element.60.columns_ref, ...), custom_call_target="tpu_custom_call" | custom-call | flops 1048576 | bytes 1048576 | tf_op jit(solution)/shard_map/order_next/pallas_call | solution.py:221
  30.6 0.0 collective-permute-done.4.refs_3_
  30.6 0.0 collective-permute-done.3.refs_2_
  30.6 0.0 collective-permute-done.2.refs_1_
  30.6 0.0 collective-permute-done.refs_3_.refs_7_
  30.6 0.0 collective-permute-done.1.refs_3_.refs_8_
  30.7 0.1 pad_maximum_fusion
  30.8 0.0 copy-start.2
  30.8 0.0 copy-start.3
  30.8 0.1 collective-permute-start.5
  30.9 0.5 collective-permute-start.6
  31.4 6.4 %order_next.3 = (bf16[2048,512]{1,0:T(8,128)(2,1)S(1)}, f32[16,512]{1,0:T(8,128)S(1)}) custom-call(s32[2]{0:T(128)S(1)} %pad_add_fusion.scalars, bf16[2048,2048]{1,0:T(8,128)(2,1)S(1)} %get-tuple-element.63.shifted_ref, f32[128,128]{1,0:T(8,128)S(1)} %get-tuple-element.60.columns_ref, f32[32,2048]{1,0:T(8,128)S(1)} %get-tuple-element.61.values_ref), custom_call_target="tpu_custom_call" | custom-call | flops 1048576 | bytes 1048576 | tf_op jit(solution)/shard_map/order_next/pallas_call | solution.py:221
  37.9 0.0 collective-permute-done.5.refs_4_
  37.9 0.0 copy-done.2
  37.9 0.0 copy-done.3
  37.9 5.3 %take_rows.1 = (bf16[2048,512]{1,0:T(8,128)(2,1)S(1)}, bf16[512,2048]{1,0:T(8,128)(2,1)S(1)}, f32[2048,128]{1,0:T(8,128)S(1)}) custom-call(s32[2]{0:T(128)S(1)} %pad_add_fusion.scalars, s32[16,128]{1,0:T(8,128)S(1)} %bitcast.29, f32[16,128]{1,0:T(8,128)S(1)} %bitcast.33, bf16[256,512]{1,0:T(8,128)(2,1)S(1)} %copy-done.1, ...), custom_call_target="tpu_custom_call" | custom-call | flops 4294967296 | bytes 4194304 | tf_op jit(solution)/shard_map/take_rows/pallas_call | solution.py:265
  43.2 2.0 %collective-permute-done.6.refs_3_.refs_6_ = bf16[512,512]{1,0:T(8,128)(2,1)S(1)} collective-permute-done((bf16[512,512]{1,0:T(8,128)(2,1)S(1)}, bf16[512,512]{1,0:T(8,128)(2,1)S(1)}, u32[]{:S(2)}, u32[]{:S(2)}) %collective-permute-start.6) | collective-permute-done | bytes 524320 | tf_op jit(solution)/shard_map/ppermute | solution.py:442
  45.2 4.4 %cells.4 = (bf16[2048,512]{1,0:T(8,128)(2,1)S(1)}, bf16[256,512]{1,0:T(8,128)(2,1)S(1)}, bf16[256,512]{1,0:T(8,128)(2,1)S(1)}) custom-call(bf16[2048,512]{1,0:T(8,128)(2,1)S(1)} %get-tuple-element.88.refs_0_, bf16[512,2048]{1,0:T(8,128)(2,1)S(1)} %get-tuple-element.89.refs_1_, f32[2048,128]{1,0:T(8,128)S(1)} %get-tuple-element.90.refs_2_, ...), custom_call_target="tpu_custom_call" | custom-call | flops 1048576 | bytes 1048576 | tf_op jit(solution)/shard_map/cells/pallas_call | solution.py:374
  49.7 0.5 collective-permute-start.7
  50.2 1.6 %collective-permute-start.8 = (bf16[256,512]{1,0:T(8,128)(2,1)S(1)}, bf16[256,512]{1,0:T(8,128)(2,1)S(1)}, u32[]{:S(2)}, u32[]{:S(2)}) collective-permute-start(bf16[256,512]{1,0:T(8,128)(2,1)S(1)} %get-tuple-element.100), channel_id=1, source_target_pairs={{0,8},{8,0},{16,24},{24,16},{1,9},{9,1},{17,25},{25,17},{2,10},{10... | collective-permute-start | bytes 786440 | tf_op jit(solution)/shard_map/ppermute | solution.py:442
  51.8 4.4 %cells.5 = (bf16[2048,512]{1,0:T(8,128)(2,1)S(1)}, f32[512,512]{1,0:T(8,128)S(1)}) custom-call(bf16[2048,512]{1,0:T(8,128)(2,1)S(1)} %get-tuple-element.88.refs_0_, bf16[512,2048]{1,0:T(8,128)(2,1)S(1)} %get-tuple-element.89.refs_1_, f32[2048,128]{1,0:T(8,128)S(1)} %get-tuple-element.90.refs_2_, bf16[512,512]{1,0:T(8,128)(2,1)S(1)} %collective-permute-done.refs_3_.refs_7_, ...), custom_call_target="tpu_custom_call" | custom-call | flops 1048576 | bytes 1048576 | tf_op jit(solution)/shard_map/cells/pallas_call | solution.py:374
  56.2 2.8 %collective-permute-done.7 = bf16[256,512]{1,0:T(8,128)(2,1)S(1)} collective-permute-done((bf16[256,512]{1,0:T(8,128)(2,1)S(1)}, bf16[256,512]{1,0:T(8,128)(2,1)S(1)}, u32[]{:S(2)}, u32[]{:S(2)}) %collective-permute-start.7) | collective-permute-done | bytes 262176 | tf_op jit(solution)/shard_map/ppermute | solution.py:442
  59.0 0.1 add_convert_fusion.2
  59.1 0.4 collective-permute-start.9
  59.5 0.0 copy-start
  59.5 4.6 %cells.6 = (bf16[2048,512]{1,0:T(8,128)(2,1)S(1)}, bf16[512,512]{1,0:T(8,128)(2,1)S(1)}) custom-call(bf16[2048,512]{1,0:T(8,128)(2,1)S(1)} %get-tuple-element.88.refs_0_, bf16[512,2048]{1,0:T(8,128)(2,1)S(1)} %get-tuple-element.89.refs_1_, f32[2048,128]{1,0:T(8,128)S(1)} %get-tuple-element.90.refs_2_, ...), custom_call_target="tpu_custom_call" | custom-call | flops 1048576 | bytes 1048576 | tf_op jit(solution)/shard_map/cells/pallas_call | solution.py:374
  64.1 0.0 copy-done
  64.1 8.9 %cells.7 = (f32[2048,512]{1,0:T(8,128)S(1)}, f32[512,512]{1,0:T(8,128)S(1)}) custom-call(bf16[2048,512]{1,0:T(8,128)(2,1)S(1)} %get-tuple-element.88.refs_0_, bf16[512,2048]{1,0:T(8,128)(2,1)S(1)} %get-tuple-element.89.refs_1_, f32[2048,128]{1,0:T(8,128)S(1)} %get-tuple-element.90.refs_2_, bf16[512,512]{1,0:T(8,128)(2,1)S(1)} %copy-done, ...), custom_call_target="tpu_custom_call" | custom-call | flops 1048576 | bytes 1048576 | tf_op jit(solution)/shard_map/cells/pallas_call | solution.py:374
  73.0 0.0 collective-permute-done.8
  73.0 0.0 collective-permute-done.9.refs_2_
  73.1 0.1 add_convert_fusion.1
  73.1 2.9 %put_rows.3 = bf16[4,256,512]{2,1,0:T(8,128)(2,1)S(1)} custom-call(s32[2]{0:T(128)S(1)} %pad_add_fusion.scalars, s32[1,2048]{1,0:T(1,128)S(1)} %bitcast.30, f32[2048,512]{1,0:T(8,128)S(1)} %get-tuple-element.106.grad_ref), custom_call_target="tpu_custom_call" | custom-call | flops 1048576 | bytes 65536 | tf_op jit(solution)/shard_map/put_rows/pallas_call | solution.py:428
  76.0 0.1 collective-permute-start.10
  76.1 1.3 %collective-permute-start.14 = (bf16[512,512]{1,0:T(8,128)(2,1)S(1)}, bf16[512,512]{1,0:T(8,128)(2,1)S(1)}, u32[]{:S(2)}, u32[]{:S(2)}) collective-permute-start(bf16[512,512]{1,0:T(8,128)(2,1)S(1)} %get-tuple-element.110), channel_id=1, source_target_pairs={{0,8},{8,0},{16,24},{24,16},{1,9},{9,1},{17,25},{25,17},{2,10},{10... | collective-permute-start | bytes 1572872 | tf_op jit(solution)/shard_map/ppermute | solution.py:442
  77.4 1.8 %collective-permute-start.15 = (bf16[256,512]{1,0:T(8,128)(2,1)S(1)}, bf16[256,512]{1,0:T(8,128)(2,1)S(1)}, u32[]{:S(2)}, u32[]{:S(2)}) collective-permute-start(bf16[256,512]{1,0:T(8,128)(2,1)S(1)} %add_convert_fusion.1), channel_id=1, source_target_pairs={{0,16},{8,24},{16,0},{24,8},{1,17},{9,25},{17,1},{25,9},{2,18},{10... | collective-permute-start | bytes 786440 | tf_op jit(solution)/shard_map/ppermute | solution.py:442
  79.2 3.9 %put_rows.4 = f32[3,256,512]{2,1,0:T(8,128)S(1)} custom-call(s32[2]{0:T(128)S(1)} %pad_add_fusion.scalars, s32[1,2048]{1,0:T(1,128)S(1)} %bitcast.31, f32[2048,512]{1,0:T(8,128)S(1)} %get-tuple-element.106.grad_ref), custom_call_target="tpu_custom_call" | custom-call | flops 4294967296 | bytes 65536 | tf_op jit(solution)/shard_map/put_rows/pallas_call | solution.py:428
  83.2 0.0 collective-permute-done.10
  83.2 0.3 add_convert_fusion
  83.5 0.1 slice_bitcast_fusion.1
  83.5 1.6 %collective-permute-start.11 = (bf16[256,512]{1,0:T(8,128)(2,1)S(1)}, bf16[256,512]{1,0:T(8,128)(2,1)S(1)}, u32[]{:S(2)}, u32[]{:S(2)}) collective-permute-start(bf16[256,512]{1,0:T(8,128)(2,1)S(1)} %get-tuple-element.112), channel_id=1, source_target_pairs={{0,4},{1,5},{2,6},{3,7},{4,0},{5,1},{6,2},{7,3},{8,12},{9,13},{10,... | collective-permute-start | bytes 786440 | tf_op jit(solution)/shard_map/ppermute | solution.py:442
  85.1 1.4 %collective-permute-start.12 = (bf16[256,512]{1,0:T(8,128)(2,1)S(1)}, bf16[256,512]{1,0:T(8,128)(2,1)S(1)}, u32[]{:S(2)}, u32[]{:S(2)}) collective-permute-start(bf16[256,512]{1,0:T(8,128)(2,1)S(1)} %get-tuple-element.113), channel_id=1, source_target_pairs={{0,6},{1,7},{2,4},{3,5},{4,2},{5,3},{6,0},{7,1},{8,14},{9,15},{10,... | collective-permute-start | bytes 786440 | tf_op jit(solution)/shard_map/ppermute | solution.py:442
  86.5 0.6 collective-permute-start.13
  87.1 1.8 %put_rows.5 = f32[1,256,512]{2,1,0:T(8,128)S(1)} custom-call(s32[2]{0:T(128)S(1)} %pad_add_fusion.scalars, s32[1,2048]{1,0:T(1,128)S(1)} %bitcast.32, f32[2048,512]{1,0:T(8,128)S(1)} %get-tuple-element.106.grad_ref), custom_call_target="tpu_custom_call" | custom-call | flops 1048576 | bytes 65536 | tf_op jit(solution)/shard_map/put_rows/pallas_call | solution.py:428
  88.9 5.9 %collective-permute-done.15.refs_3_ = bf16[256,512]{1,0:T(8,128)(2,1)S(1)} collective-permute-done((bf16[256,512]{1,0:T(8,128)(2,1)S(1)}, bf16[256,512]{1,0:T(8,128)(2,1)S(1)}, u32[]{:S(2)}, u32[]{:S(2)}) %collective-permute-start.15) | collective-permute-done | bytes 262176 | tf_op jit(solution)/shard_map/ppermute | solution.py:442
  94.8 1.3 %collective-permute-done.14.refs_1_ = bf16[512,512]{1,0:T(8,128)(2,1)S(1)} collective-permute-done((bf16[512,512]{1,0:T(8,128)(2,1)S(1)}, bf16[512,512]{1,0:T(8,128)(2,1)S(1)}, u32[]{:S(2)}, u32[]{:S(2)}) %collective-permute-start.14) | collective-permute-done | bytes 524320 | tf_op jit(solution)/shard_map/ppermute | solution.py:442
  96.0 1.3 %finish.1 = f32[512,512]{1,0:T(8,128)} custom-call(f32[512,512]{1,0:T(8,128)S(1)} %get-tuple-element.109.refs_0_, bf16[512,512]{1,0:T(8,128)(2,1)S(1)} %collective-permute-done.14.refs_1_, bf16[256,512]{1,0:T(8,128)(2,1)S(1)} %collective-permute-done.9.refs_2_, bf16[256,512]{1,0:T(8,128)(2,1)S(1)} %collective-permute-done.15.refs_3_), custom_call_target="tpu_custom_call" | custom-call | flops 262144 | bytes 16384 | tf_op jit(solution)/shard_map/finish/pallas_call | solution.py:396
  97.4 0.0 collective-permute-done.11
  97.4 0.0 collective-permute-done.12
  97.4 1.1 %collective-permute-done.13 = bf16[256,512]{1,0:T(8,128)(2,1)S(1)} collective-permute-done((bf16[256,512]{1,0:T(8,128)(2,1)S(1)}, bf16[256,512]{1,0:T(8,128)(2,1)S(1)}, u32[]{:S(2)}, u32[]{:S(2)}) %collective-permute-start.13) | collective-permute-done | bytes 262176 | tf_op jit(solution)/shard_map/ppermute | solution.py:442
  98.5 1.0 fusion.2
Async XLA Ops:
  0.6 30.0 %collective-permute-start = (bf16[512,512]{1,0:T(8,128)(2,1)}, bf16[512,512]{1,0:T(8,128)(2,1)S(1)}, u32[]{:S(2)}, u32[]{:S(2)}) collective-permute-start(bf16[512,512]{1,0:T(8,128)(2,1)} %refs_3_.1), channel_id=1, source_target_pairs={{0,16},{8,24},{16,0},{24,8},{1,17},{9,25},{17,1},{25,9},{2,18},{10... | collective-permute-start | bytes 1572872 | tf_op jit(solution)/shard_map/ppermute | solution.py:442
  4.7 25.9 %collective-permute-start.1 = (bf16[512,512]{1,0:T(8,128)(2,1)}, bf16[512,512]{1,0:T(8,128)(2,1)S(1)}, u32[]{:S(2)}, u32[]{:S(2)}) collective-permute-start(bf16[512,512]{1,0:T(8,128)(2,1)} %refs_3_.1), channel_id=1, source_target_pairs={{0,8},{8,0},{16,24},{24,16},{1,9},{9,1},{17,25},{25,17},{2,10},{10... | collective-permute-start | bytes 1572872 | tf_op jit(solution)/shard_map/ppermute | solution.py:442
  6.4 9.5 %copy-start.1 = (bf16[256,512]{1,0:T(8,128)(2,1)S(1)}, bf16[256,512]{1,0:T(8,128)(2,1)}, u32[]{:S(2)}) copy-start(bf16[256,512]{1,0:T(8,128)(2,1)} %refs_0_.1) | copy-start | bytes 786436
  15.9 14.7 %collective-permute-start.4 = (bf16[256,512]{1,0:T(8,128)(2,1)S(1)}, bf16[256,512]{1,0:T(8,128)(2,1)S(1)}, u32[]{:S(2)}, u32[]{:S(2)}) collective-permute-start(bf16[256,512]{1,0:T(8,128)(2,1)S(1)} %copy-done.1), channel_id=1, source_target_pairs={{0,6},{1,7},{2,4},{3,5},{4,2},{5,3},{6,0},{7,1},{8,14},{9,15},{10,... | collective-permute-start | bytes 786440 | tf_op jit(solution)/shard_map/ppermute | solution.py:442
  18.4 12.2 %collective-permute-start.3 = (bf16[256,512]{1,0:T(8,128)(2,1)S(1)}, bf16[256,512]{1,0:T(8,128)(2,1)S(1)}, u32[]{:S(2)}, u32[]{:S(2)}) collective-permute-start(bf16[256,512]{1,0:T(8,128)(2,1)S(1)} %copy-done.1), channel_id=1, source_target_pairs={{0,4},{1,5},{2,6},{3,7},{4,0},{5,1},{6,2},{7,3},{8,12},{9,13},{10,... | collective-permute-start | bytes 786440 | tf_op jit(solution)/shard_map/ppermute | solution.py:442
  18.9 11.7 %collective-permute-start.2 = (bf16[256,512]{1,0:T(8,128)(2,1)S(1)}, bf16[256,512]{1,0:T(8,128)(2,1)S(1)}, u32[]{:S(2)}, u32[]{:S(2)}) collective-permute-start(bf16[256,512]{1,0:T(8,128)(2,1)S(1)} %copy-done.1), channel_id=1, source_target_pairs={{0,2},{1,3},{2,0},{3,1},{4,6},{5,7},{6,4},{7,5},{8,10},{9,11},{10,... | collective-permute-start | bytes 786440 | tf_op jit(solution)/shard_map/ppermute | solution.py:442
  30.8 7.1 %copy-start.2 = (s32[2048]{0:T(1024)S(1)}, s32[2048]{0:T(1024)}, u32[]{:S(2)}) copy-start(s32[2048]{0:T(1024)} %param.10) | copy-start | bytes 24580
  30.8 7.1 %copy-start.3 = (f32[2048]{0:T(1024)S(1)}, f32[2048]{0:T(1024)}, u32[]{:S(2)}) copy-start(f32[2048]{0:T(1024)} %param.12) | copy-start | bytes 24580
  30.8 7.0 %collective-permute-start.5 = (bf16[4,256,512]{2,1,0:T(8,128)(2,1)S(1)}, bf16[4,256,512]{2,1,0:T(8,128)(2,1)S(1)}, u32[]{:S(2)}, u32[]{:S(2)}) collective-permute-start(bf16[4,256,512]{2,1,0:T(8,128)(2,1)S(1)} %pad_maximum_fusion), channel_id=1, source_target_pairs={{0,1},{1,0},{2,3},{3,2},{4,5},{5,4},{6,7},{7,6},{8,9},{9,8},{10,11... | collective-permute-start | bytes 3145736 | tf_op jit(solution)/shard_map/ppermute | solution.py:442
  30.9 14.3 %collective-permute-start.6 = (bf16[512,512]{1,0:T(8,128)(2,1)S(1)}, bf16[512,512]{1,0:T(8,128)(2,1)S(1)}, u32[]{:S(2)}, u32[]{:S(2)}) collective-permute-start(bf16[512,512]{1,0:T(8,128)(2,1)S(1)} %collective-permute-done.refs_3_.refs_7_), channel_id=1, source_target_pairs={{0,8},{8,0},{16,24},{24,16},{1,9},{9,1},{17,25},{25,17},{2,10},{10... | collective-permute-start | bytes 1572872 | tf_op jit(solution)/shard_map/ppermute | solution.py:442
  49.7 9.3 %collective-permute-start.7 = (bf16[256,512]{1,0:T(8,128)(2,1)S(1)}, bf16[256,512]{1,0:T(8,128)(2,1)S(1)}, u32[]{:S(2)}, u32[]{:S(2)}) collective-permute-start(bf16[256,512]{1,0:T(8,128)(2,1)S(1)} %get-tuple-element.82), channel_id=1, source_target_pairs={{0,8},{8,0},{16,24},{24,16},{1,9},{9,1},{17,25},{25,17},{2,10},{10... | collective-permute-start | bytes 786440 | tf_op jit(solution)/shard_map/ppermute | solution.py:442
  50.2 22.8 %collective-permute-start.8 = (bf16[256,512]{1,0:T(8,128)(2,1)S(1)}, bf16[256,512]{1,0:T(8,128)(2,1)S(1)}, u32[]{:S(2)}, u32[]{:S(2)}) collective-permute-start(bf16[256,512]{1,0:T(8,128)(2,1)S(1)} %get-tuple-element.100), channel_id=1, source_target_pairs={{0,8},{8,0},{16,24},{24,16},{1,9},{9,1},{17,25},{25,17},{2,10},{10... | collective-permute-start | bytes 786440 | tf_op jit(solution)/shard_map/ppermute | solution.py:442
  59.1 14.0 %collective-permute-start.9 = (bf16[256,512]{1,0:T(8,128)(2,1)S(1)}, bf16[256,512]{1,0:T(8,128)(2,1)S(1)}, u32[]{:S(2)}, u32[]{:S(2)}) collective-permute-start(bf16[256,512]{1,0:T(8,128)(2,1)S(1)} %add_convert_fusion.2), channel_id=1, source_target_pairs={{0,16},{8,24},{16,0},{24,8},{1,17},{9,25},{17,1},{25,9},{2,18},{10... | collective-permute-start | bytes 786440 | tf_op jit(solution)/shard_map/ppermute | solution.py:442
  59.5 4.6 %copy-start = (bf16[512,512]{1,0:T(8,128)(2,1)S(1)}, bf16[512,512]{1,0:T(8,128)(2,1)}, u32[]{:S(2)}) copy-start(bf16[512,512]{1,0:T(8,128)(2,1)} %refs_3_.1) | copy-start | bytes 1572868
  76.0 7.2 %collective-permute-start.10 = (bf16[4,256,512]{2,1,0:T(8,128)(2,1)S(1)}, bf16[4,256,512]{2,1,0:T(8,128)(2,1)S(1)}, u32[]{:S(2)}, u32[]{:S(2)}) collective-permute-start(bf16[4,256,512]{2,1,0:T(8,128)(2,1)S(1)} %put_rows.3), channel_id=1, source_target_pairs={{0,1},{1,0},{2,3},{3,2},{4,5},{5,4},{6,7},{7,6},{8,9},{9,8},{10,11... | collective-permute-start | bytes 3145736 | tf_op jit(solution)/shard_map/ppermute | solution.py:442
  76.1 20.0 %collective-permute-start.14 = (bf16[512,512]{1,0:T(8,128)(2,1)S(1)}, bf16[512,512]{1,0:T(8,128)(2,1)S(1)}, u32[]{:S(2)}, u32[]{:S(2)}) collective-permute-start(bf16[512,512]{1,0:T(8,128)(2,1)S(1)} %get-tuple-element.110), channel_id=1, source_target_pairs={{0,8},{8,0},{16,24},{24,16},{1,9},{9,1},{17,25},{25,17},{2,10},{10... | collective-permute-start | bytes 1572872 | tf_op jit(solution)/shard_map/ppermute | solution.py:442
  77.4 17.4 %collective-permute-start.15 = (bf16[256,512]{1,0:T(8,128)(2,1)S(1)}, bf16[256,512]{1,0:T(8,128)(2,1)S(1)}, u32[]{:S(2)}, u32[]{:S(2)}) collective-permute-start(bf16[256,512]{1,0:T(8,128)(2,1)S(1)} %add_convert_fusion.1), channel_id=1, source_target_pairs={{0,16},{8,24},{16,0},{24,8},{1,17},{9,25},{17,1},{25,9},{2,18},{10... | collective-permute-start | bytes 786440 | tf_op jit(solution)/shard_map/ppermute | solution.py:442
  83.5 13.9 %collective-permute-start.11 = (bf16[256,512]{1,0:T(8,128)(2,1)S(1)}, bf16[256,512]{1,0:T(8,128)(2,1)S(1)}, u32[]{:S(2)}, u32[]{:S(2)}) collective-permute-start(bf16[256,512]{1,0:T(8,128)(2,1)S(1)} %get-tuple-element.112), channel_id=1, source_target_pairs={{0,4},{1,5},{2,6},{3,7},{4,0},{5,1},{6,2},{7,3},{8,12},{9,13},{10,... | collective-permute-start | bytes 786440 | tf_op jit(solution)/shard_map/ppermute | solution.py:442
  85.1 12.3 %collective-permute-start.12 = (bf16[256,512]{1,0:T(8,128)(2,1)S(1)}, bf16[256,512]{1,0:T(8,128)(2,1)S(1)}, u32[]{:S(2)}, u32[]{:S(2)}) collective-permute-start(bf16[256,512]{1,0:T(8,128)(2,1)S(1)} %get-tuple-element.113), channel_id=1, source_target_pairs={{0,6},{1,7},{2,4},{3,5},{4,2},{5,3},{6,0},{7,1},{8,14},{9,15},{10,... | collective-permute-start | bytes 786440 | tf_op jit(solution)/shard_map/ppermute | solution.py:442
  86.5 12.0 %collective-permute-start.13 = (bf16[256,512]{1,0:T(8,128)(2,1)S(1)}, bf16[256,512]{1,0:T(8,128)(2,1)S(1)}, u32[]{:S(2)}, u32[]{:S(2)}) collective-permute-start(bf16[256,512]{1,0:T(8,128)(2,1)S(1)} %get-tuple-element.114), channel_id=1, source_target_pairs={{0,2},{1,3},{2,0},{3,1},{4,6},{5,7},{6,4},{7,5},{8,10},{9,11},{10,... | collective-permute-start | bytes 786440 | tf_op jit(solution)/shard_map/ppermute | solution.py:442

commit v7 on v6

--- a/solution.py
+++ b/solution.py
@@ -124,8 +124,7 @@
         )
 
     small = copies([(perm_hbm, perm), (mask_hbm, mask_ref), (logm_hbm, logm_ref)], sems)
-    for at in range(slots):
-        tile_copy(at).start()
+    tile_copy(0).start()
     for copy in small:
         copy.wait()
     columns = along_sublanes((perm[...] - scalars[COL_AT] * depth).astype(F32))
@@ -143,6 +142,7 @@
     for part, offset in enumerate(offsets):
         fill_pick(pick.at[part], columns, chunk_base(scalars, offset, width), range(depth // LANES))
         move_values(values, pick.at[part], auxes[part])
+    tile_copy(1).start()
 
     @pl.loop(0, steps)
     def _(at):
@@ -281,7 +281,8 @@
 def cells_kernel(others, pieces, *refs):
     wvec_ref, turned_ref, logm_ref, chunk, count_ref, aux_ref, refs = *refs[:6], refs[6:]
     chunk_refs, delta_refs, refs = refs[:others], refs[others : 2 * others], refs[2 * others :]
-    main_ref, out_refs, refs = refs[0], refs[1 : 1 + max(pieces, 1)], refs[1 + max(pieces, 1) :]
+    outs = max(len(pieces), 1)
+    main_ref, out_refs, refs = refs[0], refs[1 : 1 + outs], refs[1 + outs :]
     chunk_turned, term_ref, refs = refs[0], refs[1], refs[2:]
     chunk_turned[...] = chunk[...].T
     rows = wvec_ref.shape[0]
@@ -351,12 +352,13 @@
         pl.loop(0, blocks // joined)(part)
     else:
         part(0)
-    for piece, out_ref in enumerate(out_refs):
-        size = out_ref.shape[0]
-        out_ref[...] = term_ref[pl.ds(piece * size, size), :].astype(out_ref.dtype)
-
-
-def cells(rows_in, chunk, pieces, others=()):
+    first = 0
+    for out_ref in out_refs:
+        out_ref[...] = term_ref[pl.ds(first, out_ref.shape[0]), :].astype(out_ref.dtype)
+        first += out_ref.shape[0]
+
+
+def cells(rows_in, chunk, pieces=(), others=()):
     wvec = rows_in[0]
     rows, depth = wvec.shape
     width = chunk[0].shape[0]
@@ -368,7 +370,7 @@
         main = jax.ShapeDtypeStruct((rows, width), BF16)
         scratch = []
     if pieces:
-        outs = [jax.ShapeDtypeStruct((depth // pieces, width), BF16) for _ in range(pieces)]
+        outs = [jax.ShapeDtypeStruct((size, width), BF16) for size in pieces]
     else:
         outs = [jax.ShapeDtypeStruct((depth, width), F32)]
     return pl.pallas_call(
@@ -384,12 +386,14 @@
 
 
 def finish_kernel(scale, *refs):
-    own_ref, near_ref, cross_refs, out_ref = refs[0], refs[1], refs[2:-1], refs[-1]
-    size = cross_refs[0].shape[0]
-    for at, cross_ref in enumerate(cross_refs):
-        here = pl.ds(at * size, size)
+    own_ref, near_ref, cross_refs, out_ref, sum_ref = refs[0], refs[1], refs[2:-2], refs[-2], refs[-1]
+    first = 0
+    for cross_ref in cross_refs:
+        here = pl.ds(first, cross_ref.shape[0])
+        first += cross_ref.shape[0]
         total = own_ref[here, :] + near_ref[here, :].astype(F32) + cross_ref[...].astype(F32)
-        out_ref[:, here] = (total * scale).T
+        sum_ref[here, :] = total * scale
+    out_ref[...] = sum_ref[...].T
 
 
 def finish(scale, own, near, *crosses):
@@ -398,6 +402,7 @@
         in_specs=[WHOLE] * (2 + len(crosses)),
         out_specs=WHOLE,
         out_shape=jax.ShapeDtypeStruct(own.shape[::-1], F32),
+        scratch_shapes=[pltpu.VMEM(own.shape, F32)],
         compiler_params=params(8),
         cost_estimate=cost(own.size, own.size // 16),
         name="finish",
@@ -476,23 +481,25 @@
     rows_in = (wvec, turned, logm)
     of_far, of_cross = (far, count_far, aux_far), (cross, count_cross, aux_cross)
     of_near, of_own = (near, count_near, aux_near), (col_emb, count_own, aux_own)
-    delta_far, sent_0, sent_1 = cells(rows_in, of_far, 2)
+    depth = col_emb.shape[1]
+    early = depth * 5 // 16
+    delta_far, sent_0, sent_1 = cells(rows_in, of_far, (early, depth - early))
     far_0 = swap(sent_0, "row", 1)
     far_1 = swap(sent_1, "row", 1)
     rows_in, delta_far = together((rows_in, delta_far))
-    delta_cross, term_cross = cells(rows_in, of_cross, 0)
-    rows_in, term_cross, far_0 = together((rows_in, term_cross, far_0))
-
-    half = term_cross.shape[0] // 2
-    sum_0 = (term_cross[:half] + far_0.astype(F32)).astype(BF16)
+    delta_cross, term_cross = cells(rows_in, of_cross)
+    rows_in, delta_cross = together((rows_in, delta_cross))
+    delta_near, sent_near = cells(rows_in, of_near, (depth,))
+    got_near = swap(sent_near, "row", 1)
+    rows_in, delta_near, far_0 = together((rows_in, delta_near, far_0))
+
+    sum_0 = (term_cross[:early] + far_0.astype(F32)).astype(BF16)
     rows_in, sum_0 = together((rows_in, sum_0))
     cross_0 = swap(sum_0, "row", 2)
-    delta_near, sent_near = cells(rows_in, of_near, 1)
-    got_near = swap(sent_near, "row", 1)
     others = ((far, delta_far), (cross, delta_cross), (near, delta_near))
-    grad, term_own = cells(rows_in, of_own, 0, others)
+    grad, term_own = cells(rows_in, of_own, (), others)
     grad, far_1, cross_0 = together((grad, far_1, cross_0))
-    sum_1 = (term_cross[half:] + far_1.astype(F32)).astype(BF16)
+    sum_1 = (term_cross[early:] + far_1.astype(F32)).astype(BF16)
     cross_1 = swap(sum_1, "row", 2)
     grad, sum_1 = together((grad, sum_1))
 

time: 99.7 us -> 97.7 us (0.980)
  waiting for transfers between devices: 13.1 us -> 11.8 us
    ppermute x16, waiting for transfers between devices: 13.1 us -> 11.8 us  [swap(): return lax.ppermute(value, axis, pairs)]
  transfers between devices with their start and end apart: 16 -> 16, of which waited for: 5 -> 3; matrix products, arithmetic and copies ran while one was open for 0% -> 0% of each run, Pallas kernels for 58% -> 58%
where the time goes in v7:
time: 97.7 us; the launch traced here: 97.6 us
  Pallas kernels  64.4 us (66%)
  starting transfers between devices  18.8 us (19%)
  waiting for transfers between devices  11.8 us (12%)
  other arithmetic  1.61 us (2%)
    pallas_call x4, Pallas kernels, cells(): pl.pallas_call(functools.partial(cells_kernel, len(others), pieces), in_s...  22.4 us
    ppermute x16, starting transfers between devices, swap(): return lax.ppermute(value, axis, pairs)  18.8 us
    pallas_call x2, Pallas kernels, order_next(): pl.pallas_call(functools.partial(order_next_kernel, offsets), in_specs=[S...  17.6 us
    ppermute x16, waiting for transfers between devices, swap(): return lax.ppermute(value, axis, pairs)  11.8 us
    pallas_call x1, Pallas kernels, order_first(): pl.pallas_call(functools.partial(order_first_kernel, offsets), in_specs=[...  9.09 us
    pallas_call x3, Pallas kernels, put_rows(): pl.pallas_call(functools.partial(put_kernel, offsets, exact), in_specs=[S...  8.61 us
    pallas_call x1, Pallas kernels, take_rows(): pl.pallas_call(take_kernel, in_specs=[SCALARS] + [WHOLE] * 7, out_specs=[...  5.32 us
  transfers between devices with their start and end apart: 16, of which 3 were waited for; matrix products, arithmetic and copies ran while one was open for 0% of the time, Pallas kernels for 58%

profile of v7, /device:TPU:0, one launch (start us, length us, event | category | flops | bytes accessed | tf_op | source)
XLA Modules:
  0.0 97.6 jit_solution(2267520862103776658)
XLA Ops:
  0.6 4.1 %collective-permute-start = (bf16[512,512]{1,0:T(8,128)(2,1)}, bf16[512,512]{1,0:T(8,128)(2,1)S(1)}, u32[]{:S(2)}, u32[]{:S(2)}) collective-permute-start(bf16[512,512]{1,0:T(8,128)(2,1)} %refs_3_.1), channel_id=1, source_target_pairs={{0,16},{8,24},{16,0},{24,8},{1,17},{9,25},{17,1},{25,9},{2,18},{10... | collective-permute-start | bytes 1572872 | tf_op jit(solution)/shard_map/ppermute | solution.py:447
  4.7 1.6 %collective-permute-start.1 = (bf16[512,512]{1,0:T(8,128)(2,1)}, bf16[512,512]{1,0:T(8,128)(2,1)S(1)}, u32[]{:S(2)}, u32[]{:S(2)}) collective-permute-start(bf16[512,512]{1,0:T(8,128)(2,1)} %refs_3_.1), channel_id=1, source_target_pairs={{0,8},{8,0},{16,24},{24,16},{1,9},{9,1},{17,25},{25,17},{2,10},{10... | collective-permute-start | bytes 1572872 | tf_op jit(solution)/shard_map/ppermute | solution.py:447
  6.3 0.1 pad_add_fusion.scalars
  6.4 0.0 copy-start.1
  6.4 9.1 %order_first.1 = (bf16[2048,512]{1,0:T(8,128)(2,1)S(1)}, f32[16,512]{1,0:T(8,128)S(1)}, bf16[2048,2048]{1,0:T(8,128)(2,1)S(1)}, f32[128,128]{1,0:T(8,128)S(1)}, f32[32,2048]{1,0:T(8,128)S(1)}) custom-call(s32[2]{0:T(128)S(1)} %pad_add_fusion.scalars, s32[16,128]{1,0:T(8,128)} %bitcast.34, s32[8,8]{1,0:T(8,128)} %mask_hbm.1, f32[1,2048]{1,0:T(1,128)} %bitcast.35, ...), custom_call_target="tpu_custom_call" | custom-call | flops 4294967296 | bytes 16777216 | tf_op jit(solution)/shard_map/order_first/pallas_call | solution.py:173
  15.5 0.0 copy-done.1
  15.5 2.5 %collective-permute-start.4 = (bf16[256,512]{1,0:T(8,128)(2,1)S(1)}, bf16[256,512]{1,0:T(8,128)(2,1)S(1)}, u32[]{:S(2)}, u32[]{:S(2)}) collective-permute-start(bf16[256,512]{1,0:T(8,128)(2,1)S(1)} %copy-done.1), channel_id=1, source_target_pairs={{0,6},{1,7},{2,4},{3,5},{4,2},{5,3},{6,0},{7,1},{8,14},{9,15},{10,... | collective-permute-start | bytes 786440 | tf_op jit(solution)/shard_map/ppermute | solution.py:447
  18.0 0.5 collective-permute-start.3
  18.5 0.5 collective-permute-start.2
  19.0 11.2 %order_next.2 = (bf16[2048,512]{1,0:T(8,128)(2,1)S(1)}, bf16[2048,512]{1,0:T(8,128)(2,1)S(1)}, f32[16,512]{1,0:T(8,128)S(1)}, f32[16,512]{1,0:T(8,128)S(1)}) custom-call(s32[2]{0:T(128)S(1)} %pad_add_fusion.scalars, bf16[2048,2048]{1,0:T(8,128)(2,1)S(1)} %get-tuple-element.67.shifted_ref, f32[128,128]{1,0:T(8,128)S(1)} %get-tuple-element.64.columns_ref, ...), custom_call_target="tpu_custom_call" | custom-call | flops 1048576 | bytes 1048576 | tf_op jit(solution)/shard_map/order_next/pallas_call | solution.py:221
  30.2 0.0 collective-permute-done.4.refs_3_
  30.2 0.0 collective-permute-done.3.refs_2_
  30.2 0.0 collective-permute-done.2.refs_1_
  30.3 0.0 collective-permute-done.refs_3_.refs_7_
  30.3 0.0 collective-permute-done.1.refs_3_.refs_8_
  30.3 0.1 pad_maximum_fusion
  30.4 0.0 copy-start.2
  30.4 0.0 copy-start.3
  30.4 0.1 collective-permute-start.5
  30.5 0.5 collective-permute-start.6
  31.0 6.4 %order_next.3 = (bf16[2048,512]{1,0:T(8,128)(2,1)S(1)}, f32[16,512]{1,0:T(8,128)S(1)}) custom-call(s32[2]{0:T(128)S(1)} %pad_add_fusion.scalars, bf16[2048,2048]{1,0:T(8,128)(2,1)S(1)} %get-tuple-element.67.shifted_ref, f32[128,128]{1,0:T(8,128)S(1)} %get-tuple-element.64.columns_ref, f32[32,2048]{1,0:T(8,128)S(1)} %get-tuple-element.65.values_ref), custom_call_target="tpu_custom_call" | custom-call | flops 1048576 | bytes 1048576 | tf_op jit(solution)/shard_map/order_next/pallas_call | solution.py:221
  37.5 0.0 collective-permute-done.5.refs_4_
  37.5 0.0 copy-done.2
  37.5 0.0 copy-done.3
  37.5 5.3 %take_rows.1 = (bf16[2048,512]{1,0:T(8,128)(2,1)S(1)}, bf16[512,2048]{1,0:T(8,128)(2,1)S(1)}, f32[2048,128]{1,0:T(8,128)S(1)}) custom-call(s32[2]{0:T(128)S(1)} %pad_add_fusion.scalars, s32[16,128]{1,0:T(8,128)S(1)} %bitcast.29, f32[16,128]{1,0:T(8,128)S(1)} %bitcast.33, bf16[256,512]{1,0:T(8,128)(2,1)S(1)} %copy-done.1, ...), custom_call_target="tpu_custom_call" | custom-call | flops 4294967296 | bytes 4194304 | tf_op jit(solution)/shard_map/take_rows/pallas_call | solution.py:265
  42.8 2.0 %collective-permute-done.6.refs_3_.refs_6_ = bf16[512,512]{1,0:T(8,128)(2,1)S(1)} collective-permute-done((bf16[512,512]{1,0:T(8,128)(2,1)S(1)}, bf16[512,512]{1,0:T(8,128)(2,1)S(1)}, u32[]{:S(2)}, u32[]{:S(2)}) %collective-permute-start.6) | collective-permute-done | bytes 524320 | tf_op jit(solution)/shard_map/ppermute | solution.py:447
  44.9 4.4 %cells.4 = (bf16[2048,512]{1,0:T(8,128)(2,1)S(1)}, bf16[160,512]{1,0:T(8,128)(2,1)S(1)}, bf16[352,512]{1,0:T(8,128)(2,1)S(1)}) custom-call(bf16[2048,512]{1,0:T(8,128)(2,1)S(1)} %get-tuple-element.99.refs_0_, bf16[512,2048]{1,0:T(8,128)(2,1)S(1)} %get-tuple-element.100.refs_1_, f32[2048,128]{1,0:T(8,128)S(1)} %get-tuple-element.101.refs_2_, ...), custom_call_target="tpu_custom_call" | custom-call | flops 1048576 | bytes 1048576 | tf_op jit(solution)/shard_map/cells/pallas_call | solution.py:376
  49.3 0.5 collective-permute-start.7
  49.8 1.6 %collective-permute-start.8 = (bf16[352,512]{1,0:T(8,128)(2,1)S(1)}, bf16[352,512]{1,0:T(8,128)(2,1)S(1)}, u32[]{:S(2)}, u32[]{:S(2)}) collective-permute-start(bf16[352,512]{1,0:T(8,128)(2,1)S(1)} %get-tuple-element.108), channel_id=1, source_target_pairs={{0,8},{8,0},{16,24},{24,16},{1,9},{9,1},{17,25},{25,17},{2,10},{10... | collective-permute-start | bytes 1081352 | tf_op jit(solution)/shard_map/ppermute | solution.py:447
  51.4 4.4 %cells.5 = (bf16[2048,512]{1,0:T(8,128)(2,1)S(1)}, f32[512,512]{1,0:T(8,128)S(1)}) custom-call(bf16[2048,512]{1,0:T(8,128)(2,1)S(1)} %get-tuple-element.99.refs_0_, bf16[512,2048]{1,0:T(8,128)(2,1)S(1)} %get-tuple-element.100.refs_1_, f32[2048,128]{1,0:T(8,128)S(1)} %get-tuple-element.101.refs_2_, bf16[512,512]{1,0:T(8,128)(2,1)S(1)} %collective-permute-done.refs_3_.refs_7_, ...), custom_call_target="tpu_custom_call" | custom-call | flops 1048576 | bytes 1048576 | tf_op jit(solution)/shard_map/cells/pallas_call | solution.py:376
  55.8 0.0 copy-start
  55.8 4.6 %cells.6 = (bf16[2048,512]{1,0:T(8,128)(2,1)S(1)}, bf16[512,512]{1,0:T(8,128)(2,1)S(1)}) custom-call(bf16[2048,512]{1,0:T(8,128)(2,1)S(1)} %get-tuple-element.99.refs_0_, bf16[512,2048]{1,0:T(8,128)(2,1)S(1)} %get-tuple-element.100.refs_1_, f32[2048,128]{1,0:T(8,128)S(1)} %get-tuple-element.101.refs_2_, ...), custom_call_target="tpu_custom_call" | custom-call | flops 1048576 | bytes 1048576 | tf_op jit(solution)/shard_map/cells/pallas_call | solution.py:376
  60.5 0.0 collective-permute-done.7
  60.5 0.4 collective-permute-start.9
  60.9 0.0 copy-done
  60.9 8.9 %cells.7 = (f32[2048,512]{1,0:T(8,128)S(1)}, f32[512,512]{1,0:T(8,128)S(1)}) custom-call(bf16[2048,512]{1,0:T(8,128)(2,1)S(1)} %get-tuple-element.99.refs_0_, bf16[512,2048]{1,0:T(8,128)(2,1)S(1)} %get-tuple-element.100.refs_1_, f32[2048,128]{1,0:T(8,128)S(1)} %get-tuple-element.101.refs_2_, bf16[512,512]{1,0:T(8,128)(2,1)S(1)} %copy-done, ...), custom_call_target="tpu_custom_call" | custom-call | flops 1048576 | bytes 1048576 | tf_op jit(solution)/shard_map/cells/pallas_call | solution.py:376
  69.8 0.3 collective-permute-done.9.refs_2_
  70.1 0.0 collective-permute-done.8
  70.1 0.1 add_convert_fusion.1
  70.2 2.9 %put_rows.3 = bf16[4,256,512]{2,1,0:T(8,128)(2,1)S(1)} custom-call(s32[2]{0:T(128)S(1)} %pad_add_fusion.scalars, s32[1,2048]{1,0:T(1,128)S(1)} %bitcast.30, f32[2048,512]{1,0:T(8,128)S(1)} %get-tuple-element.114.grad_ref), custom_call_target="tpu_custom_call" | custom-call | flops 1048576 | bytes 65536 | tf_op jit(solution)/shard_map/put_rows/pallas_call | solution.py:433
  73.1 0.1 collective-permute-start.10
  73.2 1.4 %collective-permute-start.14 = (bf16[512,512]{1,0:T(8,128)(2,1)S(1)}, bf16[512,512]{1,0:T(8,128)(2,1)S(1)}, u32[]{:S(2)}, u32[]{:S(2)}) collective-permute-start(bf16[512,512]{1,0:T(8,128)(2,1)S(1)} %get-tuple-element.118), channel_id=1, source_target_pairs={{0,8},{8,0},{16,24},{24,16},{1,9},{9,1},{17,25},{25,17},{2,10},{10... | collective-permute-start | bytes 1572872 | tf_op jit(solution)/shard_map/ppermute | solution.py:447
  74.6 1.5 %collective-permute-start.15 = (bf16[352,512]{1,0:T(8,128)(2,1)S(1)}, bf16[352,512]{1,0:T(8,128)(2,1)S(1)}, u32[]{:S(2)}, u32[]{:S(2)}) collective-permute-start(bf16[352,512]{1,0:T(8,128)(2,1)S(1)} %add_convert_fusion.1), channel_id=1, source_target_pairs={{0,16},{8,24},{16,0},{24,8},{1,17},{9,25},{17,1},{25,9},{2,18},{10... | collective-permute-start | bytes 1081352 | tf_op jit(solution)/shard_map/ppermute | solution.py:447
  76.1 3.9 %put_rows.4 = f32[3,256,512]{2,1,0:T(8,128)S(1)} custom-call(s32[2]{0:T(128)S(1)} %pad_add_fusion.scalars, s32[1,2048]{1,0:T(1,128)S(1)} %bitcast.31, f32[2048,512]{1,0:T(8,128)S(1)} %get-tuple-element.114.grad_ref), custom_call_target="tpu_custom_call" | custom-call | flops 4294967296 | bytes 65536 | tf_op jit(solution)/shard_map/put_rows/pallas_call | solution.py:433
  80.0 0.0 collective-permute-done.10
  80.0 0.3 add_convert_fusion
  80.3 0.1 slice_bitcast_fusion.1
  80.4 1.6 %collective-permute-start.11 = (bf16[256,512]{1,0:T(8,128)(2,1)S(1)}, bf16[256,512]{1,0:T(8,128)(2,1)S(1)}, u32[]{:S(2)}, u32[]{:S(2)}) collective-permute-start(bf16[256,512]{1,0:T(8,128)(2,1)S(1)} %get-tuple-element.120), channel_id=1, source_target_pairs={{0,4},{1,5},{2,6},{3,7},{4,0},{5,1},{6,2},{7,3},{8,12},{9,13},{10,... | collective-permute-start | bytes 786440 | tf_op jit(solution)/shard_map/ppermute | solution.py:447
  81.9 1.5 %collective-permute-start.12 = (bf16[256,512]{1,0:T(8,128)(2,1)S(1)}, bf16[256,512]{1,0:T(8,128)(2,1)S(1)}, u32[]{:S(2)}, u32[]{:S(2)}) collective-permute-start(bf16[256,512]{1,0:T(8,128)(2,1)S(1)} %get-tuple-element.121), channel_id=1, source_target_pairs={{0,6},{1,7},{2,4},{3,5},{4,2},{5,3},{6,0},{7,1},{8,14},{9,15},{10,... | collective-permute-start | bytes 786440 | tf_op jit(solution)/shard_map/ppermute | solution.py:447
  83.4 0.5 collective-permute-start.13
  83.9 1.8 %put_rows.5 = f32[1,256,512]{2,1,0:T(8,128)S(1)} custom-call(s32[2]{0:T(128)S(1)} %pad_add_fusion.scalars, s32[1,2048]{1,0:T(1,128)S(1)} %bitcast.32, f32[2048,512]{1,0:T(8,128)S(1)} %get-tuple-element.114.grad_ref), custom_call_target="tpu_custom_call" | custom-call | flops 1048576 | bytes 65536 | tf_op jit(solution)/shard_map/put_rows/pallas_call | solution.py:433
  85.7 9.5 %collective-permute-done.14.refs_1_ = bf16[512,512]{1,0:T(8,128)(2,1)S(1)} collective-permute-done((bf16[512,512]{1,0:T(8,128)(2,1)S(1)}, bf16[512,512]{1,0:T(8,128)(2,1)S(1)}, u32[]{:S(2)}, u32[]{:S(2)}) %collective-permute-start.14) | collective-permute-done | bytes 524320 | tf_op jit(solution)/shard_map/ppermute | solution.py:447
  95.2 0.0 collective-permute-done.15.refs_3_
  95.2 1.3 %finish.1 = f32[512,512]{1,0:T(8,128)} custom-call(f32[512,512]{1,0:T(8,128)S(1)} %get-tuple-element.117.refs_0_, bf16[512,512]{1,0:T(8,128)(2,1)S(1)} %collective-permute-done.14.refs_1_, bf16[160,512]{1,0:T(8,128)(2,1)S(1)} %collective-permute-done.9.refs_2_, bf16[352,512]{1,0:T(8,128)(2,1)S(1)} %collective-permute-done.15.refs_3_), custom_call_target="tpu_custom_call" | custom-call | flops 262144 | bytes 16384 | tf_op jit(solution)/shard_map/finish/pallas_call | solution.py:400
  96.6 0.0 collective-permute-done.11
  96.6 0.0 collective-permute-done.12
  96.6 0.0 collective-permute-done.13
  96.6 1.0 fusion.2
  (1 shorter events, 0.0 us)
Async XLA Ops:
  0.6 29.6 %collective-permute-start = (bf16[512,512]{1,0:T(8,128)(2,1)}, bf16[512,512]{1,0:T(8,128)(2,1)S(1)}, u32[]{:S(2)}, u32[]{:S(2)}) collective-permute-start(bf16[512,512]{1,0:T(8,128)(2,1)} %refs_3_.1), channel_id=1, source_target_pairs={{0,16},{8,24},{16,0},{24,8},{1,17},{9,25},{17,1},{25,9},{2,18},{10... | collective-permute-start | bytes 1572872 | tf_op jit(solution)/shard_map/ppermute | solution.py:447
  4.7 25.5 %collective-permute-start.1 = (bf16[512,512]{1,0:T(8,128)(2,1)}, bf16[512,512]{1,0:T(8,128)(2,1)S(1)}, u32[]{:S(2)}, u32[]{:S(2)}) collective-permute-start(bf16[512,512]{1,0:T(8,128)(2,1)} %refs_3_.1), channel_id=1, source_target_pairs={{0,8},{8,0},{16,24},{24,16},{1,9},{9,1},{17,25},{25,17},{2,10},{10... | collective-permute-start | bytes 1572872 | tf_op jit(solution)/shard_map/ppermute | solution.py:447
  6.4 9.1 %copy-start.1 = (bf16[256,512]{1,0:T(8,128)(2,1)S(1)}, bf16[256,512]{1,0:T(8,128)(2,1)}, u32[]{:S(2)}) copy-start(bf16[256,512]{1,0:T(8,128)(2,1)} %refs_0_.1) | copy-start | bytes 786436
  15.5 14.7 %collective-permute-start.4 = (bf16[256,512]{1,0:T(8,128)(2,1)S(1)}, bf16[256,512]{1,0:T(8,128)(2,1)S(1)}, u32[]{:S(2)}, u32[]{:S(2)}) collective-permute-start(bf16[256,512]{1,0:T(8,128)(2,1)S(1)} %copy-done.1), channel_id=1, source_target_pairs={{0,6},{1,7},{2,4},{3,5},{4,2},{5,3},{6,0},{7,1},{8,14},{9,15},{10,... | collective-permute-start | bytes 786440 | tf_op jit(solution)/shard_map/ppermute | solution.py:447
  18.0 12.2 %collective-permute-start.3 = (bf16[256,512]{1,0:T(8,128)(2,1)S(1)}, bf16[256,512]{1,0:T(8,128)(2,1)S(1)}, u32[]{:S(2)}, u32[]{:S(2)}) collective-permute-start(bf16[256,512]{1,0:T(8,128)(2,1)S(1)} %copy-done.1), channel_id=1, source_target_pairs={{0,4},{1,5},{2,6},{3,7},{4,0},{5,1},{6,2},{7,3},{8,12},{9,13},{10,... | collective-permute-start | bytes 786440 | tf_op jit(solution)/shard_map/ppermute | solution.py:447
  18.5 11.7 %collective-permute-start.2 = (bf16[256,512]{1,0:T(8,128)(2,1)S(1)}, bf16[256,512]{1,0:T(8,128)(2,1)S(1)}, u32[]{:S(2)}, u32[]{:S(2)}) collective-permute-start(bf16[256,512]{1,0:T(8,128)(2,1)S(1)} %copy-done.1), channel_id=1, source_target_pairs={{0,2},{1,3},{2,0},{3,1},{4,6},{5,7},{6,4},{7,5},{8,10},{9,11},{10,... | collective-permute-start | bytes 786440 | tf_op jit(solution)/shard_map/ppermute | solution.py:447
  30.4 7.1 %copy-start.2 = (s32[2048]{0:T(1024)S(1)}, s32[2048]{0:T(1024)}, u32[]{:S(2)}) copy-start(s32[2048]{0:T(1024)} %param.10) | copy-start | bytes 24580
  30.4 7.1 %copy-start.3 = (f32[2048]{0:T(1024)S(1)}, f32[2048]{0:T(1024)}, u32[]{:S(2)}) copy-start(f32[2048]{0:T(1024)} %param.12) | copy-start | bytes 24580
  30.4 7.0 %collective-permute-start.5 = (bf16[4,256,512]{2,1,0:T(8,128)(2,1)S(1)}, bf16[4,256,512]{2,1,0:T(8,128)(2,1)S(1)}, u32[]{:S(2)}, u32[]{:S(2)}) collective-permute-start(bf16[4,256,512]{2,1,0:T(8,128)(2,1)S(1)} %pad_maximum_fusion), channel_id=1, source_target_pairs={{0,1},{1,0},{2,3},{3,2},{4,5},{5,4},{6,7},{7,6},{8,9},{9,8},{10,11... | collective-permute-start | bytes 3145736 | tf_op jit(solution)/shard_map/ppermute | solution.py:447
  30.5 14.3 %collective-permute-start.6 = (bf16[512,512]{1,0:T(8,128)(2,1)S(1)}, bf16[512,512]{1,0:T(8,128)(2,1)S(1)}, u32[]{:S(2)}, u32[]{:S(2)}) collective-permute-start(bf16[512,512]{1,0:T(8,128)(2,1)S(1)} %collective-permute-done.refs_3_.refs_7_), channel_id=1, source_target_pairs={{0,8},{8,0},{16,24},{24,16},{1,9},{9,1},{17,25},{25,17},{2,10},{10... | collective-permute-start | bytes 1572872 | tf_op jit(solution)/shard_map/ppermute | solution.py:447
  49.3 11.2 %collective-permute-start.7 = (bf16[160,512]{1,0:T(8,128)(2,1)S(1)}, bf16[160,512]{1,0:T(8,128)(2,1)S(1)}, u32[]{:S(2)}, u32[]{:S(2)}) collective-permute-start(bf16[160,512]{1,0:T(8,128)(2,1)S(1)} %get-tuple-element.93), channel_id=1, source_target_pairs={{0,8},{8,0},{16,24},{24,16},{1,9},{9,1},{17,25},{25,17},{2,10},{10... | collective-permute-start | bytes 491528 | tf_op jit(solution)/shard_map/ppermute | solution.py:447
  49.8 20.3 %collective-permute-start.8 = (bf16[352,512]{1,0:T(8,128)(2,1)S(1)}, bf16[352,512]{1,0:T(8,128)(2,1)S(1)}, u32[]{:S(2)}, u32[]{:S(2)}) collective-permute-start(bf16[352,512]{1,0:T(8,128)(2,1)S(1)} %get-tuple-element.108), channel_id=1, source_target_pairs={{0,8},{8,0},{16,24},{24,16},{1,9},{9,1},{17,25},{25,17},{2,10},{10... | collective-permute-start | bytes 1081352 | tf_op jit(solution)/shard_map/ppermute | solution.py:447
  55.8 5.1 %copy-start = (bf16[512,512]{1,0:T(8,128)(2,1)S(1)}, bf16[512,512]{1,0:T(8,128)(2,1)}, u32[]{:S(2)}) copy-start(bf16[512,512]{1,0:T(8,128)(2,1)} %refs_3_.1) | copy-start | bytes 1572868
  60.5 9.6 %collective-permute-start.9 = (bf16[160,512]{1,0:T(8,128)(2,1)S(1)}, bf16[160,512]{1,0:T(8,128)(2,1)S(1)}, u32[]{:S(2)}, u32[]{:S(2)}) collective-permute-start(bf16[160,512]{1,0:T(8,128)(2,1)S(1)} %add_convert_fusion.2), channel_id=1, source_target_pairs={{0,16},{8,24},{16,0},{24,8},{1,17},{9,25},{17,1},{25,9},{2,18},{10... | collective-permute-start | bytes 491528 | tf_op jit(solution)/shard_map/ppermute | solution.py:447
  73.1 6.9 %collective-permute-start.10 = (bf16[4,256,512]{2,1,0:T(8,128)(2,1)S(1)}, bf16[4,256,512]{2,1,0:T(8,128)(2,1)S(1)}, u32[]{:S(2)}, u32[]{:S(2)}) collective-permute-start(bf16[4,256,512]{2,1,0:T(8,128)(2,1)S(1)} %put_rows.3), channel_id=1, source_target_pairs={{0,1},{1,0},{2,3},{3,2},{4,5},{5,4},{6,7},{7,6},{8,9},{9,8},{10,11... | collective-permute-start | bytes 3145736 | tf_op jit(solution)/shard_map/ppermute | solution.py:447
  73.2 22.1 %collective-permute-start.14 = (bf16[512,512]{1,0:T(8,128)(2,1)S(1)}, bf16[512,512]{1,0:T(8,128)(2,1)S(1)}, u32[]{:S(2)}, u32[]{:S(2)}) collective-permute-start(bf16[512,512]{1,0:T(8,128)(2,1)S(1)} %get-tuple-element.118), channel_id=1, source_target_pairs={{0,8},{8,0},{16,24},{24,16},{1,9},{9,1},{17,25},{25,17},{2,10},{10... | collective-permute-start | bytes 1572872 | tf_op jit(solution)/shard_map/ppermute | solution.py:447
  74.6 20.6 %collective-permute-start.15 = (bf16[352,512]{1,0:T(8,128)(2,1)S(1)}, bf16[352,512]{1,0:T(8,128)(2,1)S(1)}, u32[]{:S(2)}, u32[]{:S(2)}) collective-permute-start(bf16[352,512]{1,0:T(8,128)(2,1)S(1)} %add_convert_fusion.1), channel_id=1, source_target_pairs={{0,16},{8,24},{16,0},{24,8},{1,17},{9,25},{17,1},{25,9},{2,18},{10... | collective-permute-start | bytes 1081352 | tf_op jit(solution)/shard_map/ppermute | solution.py:447
  80.4 16.2 %collective-permute-start.11 = (bf16[256,512]{1,0:T(8,128)(2,1)S(1)}, bf16[256,512]{1,0:T(8,128)(2,1)S(1)}, u32[]{:S(2)}, u32[]{:S(2)}) collective-permute-start(bf16[256,512]{1,0:T(8,128)(2,1)S(1)} %get-tuple-element.120), channel_id=1, source_target_pairs={{0,4},{1,5},{2,6},{3,7},{4,0},{5,1},{6,2},{7,3},{8,12},{9,13},{10,... | collective-permute-start | bytes 786440 | tf_op jit(solution)/shard_map/ppermute | solution.py:447
  81.9 14.7 %collective-permute-start.12 = (bf16[256,512]{1,0:T(8,128)(2,1)S(1)}, bf16[256,512]{1,0:T(8,128)(2,1)S(1)}, u32[]{:S(2)}, u32[]{:S(2)}) collective-permute-start(bf16[256,512]{1,0:T(8,128)(2,1)S(1)} %get-tuple-element.121), channel_id=1, source_target_pairs={{0,6},{1,7},{2,4},{3,5},{4,2},{5,3},{6,0},{7,1},{8,14},{9,15},{10,... | collective-permute-start | bytes 786440 | tf_op jit(solution)/shard_map/ppermute | solution.py:447
  83.4 13.2 %collective-permute-start.13 = (bf16[256,512]{1,0:T(8,128)(2,1)S(1)}, bf16[256,512]{1,0:T(8,128)(2,1)S(1)}, u32[]{:S(2)}, u32[]{:S(2)}) collective-permute-start(bf16[256,512]{1,0:T(8,128)(2,1)S(1)} %get-tuple-element.122), channel_id=1, source_target_pairs={{0,2},{1,3},{2,0},{3,1},{4,6},{5,7},{6,4},{7,5},{8,10},{9,11},{10,... | collective-permute-start | bytes 786440 | tf_op jit(solution)/shard_map/ppermute | solution.py:447

commit v8 on v7

--- a/solution.py
+++ b/solution.py
@@ -380,7 +380,7 @@
         out_shape=[main, *outs],
         scratch_shapes=[pltpu.VMEM((depth, width), BF16), pltpu.VMEM((depth, width), F32), *scratch],
         compiler_params=params(24),
-        cost_estimate=cost(rows * width, rows * depth),
+        cost_estimate=cost(rows, rows),
         name="cells",
     )(*args)
 
@@ -437,7 +437,7 @@
         out_shape=jax.ShapeDtypeStruct((len(offsets), side, width), F32 if exact else BF16),
         scratch_shapes=[pltpu.VMEM((len(offsets) * side, grad.shape[0]), BF16)],
         compiler_params=params(24),
-        cost_estimate=cost((4096 if exact and len(offsets) > 1 else 1) * grad.size, grad.size // 16),
+        cost_estimate=cost((16384 if exact and len(offsets) > 1 else 1) * grad.size, grad.size // 16),
         name="put_rows",
     )(scalars, row_perm[None, :], grad)
 
@@ -506,7 +506,7 @@
     ordered = functools.partial(put_rows, scalars, row_perm)
     away = ordered(grad, (1, 3, 5, 7), side, False)
     core = swap(away, "col", 1)
-    grad, away = together((grad, away))
+    grad, away, got_near = together((grad, away, got_near))
     both = ordered(grad, (2, 4, 6), side, True) + core[1:].astype(F32)
     sends = [both[at].astype(BF16) for at in range(3)]
     got = [swap(sends[at], "col", bit) for at, bit in ((1, 4), (2, 6), (0, 2))]

time: 97.7 us -> 103 us (1.054)
  waiting for transfers between devices: 11.8 us -> 15 us
  starting transfers between devices: 18.8 us -> 21 us
    ppermute x16, waiting for transfers between devices: 11.8 us -> 15 us  [swap(): return lax.ppermute(value, axis, pairs)]
    ppermute x16, starting transfers between devices: 18.8 us -> 21 us  [swap(): return lax.ppermute(value, axis, pairs)]
  transfers between devices with their start and end apart: 16 -> 16, of which waited for: 3 -> 5; matrix products, arithmetic and copies ran while one was open for 0% -> 1% of each run, Pallas kernels for 58% -> 58%
where the time goes in v8:
time: 103 us
  Pallas kernels  64.4 us (63%)
  starting transfers between devices  21 us (20%)
  waiting for transfers between devices  15 us (15%)
  other arithmetic  1.6 us (2%)
    pallas_call x4, Pallas kernels, cells(): pl.pallas_call(functools.partial(cells_kernel, len(others), pieces), in_s...  22.4 us
    ppermute x16, starting transfers between devices, swap(): return lax.ppermute(value, axis, pairs)  21 us
    pallas_call x2, Pallas kernels, order_next(): pl.pallas_call(functools.partial(order_next_kernel, offsets), in_specs=[S...  17.6 us
    ppermute x16, waiting for transfers between devices, swap(): return lax.ppermute(value, axis, pairs)  15 us
    pallas_call x1, Pallas kernels, order_first(): pl.pallas_call(functools.partial(order_first_kernel, offsets), in_specs=[...  9.09 us
    pallas_call x3, Pallas kernels, put_rows(): pl.pallas_call(functools.partial(put_kernel, offsets, exact), in_specs=[S...  8.62 us
    pallas_call x1, Pallas kernels, take_rows(): pl.pallas_call(take_kernel, in_specs=[SCALARS] + [WHOLE] * 7, out_specs=[...  5.32 us
  transfers between devices with their start and end apart: 16, of which 5 were waited for; matrix products, arithmetic and copies ran while one was open for 1% of the time, Pallas kernels for 58%

profile of v8, /device:TPU:0, one launch (start us, length us, event | category | flops | bytes accessed | tf_op | source)
XLA Modules:
  0.0 103.0 jit_solution(7566246140665533821)
XLA Ops:
  0.6 4.1 %collective-permute-start = (bf16[512,512]{1,0:T(8,128)(2,1)}, bf16[512,512]{1,0:T(8,128)(2,1)S(1)}, u32[]{:S(2)}, u32[]{:S(2)}) collective-permute-start(bf16[512,512]{1,0:T(8,128)(2,1)} %refs_3_.1), channel_id=1, source_target_pairs={{0,16},{8,24},{16,0},{24,8},{1,17},{9,25},{17,1},{25,9},{2,18},{10... | collective-permute-start | bytes 1572872 | tf_op jit(solution)/shard_map/ppermute | solution.py:447
  4.7 1.6 %collective-permute-start.1 = (bf16[512,512]{1,0:T(8,128)(2,1)}, bf16[512,512]{1,0:T(8,128)(2,1)S(1)}, u32[]{:S(2)}, u32[]{:S(2)}) collective-permute-start(bf16[512,512]{1,0:T(8,128)(2,1)} %refs_3_.1), channel_id=1, source_target_pairs={{0,8},{8,0},{16,24},{24,16},{1,9},{9,1},{17,25},{25,17},{2,10},{10... | collective-permute-start | bytes 1572872 | tf_op jit(solution)/shard_map/ppermute | solution.py:447
  6.3 0.1 pad_add_fusion.scalars
  6.4 0.0 copy-start.1
  6.4 9.1 %order_first.1 = (bf16[2048,512]{1,0:T(8,128)(2,1)S(1)}, f32[16,512]{1,0:T(8,128)S(1)}, bf16[2048,2048]{1,0:T(8,128)(2,1)S(1)}, f32[128,128]{1,0:T(8,128)S(1)}, f32[32,2048]{1,0:T(8,128)S(1)}) custom-call(s32[2]{0:T(128)S(1)} %pad_add_fusion.scalars, s32[16,128]{1,0:T(8,128)} %bitcast.34, s32[8,8]{1,0:T(8,128)} %mask_hbm.1, f32[1,2048]{1,0:T(1,128)} %bitcast.35, ...), custom_call_target="tpu_custom_call" | custom-call | flops 4294967296 | bytes 16777216 | tf_op jit(solution)/shard_map/order_first/pallas_call | solution.py:173
  15.5 0.0 copy-done.1
  15.5 2.5 %collective-permute-start.4 = (bf16[256,512]{1,0:T(8,128)(2,1)S(1)}, bf16[256,512]{1,0:T(8,128)(2,1)S(1)}, u32[]{:S(2)}, u32[]{:S(2)}) collective-permute-start(bf16[256,512]{1,0:T(8,128)(2,1)S(1)} %copy-done.1), channel_id=1, source_target_pairs={{0,6},{1,7},{2,4},{3,5},{4,2},{5,3},{6,0},{7,1},{8,14},{9,15},{10,... | collective-permute-start | bytes 786440 | tf_op jit(solution)/shard_map/ppermute | solution.py:447
  18.0 0.5 collective-permute-start.3
  18.5 0.5 collective-permute-start.2
  19.0 11.2 %order_next.2 = (bf16[2048,512]{1,0:T(8,128)(2,1)S(1)}, bf16[2048,512]{1,0:T(8,128)(2,1)S(1)}, f32[16,512]{1,0:T(8,128)S(1)}, f32[16,512]{1,0:T(8,128)S(1)}) custom-call(s32[2]{0:T(128)S(1)} %pad_add_fusion.scalars, bf16[2048,2048]{1,0:T(8,128)(2,1)S(1)} %get-tuple-element.68.shifted_ref, f32[128,128]{1,0:T(8,128)S(1)} %get-tuple-element.65.columns_ref, ...), custom_call_target="tpu_custom_call" | custom-call | flops 1048576 | bytes 1048576 | tf_op jit(solution)/shard_map/order_next/pallas_call | solution.py:221
  30.2 0.0 collective-permute-done.4.refs_3_
  30.2 0.0 collective-permute-done.3.refs_2_
  30.2 0.0 collective-permute-done.2.refs_1_
  30.3 0.0 collective-permute-done.refs_3_.refs_7_
  30.3 0.0 collective-permute-done.1.refs_3_.refs_8_
  30.3 0.1 pad_maximum_fusion
  30.4 0.0 copy-start.2
  30.4 0.0 copy-start.3
  30.4 0.1 collective-permute-start.5
  30.5 0.5 collective-permute-start.6
  31.0 6.4 %order_next.3 = (bf16[2048,512]{1,0:T(8,128)(2,1)S(1)}, f32[16,512]{1,0:T(8,128)S(1)}) custom-call(s32[2]{0:T(128)S(1)} %pad_add_fusion.scalars, bf16[2048,2048]{1,0:T(8,128)(2,1)S(1)} %get-tuple-element.68.shifted_ref, f32[128,128]{1,0:T(8,128)S(1)} %get-tuple-element.65.columns_ref, f32[32,2048]{1,0:T(8,128)S(1)} %get-tuple-element.66.values_ref), custom_call_target="tpu_custom_call" | custom-call | flops 1048576 | bytes 1048576 | tf_op jit(solution)/shard_map/order_next/pallas_call | solution.py:221
  37.5 0.0 collective-permute-done.5.refs_4_
  37.5 0.0 copy-done.2
  37.5 0.0 copy-done.3
  37.5 5.3 %take_rows.1 = (bf16[2048,512]{1,0:T(8,128)(2,1)S(1)}, bf16[512,2048]{1,0:T(8,128)(2,1)S(1)}, f32[2048,128]{1,0:T(8,128)S(1)}) custom-call(s32[2]{0:T(128)S(1)} %pad_add_fusion.scalars, s32[16,128]{1,0:T(8,128)S(1)} %bitcast.29, f32[16,128]{1,0:T(8,128)S(1)} %bitcast.33, bf16[256,512]{1,0:T(8,128)(2,1)S(1)} %copy-done.1, ...), custom_call_target="tpu_custom_call" | custom-call | flops 4294967296 | bytes 4194304 | tf_op jit(solution)/shard_map/take_rows/pallas_call | solution.py:265
  42.8 2.0 %collective-permute-done.6.refs_3_.refs_6_ = bf16[512,512]{1,0:T(8,128)(2,1)S(1)} collective-permute-done((bf16[512,512]{1,0:T(8,128)(2,1)S(1)}, bf16[512,512]{1,0:T(8,128)(2,1)S(1)}, u32[]{:S(2)}, u32[]{:S(2)}) %collective-permute-start.6) | collective-permute-done | bytes 524320 | tf_op jit(solution)/shard_map/ppermute | solution.py:447
  44.9 4.4 %cells.4 = (bf16[2048,512]{1,0:T(8,128)(2,1)S(1)}, bf16[160,512]{1,0:T(8,128)(2,1)S(1)}, bf16[352,512]{1,0:T(8,128)(2,1)S(1)}) custom-call(bf16[2048,512]{1,0:T(8,128)(2,1)S(1)} %get-tuple-element.100.refs_0_, bf16[512,2048]{1,0:T(8,128)(2,1)S(1)} %get-tuple-element.101.refs_1_, f32[2048,128]{1,0:T(8,128)S(1)} %get-tuple-element.102.refs_2_, ...), custom_call_target="tpu_custom_call" | custom-call | flops 2048 | bytes 2048 | tf_op jit(solution)/shard_map/cells/pallas_call | solution.py:376
  49.3 0.5 collective-permute-start.7
  49.8 1.6 %collective-permute-start.8 = (bf16[352,512]{1,0:T(8,128)(2,1)S(1)}, bf16[352,512]{1,0:T(8,128)(2,1)S(1)}, u32[]{:S(2)}, u32[]{:S(2)}) collective-permute-start(bf16[352,512]{1,0:T(8,128)(2,1)S(1)} %get-tuple-element.109), channel_id=1, source_target_pairs={{0,8},{8,0},{16,24},{24,16},{1,9},{9,1},{17,25},{25,17},{2,10},{10... | collective-permute-start | bytes 1081352 | tf_op jit(solution)/shard_map/ppermute | solution.py:447
  51.4 4.4 %cells.5 = (bf16[2048,512]{1,0:T(8,128)(2,1)S(1)}, f32[512,512]{1,0:T(8,128)S(1)}) custom-call(bf16[2048,512]{1,0:T(8,128)(2,1)S(1)} %get-tuple-element.100.refs_0_, bf16[512,2048]{1,0:T(8,128)(2,1)S(1)} %get-tuple-element.101.refs_1_, f32[2048,128]{1,0:T(8,128)S(1)} %get-tuple-element.102.refs_2_, ...), custom_call_target="tpu_custom_call" | custom-call | flops 2048 | bytes 2048 | tf_op jit(solution)/shard_map/cells/pallas_call | solution.py:376
  55.8 0.0 copy-start
  55.8 4.6 %cells.6 = (bf16[2048,512]{1,0:T(8,128)(2,1)S(1)}, bf16[512,512]{1,0:T(8,128)(2,1)S(1)}) custom-call(bf16[2048,512]{1,0:T(8,128)(2,1)S(1)} %get-tuple-element.100.refs_0_, bf16[512,2048]{1,0:T(8,128)(2,1)S(1)} %get-tuple-element.101.refs_1_, f32[2048,128]{1,0:T(8,128)S(1)} %get-tuple-element.102.refs_2_, ...), custom_call_target="tpu_custom_call" | custom-call | flops 2048 | bytes 2048 | tf_op jit(solution)/shard_map/cells/pallas_call | solution.py:376
  60.5 0.5 collective-permute-start.10
  61.0 0.0 collective-permute-done.7
  61.0 1.5 %collective-permute-start.9 = (bf16[160,512]{1,0:T(8,128)(2,1)S(1)}, bf16[160,512]{1,0:T(8,128)(2,1)S(1)}, u32[]{:S(2)}, u32[]{:S(2)}) collective-permute-start(bf16[160,512]{1,0:T(8,128)(2,1)S(1)} %add_convert_fusion.2), channel_id=1, source_target_pairs={{0,16},{8,24},{16,0},{24,8},{1,17},{9,25},{17,1},{25,9},{2,18},{10... | collective-permute-start | bytes 491528 | tf_op jit(solution)/shard_map/ppermute | solution.py:447
  62.6 0.0 copy-done
  62.6 8.9 %cells.7 = (f32[2048,512]{1,0:T(8,128)S(1)}, f32[512,512]{1,0:T(8,128)S(1)}) custom-call(bf16[2048,512]{1,0:T(8,128)(2,1)S(1)} %get-tuple-element.100.refs_0_, bf16[512,2048]{1,0:T(8,128)(2,1)S(1)} %get-tuple-element.101.refs_1_, f32[2048,128]{1,0:T(8,128)S(1)} %get-tuple-element.102.refs_2_, bf16[512,512]{1,0:T(8,128)(2,1)S(1)} %copy-done, ...), custom_call_target="tpu_custom_call" | custom-call | flops 2048 | bytes 2048 | tf_op jit(solution)/shard_map/cells/pallas_call | solution.py:376
  71.5 4.1 %collective-permute-done.9.refs_2_ = bf16[160,512]{1,0:T(8,128)(2,1)S(1)} collective-permute-done((bf16[160,512]{1,0:T(8,128)(2,1)S(1)}, bf16[160,512]{1,0:T(8,128)(2,1)S(1)}, u32[]{:S(2)}, u32[]{:S(2)}) %collective-permute-start.9) | collective-permute-done | bytes 163872 | tf_op jit(solution)/shard_map/ppermute | solution.py:447
  75.6 0.0 collective-permute-done.8
  75.6 0.1 add_convert_fusion.1
  75.7 3.4 %collective-permute-start.15 = (bf16[352,512]{1,0:T(8,128)(2,1)S(1)}, bf16[352,512]{1,0:T(8,128)(2,1)S(1)}, u32[]{:S(2)}, u32[]{:S(2)}) collective-permute-start(bf16[352,512]{1,0:T(8,128)(2,1)S(1)} %add_convert_fusion.1), channel_id=1, source_target_pairs={{0,16},{8,24},{16,0},{24,8},{1,17},{9,25},{17,1},{25,9},{2,18},{10... | collective-permute-start | bytes 1081352 | tf_op jit(solution)/shard_map/ppermute | solution.py:447
  79.1 2.9 %put_rows.3 = bf16[4,256,512]{2,1,0:T(8,128)(2,1)S(1)} custom-call(s32[2]{0:T(128)S(1)} %pad_add_fusion.scalars, s32[1,2048]{1,0:T(1,128)S(1)} %bitcast.30, f32[2048,512]{1,0:T(8,128)S(1)} %get-tuple-element.116.grad_ref), custom_call_target="tpu_custom_call" | custom-call | flops 1048576 | bytes 65536 | tf_op jit(solution)/shard_map/put_rows/pallas_call | solution.py:433
  82.0 0.1 collective-permute-start.11
  82.1 0.0 collective-permute-done.10.refs_1_
  82.1 3.9 %put_rows.4 = f32[3,256,512]{2,1,0:T(8,128)S(1)} custom-call(s32[2]{0:T(128)S(1)} %pad_add_fusion.scalars, s32[1,2048]{1,0:T(1,128)S(1)} %bitcast.31, f32[2048,512]{1,0:T(8,128)S(1)} %get-tuple-element.116.grad_ref), custom_call_target="tpu_custom_call" | custom-call | flops 17179869184 | bytes 65536 | tf_op jit(solution)/shard_map/put_rows/pallas_call | solution.py:433
  86.1 0.0 collective-permute-done.11
  86.1 0.3 add_convert_fusion
  86.3 0.1 slice_bitcast_fusion.1
  86.4 1.6 %collective-permute-start.12 = (bf16[256,512]{1,0:T(8,128)(2,1)S(1)}, bf16[256,512]{1,0:T(8,128)(2,1)S(1)}, u32[]{:S(2)}, u32[]{:S(2)}) collective-permute-start(bf16[256,512]{1,0:T(8,128)(2,1)S(1)} %get-tuple-element.122), channel_id=1, source_target_pairs={{0,4},{1,5},{2,6},{3,7},{4,0},{5,1},{6,2},{7,3},{8,12},{9,13},{10,... | collective-permute-start | bytes 786440 | tf_op jit(solution)/shard_map/ppermute | solution.py:447
  88.0 1.4 %collective-permute-start.13 = (bf16[256,512]{1,0:T(8,128)(2,1)S(1)}, bf16[256,512]{1,0:T(8,128)(2,1)S(1)}, u32[]{:S(2)}, u32[]{:S(2)}) collective-permute-start(bf16[256,512]{1,0:T(8,128)(2,1)S(1)} %get-tuple-element.123), channel_id=1, source_target_pairs={{0,6},{1,7},{2,4},{3,5},{4,2},{5,3},{6,0},{7,1},{8,14},{9,15},{10,... | collective-permute-start | bytes 786440 | tf_op jit(solution)/shard_map/ppermute | solution.py:447
  89.4 0.5 collective-permute-start.14
  90.0 1.8 %put_rows.5 = f32[1,256,512]{2,1,0:T(8,128)S(1)} custom-call(s32[2]{0:T(128)S(1)} %pad_add_fusion.scalars, s32[1,2048]{1,0:T(1,128)S(1)} %bitcast.32, f32[2048,512]{1,0:T(8,128)S(1)} %get-tuple-element.116.grad_ref), custom_call_target="tpu_custom_call" | custom-call | flops 1048576 | bytes 65536 | tf_op jit(solution)/shard_map/put_rows/pallas_call | solution.py:433
  91.8 2.5 %collective-permute-done.15.refs_3_ = bf16[352,512]{1,0:T(8,128)(2,1)S(1)} collective-permute-done((bf16[352,512]{1,0:T(8,128)(2,1)S(1)}, bf16[352,512]{1,0:T(8,128)(2,1)S(1)}, u32[]{:S(2)}, u32[]{:S(2)}) %collective-permute-start.15) | collective-permute-done | bytes 360480 | tf_op jit(solution)/shard_map/ppermute | solution.py:447
  94.3 1.3 %finish.1 = f32[512,512]{1,0:T(8,128)} custom-call(f32[512,512]{1,0:T(8,128)S(1)} %get-tuple-element.119.refs_0_, bf16[512,512]{1,0:T(8,128)(2,1)S(1)} %collective-permute-done.10.refs_1_, bf16[160,512]{1,0:T(8,128)(2,1)S(1)} %collective-permute-done.9.refs_2_, bf16[352,512]{1,0:T(8,128)(2,1)S(1)} %collective-permute-done.15.refs_3_), custom_call_target="tpu_custom_call" | custom-call | flops 262144 | bytes 16384 | tf_op jit(solution)/shard_map/finish/pallas_call | solution.py:400
  95.6 5.2 %collective-permute-done.12 = bf16[256,512]{1,0:T(8,128)(2,1)S(1)} collective-permute-done((bf16[256,512]{1,0:T(8,128)(2,1)S(1)}, bf16[256,512]{1,0:T(8,128)(2,1)S(1)}, u32[]{:S(2)}, u32[]{:S(2)}) %collective-permute-start.12) | collective-permute-done | bytes 262176 | tf_op jit(solution)/shard_map/ppermute | solution.py:447
  100.8 0.0 collective-permute-done.13
  100.8 1.2 %collective-permute-done.14 = bf16[256,512]{1,0:T(8,128)(2,1)S(1)} collective-permute-done((bf16[256,512]{1,0:T(8,128)(2,1)S(1)}, bf16[256,512]{1,0:T(8,128)(2,1)S(1)}, u32[]{:S(2)}, u32[]{:S(2)}) %collective-permute-start.14) | collective-permute-done | bytes 262176 | tf_op jit(solution)/shard_map/ppermute | solution.py:447
  102.0 1.0 fusion.2
  (1 shorter events, 0.0 us)
Async XLA Ops:
  0.6 29.6 %collective-permute-start = (bf16[512,512]{1,0:T(8,128)(2,1)}, bf16[512,512]{1,0:T(8,128)(2,1)S(1)}, u32[]{:S(2)}, u32[]{:S(2)}) collective-permute-start(bf16[512,512]{1,0:T(8,128)(2,1)} %refs_3_.1), channel_id=1, source_target_pairs={{0,16},{8,24},{16,0},{24,8},{1,17},{9,25},{17,1},{25,9},{2,18},{10... | collective-permute-start | bytes 1572872 | tf_op jit(solution)/shard_map/ppermute | solution.py:447
  4.7 25.5 %collective-permute-start.1 = (bf16[512,512]{1,0:T(8,128)(2,1)}, bf16[512,512]{1,0:T(8,128)(2,1)S(1)}, u32[]{:S(2)}, u32[]{:S(2)}) collective-permute-start(bf16[512,512]{1,0:T(8,128)(2,1)} %refs_3_.1), channel_id=1, source_target_pairs={{0,8},{8,0},{16,24},{24,16},{1,9},{9,1},{17,25},{25,17},{2,10},{10... | collective-permute-start | bytes 1572872 | tf_op jit(solution)/shard_map/ppermute | solution.py:447
  6.4 9.1 %copy-start.1 = (bf16[256,512]{1,0:T(8,128)(2,1)S(1)}, bf16[256,512]{1,0:T(8,128)(2,1)}, u32[]{:S(2)}) copy-start(bf16[256,512]{1,0:T(8,128)(2,1)} %refs_0_.1) | copy-start | bytes 786436
  15.5 14.7 %collective-permute-start.4 = (bf16[256,512]{1,0:T(8,128)(2,1)S(1)}, bf16[256,512]{1,0:T(8,128)(2,1)S(1)}, u32[]{:S(2)}, u32[]{:S(2)}) collective-permute-start(bf16[256,512]{1,0:T(8,128)(2,1)S(1)} %copy-done.1), channel_id=1, source_target_pairs={{0,6},{1,7},{2,4},{3,5},{4,2},{5,3},{6,0},{7,1},{8,14},{9,15},{10,... | collective-permute-start | bytes 786440 | tf_op jit(solution)/shard_map/ppermute | solution.py:447
  18.0 12.2 %collective-permute-start.3 = (bf16[256,512]{1,0:T(8,128)(2,1)S(1)}, bf16[256,512]{1,0:T(8,128)(2,1)S(1)}, u32[]{:S(2)}, u32[]{:S(2)}) collective-permute-start(bf16[256,512]{1,0:T(8,128)(2,1)S(1)} %copy-done.1), channel_id=1, source_target_pairs={{0,4},{1,5},{2,6},{3,7},{4,0},{5,1},{6,2},{7,3},{8,12},{9,13},{10,... | collective-permute-start | bytes 786440 | tf_op jit(solution)/shard_map/ppermute | solution.py:447
  18.5 11.7 %collective-permute-start.2 = (bf16[256,512]{1,0:T(8,128)(2,1)S(1)}, bf16[256,512]{1,0:T(8,128)(2,1)S(1)}, u32[]{:S(2)}, u32[]{:S(2)}) collective-permute-start(bf16[256,512]{1,0:T(8,128)(2,1)S(1)} %copy-done.1), channel_id=1, source_target_pairs={{0,2},{1,3},{2,0},{3,1},{4,6},{5,7},{6,4},{7,5},{8,10},{9,11},{10,... | collective-permute-start | bytes 786440 | tf_op jit(solution)/shard_map/ppermute | solution.py:447
  30.4 7.1 %copy-start.2 = (s32[2048]{0:T(1024)S(1)}, s32[2048]{0:T(1024)}, u32[]{:S(2)}) copy-start(s32[2048]{0:T(1024)} %param.10) | copy-start | bytes 24580
  30.4 7.1 %copy-start.3 = (f32[2048]{0:T(1024)S(1)}, f32[2048]{0:T(1024)}, u32[]{:S(2)}) copy-start(f32[2048]{0:T(1024)} %param.12) | copy-start | bytes 24580
  30.4 7.0 %collective-permute-start.5 = (bf16[4,256,512]{2,1,0:T(8,128)(2,1)S(1)}, bf16[4,256,512]{2,1,0:T(8,128)(2,1)S(1)}, u32[]{:S(2)}, u32[]{:S(2)}) collective-permute-start(bf16[4,256,512]{2,1,0:T(8,128)(2,1)S(1)} %pad_maximum_fusion), channel_id=1, source_target_pairs={{0,1},{1,0},{2,3},{3,2},{4,5},{5,4},{6,7},{7,6},{8,9},{9,8},{10,11... | collective-permute-start | bytes 3145736 | tf_op jit(solution)/shard_map/ppermute | solution.py:447
  30.5 14.3 %collective-permute-start.6 = (bf16[512,512]{1,0:T(8,128)(2,1)S(1)}, bf16[512,512]{1,0:T(8,128)(2,1)S(1)}, u32[]{:S(2)}, u32[]{:S(2)}) collective-permute-start(bf16[512,512]{1,0:T(8,128)(2,1)S(1)} %collective-permute-done.refs_3_.refs_7_), channel_id=1, source_target_pairs={{0,8},{8,0},{16,24},{24,16},{1,9},{9,1},{17,25},{25,17},{2,10},{10... | collective-permute-start | bytes 1572872 | tf_op jit(solution)/shard_map/ppermute | solution.py:447
  49.3 11.7 %collective-permute-start.7 = (bf16[160,512]{1,0:T(8,128)(2,1)S(1)}, bf16[160,512]{1,0:T(8,128)(2,1)S(1)}, u32[]{:S(2)}, u32[]{:S(2)}) collective-permute-start(bf16[160,512]{1,0:T(8,128)(2,1)S(1)} %get-tuple-element.94), channel_id=1, source_target_pairs={{0,8},{8,0},{16,24},{24,16},{1,9},{9,1},{17,25},{25,17},{2,10},{10... | collective-permute-start | bytes 491528 | tf_op jit(solution)/shard_map/ppermute | solution.py:447
  49.8 25.8 %collective-permute-start.8 = (bf16[352,512]{1,0:T(8,128)(2,1)S(1)}, bf16[352,512]{1,0:T(8,128)(2,1)S(1)}, u32[]{:S(2)}, u32[]{:S(2)}) collective-permute-start(bf16[352,512]{1,0:T(8,128)(2,1)S(1)} %get-tuple-element.109), channel_id=1, source_target_pairs={{0,8},{8,0},{16,24},{24,16},{1,9},{9,1},{17,25},{25,17},{2,10},{10... | collective-permute-start | bytes 1081352 | tf_op jit(solution)/shard_map/ppermute | solution.py:447
  55.8 6.7 %copy-start = (bf16[512,512]{1,0:T(8,128)(2,1)S(1)}, bf16[512,512]{1,0:T(8,128)(2,1)}, u32[]{:S(2)}) copy-start(bf16[512,512]{1,0:T(8,128)(2,1)} %refs_3_.1) | copy-start | bytes 1572868
  60.5 21.6 %collective-permute-start.10 = (bf16[512,512]{1,0:T(8,128)(2,1)S(1)}, bf16[512,512]{1,0:T(8,128)(2,1)S(1)}, u32[]{:S(2)}, u32[]{:S(2)}) collective-permute-start(bf16[512,512]{1,0:T(8,128)(2,1)S(1)} %get-tuple-element.114), channel_id=1, source_target_pairs={{0,8},{8,0},{16,24},{24,16},{1,9},{9,1},{17,25},{25,17},{2,10},{10... | collective-permute-start | bytes 1572872 | tf_op jit(solution)/shard_map/ppermute | solution.py:447
  61.0 14.6 %collective-permute-start.9 = (bf16[160,512]{1,0:T(8,128)(2,1)S(1)}, bf16[160,512]{1,0:T(8,128)(2,1)S(1)}, u32[]{:S(2)}, u32[]{:S(2)}) collective-permute-start(bf16[160,512]{1,0:T(8,128)(2,1)S(1)} %add_convert_fusion.2), channel_id=1, source_target_pairs={{0,16},{8,24},{16,0},{24,8},{1,17},{9,25},{17,1},{25,9},{2,18},{10... | collective-permute-start | bytes 491528 | tf_op jit(solution)/shard_map/ppermute | solution.py:447
  75.7 18.6 %collective-permute-start.15 = (bf16[352,512]{1,0:T(8,128)(2,1)S(1)}, bf16[352,512]{1,0:T(8,128)(2,1)S(1)}, u32[]{:S(2)}, u32[]{:S(2)}) collective-permute-start(bf16[352,512]{1,0:T(8,128)(2,1)S(1)} %add_convert_fusion.1), channel_id=1, source_target_pairs={{0,16},{8,24},{16,0},{24,8},{1,17},{9,25},{17,1},{25,9},{2,18},{10... | collective-permute-start | bytes 1081352 | tf_op jit(solution)/shard_map/ppermute | solution.py:447
  82.0 4.0 %collective-permute-start.11 = (bf16[4,256,512]{2,1,0:T(8,128)(2,1)S(1)}, bf16[4,256,512]{2,1,0:T(8,128)(2,1)S(1)}, u32[]{:S(2)}, u32[]{:S(2)}) collective-permute-start(bf16[4,256,512]{2,1,0:T(8,128)(2,1)S(1)} %put_rows.3), channel_id=1, source_target_pairs={{0,1},{1,0},{2,3},{3,2},{4,5},{5,4},{6,7},{7,6},{8,9},{9,8},{10,11... | collective-permute-start | bytes 3145736 | tf_op jit(solution)/shard_map/ppermute | solution.py:447
  86.4 14.4 %collective-permute-start.12 = (bf16[256,512]{1,0:T(8,128)(2,1)S(1)}, bf16[256,512]{1,0:T(8,128)(2,1)S(1)}, u32[]{:S(2)}, u32[]{:S(2)}) collective-permute-start(bf16[256,512]{1,0:T(8,128)(2,1)S(1)} %get-tuple-element.122), channel_id=1, source_target_pairs={{0,4},{1,5},{2,6},{3,7},{4,0},{5,1},{6,2},{7,3},{8,12},{9,13},{10,... | collective-permute-start | bytes 786440 | tf_op jit(solution)/shard_map/ppermute | solution.py:447
  88.0 12.8 %collective-permute-start.13 = (bf16[256,512]{1,0:T(8,128)(2,1)S(1)}, bf16[256,512]{1,0:T(8,128)(2,1)S(1)}, u32[]{:S(2)}, u32[]{:S(2)}) collective-permute-start(bf16[256,512]{1,0:T(8,128)(2,1)S(1)} %get-tuple-element.123), channel_id=1, source_target_pairs={{0,6},{1,7},{2,4},{3,5},{4,2},{5,3},{6,0},{7,1},{8,14},{9,15},{10,... | collective-permute-start | bytes 786440 | tf_op jit(solution)/shard_map/ppermute | solution.py:447
  89.4 12.6 %collective-permute-start.14 = (bf16[256,512]{1,0:T(8,128)(2,1)S(1)}, bf16[256,512]{1,0:T(8,128)(2,1)S(1)}, u32[]{:S(2)}, u32[]{:S(2)}) collective-permute-start(bf16[256,512]{1,0:T(8,128)(2,1)S(1)} %get-tuple-element.124), channel_id=1, source_target_pairs={{0,2},{1,3},{2,0},{3,1},{4,6},{5,7},{6,4},{7,5},{8,10},{9,11},{10,... | collective-permute-start | bytes 786440 | tf_op jit(solution)/shard_map/ppermute | solution.py:447

commit v9 on v7

--- a/solution.py
+++ b/solution.py
@@ -437,7 +437,7 @@
         out_shape=jax.ShapeDtypeStruct((len(offsets), side, width), F32 if exact else BF16),
         scratch_shapes=[pltpu.VMEM((len(offsets) * side, grad.shape[0]), BF16)],
         compiler_params=params(24),
-        cost_estimate=cost((4096 if exact and len(offsets) > 1 else 1) * grad.size, grad.size // 16),
+        cost_estimate=cost((16384 if exact and len(offsets) > 1 else 1) * grad.size, grad.size // 16),
         name="put_rows",
     )(scalars, row_perm[None, :], grad)
 

time: 97.7 us -> 97.1 us (level)
  transfers between devices with their start and end apart: 16 -> 16, of which waited for: 3 -> 4; matrix products, arithmetic and copies ran while one was open for 0% -> 1% of each run, Pallas kernels for 58% -> 62%
where the time goes in v9:
time: 97.1 us; the launch traced here: 96.9 us
  Pallas kernels  64.4 us (66%)
  starting transfers between devices  19 us (20%)
  waiting for transfers between devices  11 us (11%)
  other arithmetic  1.61 us (2%)
    pallas_call x4, Pallas kernels, cells(): pl.pallas_call(functools.partial(cells_kernel, len(others), pieces), in_s...  22.4 us
    ppermute x16, starting transfers between devices, swap(): return lax.ppermute(value, axis, pairs)  19 us
    pallas_call x2, Pallas kernels, order_next(): pl.pallas_call(functools.partial(order_next_kernel, offsets), in_specs=[S...  17.6 us
    ppermute x16, waiting for transfers between devices, swap(): return lax.ppermute(value, axis, pairs)  11 us
    pallas_call x1, Pallas kernels, order_first(): pl.pallas_call(functools.partial(order_first_kernel, offsets), in_specs=[...  9.09 us
    pallas_call x3, Pallas kernels, put_rows(): pl.pallas_call(functools.partial(put_kernel, offsets, exact), in_specs=[S...  8.61 us
    pallas_call x1, Pallas kernels, take_rows(): pl.pallas_call(take_kernel, in_specs=[SCALARS] + [WHOLE] * 7, out_specs=[...  5.32 us
  transfers between devices with their start and end apart: 16, of which 4 were waited for; matrix products, arithmetic and copies ran while one was open for 1% of the time, Pallas kernels for 62%

profile of v9, /device:TPU:0, one launch (start us, length us, event | category | flops | bytes accessed | tf_op | source)
XLA Modules:
  0.0 96.9 jit_solution(8876478133014066525)
XLA Ops:
  0.6 4.1 %collective-permute-start = (bf16[512,512]{1,0:T(8,128)(2,1)}, bf16[512,512]{1,0:T(8,128)(2,1)S(1)}, u32[]{:S(2)}, u32[]{:S(2)}) collective-permute-start(bf16[512,512]{1,0:T(8,128)(2,1)} %refs_3_.1), channel_id=1, source_target_pairs={{0,16},{8,24},{16,0},{24,8},{1,17},{9,25},{17,1},{25,9},{2,18},{10... | collective-permute-start | bytes 1572872 | tf_op jit(solution)/shard_map/ppermute | solution.py:447
  4.7 1.6 %collective-permute-start.1 = (bf16[512,512]{1,0:T(8,128)(2,1)}, bf16[512,512]{1,0:T(8,128)(2,1)S(1)}, u32[]{:S(2)}, u32[]{:S(2)}) collective-permute-start(bf16[512,512]{1,0:T(8,128)(2,1)} %refs_3_.1), channel_id=1, source_target_pairs={{0,8},{8,0},{16,24},{24,16},{1,9},{9,1},{17,25},{25,17},{2,10},{10... | collective-permute-start | bytes 1572872 | tf_op jit(solution)/shard_map/ppermute | solution.py:447
  6.3 0.1 pad_add_fusion.scalars
  6.4 0.0 copy-start.1
  6.4 9.1 %order_first.1 = (bf16[2048,512]{1,0:T(8,128)(2,1)S(1)}, f32[16,512]{1,0:T(8,128)S(1)}, bf16[2048,2048]{1,0:T(8,128)(2,1)S(1)}, f32[128,128]{1,0:T(8,128)S(1)}, f32[32,2048]{1,0:T(8,128)S(1)}) custom-call(s32[2]{0:T(128)S(1)} %pad_add_fusion.scalars, s32[16,128]{1,0:T(8,128)} %bitcast.34, s32[8,8]{1,0:T(8,128)} %mask_hbm.1, f32[1,2048]{1,0:T(1,128)} %bitcast.35, ...), custom_call_target="tpu_custom_call" | custom-call | flops 4294967296 | bytes 16777216 | tf_op jit(solution)/shard_map/order_first/pallas_call | solution.py:173
  15.5 0.0 copy-done.1
  15.5 2.5 %collective-permute-start.4 = (bf16[256,512]{1,0:T(8,128)(2,1)S(1)}, bf16[256,512]{1,0:T(8,128)(2,1)S(1)}, u32[]{:S(2)}, u32[]{:S(2)}) collective-permute-start(bf16[256,512]{1,0:T(8,128)(2,1)S(1)} %copy-done.1), channel_id=1, source_target_pairs={{0,6},{1,7},{2,4},{3,5},{4,2},{5,3},{6,0},{7,1},{8,14},{9,15},{10,... | collective-permute-start | bytes 786440 | tf_op jit(solution)/shard_map/ppermute | solution.py:447
  18.0 0.5 collective-permute-start.3
  18.5 0.5 collective-permute-start.2
  19.0 11.2 %order_next.2 = (bf16[2048,512]{1,0:T(8,128)(2,1)S(1)}, bf16[2048,512]{1,0:T(8,128)(2,1)S(1)}, f32[16,512]{1,0:T(8,128)S(1)}, f32[16,512]{1,0:T(8,128)S(1)}) custom-call(s32[2]{0:T(128)S(1)} %pad_add_fusion.scalars, bf16[2048,2048]{1,0:T(8,128)(2,1)S(1)} %get-tuple-element.67.shifted_ref, f32[128,128]{1,0:T(8,128)S(1)} %get-tuple-element.64.columns_ref, ...), custom_call_target="tpu_custom_call" | custom-call | flops 1048576 | bytes 1048576 | tf_op jit(solution)/shard_map/order_next/pallas_call | solution.py:221
  30.2 0.0 collective-permute-done.4.refs_3_
  30.2 0.0 collective-permute-done.3.refs_2_
  30.2 0.0 collective-permute-done.2.refs_1_
  30.3 0.0 collective-permute-done.refs_3_.refs_7_
  30.3 0.0 collective-permute-done.1.refs_3_.refs_8_
  30.3 0.1 pad_maximum_fusion
  30.4 0.0 copy-start.2
  30.4 0.0 copy-start.3
  30.4 0.1 collective-permute-start.5
  30.5 0.5 collective-permute-start.6
  31.0 6.4 %order_next.3 = (bf16[2048,512]{1,0:T(8,128)(2,1)S(1)}, f32[16,512]{1,0:T(8,128)S(1)}) custom-call(s32[2]{0:T(128)S(1)} %pad_add_fusion.scalars, bf16[2048,2048]{1,0:T(8,128)(2,1)S(1)} %get-tuple-element.67.shifted_ref, f32[128,128]{1,0:T(8,128)S(1)} %get-tuple-element.64.columns_ref, f32[32,2048]{1,0:T(8,128)S(1)} %get-tuple-element.65.values_ref), custom_call_target="tpu_custom_call" | custom-call | flops 1048576 | bytes 1048576 | tf_op jit(solution)/shard_map/order_next/pallas_call | solution.py:221
  37.5 0.0 collective-permute-done.5.refs_4_
  37.5 0.0 copy-done.2
  37.5 0.0 copy-done.3
  37.5 5.3 %take_rows.1 = (bf16[2048,512]{1,0:T(8,128)(2,1)S(1)}, bf16[512,2048]{1,0:T(8,128)(2,1)S(1)}, f32[2048,128]{1,0:T(8,128)S(1)}) custom-call(s32[2]{0:T(128)S(1)} %pad_add_fusion.scalars, s32[16,128]{1,0:T(8,128)S(1)} %bitcast.29, f32[16,128]{1,0:T(8,128)S(1)} %bitcast.33, bf16[256,512]{1,0:T(8,128)(2,1)S(1)} %copy-done.1, ...), custom_call_target="tpu_custom_call" | custom-call | flops 4294967296 | bytes 4194304 | tf_op jit(solution)/shard_map/take_rows/pallas_call | solution.py:265
  42.8 2.0 %collective-permute-done.6.refs_3_.refs_6_ = bf16[512,512]{1,0:T(8,128)(2,1)S(1)} collective-permute-done((bf16[512,512]{1,0:T(8,128)(2,1)S(1)}, bf16[512,512]{1,0:T(8,128)(2,1)S(1)}, u32[]{:S(2)}, u32[]{:S(2)}) %collective-permute-start.6) | collective-permute-done | bytes 524320 | tf_op jit(solution)/shard_map/ppermute | solution.py:447
  44.9 4.4 %cells.4 = (bf16[2048,512]{1,0:T(8,128)(2,1)S(1)}, bf16[160,512]{1,0:T(8,128)(2,1)S(1)}, bf16[352,512]{1,0:T(8,128)(2,1)S(1)}) custom-call(bf16[2048,512]{1,0:T(8,128)(2,1)S(1)} %get-tuple-element.99.refs_0_, bf16[512,2048]{1,0:T(8,128)(2,1)S(1)} %get-tuple-element.100.refs_1_, f32[2048,128]{1,0:T(8,128)S(1)} %get-tuple-element.101.refs_2_, ...), custom_call_target="tpu_custom_call" | custom-call | flops 1048576 | bytes 1048576 | tf_op jit(solution)/shard_map/cells/pallas_call | solution.py:376
  49.3 0.5 collective-permute-start.7
  49.8 1.6 %collective-permute-start.8 = (bf16[352,512]{1,0:T(8,128)(2,1)S(1)}, bf16[352,512]{1,0:T(8,128)(2,1)S(1)}, u32[]{:S(2)}, u32[]{:S(2)}) collective-permute-start(bf16[352,512]{1,0:T(8,128)(2,1)S(1)} %get-tuple-element.108), channel_id=1, source_target_pairs={{0,8},{8,0},{16,24},{24,16},{1,9},{9,1},{17,25},{25,17},{2,10},{10... | collective-permute-start | bytes 1081352 | tf_op jit(solution)/shard_map/ppermute | solution.py:447
  51.4 4.4 %cells.5 = (bf16[2048,512]{1,0:T(8,128)(2,1)S(1)}, f32[512,512]{1,0:T(8,128)S(1)}) custom-call(bf16[2048,512]{1,0:T(8,128)(2,1)S(1)} %get-tuple-element.99.refs_0_, bf16[512,2048]{1,0:T(8,128)(2,1)S(1)} %get-tuple-element.100.refs_1_, f32[2048,128]{1,0:T(8,128)S(1)} %get-tuple-element.101.refs_2_, bf16[512,512]{1,0:T(8,128)(2,1)S(1)} %collective-permute-done.refs_3_.refs_7_, ...), custom_call_target="tpu_custom_call" | custom-call | flops 1048576 | bytes 1048576 | tf_op jit(solution)/shard_map/cells/pallas_call | solution.py:376
  55.8 0.0 copy-start
  55.8 4.6 %cells.6 = (bf16[2048,512]{1,0:T(8,128)(2,1)S(1)}, bf16[512,512]{1,0:T(8,128)(2,1)S(1)}) custom-call(bf16[2048,512]{1,0:T(8,128)(2,1)S(1)} %get-tuple-element.99.refs_0_, bf16[512,2048]{1,0:T(8,128)(2,1)S(1)} %get-tuple-element.100.refs_1_, f32[2048,128]{1,0:T(8,128)S(1)} %get-tuple-element.101.refs_2_, ...), custom_call_target="tpu_custom_call" | custom-call | flops 1048576 | bytes 1048576 | tf_op jit(solution)/shard_map/cells/pallas_call | solution.py:376
  60.5 0.0 collective-permute-done.7
  60.5 0.4 collective-permute-start.9
  60.9 1.6 %collective-permute-start.14 = (bf16[512,512]{1,0:T(8,128)(2,1)S(1)}, bf16[512,512]{1,0:T(8,128)(2,1)S(1)}, u32[]{:S(2)}, u32[]{:S(2)}) collective-permute-start(bf16[512,512]{1,0:T(8,128)(2,1)S(1)} %get-tuple-element.118), channel_id=1, source_target_pairs={{0,8},{8,0},{16,24},{24,16},{1,9},{9,1},{17,25},{25,17},{2,10},{10... | collective-permute-start | bytes 1572872 | tf_op jit(solution)/shard_map/ppermute | solution.py:447
  62.5 0.0 copy-done
  62.5 8.9 %cells.7 = (f32[2048,512]{1,0:T(8,128)S(1)}, f32[512,512]{1,0:T(8,128)S(1)}) custom-call(bf16[2048,512]{1,0:T(8,128)(2,1)S(1)} %get-tuple-element.99.refs_0_, bf16[512,2048]{1,0:T(8,128)(2,1)S(1)} %get-tuple-element.100.refs_1_, f32[2048,128]{1,0:T(8,128)S(1)} %get-tuple-element.101.refs_2_, bf16[512,512]{1,0:T(8,128)(2,1)S(1)} %copy-done, ...), custom_call_target="tpu_custom_call" | custom-call | flops 1048576 | bytes 1048576 | tf_op jit(solution)/shard_map/cells/pallas_call | solution.py:376
  71.4 0.0 collective-permute-done.9.refs_2_
  71.4 0.0 collective-permute-done.8
  71.4 0.1 add_convert_fusion.1
  71.6 1.5 %collective-permute-start.15 = (bf16[352,512]{1,0:T(8,128)(2,1)S(1)}, bf16[352,512]{1,0:T(8,128)(2,1)S(1)}, u32[]{:S(2)}, u32[]{:S(2)}) collective-permute-start(bf16[352,512]{1,0:T(8,128)(2,1)S(1)} %add_convert_fusion.1), channel_id=1, source_target_pairs={{0,16},{8,24},{16,0},{24,8},{1,17},{9,25},{17,1},{25,9},{2,18},{10... | collective-permute-start | bytes 1081352 | tf_op jit(solution)/shard_map/ppermute | solution.py:447
  73.1 2.9 %put_rows.3 = bf16[4,256,512]{2,1,0:T(8,128)(2,1)S(1)} custom-call(s32[2]{0:T(128)S(1)} %pad_add_fusion.scalars, s32[1,2048]{1,0:T(1,128)S(1)} %bitcast.30, f32[2048,512]{1,0:T(8,128)S(1)} %get-tuple-element.114.grad_ref), custom_call_target="tpu_custom_call" | custom-call | flops 1048576 | bytes 65536 | tf_op jit(solution)/shard_map/put_rows/pallas_call | solution.py:433
  76.0 0.1 collective-permute-start.10
  76.0 3.9 %put_rows.4 = f32[3,256,512]{2,1,0:T(8,128)S(1)} custom-call(s32[2]{0:T(128)S(1)} %pad_add_fusion.scalars, s32[1,2048]{1,0:T(1,128)S(1)} %bitcast.31, f32[2048,512]{1,0:T(8,128)S(1)} %get-tuple-element.114.grad_ref), custom_call_target="tpu_custom_call" | custom-call | flops 17179869184 | bytes 65536 | tf_op jit(solution)/shard_map/put_rows/pallas_call | solution.py:433
  80.0 0.0 collective-permute-done.10
  80.0 0.3 add_convert_fusion
  80.3 0.1 slice_bitcast_fusion.1
  80.3 1.6 %collective-permute-start.11 = (bf16[256,512]{1,0:T(8,128)(2,1)S(1)}, bf16[256,512]{1,0:T(8,128)(2,1)S(1)}, u32[]{:S(2)}, u32[]{:S(2)}) collective-permute-start(bf16[256,512]{1,0:T(8,128)(2,1)S(1)} %get-tuple-element.120), channel_id=1, source_target_pairs={{0,4},{1,5},{2,6},{3,7},{4,0},{5,1},{6,2},{7,3},{8,12},{9,13},{10,... | collective-permute-start | bytes 786440 | tf_op jit(solution)/shard_map/ppermute | solution.py:447
  81.9 1.4 %collective-permute-start.12 = (bf16[256,512]{1,0:T(8,128)(2,1)S(1)}, bf16[256,512]{1,0:T(8,128)(2,1)S(1)}, u32[]{:S(2)}, u32[]{:S(2)}) collective-permute-start(bf16[256,512]{1,0:T(8,128)(2,1)S(1)} %get-tuple-element.121), channel_id=1, source_target_pairs={{0,6},{1,7},{2,4},{3,5},{4,2},{5,3},{6,0},{7,1},{8,14},{9,15},{10,... | collective-permute-start | bytes 786440 | tf_op jit(solution)/shard_map/ppermute | solution.py:447
  83.4 0.5 collective-permute-start.13
  83.9 1.8 %put_rows.5 = f32[1,256,512]{2,1,0:T(8,128)S(1)} custom-call(s32[2]{0:T(128)S(1)} %pad_add_fusion.scalars, s32[1,2048]{1,0:T(1,128)S(1)} %bitcast.32, f32[2048,512]{1,0:T(8,128)S(1)} %get-tuple-element.114.grad_ref), custom_call_target="tpu_custom_call" | custom-call | flops 1048576 | bytes 65536 | tf_op jit(solution)/shard_map/put_rows/pallas_call | solution.py:433
  85.7 0.0 collective-permute-done.14.refs_1_
  85.7 3.5 %collective-permute-done.15.refs_3_ = bf16[352,512]{1,0:T(8,128)(2,1)S(1)} collective-permute-done((bf16[352,512]{1,0:T(8,128)(2,1)S(1)}, bf16[352,512]{1,0:T(8,128)(2,1)S(1)}, u32[]{:S(2)}, u32[]{:S(2)}) %collective-permute-start.15) | collective-permute-done | bytes 360480 | tf_op jit(solution)/shard_map/ppermute | solution.py:447
  89.2 1.3 %finish.1 = f32[512,512]{1,0:T(8,128)} custom-call(f32[512,512]{1,0:T(8,128)S(1)} %get-tuple-element.117.refs_0_, bf16[512,512]{1,0:T(8,128)(2,1)S(1)} %collective-permute-done.14.refs_1_, bf16[160,512]{1,0:T(8,128)(2,1)S(1)} %collective-permute-done.9.refs_2_, bf16[352,512]{1,0:T(8,128)(2,1)S(1)} %collective-permute-done.15.refs_3_), custom_call_target="tpu_custom_call" | custom-call | flops 262144 | bytes 16384 | tf_op jit(solution)/shard_map/finish/pallas_call | solution.py:400
  90.5 4.2 %collective-permute-done.11 = bf16[256,512]{1,0:T(8,128)(2,1)S(1)} collective-permute-done((bf16[256,512]{1,0:T(8,128)(2,1)S(1)}, bf16[256,512]{1,0:T(8,128)(2,1)S(1)}, u32[]{:S(2)}, u32[]{:S(2)}) %collective-permute-start.11) | collective-permute-done | bytes 262176 | tf_op jit(solution)/shard_map/ppermute | solution.py:447
  94.7 0.0 collective-permute-done.12
  94.7 1.2 %collective-permute-done.13 = bf16[256,512]{1,0:T(8,128)(2,1)S(1)} collective-permute-done((bf16[256,512]{1,0:T(8,128)(2,1)S(1)}, bf16[256,512]{1,0:T(8,128)(2,1)S(1)}, u32[]{:S(2)}, u32[]{:S(2)}) %collective-permute-start.13) | collective-permute-done | bytes 262176 | tf_op jit(solution)/shard_map/ppermute | solution.py:447
  96.0 1.0 fusion.2
  (1 shorter events, 0.0 us)
Async XLA Ops:
  0.6 29.6 %collective-permute-start = (bf16[512,512]{1,0:T(8,128)(2,1)}, bf16[512,512]{1,0:T(8,128)(2,1)S(1)}, u32[]{:S(2)}, u32[]{:S(2)}) collective-permute-start(bf16[512,512]{1,0:T(8,128)(2,1)} %refs_3_.1), channel_id=1, source_target_pairs={{0,16},{8,24},{16,0},{24,8},{1,17},{9,25},{17,1},{25,9},{2,18},{10... | collective-permute-start | bytes 1572872 | tf_op jit(solution)/shard_map/ppermute | solution.py:447
  4.7 25.5 %collective-permute-start.1 = (bf16[512,512]{1,0:T(8,128)(2,1)}, bf16[512,512]{1,0:T(8,128)(2,1)S(1)}, u32[]{:S(2)}, u32[]{:S(2)}) collective-permute-start(bf16[512,512]{1,0:T(8,128)(2,1)} %refs_3_.1), channel_id=1, source_target_pairs={{0,8},{8,0},{16,24},{24,16},{1,9},{9,1},{17,25},{25,17},{2,10},{10... | collective-permute-start | bytes 1572872 | tf_op jit(solution)/shard_map/ppermute | solution.py:447
  6.4 9.1 %copy-start.1 = (bf16[256,512]{1,0:T(8,128)(2,1)S(1)}, bf16[256,512]{1,0:T(8,128)(2,1)}, u32[]{:S(2)}) copy-start(bf16[256,512]{1,0:T(8,128)(2,1)} %refs_0_.1) | copy-start | bytes 786436
  15.5 14.7 %collective-permute-start.4 = (bf16[256,512]{1,0:T(8,128)(2,1)S(1)}, bf16[256,512]{1,0:T(8,128)(2,1)S(1)}, u32[]{:S(2)}, u32[]{:S(2)}) collective-permute-start(bf16[256,512]{1,0:T(8,128)(2,1)S(1)} %copy-done.1), channel_id=1, source_target_pairs={{0,6},{1,7},{2,4},{3,5},{4,2},{5,3},{6,0},{7,1},{8,14},{9,15},{10,... | collective-permute-start | bytes 786440 | tf_op jit(solution)/shard_map/ppermute | solution.py:447
  18.0 12.2 %collective-permute-start.3 = (bf16[256,512]{1,0:T(8,128)(2,1)S(1)}, bf16[256,512]{1,0:T(8,128)(2,1)S(1)}, u32[]{:S(2)}, u32[]{:S(2)}) collective-permute-start(bf16[256,512]{1,0:T(8,128)(2,1)S(1)} %copy-done.1), channel_id=1, source_target_pairs={{0,4},{1,5},{2,6},{3,7},{4,0},{5,1},{6,2},{7,3},{8,12},{9,13},{10,... | collective-permute-start | bytes 786440 | tf_op jit(solution)/shard_map/ppermute | solution.py:447
  18.5 11.7 %collective-permute-start.2 = (bf16[256,512]{1,0:T(8,128)(2,1)S(1)}, bf16[256,512]{1,0:T(8,128)(2,1)S(1)}, u32[]{:S(2)}, u32[]{:S(2)}) collective-permute-start(bf16[256,512]{1,0:T(8,128)(2,1)S(1)} %copy-done.1), channel_id=1, source_target_pairs={{0,2},{1,3},{2,0},{3,1},{4,6},{5,7},{6,4},{7,5},{8,10},{9,11},{10,... | collective-permute-start | bytes 786440 | tf_op jit(solution)/shard_map/ppermute | solution.py:447
  30.4 7.1 %copy-start.2 = (s32[2048]{0:T(1024)S(1)}, s32[2048]{0:T(1024)}, u32[]{:S(2)}) copy-start(s32[2048]{0:T(1024)} %param.10) | copy-start | bytes 24580
  30.4 7.1 %copy-start.3 = (f32[2048]{0:T(1024)S(1)}, f32[2048]{0:T(1024)}, u32[]{:S(2)}) copy-start(f32[2048]{0:T(1024)} %param.12) | copy-start | bytes 24580
  30.4 7.0 %collective-permute-start.5 = (bf16[4,256,512]{2,1,0:T(8,128)(2,1)S(1)}, bf16[4,256,512]{2,1,0:T(8,128)(2,1)S(1)}, u32[]{:S(2)}, u32[]{:S(2)}) collective-permute-start(bf16[4,256,512]{2,1,0:T(8,128)(2,1)S(1)} %pad_maximum_fusion), channel_id=1, source_target_pairs={{0,1},{1,0},{2,3},{3,2},{4,5},{5,4},{6,7},{7,6},{8,9},{9,8},{10,11... | collective-permute-start | bytes 3145736 | tf_op jit(solution)/shard_map/ppermute | solution.py:447
  30.5 14.3 %collective-permute-start.6 = (bf16[512,512]{1,0:T(8,128)(2,1)S(1)}, bf16[512,512]{1,0:T(8,128)(2,1)S(1)}, u32[]{:S(2)}, u32[]{:S(2)}) collective-permute-start(bf16[512,512]{1,0:T(8,128)(2,1)S(1)} %collective-permute-done.refs_3_.refs_7_), channel_id=1, source_target_pairs={{0,8},{8,0},{16,24},{24,16},{1,9},{9,1},{17,25},{25,17},{2,10},{10... | collective-permute-start | bytes 1572872 | tf_op jit(solution)/shard_map/ppermute | solution.py:447
  49.3 11.2 %collective-permute-start.7 = (bf16[160,512]{1,0:T(8,128)(2,1)S(1)}, bf16[160,512]{1,0:T(8,128)(2,1)S(1)}, u32[]{:S(2)}, u32[]{:S(2)}) collective-permute-start(bf16[160,512]{1,0:T(8,128)(2,1)S(1)} %get-tuple-element.93), channel_id=1, source_target_pairs={{0,8},{8,0},{16,24},{24,16},{1,9},{9,1},{17,25},{25,17},{2,10},{10... | collective-permute-start | bytes 491528 | tf_op jit(solution)/shard_map/ppermute | solution.py:447
  49.8 21.6 %collective-permute-start.8 = (bf16[352,512]{1,0:T(8,128)(2,1)S(1)}, bf16[352,512]{1,0:T(8,128)(2,1)S(1)}, u32[]{:S(2)}, u32[]{:S(2)}) collective-permute-start(bf16[352,512]{1,0:T(8,128)(2,1)S(1)} %get-tuple-element.108), channel_id=1, source_target_pairs={{0,8},{8,0},{16,24},{24,16},{1,9},{9,1},{17,25},{25,17},{2,10},{10... | collective-permute-start | bytes 1081352 | tf_op jit(solution)/shard_map/ppermute | solution.py:447
  55.8 6.7 %copy-start = (bf16[512,512]{1,0:T(8,128)(2,1)S(1)}, bf16[512,512]{1,0:T(8,128)(2,1)}, u32[]{:S(2)}) copy-start(bf16[512,512]{1,0:T(8,128)(2,1)} %refs_3_.1) | copy-start | bytes 1572868
  60.5 10.9 %collective-permute-start.9 = (bf16[160,512]{1,0:T(8,128)(2,1)S(1)}, bf16[160,512]{1,0:T(8,128)(2,1)S(1)}, u32[]{:S(2)}, u32[]{:S(2)}) collective-permute-start(bf16[160,512]{1,0:T(8,128)(2,1)S(1)} %add_convert_fusion.2), channel_id=1, source_target_pairs={{0,16},{8,24},{16,0},{24,8},{1,17},{9,25},{17,1},{25,9},{2,18},{10... | collective-permute-start | bytes 491528 | tf_op jit(solution)/shard_map/ppermute | solution.py:447
  60.9 24.8 %collective-permute-start.14 = (bf16[512,512]{1,0:T(8,128)(2,1)S(1)}, bf16[512,512]{1,0:T(8,128)(2,1)S(1)}, u32[]{:S(2)}, u32[]{:S(2)}) collective-permute-start(bf16[512,512]{1,0:T(8,128)(2,1)S(1)} %get-tuple-element.118), channel_id=1, source_target_pairs={{0,8},{8,0},{16,24},{24,16},{1,9},{9,1},{17,25},{25,17},{2,10},{10... | collective-permute-start | bytes 1572872 | tf_op jit(solution)/shard_map/ppermute | solution.py:447
  71.6 17.6 %collective-permute-start.15 = (bf16[352,512]{1,0:T(8,128)(2,1)S(1)}, bf16[352,512]{1,0:T(8,128)(2,1)S(1)}, u32[]{:S(2)}, u32[]{:S(2)}) collective-permute-start(bf16[352,512]{1,0:T(8,128)(2,1)S(1)} %add_convert_fusion.1), channel_id=1, source_target_pairs={{0,16},{8,24},{16,0},{24,8},{1,17},{9,25},{17,1},{25,9},{2,18},{10... | collective-permute-start | bytes 1081352 | tf_op jit(solution)/shard_map/ppermute | solution.py:447
  76.0 4.0 %collective-permute-start.10 = (bf16[4,256,512]{2,1,0:T(8,128)(2,1)S(1)}, bf16[4,256,512]{2,1,0:T(8,128)(2,1)S(1)}, u32[]{:S(2)}, u32[]{:S(2)}) collective-permute-start(bf16[4,256,512]{2,1,0:T(8,128)(2,1)S(1)} %put_rows.3), channel_id=1, source_target_pairs={{0,1},{1,0},{2,3},{3,2},{4,5},{5,4},{6,7},{7,6},{8,9},{9,8},{10,11... | collective-permute-start | bytes 3145736 | tf_op jit(solution)/shard_map/ppermute | solution.py:447
  80.3 14.4 %collective-permute-start.11 = (bf16[256,512]{1,0:T(8,128)(2,1)S(1)}, bf16[256,512]{1,0:T(8,128)(2,1)S(1)}, u32[]{:S(2)}, u32[]{:S(2)}) collective-permute-start(bf16[256,512]{1,0:T(8,128)(2,1)S(1)} %get-tuple-element.120), channel_id=1, source_target_pairs={{0,4},{1,5},{2,6},{3,7},{4,0},{5,1},{6,2},{7,3},{8,12},{9,13},{10,... | collective-permute-start | bytes 786440 | tf_op jit(solution)/shard_map/ppermute | solution.py:447
  81.9 12.8 %collective-permute-start.12 = (bf16[256,512]{1,0:T(8,128)(2,1)S(1)}, bf16[256,512]{1,0:T(8,128)(2,1)S(1)}, u32[]{:S(2)}, u32[]{:S(2)}) collective-permute-start(bf16[256,512]{1,0:T(8,128)(2,1)S(1)} %get-tuple-element.121), channel_id=1, source_target_pairs={{0,6},{1,7},{2,4},{3,5},{4,2},{5,3},{6,0},{7,1},{8,14},{9,15},{10,... | collective-permute-start | bytes 786440 | tf_op jit(solution)/shard_map/ppermute | solution.py:447
  83.4 12.6 %collective-permute-start.13 = (bf16[256,512]{1,0:T(8,128)(2,1)S(1)}, bf16[256,512]{1,0:T(8,128)(2,1)S(1)}, u32[]{:S(2)}, u32[]{:S(2)}) collective-permute-start(bf16[256,512]{1,0:T(8,128)(2,1)S(1)} %get-tuple-element.122), channel_id=1, source_target_pairs={{0,2},{1,3},{2,0},{3,1},{4,6},{5,7},{6,4},{7,5},{8,10},{9,11},{10,... | collective-permute-start | bytes 786440 | tf_op jit(solution)/shard_map/ppermute | solution.py:447

commit v10 on v9

--- a/solution.py
+++ b/solution.py
@@ -226,7 +226,7 @@
         + [jax.ShapeDtypeStruct((values.shape[0] - 16, width), F32)] * parts,
         scratch_shapes=[pltpu.VMEM((parts, cols, width), BF16)],
         compiler_params=params(24),
-        cost_estimate=cost(rows * width, rows * width),
+        cost_estimate=cost((16384 if parts == 1 else 1) * rows * width, rows * width),
         name="order_next",
     )(scalars, shifted, columns, values)
 
@@ -509,7 +509,7 @@
     grad, away = together((grad, away))
     both = ordered(grad, (2, 4, 6), side, True) + core[1:].astype(F32)
     sends = [both[at].astype(BF16) for at in range(3)]
-    got = [swap(sends[at], "col", bit) for at, bit in ((1, 4), (2, 6), (0, 2))]
+    got = [swap(sends[at], "col", bit) for at, bit in ((2, 6), (1, 4), (0, 2))]
     grad, sends = together((grad, sends))
     home = ordered(grad, (0,), side, True)
     home, term_own = together((home, term_own))

time: 97.1 us -> 96 us (0.989)
  waiting for transfers between devices: 11 us -> 9.33 us
    ppermute x16, waiting for transfers between devices: 11 us -> 9.33 us  [swap(): return lax.ppermute(value, axis, pairs)]
  transfers between devices with their start and end apart: 16 -> 16, of which waited for: 4 -> 5; matrix products, arithmetic and copies ran while one was open for 1% -> 1% of each run, Pallas kernels for 62% -> 63%
where the time goes in v10:
time: 96 us; the launch traced here: 95.8 us
  Pallas kernels  64.4 us (67%)
  starting transfers between devices  19.5 us (20%)
  waiting for transfers between devices  9.33 us (10%)
  other arithmetic  1.6 us (2%)
    pallas_call x4, Pallas kernels, cells(): pl.pallas_call(functools.partial(cells_kernel, len(others), pieces), in_s...  22.4 us
    ppermute x16, starting transfers between devices, swap(): return lax.ppermute(value, axis, pairs)  19.5 us
    pallas_call x2, Pallas kernels, order_next(): pl.pallas_call(functools.partial(order_next_kernel, offsets), in_specs=[S...  17.6 us
    ppermute x16, waiting for transfers between devices, swap(): return lax.ppermute(value, axis, pairs)  9.33 us
    pallas_call x1, Pallas kernels, order_first(): pl.pallas_call(functools.partial(order_first_kernel, offsets), in_specs=[...  9.09 us
    pallas_call x3, Pallas kernels, put_rows(): pl.pallas_call(functools.partial(put_kernel, offsets, exact), in_specs=[S...  8.61 us
    pallas_call x1, Pallas kernels, take_rows(): pl.pallas_call(take_kernel, in_specs=[SCALARS] + [WHOLE] * 7, out_specs=[...  5.32 us
  transfers between devices with their start and end apart: 16, of which 5 were waited for; matrix products, arithmetic and copies ran while one was open for 1% of the time, Pallas kernels for 63%

profile of v10, /device:TPU:0, one launch (start us, length us, event | category | flops | bytes accessed | tf_op | source)
XLA Modules:
  0.0 95.8 jit_solution(7372287279169174806)
XLA Ops:
  0.6 4.1 %collective-permute-start = (bf16[512,512]{1,0:T(8,128)(2,1)}, bf16[512,512]{1,0:T(8,128)(2,1)S(1)}, u32[]{:S(2)}, u32[]{:S(2)}) collective-permute-start(bf16[512,512]{1,0:T(8,128)(2,1)} %refs_3_.1), channel_id=1, source_target_pairs={{0,16},{8,24},{16,0},{24,8},{1,17},{9,25},{17,1},{25,9},{2,18},{10... | collective-permute-start | bytes 1572872 | tf_op jit(solution)/shard_map/ppermute | solution.py:447
  4.7 1.6 %collective-permute-start.1 = (bf16[512,512]{1,0:T(8,128)(2,1)}, bf16[512,512]{1,0:T(8,128)(2,1)S(1)}, u32[]{:S(2)}, u32[]{:S(2)}) collective-permute-start(bf16[512,512]{1,0:T(8,128)(2,1)} %refs_3_.1), channel_id=1, source_target_pairs={{0,8},{8,0},{16,24},{24,16},{1,9},{9,1},{17,25},{25,17},{2,10},{10... | collective-permute-start | bytes 1572872 | tf_op jit(solution)/shard_map/ppermute | solution.py:447
  6.3 0.1 pad_add_fusion.scalars
  6.4 0.0 copy-start.1
  6.4 9.1 %order_first.1 = (bf16[2048,512]{1,0:T(8,128)(2,1)S(1)}, f32[16,512]{1,0:T(8,128)S(1)}, bf16[2048,2048]{1,0:T(8,128)(2,1)S(1)}, f32[128,128]{1,0:T(8,128)S(1)}, f32[32,2048]{1,0:T(8,128)S(1)}) custom-call(s32[2]{0:T(128)S(1)} %pad_add_fusion.scalars, s32[16,128]{1,0:T(8,128)} %bitcast.34, s32[8,8]{1,0:T(8,128)} %mask_hbm.1, f32[1,2048]{1,0:T(1,128)} %bitcast.35, ...), custom_call_target="tpu_custom_call" | custom-call | flops 4294967296 | bytes 16777216 | tf_op jit(solution)/shard_map/order_first/pallas_call | solution.py:173
  15.5 0.0 copy-done.1
  15.5 2.5 %collective-permute-start.4 = (bf16[256,512]{1,0:T(8,128)(2,1)S(1)}, bf16[256,512]{1,0:T(8,128)(2,1)S(1)}, u32[]{:S(2)}, u32[]{:S(2)}) collective-permute-start(bf16[256,512]{1,0:T(8,128)(2,1)S(1)} %copy-done.1), channel_id=1, source_target_pairs={{0,6},{1,7},{2,4},{3,5},{4,2},{5,3},{6,0},{7,1},{8,14},{9,15},{10,... | collective-permute-start | bytes 786440 | tf_op jit(solution)/shard_map/ppermute | solution.py:447
  18.0 0.5 collective-permute-start.3
  18.5 0.5 collective-permute-start.2
  19.0 11.2 %order_next.2 = (bf16[2048,512]{1,0:T(8,128)(2,1)S(1)}, bf16[2048,512]{1,0:T(8,128)(2,1)S(1)}, f32[16,512]{1,0:T(8,128)S(1)}, f32[16,512]{1,0:T(8,128)S(1)}) custom-call(s32[2]{0:T(128)S(1)} %pad_add_fusion.scalars, bf16[2048,2048]{1,0:T(8,128)(2,1)S(1)} %get-tuple-element.67.shifted_ref, f32[128,128]{1,0:T(8,128)S(1)} %get-tuple-element.64.columns_ref, ...), custom_call_target="tpu_custom_call" | custom-call | flops 1048576 | bytes 1048576 | tf_op jit(solution)/shard_map/order_next/pallas_call | solution.py:221
  30.2 0.0 collective-permute-done.4.refs_3_
  30.2 0.0 collective-permute-done.3.refs_2_
  30.2 0.0 collective-permute-done.2.refs_1_
  30.3 0.0 collective-permute-done.refs_3_.refs_7_
  30.3 0.0 collective-permute-done.1.refs_3_.refs_8_
  30.3 0.5 collective-permute-start.6
  30.8 0.1 pad_maximum_fusion
  30.9 0.0 copy-start.2
  30.9 0.0 copy-start.3
  31.0 0.1 collective-permute-start.5
  31.0 6.4 %order_next.3 = (bf16[2048,512]{1,0:T(8,128)(2,1)S(1)}, f32[16,512]{1,0:T(8,128)S(1)}) custom-call(s32[2]{0:T(128)S(1)} %pad_add_fusion.scalars, bf16[2048,2048]{1,0:T(8,128)(2,1)S(1)} %get-tuple-element.67.shifted_ref, f32[128,128]{1,0:T(8,128)S(1)} %get-tuple-element.64.columns_ref, f32[32,2048]{1,0:T(8,128)S(1)} %get-tuple-element.65.values_ref), custom_call_target="tpu_custom_call" | custom-call | flops 17179869184 | bytes 1048576 | tf_op jit(solution)/shard_map/order_next/pallas_call | solution.py:221
  37.5 0.0 collective-permute-done.5.refs_4_
  37.5 0.0 copy-done.2
  37.5 0.0 copy-done.3
  37.5 5.3 %take_rows.1 = (bf16[2048,512]{1,0:T(8,128)(2,1)S(1)}, bf16[512,2048]{1,0:T(8,128)(2,1)S(1)}, f32[2048,128]{1,0:T(8,128)S(1)}) custom-call(s32[2]{0:T(128)S(1)} %pad_add_fusion.scalars, s32[16,128]{1,0:T(8,128)S(1)} %bitcast.29, f32[16,128]{1,0:T(8,128)S(1)} %bitcast.33, bf16[256,512]{1,0:T(8,128)(2,1)S(1)} %copy-done.1, ...), custom_call_target="tpu_custom_call" | custom-call | flops 4294967296 | bytes 4194304 | tf_op jit(solution)/shard_map/take_rows/pallas_call | solution.py:265
  42.8 0.6 collective-permute-done.6.refs_3_.refs_6_
  43.5 4.4 %cells.4 = (bf16[2048,512]{1,0:T(8,128)(2,1)S(1)}, bf16[160,512]{1,0:T(8,128)(2,1)S(1)}, bf16[352,512]{1,0:T(8,128)(2,1)S(1)}) custom-call(bf16[2048,512]{1,0:T(8,128)(2,1)S(1)} %get-tuple-element.99.refs_0_, bf16[512,2048]{1,0:T(8,128)(2,1)S(1)} %get-tuple-element.100.refs_1_, f32[2048,128]{1,0:T(8,128)S(1)} %get-tuple-element.101.refs_2_, ...), custom_call_target="tpu_custom_call" | custom-call | flops 1048576 | bytes 1048576 | tf_op jit(solution)/shard_map/cells/pallas_call | solution.py:376
  47.9 1.0 %collective-permute-start.7 = (bf16[160,512]{1,0:T(8,128)(2,1)S(1)}, bf16[160,512]{1,0:T(8,128)(2,1)S(1)}, u32[]{:S(2)}, u32[]{:S(2)}) collective-permute-start(bf16[160,512]{1,0:T(8,128)(2,1)S(1)} %get-tuple-element.93), channel_id=1, source_target_pairs={{0,8},{8,0},{16,24},{24,16},{1,9},{9,1},{17,25},{25,17},{2,10},{10... | collective-permute-start | bytes 491528 | tf_op jit(solution)/shard_map/ppermute | solution.py:447
  48.9 1.1 %collective-permute-start.8 = (bf16[352,512]{1,0:T(8,128)(2,1)S(1)}, bf16[352,512]{1,0:T(8,128)(2,1)S(1)}, u32[]{:S(2)}, u32[]{:S(2)}) collective-permute-start(bf16[352,512]{1,0:T(8,128)(2,1)S(1)} %get-tuple-element.108), channel_id=1, source_target_pairs={{0,8},{8,0},{16,24},{24,16},{1,9},{9,1},{17,25},{25,17},{2,10},{10... | collective-permute-start | bytes 1081352 | tf_op jit(solution)/shard_map/ppermute | solution.py:447
  50.0 4.4 %cells.5 = (bf16[2048,512]{1,0:T(8,128)(2,1)S(1)}, f32[512,512]{1,0:T(8,128)S(1)}) custom-call(bf16[2048,512]{1,0:T(8,128)(2,1)S(1)} %get-tuple-element.99.refs_0_, bf16[512,2048]{1,0:T(8,128)(2,1)S(1)} %get-tuple-element.100.refs_1_, f32[2048,128]{1,0:T(8,128)S(1)} %get-tuple-element.101.refs_2_, bf16[512,512]{1,0:T(8,128)(2,1)S(1)} %collective-permute-done.refs_3_.refs_7_, ...), custom_call_target="tpu_custom_call" | custom-call | flops 1048576 | bytes 1048576 | tf_op jit(solution)/shard_map/cells/pallas_call | solution.py:376
  54.4 0.0 copy-start
  54.4 4.6 %cells.6 = (bf16[2048,512]{1,0:T(8,128)(2,1)S(1)}, bf16[512,512]{1,0:T(8,128)(2,1)S(1)}) custom-call(bf16[2048,512]{1,0:T(8,128)(2,1)S(1)} %get-tuple-element.99.refs_0_, bf16[512,2048]{1,0:T(8,128)(2,1)S(1)} %get-tuple-element.100.refs_1_, f32[2048,128]{1,0:T(8,128)S(1)} %get-tuple-element.101.refs_2_, ...), custom_call_target="tpu_custom_call" | custom-call | flops 1048576 | bytes 1048576 | tf_op jit(solution)/shard_map/cells/pallas_call | solution.py:376
  59.1 0.0 collective-permute-done.7
  59.1 0.9 collective-permute-start.9
  60.0 1.7 %collective-permute-start.14 = (bf16[512,512]{1,0:T(8,128)(2,1)S(1)}, bf16[512,512]{1,0:T(8,128)(2,1)S(1)}, u32[]{:S(2)}, u32[]{:S(2)}) collective-permute-start(bf16[512,512]{1,0:T(8,128)(2,1)S(1)} %get-tuple-element.118), channel_id=1, source_target_pairs={{0,8},{8,0},{16,24},{24,16},{1,9},{9,1},{17,25},{25,17},{2,10},{10... | collective-permute-start | bytes 1572872 | tf_op jit(solution)/shard_map/ppermute | solution.py:447
  61.8 0.0 copy-done
  61.8 8.9 %cells.7 = (f32[2048,512]{1,0:T(8,128)S(1)}, f32[512,512]{1,0:T(8,128)S(1)}) custom-call(bf16[2048,512]{1,0:T(8,128)(2,1)S(1)} %get-tuple-element.99.refs_0_, bf16[512,2048]{1,0:T(8,128)(2,1)S(1)} %get-tuple-element.100.refs_1_, f32[2048,128]{1,0:T(8,128)S(1)} %get-tuple-element.101.refs_2_, bf16[512,512]{1,0:T(8,128)(2,1)S(1)} %copy-done, ...), custom_call_target="tpu_custom_call" | custom-call | flops 1048576 | bytes 1048576 | tf_op jit(solution)/shard_map/cells/pallas_call | solution.py:376
  70.7 0.0 collective-permute-done.9.refs_2_
  70.7 0.0 collective-permute-done.8
  70.7 0.1 add_convert_fusion.1
  70.8 1.4 %collective-permute-start.15 = (bf16[352,512]{1,0:T(8,128)(2,1)S(1)}, bf16[352,512]{1,0:T(8,128)(2,1)S(1)}, u32[]{:S(2)}, u32[]{:S(2)}) collective-permute-start(bf16[352,512]{1,0:T(8,128)(2,1)S(1)} %add_convert_fusion.1), channel_id=1, source_target_pairs={{0,16},{8,24},{16,0},{24,8},{1,17},{9,25},{17,1},{25,9},{2,18},{10... | collective-permute-start | bytes 1081352 | tf_op jit(solution)/shard_map/ppermute | solution.py:447
  72.2 2.9 %put_rows.3 = bf16[4,256,512]{2,1,0:T(8,128)(2,1)S(1)} custom-call(s32[2]{0:T(128)S(1)} %pad_add_fusion.scalars, s32[1,2048]{1,0:T(1,128)S(1)} %bitcast.30, f32[2048,512]{1,0:T(8,128)S(1)} %get-tuple-element.114.grad_ref), custom_call_target="tpu_custom_call" | custom-call | flops 1048576 | bytes 65536 | tf_op jit(solution)/shard_map/put_rows/pallas_call | solution.py:433
  75.1 0.1 collective-permute-start.10
  75.1 3.9 %put_rows.4 = f32[3,256,512]{2,1,0:T(8,128)S(1)} custom-call(s32[2]{0:T(128)S(1)} %pad_add_fusion.scalars, s32[1,2048]{1,0:T(1,128)S(1)} %bitcast.31, f32[2048,512]{1,0:T(8,128)S(1)} %get-tuple-element.114.grad_ref), custom_call_target="tpu_custom_call" | custom-call | flops 17179869184 | bytes 65536 | tf_op jit(solution)/shard_map/put_rows/pallas_call | solution.py:433
  79.1 0.0 collective-permute-done.10
  79.1 0.3 add_convert_fusion
  79.4 0.1 slice_bitcast_fusion
  79.5 2.5 %collective-permute-start.11 = (bf16[256,512]{1,0:T(8,128)(2,1)S(1)}, bf16[256,512]{1,0:T(8,128)(2,1)S(1)}, u32[]{:S(2)}, u32[]{:S(2)}) collective-permute-start(bf16[256,512]{1,0:T(8,128)(2,1)S(1)} %get-tuple-element.120), channel_id=1, source_target_pairs={{0,6},{1,7},{2,4},{3,5},{4,2},{5,3},{6,0},{7,1},{8,14},{9,15},{10,... | collective-permute-start | bytes 786440 | tf_op jit(solution)/shard_map/ppermute | solution.py:447
  82.0 0.5 collective-permute-start.12
  82.5 0.5 collective-permute-start.13
  83.0 1.8 %put_rows.5 = f32[1,256,512]{2,1,0:T(8,128)S(1)} custom-call(s32[2]{0:T(128)S(1)} %pad_add_fusion.scalars, s32[1,2048]{1,0:T(1,128)S(1)} %bitcast.32, f32[2048,512]{1,0:T(8,128)S(1)} %get-tuple-element.114.grad_ref), custom_call_target="tpu_custom_call" | custom-call | flops 1048576 | bytes 65536 | tf_op jit(solution)/shard_map/put_rows/pallas_call | solution.py:433
  84.8 0.0 collective-permute-done.14.refs_1_
  84.8 3.2 %collective-permute-done.15.refs_3_ = bf16[352,512]{1,0:T(8,128)(2,1)S(1)} collective-permute-done((bf16[352,512]{1,0:T(8,128)(2,1)S(1)}, bf16[352,512]{1,0:T(8,128)(2,1)S(1)}, u32[]{:S(2)}, u32[]{:S(2)}) %collective-permute-start.15) | collective-permute-done | bytes 360480 | tf_op jit(solution)/shard_map/ppermute | solution.py:447
  88.0 1.3 %finish.1 = f32[512,512]{1,0:T(8,128)} custom-call(f32[512,512]{1,0:T(8,128)S(1)} %get-tuple-element.117.refs_0_, bf16[512,512]{1,0:T(8,128)(2,1)S(1)} %collective-permute-done.14.refs_1_, bf16[160,512]{1,0:T(8,128)(2,1)S(1)} %collective-permute-done.9.refs_2_, bf16[352,512]{1,0:T(8,128)(2,1)S(1)} %collective-permute-done.15.refs_3_), custom_call_target="tpu_custom_call" | custom-call | flops 262144 | bytes 16384 | tf_op jit(solution)/shard_map/finish/pallas_call | solution.py:400
  89.3 0.2 collective-permute-done.11
  89.6 5.2 %collective-permute-done.12 = bf16[256,512]{1,0:T(8,128)(2,1)S(1)} collective-permute-done((bf16[256,512]{1,0:T(8,128)(2,1)S(1)}, bf16[256,512]{1,0:T(8,128)(2,1)S(1)}, u32[]{:S(2)}, u32[]{:S(2)}) %collective-permute-start.12) | collective-permute-done | bytes 262176 | tf_op jit(solution)/shard_map/ppermute | solution.py:447
  94.7 0.1 collective-permute-done.13
  94.8 1.0 %fusion.2 = f32[256,512]{1,0:T(8,128)} fusion(bf16[256,512]{1,0:T(8,128)(2,1)S(1)} %collective-permute-done.13, bf16[256,512]{1,0:T(8,128)(2,1)S(1)} %collective-permute-done.12, bf16[256,512]{1,0:T(8,128)(2,1)S(1)} %collective-permute-done.11, f32[1,256,512]{2,1,0:T(8,128)S(1)} %put_rows.5, bf16[4,256,512]{2,1,0:T(8,128)(2,1)S(1)} %collective-permute-done.10), kind=kLoop, calls=%fused_computation.6 | loop fusion | flops 1179648 | bytes 2097152 | tf_op jit(solution)/shard_map/mul | solution.py:521
  (1 shorter events, 0.0 us)
Async XLA Ops:
  0.6 29.6 %collective-permute-start = (bf16[512,512]{1,0:T(8,128)(2,1)}, bf16[512,512]{1,0:T(8,128)(2,1)S(1)}, u32[]{:S(2)}, u32[]{:S(2)}) collective-permute-start(bf16[512,512]{1,0:T(8,128)(2,1)} %refs_3_.1), channel_id=1, source_target_pairs={{0,16},{8,24},{16,0},{24,8},{1,17},{9,25},{17,1},{25,9},{2,18},{10... | collective-permute-start | bytes 1572872 | tf_op jit(solution)/shard_map/ppermute | solution.py:447
  4.7 25.5 %collective-permute-start.1 = (bf16[512,512]{1,0:T(8,128)(2,1)}, bf16[512,512]{1,0:T(8,128)(2,1)S(1)}, u32[]{:S(2)}, u32[]{:S(2)}) collective-permute-start(bf16[512,512]{1,0:T(8,128)(2,1)} %refs_3_.1), channel_id=1, source_target_pairs={{0,8},{8,0},{16,24},{24,16},{1,9},{9,1},{17,25},{25,17},{2,10},{10... | collective-permute-start | bytes 1572872 | tf_op jit(solution)/shard_map/ppermute | solution.py:447
  6.4 9.1 %copy-start.1 = (bf16[256,512]{1,0:T(8,128)(2,1)S(1)}, bf16[256,512]{1,0:T(8,128)(2,1)}, u32[]{:S(2)}) copy-start(bf16[256,512]{1,0:T(8,128)(2,1)} %refs_0_.1) | copy-start | bytes 786436
  15.5 14.7 %collective-permute-start.4 = (bf16[256,512]{1,0:T(8,128)(2,1)S(1)}, bf16[256,512]{1,0:T(8,128)(2,1)S(1)}, u32[]{:S(2)}, u32[]{:S(2)}) collective-permute-start(bf16[256,512]{1,0:T(8,128)(2,1)S(1)} %copy-done.1), channel_id=1, source_target_pairs={{0,6},{1,7},{2,4},{3,5},{4,2},{5,3},{6,0},{7,1},{8,14},{9,15},{10,... | collective-permute-start | bytes 786440 | tf_op jit(solution)/shard_map/ppermute | solution.py:447
  18.0 12.2 %collective-permute-start.3 = (bf16[256,512]{1,0:T(8,128)(2,1)S(1)}, bf16[256,512]{1,0:T(8,128)(2,1)S(1)}, u32[]{:S(2)}, u32[]{:S(2)}) collective-permute-start(bf16[256,512]{1,0:T(8,128)(2,1)S(1)} %copy-done.1), channel_id=1, source_target_pairs={{0,4},{1,5},{2,6},{3,7},{4,0},{5,1},{6,2},{7,3},{8,12},{9,13},{10,... | collective-permute-start | bytes 786440 | tf_op jit(solution)/shard_map/ppermute | solution.py:447
  18.5 11.7 %collective-permute-start.2 = (bf16[256,512]{1,0:T(8,128)(2,1)S(1)}, bf16[256,512]{1,0:T(8,128)(2,1)S(1)}, u32[]{:S(2)}, u32[]{:S(2)}) collective-permute-start(bf16[256,512]{1,0:T(8,128)(2,1)S(1)} %copy-done.1), channel_id=1, source_target_pairs={{0,2},{1,3},{2,0},{3,1},{4,6},{5,7},{6,4},{7,5},{8,10},{9,11},{10,... | collective-permute-start | bytes 786440 | tf_op jit(solution)/shard_map/ppermute | solution.py:447
  30.3 13.2 %collective-permute-start.6 = (bf16[512,512]{1,0:T(8,128)(2,1)S(1)}, bf16[512,512]{1,0:T(8,128)(2,1)S(1)}, u32[]{:S(2)}, u32[]{:S(2)}) collective-permute-start(bf16[512,512]{1,0:T(8,128)(2,1)S(1)} %collective-permute-done.refs_3_.refs_7_), channel_id=1, source_target_pairs={{0,8},{8,0},{16,24},{24,16},{1,9},{9,1},{17,25},{25,17},{2,10},{10... | collective-permute-start | bytes 1572872 | tf_op jit(solution)/shard_map/ppermute | solution.py:447
  30.9 6.6 %copy-start.2 = (s32[2048]{0:T(1024)S(1)}, s32[2048]{0:T(1024)}, u32[]{:S(2)}) copy-start(s32[2048]{0:T(1024)} %param.10) | copy-start | bytes 24580
  30.9 6.6 %copy-start.3 = (f32[2048]{0:T(1024)S(1)}, f32[2048]{0:T(1024)}, u32[]{:S(2)}) copy-start(f32[2048]{0:T(1024)} %param.12) | copy-start | bytes 24580
  31.0 6.5 %collective-permute-start.5 = (bf16[4,256,512]{2,1,0:T(8,128)(2,1)S(1)}, bf16[4,256,512]{2,1,0:T(8,128)(2,1)S(1)}, u32[]{:S(2)}, u32[]{:S(2)}) collective-permute-start(bf16[4,256,512]{2,1,0:T(8,128)(2,1)S(1)} %pad_maximum_fusion), channel_id=1, source_target_pairs={{0,1},{1,0},{2,3},{3,2},{4,5},{5,4},{6,7},{7,6},{8,9},{9,8},{10,11... | collective-permute-start | bytes 3145736 | tf_op jit(solution)/shard_map/ppermute | solution.py:447
  47.9 11.2 %collective-permute-start.7 = (bf16[160,512]{1,0:T(8,128)(2,1)S(1)}, bf16[160,512]{1,0:T(8,128)(2,1)S(1)}, u32[]{:S(2)}, u32[]{:S(2)}) collective-permute-start(bf16[160,512]{1,0:T(8,128)(2,1)S(1)} %get-tuple-element.93), channel_id=1, source_target_pairs={{0,8},{8,0},{16,24},{24,16},{1,9},{9,1},{17,25},{25,17},{2,10},{10... | collective-permute-start | bytes 491528 | tf_op jit(solution)/shard_map/ppermute | solution.py:447
  48.9 21.8 %collective-permute-start.8 = (bf16[352,512]{1,0:T(8,128)(2,1)S(1)}, bf16[352,512]{1,0:T(8,128)(2,1)S(1)}, u32[]{:S(2)}, u32[]{:S(2)}) collective-permute-start(bf16[352,512]{1,0:T(8,128)(2,1)S(1)} %get-tuple-element.108), channel_id=1, source_target_pairs={{0,8},{8,0},{16,24},{24,16},{1,9},{9,1},{17,25},{25,17},{2,10},{10... | collective-permute-start | bytes 1081352 | tf_op jit(solution)/shard_map/ppermute | solution.py:447
  54.4 7.3 %copy-start = (bf16[512,512]{1,0:T(8,128)(2,1)S(1)}, bf16[512,512]{1,0:T(8,128)(2,1)}, u32[]{:S(2)}) copy-start(bf16[512,512]{1,0:T(8,128)(2,1)} %refs_3_.1) | copy-start | bytes 1572868
  59.1 11.6 %collective-permute-start.9 = (bf16[160,512]{1,0:T(8,128)(2,1)S(1)}, bf16[160,512]{1,0:T(8,128)(2,1)S(1)}, u32[]{:S(2)}, u32[]{:S(2)}) collective-permute-start(bf16[160,512]{1,0:T(8,128)(2,1)S(1)} %add_convert_fusion.2), channel_id=1, source_target_pairs={{0,16},{8,24},{16,0},{24,8},{1,17},{9,25},{17,1},{25,9},{2,18},{10... | collective-permute-start | bytes 491528 | tf_op jit(solution)/shard_map/ppermute | solution.py:447
  60.0 24.8 %collective-permute-start.14 = (bf16[512,512]{1,0:T(8,128)(2,1)S(1)}, bf16[512,512]{1,0:T(8,128)(2,1)S(1)}, u32[]{:S(2)}, u32[]{:S(2)}) collective-permute-start(bf16[512,512]{1,0:T(8,128)(2,1)S(1)} %get-tuple-element.118), channel_id=1, source_target_pairs={{0,8},{8,0},{16,24},{24,16},{1,9},{9,1},{17,25},{25,17},{2,10},{10... | collective-permute-start | bytes 1572872 | tf_op jit(solution)/shard_map/ppermute | solution.py:447
  70.8 17.2 %collective-permute-start.15 = (bf16[352,512]{1,0:T(8,128)(2,1)S(1)}, bf16[352,512]{1,0:T(8,128)(2,1)S(1)}, u32[]{:S(2)}, u32[]{:S(2)}) collective-permute-start(bf16[352,512]{1,0:T(8,128)(2,1)S(1)} %add_convert_fusion.1), channel_id=1, source_target_pairs={{0,16},{8,24},{16,0},{24,8},{1,17},{9,25},{17,1},{25,9},{2,18},{10... | collective-permute-start | bytes 1081352 | tf_op jit(solution)/shard_map/ppermute | solution.py:447
  75.1 4.0 %collective-permute-start.10 = (bf16[4,256,512]{2,1,0:T(8,128)(2,1)S(1)}, bf16[4,256,512]{2,1,0:T(8,128)(2,1)S(1)}, u32[]{:S(2)}, u32[]{:S(2)}) collective-permute-start(bf16[4,256,512]{2,1,0:T(8,128)(2,1)S(1)} %put_rows.3), channel_id=1, source_target_pairs={{0,1},{1,0},{2,3},{3,2},{4,5},{5,4},{6,7},{7,6},{8,9},{9,8},{10,11... | collective-permute-start | bytes 3145736 | tf_op jit(solution)/shard_map/ppermute | solution.py:447
  79.5 10.1 %collective-permute-start.11 = (bf16[256,512]{1,0:T(8,128)(2,1)S(1)}, bf16[256,512]{1,0:T(8,128)(2,1)S(1)}, u32[]{:S(2)}, u32[]{:S(2)}) collective-permute-start(bf16[256,512]{1,0:T(8,128)(2,1)S(1)} %get-tuple-element.120), channel_id=1, source_target_pairs={{0,6},{1,7},{2,4},{3,5},{4,2},{5,3},{6,0},{7,1},{8,14},{9,15},{10,... | collective-permute-start | bytes 786440 | tf_op jit(solution)/shard_map/ppermute | solution.py:447
  82.0 12.8 %collective-permute-start.12 = (bf16[256,512]{1,0:T(8,128)(2,1)S(1)}, bf16[256,512]{1,0:T(8,128)(2,1)S(1)}, u32[]{:S(2)}, u32[]{:S(2)}) collective-permute-start(bf16[256,512]{1,0:T(8,128)(2,1)S(1)} %get-tuple-element.121), channel_id=1, source_target_pairs={{0,4},{1,5},{2,6},{3,7},{4,0},{5,1},{6,2},{7,3},{8,12},{9,13},{10,... | collective-permute-start | bytes 786440 | tf_op jit(solution)/shard_map/ppermute | solution.py:447
  82.5 12.4 %collective-permute-start.13 = (bf16[256,512]{1,0:T(8,128)(2,1)S(1)}, bf16[256,512]{1,0:T(8,128)(2,1)S(1)}, u32[]{:S(2)}, u32[]{:S(2)}) collective-permute-start(bf16[256,512]{1,0:T(8,128)(2,1)S(1)} %get-tuple-element.122), channel_id=1, source_target_pairs={{0,2},{1,3},{2,0},{3,1},{4,6},{5,7},{6,4},{7,5},{8,10},{9,11},{10,... | collective-permute-start | bytes 786440 | tf_op jit(solution)/shard_map/ppermute | solution.py:447

commit v11 on v10

--- a/solution.py
+++ b/solution.py
@@ -91,7 +91,9 @@
 def fill_pick(pick, columns, base, groups):
     vocab = (lax.broadcasted_iota(jnp.int32, (LANES, pick.shape[1]), 1) + base).astype(F32)
     for group in groups:
-        pick[pl.ds(group * LANES, LANES), :] = onehot(columns[:, group : group + 1] == vocab)
+        here = pl.ds(group * LANES, LANES)
+        index = jnp.concatenate([columns[here, :]] * (pick.shape[1] // LANES), axis=1)
+        pick[here, :] = onehot(index == vocab)
 
 
 def chunk_base(scalars, offset, width):
@@ -128,7 +130,10 @@
     for copy in small:
         copy.wait()
     columns = along_sublanes((perm[...] - scalars[COL_AT] * depth).astype(F32))
-    columns_ref[...] = columns
+    for group in range(depth // LANES):
+        columns_ref[pl.ds(group * LANES, LANES), :] = jnp.broadcast_to(
+            columns[:, group : group + 1], (LANES, LANES)
+        )
     blocks_r, blocks_c = mask_ref.shape
     mask = mask_ref[...].astype(F32)
     side = (blocks_r, depth // blocks_c)
@@ -140,7 +145,7 @@
     values_ref[...] = values
     values = values.astype(BF16)
     for part, offset in enumerate(offsets):
-        fill_pick(pick.at[part], columns, chunk_base(scalars, offset, width), range(depth // LANES))
+        fill_pick(pick.at[part], columns_ref, chunk_base(scalars, offset, width), range(depth // LANES))
         move_values(values, pick.at[part], auxes[part])
     tile_copy(1).start()
 
@@ -178,7 +183,7 @@
         + [jax.ShapeDtypeStruct((blocks + 8, width), F32)] * parts
         + [
             jax.ShapeDtypeStruct((rows, cols), BF16),
-            jax.ShapeDtypeStruct((LANES, LANES), F32),
+            jax.ShapeDtypeStruct((cols, LANES), F32),
             jax.ShapeDtypeStruct((blocks + 24, cols), F32),
         ],
         scratch_shapes=[
@@ -203,7 +208,7 @@
     values = values_ref[...].astype(BF16)
     for part, offset in enumerate(offsets):
         base = chunk_base(scalars, offset, width)
-        fill_pick(pick.at[part], columns_ref[...], base, range(depth // LANES))
+        fill_pick(pick.at[part], columns_ref, base, range(depth // LANES))
         move_values(values, pick.at[part], auxes[part])
     step = 512
 

time: 96 us -> 95.5 us (level)
  transfers between devices with their start and end apart: 16 -> 16, of which waited for: 5 -> 4; matrix products, arithmetic and copies ran while one was open for 1% -> 1% of each run, Pallas kernels for 63% -> 62%
where the time goes in v11:
time: 95.5 us; the launch traced here: 95.4 us
  Pallas kernels  63.9 us (67%)
  starting transfers between devices  19.1 us (20%)
  waiting for transfers between devices  9.79 us (10%)
  other arithmetic  1.62 us (2%)
    pallas_call x4, Pallas kernels, cells(): pl.pallas_call(functools.partial(cells_kernel, len(others), pieces), in_s...  22.4 us
    ppermute x16, starting transfers between devices, swap(): return lax.ppermute(value, axis, pairs)  19.1 us
    pallas_call x2, Pallas kernels, order_next(): pl.pallas_call(functools.partial(order_next_kernel, offsets), in_specs=[S...  17.2 us
    ppermute x16, waiting for transfers between devices, swap(): return lax.ppermute(value, axis, pairs)  9.79 us
    pallas_call x1, Pallas kernels, order_first(): pl.pallas_call(functools.partial(order_first_kernel, offsets), in_specs=[...  9.09 us
    pallas_call x3, Pallas kernels, put_rows(): pl.pallas_call(functools.partial(put_kernel, offsets, exact), in_specs=[S...  8.61 us
    pallas_call x1, Pallas kernels, take_rows(): pl.pallas_call(take_kernel, in_specs=[SCALARS] + [WHOLE] * 7, out_specs=[...  5.32 us
  transfers between devices with their start and end apart: 16, of which 4 were waited for; matrix products, arithmetic and copies ran while one was open for 1% of the time, Pallas kernels for 62%

profile of v11, /device:TPU:0, one launch (start us, length us, event | category | flops | bytes accessed | tf_op | source)
XLA Modules:
  0.0 95.4 jit_solution(5460320567681150521)
XLA Ops:
  0.6 4.1 %collective-permute-start = (bf16[512,512]{1,0:T(8,128)(2,1)}, bf16[512,512]{1,0:T(8,128)(2,1)S(1)}, u32[]{:S(2)}, u32[]{:S(2)}) collective-permute-start(bf16[512,512]{1,0:T(8,128)(2,1)} %refs_3_.1), channel_id=1, source_target_pairs={{0,16},{8,24},{16,0},{24,8},{1,17},{9,25},{17,1},{25,9},{2,18},{10... | collective-permute-start | bytes 1572872 | tf_op jit(solution)/shard_map/ppermute | solution.py:452
  4.7 1.6 %collective-permute-start.1 = (bf16[512,512]{1,0:T(8,128)(2,1)}, bf16[512,512]{1,0:T(8,128)(2,1)S(1)}, u32[]{:S(2)}, u32[]{:S(2)}) collective-permute-start(bf16[512,512]{1,0:T(8,128)(2,1)} %refs_3_.1), channel_id=1, source_target_pairs={{0,8},{8,0},{16,24},{24,16},{1,9},{9,1},{17,25},{25,17},{2,10},{10... | collective-permute-start | bytes 1572872 | tf_op jit(solution)/shard_map/ppermute | solution.py:452
  6.3 0.1 pad_add_fusion.scalars
  6.4 0.0 copy-start.1
  6.4 9.1 %order_first.1 = (bf16[2048,512]{1,0:T(8,128)(2,1)S(1)}, f32[16,512]{1,0:T(8,128)S(1)}, bf16[2048,2048]{1,0:T(8,128)(2,1)S(1)}, f32[2048,128]{1,0:T(8,128)S(1)}, f32[32,2048]{1,0:T(8,128)S(1)}) custom-call(s32[2]{0:T(128)S(1)} %pad_add_fusion.scalars, s32[16,128]{1,0:T(8,128)} %bitcast.34, s32[8,8]{1,0:T(8,128)} %mask_hbm.1, f32[1,2048]{1,0:T(1,128)} %bitcast.35, ...), custom_call_target="tpu_custom_call" | custom-call | flops 4294967296 | bytes 16777216 | tf_op jit(solution)/shard_map/order_first/pallas_call | solution.py:178
  15.5 0.0 copy-done.1
  15.5 2.5 %collective-permute-start.4 = (bf16[256,512]{1,0:T(8,128)(2,1)S(1)}, bf16[256,512]{1,0:T(8,128)(2,1)S(1)}, u32[]{:S(2)}, u32[]{:S(2)}) collective-permute-start(bf16[256,512]{1,0:T(8,128)(2,1)S(1)} %copy-done.1), channel_id=1, source_target_pairs={{0,6},{1,7},{2,4},{3,5},{4,2},{5,3},{6,0},{7,1},{8,14},{9,15},{10,... | collective-permute-start | bytes 786440 | tf_op jit(solution)/shard_map/ppermute | solution.py:452
  18.0 0.5 collective-permute-start.3
  18.5 0.5 collective-permute-start.2
  19.0 10.9 %order_next.2 = (bf16[2048,512]{1,0:T(8,128)(2,1)S(1)}, bf16[2048,512]{1,0:T(8,128)(2,1)S(1)}, f32[16,512]{1,0:T(8,128)S(1)}, f32[16,512]{1,0:T(8,128)S(1)}) custom-call(s32[2]{0:T(128)S(1)} %pad_add_fusion.scalars, bf16[2048,2048]{1,0:T(8,128)(2,1)S(1)} %get-tuple-element.67.shifted_ref, f32[2048,128]{1,0:T(8,128)S(1)} %get-tuple-element.64.columns_ref, ...), custom_call_target="tpu_custom_call" | custom-call | flops 1048576 | bytes 1048576 | tf_op jit(solution)/shard_map/order_next/pallas_call | solution.py:226
  30.0 0.0 collective-permute-done.4.refs_3_
  30.0 0.0 collective-permute-done.3.refs_2_
  30.0 0.0 collective-permute-done.2.refs_1_
  30.0 0.0 collective-permute-done.refs_3_.refs_7_
  30.0 0.0 collective-permute-done.1.refs_3_.refs_8_
  30.0 0.5 collective-permute-start.6
  30.5 0.1 pad_maximum_fusion
  30.7 0.0 copy-start.2
  30.7 0.0 copy-start.3
  30.7 0.1 collective-permute-start.5
  30.8 6.3 %order_next.3 = (bf16[2048,512]{1,0:T(8,128)(2,1)S(1)}, f32[16,512]{1,0:T(8,128)S(1)}) custom-call(s32[2]{0:T(128)S(1)} %pad_add_fusion.scalars, bf16[2048,2048]{1,0:T(8,128)(2,1)S(1)} %get-tuple-element.67.shifted_ref, f32[2048,128]{1,0:T(8,128)S(1)} %get-tuple-element.64.columns_ref, f32[32,2048]{1,0:T(8,128)S(1)} %get-tuple-element.65.values_ref), custom_call_target="tpu_custom_call" | custom-call | flops 17179869184 | bytes 1048576 | tf_op jit(solution)/shard_map/order_next/pallas_call | solution.py:226
  37.0 0.0 collective-permute-done.5.refs_4_
  37.1 0.0 copy-done.2
  37.1 0.0 copy-done.3
  37.1 5.3 %take_rows.1 = (bf16[2048,512]{1,0:T(8,128)(2,1)S(1)}, bf16[512,2048]{1,0:T(8,128)(2,1)S(1)}, f32[2048,128]{1,0:T(8,128)S(1)}) custom-call(s32[2]{0:T(128)S(1)} %pad_add_fusion.scalars, s32[16,128]{1,0:T(8,128)S(1)} %bitcast.29, f32[16,128]{1,0:T(8,128)S(1)} %bitcast.33, bf16[256,512]{1,0:T(8,128)(2,1)S(1)} %copy-done.1, ...), custom_call_target="tpu_custom_call" | custom-call | flops 4294967296 | bytes 4194304 | tf_op jit(solution)/shard_map/take_rows/pallas_call | solution.py:270
  42.4 1.1 %collective-permute-done.6.refs_3_.refs_6_ = bf16[512,512]{1,0:T(8,128)(2,1)S(1)} collective-permute-done((bf16[512,512]{1,0:T(8,128)(2,1)S(1)}, bf16[512,512]{1,0:T(8,128)(2,1)S(1)}, u32[]{:S(2)}, u32[]{:S(2)}) %collective-permute-start.6) | collective-permute-done | bytes 524320 | tf_op jit(solution)/shard_map/ppermute | solution.py:452
  43.5 4.4 %cells.4 = (bf16[2048,512]{1,0:T(8,128)(2,1)S(1)}, bf16[160,512]{1,0:T(8,128)(2,1)S(1)}, bf16[352,512]{1,0:T(8,128)(2,1)S(1)}) custom-call(bf16[2048,512]{1,0:T(8,128)(2,1)S(1)} %get-tuple-element.99.refs_0_, bf16[512,2048]{1,0:T(8,128)(2,1)S(1)} %get-tuple-element.100.refs_1_, f32[2048,128]{1,0:T(8,128)S(1)} %get-tuple-element.101.refs_2_, ...), custom_call_target="tpu_custom_call" | custom-call | flops 1048576 | bytes 1048576 | tf_op jit(solution)/shard_map/cells/pallas_call | solution.py:381
  47.9 0.6 collective-permute-start.7
  48.5 1.5 %collective-permute-start.8 = (bf16[352,512]{1,0:T(8,128)(2,1)S(1)}, bf16[352,512]{1,0:T(8,128)(2,1)S(1)}, u32[]{:S(2)}, u32[]{:S(2)}) collective-permute-start(bf16[352,512]{1,0:T(8,128)(2,1)S(1)} %get-tuple-element.108), channel_id=1, source_target_pairs={{0,8},{8,0},{16,24},{24,16},{1,9},{9,1},{17,25},{25,17},{2,10},{10... | collective-permute-start | bytes 1081352 | tf_op jit(solution)/shard_map/ppermute | solution.py:452
  50.0 4.4 %cells.5 = (bf16[2048,512]{1,0:T(8,128)(2,1)S(1)}, f32[512,512]{1,0:T(8,128)S(1)}) custom-call(bf16[2048,512]{1,0:T(8,128)(2,1)S(1)} %get-tuple-element.99.refs_0_, bf16[512,2048]{1,0:T(8,128)(2,1)S(1)} %get-tuple-element.100.refs_1_, f32[2048,128]{1,0:T(8,128)S(1)} %get-tuple-element.101.refs_2_, bf16[512,512]{1,0:T(8,128)(2,1)S(1)} %collective-permute-done.refs_3_.refs_7_, ...), custom_call_target="tpu_custom_call" | custom-call | flops 1048576 | bytes 1048576 | tf_op jit(solution)/shard_map/cells/pallas_call | solution.py:381
  54.4 0.0 copy-start
  54.4 4.6 %cells.6 = (bf16[2048,512]{1,0:T(8,128)(2,1)S(1)}, bf16[512,512]{1,0:T(8,128)(2,1)S(1)}) custom-call(bf16[2048,512]{1,0:T(8,128)(2,1)S(1)} %get-tuple-element.99.refs_0_, bf16[512,2048]{1,0:T(8,128)(2,1)S(1)} %get-tuple-element.100.refs_1_, f32[2048,128]{1,0:T(8,128)S(1)} %get-tuple-element.101.refs_2_, ...), custom_call_target="tpu_custom_call" | custom-call | flops 1048576 | bytes 1048576 | tf_op jit(solution)/shard_map/cells/pallas_call | solution.py:381
  59.1 0.0 collective-permute-done.7
  59.1 0.9 collective-permute-start.9
  60.0 1.7 %collective-permute-start.14 = (bf16[512,512]{1,0:T(8,128)(2,1)S(1)}, bf16[512,512]{1,0:T(8,128)(2,1)S(1)}, u32[]{:S(2)}, u32[]{:S(2)}) collective-permute-start(bf16[512,512]{1,0:T(8,128)(2,1)S(1)} %get-tuple-element.118), channel_id=1, source_target_pairs={{0,8},{8,0},{16,24},{24,16},{1,9},{9,1},{17,25},{25,17},{2,10},{10... | collective-permute-start | bytes 1572872 | tf_op jit(solution)/shard_map/ppermute | solution.py:452
  61.8 0.0 copy-done
  61.8 8.9 %cells.7 = (f32[2048,512]{1,0:T(8,128)S(1)}, f32[512,512]{1,0:T(8,128)S(1)}) custom-call(bf16[2048,512]{1,0:T(8,128)(2,1)S(1)} %get-tuple-element.99.refs_0_, bf16[512,2048]{1,0:T(8,128)(2,1)S(1)} %get-tuple-element.100.refs_1_, f32[2048,128]{1,0:T(8,128)S(1)} %get-tuple-element.101.refs_2_, bf16[512,512]{1,0:T(8,128)(2,1)S(1)} %copy-done, ...), custom_call_target="tpu_custom_call" | custom-call | flops 1048576 | bytes 1048576 | tf_op jit(solution)/shard_map/cells/pallas_call | solution.py:381
  70.7 0.0 collective-permute-done.9.refs_2_
  70.7 0.0 collective-permute-done.8
  70.7 0.1 add_convert_fusion.1
  70.8 0.9 collective-permute-start.15
  71.7 2.9 %put_rows.3 = bf16[4,256,512]{2,1,0:T(8,128)(2,1)S(1)} custom-call(s32[2]{0:T(128)S(1)} %pad_add_fusion.scalars, s32[1,2048]{1,0:T(1,128)S(1)} %bitcast.30, f32[2048,512]{1,0:T(8,128)S(1)} %get-tuple-element.114.grad_ref), custom_call_target="tpu_custom_call" | custom-call | flops 1048576 | bytes 65536 | tf_op jit(solution)/shard_map/put_rows/pallas_call | solution.py:438
  74.6 0.1 collective-permute-start.10
  74.7 3.9 %put_rows.4 = f32[3,256,512]{2,1,0:T(8,128)S(1)} custom-call(s32[2]{0:T(128)S(1)} %pad_add_fusion.scalars, s32[1,2048]{1,0:T(1,128)S(1)} %bitcast.31, f32[2048,512]{1,0:T(8,128)S(1)} %get-tuple-element.114.grad_ref), custom_call_target="tpu_custom_call" | custom-call | flops 17179869184 | bytes 65536 | tf_op jit(solution)/shard_map/put_rows/pallas_call | solution.py:438
  78.6 0.0 collective-permute-done.10
  78.7 0.3 add_convert_fusion
  78.9 0.1 slice_bitcast_fusion
  79.0 2.5 %collective-permute-start.11 = (bf16[256,512]{1,0:T(8,128)(2,1)S(1)}, bf16[256,512]{1,0:T(8,128)(2,1)S(1)}, u32[]{:S(2)}, u32[]{:S(2)}) collective-permute-start(bf16[256,512]{1,0:T(8,128)(2,1)S(1)} %get-tuple-element.120), channel_id=1, source_target_pairs={{0,6},{1,7},{2,4},{3,5},{4,2},{5,3},{6,0},{7,1},{8,14},{9,15},{10,... | collective-permute-start | bytes 786440 | tf_op jit(solution)/shard_map/ppermute | solution.py:452
  81.5 0.5 collective-permute-start.12
  82.0 0.5 collective-permute-start.13
  82.6 1.8 %put_rows.5 = f32[1,256,512]{2,1,0:T(8,128)S(1)} custom-call(s32[2]{0:T(128)S(1)} %pad_add_fusion.scalars, s32[1,2048]{1,0:T(1,128)S(1)} %bitcast.32, f32[2048,512]{1,0:T(8,128)S(1)} %get-tuple-element.114.grad_ref), custom_call_target="tpu_custom_call" | custom-call | flops 1048576 | bytes 65536 | tf_op jit(solution)/shard_map/put_rows/pallas_call | solution.py:438
  84.4 0.0 collective-permute-done.14.refs_1_
  84.4 3.6 %collective-permute-done.15.refs_3_ = bf16[352,512]{1,0:T(8,128)(2,1)S(1)} collective-permute-done((bf16[352,512]{1,0:T(8,128)(2,1)S(1)}, bf16[352,512]{1,0:T(8,128)(2,1)S(1)}, u32[]{:S(2)}, u32[]{:S(2)}) %collective-permute-start.15) | collective-permute-done | bytes 360480 | tf_op jit(solution)/shard_map/ppermute | solution.py:452
  87.9 1.3 %finish.1 = f32[512,512]{1,0:T(8,128)} custom-call(f32[512,512]{1,0:T(8,128)S(1)} %get-tuple-element.117.refs_0_, bf16[512,512]{1,0:T(8,128)(2,1)S(1)} %collective-permute-done.14.refs_1_, bf16[160,512]{1,0:T(8,128)(2,1)S(1)} %collective-permute-done.9.refs_2_, bf16[352,512]{1,0:T(8,128)(2,1)S(1)} %collective-permute-done.15.refs_3_), custom_call_target="tpu_custom_call" | custom-call | flops 262144 | bytes 16384 | tf_op jit(solution)/shard_map/finish/pallas_call | solution.py:405
  89.2 0.0 collective-permute-done.11
  89.2 5.1 %collective-permute-done.12 = bf16[256,512]{1,0:T(8,128)(2,1)S(1)} collective-permute-done((bf16[256,512]{1,0:T(8,128)(2,1)S(1)}, bf16[256,512]{1,0:T(8,128)(2,1)S(1)}, u32[]{:S(2)}, u32[]{:S(2)}) %collective-permute-start.12) | collective-permute-done | bytes 262176 | tf_op jit(solution)/shard_map/ppermute | solution.py:452
  94.3 0.1 collective-permute-done.13
  94.4 1.0 %fusion.2 = f32[256,512]{1,0:T(8,128)} fusion(bf16[256,512]{1,0:T(8,128)(2,1)S(1)} %collective-permute-done.13, bf16[256,512]{1,0:T(8,128)(2,1)S(1)} %collective-permute-done.12, bf16[256,512]{1,0:T(8,128)(2,1)S(1)} %collective-permute-done.11, f32[1,256,512]{2,1,0:T(8,128)S(1)} %put_rows.5, bf16[4,256,512]{2,1,0:T(8,128)(2,1)S(1)} %collective-permute-done.10), kind=kLoop, calls=%fused_computation.6 | loop fusion | flops 1179648 | bytes 2097152 | tf_op jit(solution)/shard_map/mul | solution.py:526
  (1 shorter events, 0.0 us)
Async XLA Ops:
  0.6 29.4 %collective-permute-start = (bf16[512,512]{1,0:T(8,128)(2,1)}, bf16[512,512]{1,0:T(8,128)(2,1)S(1)}, u32[]{:S(2)}, u32[]{:S(2)}) collective-permute-start(bf16[512,512]{1,0:T(8,128)(2,1)} %refs_3_.1), channel_id=1, source_target_pairs={{0,16},{8,24},{16,0},{24,8},{1,17},{9,25},{17,1},{25,9},{2,18},{10... | collective-permute-start | bytes 1572872 | tf_op jit(solution)/shard_map/ppermute | solution.py:452
  4.7 25.3 %collective-permute-start.1 = (bf16[512,512]{1,0:T(8,128)(2,1)}, bf16[512,512]{1,0:T(8,128)(2,1)S(1)}, u32[]{:S(2)}, u32[]{:S(2)}) collective-permute-start(bf16[512,512]{1,0:T(8,128)(2,1)} %refs_3_.1), channel_id=1, source_target_pairs={{0,8},{8,0},{16,24},{24,16},{1,9},{9,1},{17,25},{25,17},{2,10},{10... | collective-permute-start | bytes 1572872 | tf_op jit(solution)/shard_map/ppermute | solution.py:452
  6.4 9.1 %copy-start.1 = (bf16[256,512]{1,0:T(8,128)(2,1)S(1)}, bf16[256,512]{1,0:T(8,128)(2,1)}, u32[]{:S(2)}) copy-start(bf16[256,512]{1,0:T(8,128)(2,1)} %refs_0_.1) | copy-start | bytes 786436
  15.5 14.5 %collective-permute-start.4 = (bf16[256,512]{1,0:T(8,128)(2,1)S(1)}, bf16[256,512]{1,0:T(8,128)(2,1)S(1)}, u32[]{:S(2)}, u32[]{:S(2)}) collective-permute-start(bf16[256,512]{1,0:T(8,128)(2,1)S(1)} %copy-done.1), channel_id=1, source_target_pairs={{0,6},{1,7},{2,4},{3,5},{4,2},{5,3},{6,0},{7,1},{8,14},{9,15},{10,... | collective-permute-start | bytes 786440 | tf_op jit(solution)/shard_map/ppermute | solution.py:452
  18.0 12.0 %collective-permute-start.3 = (bf16[256,512]{1,0:T(8,128)(2,1)S(1)}, bf16[256,512]{1,0:T(8,128)(2,1)S(1)}, u32[]{:S(2)}, u32[]{:S(2)}) collective-permute-start(bf16[256,512]{1,0:T(8,128)(2,1)S(1)} %copy-done.1), channel_id=1, source_target_pairs={{0,4},{1,5},{2,6},{3,7},{4,0},{5,1},{6,2},{7,3},{8,12},{9,13},{10,... | collective-permute-start | bytes 786440 | tf_op jit(solution)/shard_map/ppermute | solution.py:452
  18.5 11.5 %collective-permute-start.2 = (bf16[256,512]{1,0:T(8,128)(2,1)S(1)}, bf16[256,512]{1,0:T(8,128)(2,1)S(1)}, u32[]{:S(2)}, u32[]{:S(2)}) collective-permute-start(bf16[256,512]{1,0:T(8,128)(2,1)S(1)} %copy-done.1), channel_id=1, source_target_pairs={{0,2},{1,3},{2,0},{3,1},{4,6},{5,7},{6,4},{7,5},{8,10},{9,11},{10,... | collective-permute-start | bytes 786440 | tf_op jit(solution)/shard_map/ppermute | solution.py:452
  30.0 13.5 %collective-permute-start.6 = (bf16[512,512]{1,0:T(8,128)(2,1)S(1)}, bf16[512,512]{1,0:T(8,128)(2,1)S(1)}, u32[]{:S(2)}, u32[]{:S(2)}) collective-permute-start(bf16[512,512]{1,0:T(8,128)(2,1)S(1)} %collective-permute-done.refs_3_.refs_7_), channel_id=1, source_target_pairs={{0,8},{8,0},{16,24},{24,16},{1,9},{9,1},{17,25},{25,17},{2,10},{10... | collective-permute-start | bytes 1572872 | tf_op jit(solution)/shard_map/ppermute | solution.py:452
  30.7 6.4 %copy-start.2 = (s32[2048]{0:T(1024)S(1)}, s32[2048]{0:T(1024)}, u32[]{:S(2)}) copy-start(s32[2048]{0:T(1024)} %param.10) | copy-start | bytes 24580
  30.7 6.4 %copy-start.3 = (f32[2048]{0:T(1024)S(1)}, f32[2048]{0:T(1024)}, u32[]{:S(2)}) copy-start(f32[2048]{0:T(1024)} %param.12) | copy-start | bytes 24580
  30.7 6.4 %collective-permute-start.5 = (bf16[4,256,512]{2,1,0:T(8,128)(2,1)S(1)}, bf16[4,256,512]{2,1,0:T(8,128)(2,1)S(1)}, u32[]{:S(2)}, u32[]{:S(2)}) collective-permute-start(bf16[4,256,512]{2,1,0:T(8,128)(2,1)S(1)} %pad_maximum_fusion), channel_id=1, source_target_pairs={{0,1},{1,0},{2,3},{3,2},{4,5},{5,4},{6,7},{7,6},{8,9},{9,8},{10,11... | collective-permute-start | bytes 3145736 | tf_op jit(solution)/shard_map/ppermute | solution.py:452
  47.9 11.1 %collective-permute-start.7 = (bf16[160,512]{1,0:T(8,128)(2,1)S(1)}, bf16[160,512]{1,0:T(8,128)(2,1)S(1)}, u32[]{:S(2)}, u32[]{:S(2)}) collective-permute-start(bf16[160,512]{1,0:T(8,128)(2,1)S(1)} %get-tuple-element.93), channel_id=1, source_target_pairs={{0,8},{8,0},{16,24},{24,16},{1,9},{9,1},{17,25},{25,17},{2,10},{10... | collective-permute-start | bytes 491528 | tf_op jit(solution)/shard_map/ppermute | solution.py:452
  48.5 22.2 %collective-permute-start.8 = (bf16[352,512]{1,0:T(8,128)(2,1)S(1)}, bf16[352,512]{1,0:T(8,128)(2,1)S(1)}, u32[]{:S(2)}, u32[]{:S(2)}) collective-permute-start(bf16[352,512]{1,0:T(8,128)(2,1)S(1)} %get-tuple-element.108), channel_id=1, source_target_pairs={{0,8},{8,0},{16,24},{24,16},{1,9},{9,1},{17,25},{25,17},{2,10},{10... | collective-permute-start | bytes 1081352 | tf_op jit(solution)/shard_map/ppermute | solution.py:452
  54.4 7.3 %copy-start = (bf16[512,512]{1,0:T(8,128)(2,1)S(1)}, bf16[512,512]{1,0:T(8,128)(2,1)}, u32[]{:S(2)}) copy-start(bf16[512,512]{1,0:T(8,128)(2,1)} %refs_3_.1) | copy-start | bytes 1572868
  59.1 11.5 %collective-permute-start.9 = (bf16[160,512]{1,0:T(8,128)(2,1)S(1)}, bf16[160,512]{1,0:T(8,128)(2,1)S(1)}, u32[]{:S(2)}, u32[]{:S(2)}) collective-permute-start(bf16[160,512]{1,0:T(8,128)(2,1)S(1)} %add_convert_fusion.2), channel_id=1, source_target_pairs={{0,16},{8,24},{16,0},{24,8},{1,17},{9,25},{17,1},{25,9},{2,18},{10... | collective-permute-start | bytes 491528 | tf_op jit(solution)/shard_map/ppermute | solution.py:452
  60.0 24.3 %collective-permute-start.14 = (bf16[512,512]{1,0:T(8,128)(2,1)S(1)}, bf16[512,512]{1,0:T(8,128)(2,1)S(1)}, u32[]{:S(2)}, u32[]{:S(2)}) collective-permute-start(bf16[512,512]{1,0:T(8,128)(2,1)S(1)} %get-tuple-element.118), channel_id=1, source_target_pairs={{0,8},{8,0},{16,24},{24,16},{1,9},{9,1},{17,25},{25,17},{2,10},{10... | collective-permute-start | bytes 1572872 | tf_op jit(solution)/shard_map/ppermute | solution.py:452
  70.8 17.1 %collective-permute-start.15 = (bf16[352,512]{1,0:T(8,128)(2,1)S(1)}, bf16[352,512]{1,0:T(8,128)(2,1)S(1)}, u32[]{:S(2)}, u32[]{:S(2)}) collective-permute-start(bf16[352,512]{1,0:T(8,128)(2,1)S(1)} %add_convert_fusion.1), channel_id=1, source_target_pairs={{0,16},{8,24},{16,0},{24,8},{1,17},{9,25},{17,1},{25,9},{2,18},{10... | collective-permute-start | bytes 1081352 | tf_op jit(solution)/shard_map/ppermute | solution.py:452
  74.6 4.0 %collective-permute-start.10 = (bf16[4,256,512]{2,1,0:T(8,128)(2,1)S(1)}, bf16[4,256,512]{2,1,0:T(8,128)(2,1)S(1)}, u32[]{:S(2)}, u32[]{:S(2)}) collective-permute-start(bf16[4,256,512]{2,1,0:T(8,128)(2,1)S(1)} %put_rows.3), channel_id=1, source_target_pairs={{0,1},{1,0},{2,3},{3,2},{4,5},{5,4},{6,7},{7,6},{8,9},{9,8},{10,11... | collective-permute-start | bytes 3145736 | tf_op jit(solution)/shard_map/ppermute | solution.py:452
  79.0 10.2 %collective-permute-start.11 = (bf16[256,512]{1,0:T(8,128)(2,1)S(1)}, bf16[256,512]{1,0:T(8,128)(2,1)S(1)}, u32[]{:S(2)}, u32[]{:S(2)}) collective-permute-start(bf16[256,512]{1,0:T(8,128)(2,1)S(1)} %get-tuple-element.120), channel_id=1, source_target_pairs={{0,6},{1,7},{2,4},{3,5},{4,2},{5,3},{6,0},{7,1},{8,14},{9,15},{10,... | collective-permute-start | bytes 786440 | tf_op jit(solution)/shard_map/ppermute | solution.py:452
  81.5 12.8 %collective-permute-start.12 = (bf16[256,512]{1,0:T(8,128)(2,1)S(1)}, bf16[256,512]{1,0:T(8,128)(2,1)S(1)}, u32[]{:S(2)}, u32[]{:S(2)}) collective-permute-start(bf16[256,512]{1,0:T(8,128)(2,1)S(1)} %get-tuple-element.121), channel_id=1, source_target_pairs={{0,4},{1,5},{2,6},{3,7},{4,0},{5,1},{6,2},{7,3},{8,12},{9,13},{10,... | collective-permute-start | bytes 786440 | tf_op jit(solution)/shard_map/ppermute | solution.py:452
  82.0 12.3 %collective-permute-start.13 = (bf16[256,512]{1,0:T(8,128)(2,1)S(1)}, bf16[256,512]{1,0:T(8,128)(2,1)S(1)}, u32[]{:S(2)}, u32[]{:S(2)}) collective-permute-start(bf16[256,512]{1,0:T(8,128)(2,1)S(1)} %get-tuple-element.122), channel_id=1, source_target_pairs={{0,2},{1,3},{2,0},{3,1},{4,6},{5,7},{6,4},{7,5},{8,10},{9,11},{10,... | collective-permute-start | bytes 786440 | tf_op jit(solution)/shard_map/ppermute | solution.py:452
